TPU v7x, 128 devices: a whole 4x4x4 slice. The times are simulated.
128 devices in a mesh: enc: 4 (over y), clu: 32 (over x, z, core).
Axes of the slice: x: 4, y: 4, z: 4, core: 2. Of those that a mesh axis runs over, the one named last changes fastest.
Arguments:
- states: bfloat16 [1024, 32, 1024], P(('enc', 'clu')), may hold values from -6 to 6
- lengths: int32 [1024], P(('enc', 'clu')), may hold values from 8 to 32
- w_in: bfloat16 [1024, 2048], P('clu'), may hold values from -0.1875 to 0.1875
- w_out: bfloat16 [2048, 1024], P('clu'), may hold values from -0.125 to 0.125
- norm_gain: float32 [1024], replicated, may hold values from 0.5 to 1.5
- label_tiles: float32 [8192, 1024], P('clu'), may hold values from -0.6 to 0.6
- tile_mean: float32 [8192, 1024], P('clu'), may hold values from -0.06 to 0.06
- tile_var: float32 [8192, 1024], P('clu'), may hold values from 1e-05 to 0.001
- shortlist: int32 [1024, 400], P('enc'), may hold values from 0 to 2047, as said below
- positives: int32 [1024, 4], P('enc'), may hold values from 0 to 8191, as said below
- owner_map: int32 [2048], replicated, may hold values from 0 to 2047, each once
Outputs:
- loss: float32 [1024], P(('enc', 'clu'))
- new_tiles: float32 [8192, 1024], P('clu')
- new_mean: float32 [8192, 1024], P('clu')
- new_var: float32 [8192, 1024], P('clu')
- grad_in: float32 [1024, 2048], P('clu')
- grad_out: float32 [2048, 1024], P('clu')
Inputs may be any that keep to these rules, and one draw needn't show every extreme that they name: `shortlist`: each row names 400 different clusters; some clusters are named by many more rows than others. `positives`: each row names 4 different labels, each in a cluster named in the same row of shortlist.
All inputs are finite; a program needn't handle non-finite values.
Results may differ from a plain program's by a relative error of at most 0.0045.
Values may be sent and summed in bfloat16 or wider, within the bound.
No kernel may reach another device: no remote copies, remote signals or barrier semaphores. Data moves between devices by JAX's collectives and lax.ppermute only.
A program may use at most 128 MiB of HBM per device.

v0:
```python
import jax
import jax.numpy as jnp
from jax import lax
from jax.sharding import PartitionSpec as P

LPC = 4
POS = 4


NORM_EPS = 1e-05
INV_ROOT_TWO = 0.7071067811865476
INV_ROOT_TWO_PI = 0.3989422804014327
CORR_ONE = 1.000026562104397
CORR_TWO = 10.50333528


def encode_block(block_states, w_in, w_out, norm_gain, doc_lengths):
    doc_count = block_states.shape[0]
    token_rows = block_states.reshape(-1, block_states.shape[2])
    pre_act = jnp.dot(token_rows, w_in, preferred_element_type=jnp.float32)
    normal_cdf = 0.5 * (1.0 + lax.erf(pre_act * INV_ROOT_TWO))
    hidden = (pre_act * normal_cdf).astype(jnp.bfloat16)
    summed = token_rows.astype(jnp.float32) + jnp.dot(
        hidden, w_out, preferred_element_type=jnp.float32
    )
    row_mean = jnp.mean(summed, axis=-1, keepdims=True)
    centred = summed - row_mean
    inv_scale = lax.rsqrt(jnp.mean(centred * centred, axis=-1, keepdims=True) + NORM_EPS)
    normed = centred * inv_scale
    block_out = normed * norm_gain
    positions = jnp.arange(block_states.shape[1], dtype=jnp.int32)
    live_mask = (positions[None, :] < doc_lengths[:, None]).astype(jnp.float32)
    live_share = live_mask / doc_lengths[:, None].astype(jnp.float32)
    pooled = jnp.sum(
        block_out.reshape(doc_count, block_states.shape[1], -1) * live_share[:, :, None], axis=1
    )
    embedded_tokens = pooled.astype(jnp.bfloat16)
    return (pre_act, normal_cdf, hidden, normed, inv_scale, live_share, embedded_tokens)


def backward_block(block_states, parts, emb_grad, w_out, norm_gain):
    pre_act, normal_cdf, hidden, normed, inv_scale, live_share, embedded_tokens = parts
    token_rows = block_states.reshape(-1, block_states.shape[2])
    pooled_grad = (emb_grad[:, None, :] * live_share[:, :, None]).reshape(token_rows.shape[0], -1)
    scaled = pooled_grad * norm_gain
    sum_grad = (
        scaled
        - jnp.mean(scaled, axis=-1, keepdims=True)
        - normed * jnp.mean(scaled * normed, axis=-1, keepdims=True)
    ) * inv_scale
    sum_grad = sum_grad.astype(jnp.bfloat16)
    grad_out = jnp.dot(hidden.T, sum_grad, preferred_element_type=jnp.float32)
    back_hidden = lax.dot_general(
        sum_grad, w_out, (((1,), (1,)), ((), ())), preferred_element_type=jnp.float32
    )
    slope = normal_cdf + pre_act * jnp.exp(-0.5 * pre_act * pre_act) * INV_ROOT_TWO_PI
    act_grad = (back_hidden * slope).astype(jnp.bfloat16)
    grad_in = jnp.dot(token_rows.T, act_grad, preferred_element_type=jnp.float32)
    return (grad_in, grad_out)


def on_device(
    states,
    lengths,
    w_in,
    w_out,
    norm_gain,
    label_tiles,
    tile_mean,
    tile_var,
    shortlist,
    positives,
    owner_map,
):
    in_full, out_full = (
        lax.all_gather(w_in, "clu", axis=0, tiled=True),
        lax.all_gather(w_out, "clu", axis=0, tiled=True),
    )
    parts = encode_block(states, in_full, out_full, norm_gain, lengths)
    embedded_tokens = parts[6]
    group_emb = lax.all_gather(embedded_tokens, "clu", axis=0, tiled=True)
    doc_vectors = group_emb.astype(jnp.float32)
    label_rows = label_tiles.shape[0]
    local_clusters = label_rows // LPC
    group_docs = doc_vectors.shape[0]
    first_slot = lax.axis_index("clu") * local_clusters
    scores = jnp.dot(doc_vectors, label_tiles.T, precision=lax.Precision.HIGHEST)
    slot_numbers = first_slot + jnp.arange(local_clusters, dtype=jnp.int32)
    all_clusters = jnp.arange(owner_map.shape[0], dtype=jnp.int32)
    owner_match = owner_map[:, None] == slot_numbers[None, :]
    cluster_ids = jnp.sum(jnp.where(owner_match, all_clusters[:, None], 0), axis=0)
    cluster_live = jnp.max(
        (shortlist[:, :, None] == cluster_ids[None, None, :]).astype(jnp.float32), axis=1
    )
    live = jnp.repeat(cluster_live, LPC, axis=1)
    weighted = live * jnp.exp(scores)
    pos_cluster = positives // LPC
    pos_offset = positives % LPC
    cluster_hit = (pos_cluster[:, :, None] == cluster_ids[None, None, :]).astype(jnp.float32)
    offset_hit = (pos_offset[:, :, None] == jnp.arange(LPC, dtype=jnp.int32)[None, None, :]).astype(
        jnp.float32
    )
    hits = jnp.sum(cluster_hit[:, :, :, None] * offset_hit[:, :, None, :], axis=1).reshape(
        group_docs, label_rows
    )
    picked = jnp.sum(hits * scores, axis=1)
    expsum, possum = lax.psum((jnp.sum(weighted, axis=1), picked), "clu")
    logit_grad = weighted / expsum[:, None] - hits / POS
    own_docs = states.shape[0]
    all_loss = jnp.log(expsum) - possum / POS
    loss = lax.dynamic_slice_in_dim(all_loss, lax.axis_index("clu") * own_docs, own_docs, 0)
    emb_grad = lax.psum_scatter(
        jnp.dot(logit_grad, label_tiles, precision=lax.Precision.HIGHEST),
        "clu",
        scatter_dimension=0,
        tiled=True,
    )
    local_tile_grad = jnp.dot(logit_grad.T, doc_vectors, precision=lax.Precision.HIGHEST)
    panel_derivative = lax.psum(local_tile_grad, "enc")
    new_mean = 0.9 * tile_mean + 0.1 * panel_derivative
    new_var = 0.999 * tile_var + 0.001 * panel_derivative * panel_derivative
    new_tiles = label_tiles - 0.001 * (new_mean * CORR_ONE) / (jnp.sqrt(new_var * CORR_TWO) + 1e-08)
    full_in, full_out = backward_block(states, parts, emb_grad, out_full, norm_gain)
    share_in, share_out = (
        lax.psum_scatter(full_in, "clu", scatter_dimension=0, tiled=True),
        lax.psum_scatter(full_out, "clu", scatter_dimension=0, tiled=True),
    )
    grad_in, grad_out = lax.psum((share_in, share_out), "enc")
    return (loss, new_tiles, new_mean, new_var, grad_in, grad_out)


def solution(mesh):
    return jax.shard_map(
        on_device,
        mesh=mesh,
        in_specs=(
            P(("enc", "clu"), None, None),
            P(("enc", "clu")),
            P("clu", None),
            P("clu", None),
            P(),
            P("clu", None),
            P("clu", None),
            P("clu", None),
            P("enc", None),
            P("enc", None),
            P(),
        ),
        out_specs=(
            P(("enc", "clu")),
            P("clu", None),
            P("clu", None),
            P("clu", None),
            P("clu", None),
            P("clu", None),
        ),
        check_vma=False,
    )
```

profile of v0, /device:TPU:1, one launch (start us, length us, event | category | flops | bytes accessed | tf_op | source)
XLA Modules:
  0.0 570.0 jit_solution(17074042185189650091)
XLA Ops:
  11.5 3.7 convert_reduce_fusion
  16.1 44.2 %all-gather.3.cloned.1.call-done = bf16[1024,2048]{1,0:T(8,128)(2,1)} async-done(((bf16[32,2048]{1,0:T(8,128)(2,1)}), bf16[1024,2048]{1,0:T(8,128)(2,1)}) %all-gather.3.cloned.1.call-update) | async-done | bytes 4194320 | tf_op jit(solution)/shard_map/all_gather | solution.py:76
  60.3 3.4 fusion.24
  63.8 44.5 %all-gather.5.cloned.1.call-done = bf16[2048,1024]{1,0:T(8,128)(2,1)} async-done(((bf16[64,1024]{1,0:T(8,128)(2,1)}), bf16[2048,1024]{1,0:T(8,128)(2,1)}) %all-gather.5.cloned.1.call-update) | async-done | bytes 4194320 | tf_op jit(solution)/shard_map/all_gather | solution.py:77
  108.3 3.6 fusion.23
  112.6 24.2 %all_gather.11 = bf16[256,1024]{1,0:T(8,128)(2,1)S(1)} all-gather(bf16[8,1024]{1,0:T(8,128)(2,1)S(1)} %multiply_reduce_fusion.2), channel_id=1, replica_groups=mesh['enc'=4,'clu'=32] {'clu'}, dimensions={0}, use_global_device_ids=true | all-gather | bytes 540672 | tf_op jit(solution)/shard_map/all_gather | solution.py:81
  136.9 1.4 fusion.16
  138.2 62.2 %all-reduce = (f32[256]{0:T(256)S(1)}, f32[256]{0:T(256)S(1)}) all-reduce(f32[256]{0:T(256)S(1)} %get-tuple-element.25, f32[256]{0:T(256)S(1)} %get-tuple-element.24), channel_id=1, replica_groups=mesh['enc'=4,'clu'=32] {'clu'}, use_global_device_ids=true, to_apply=%region_9.10 | all-reduce | flops 512 | bytes 4096 | tf_op jit(solution)/shard_map/psum | solution.py:107
  200.4 1.2 multiply_subtract_fusion
  201.6 3.2 fusion.26
  205.1 74.8 %reduce-scatter.6.cloned.1.call-done = f32[8,1024]{1,0:T(8,128)} async-done(((f32[256,1024]{1,0:T(8,128)}), f32[8,1024]{1,0:T(8,128)}) %reduce-scatter.6.cloned.1.call-update) | async-done | bytes 32784 | tf_op jit(solution)/shard_map/reduce_scatter | solution.py:112
  279.9 1.1 fusion.12
  281.0 1.0 multiply_reduce_fusion
  282.1 1.9 fusion.11
  284.1 8.4 %convolution_bitcast_fusion = f32[1024,2048]{0,1:T(8,128)} fusion(bf16[256,1024]{1,0:T(8,128)(2,1)} %bitcast.40, bf16[256,1024]{1,0:T(8,128)(2,1)} %fusion.11, bf16[2048,1024]{1,0:T(8,128)(2,1)} %all-gather.5.cloned.1.call-done, f32[256,2048]{1,0:T(8,128)S(1)} %fusion.24), kind=kOutput, calls=%fused_computation.1 | convolution fusion | flops 2152726528 | bytes 15728640 | tf_op jit(solution)/shard_map/dot_general | solution.py:58
  292.5 9.1 %copy.27 = f32[1024,2048]{1,0:T(8,128)} copy(f32[1024,2048]{0,1:T(8,128)} %convolution_bitcast_fusion) | data formatting | bytes 16777216
  302.7 4.5 fusion.21
  308.2 1.5 fusion.25
  309.8 84.0 %reduce-scatter.10.cloned.1.call-done = f32[32,2048]{1,0:T(8,128)} async-done(((f32[1024,2048]{1,0:T(8,128)}), f32[32,2048]{1,0:T(8,128)}) %reduce-scatter.10.cloned.1.call-update) | async-done | bytes 262160
  393.8 2.3 copy.28
  396.1 93.4 %reduce-scatter.8.cloned.1.call-done = f32[64,1024]{1,0:T(8,128)} async-done(((f32[2048,1024]{1,0:T(8,128)}), f32[64,1024]{1,0:T(8,128)}) %reduce-scatter.8.cloned.1.call-update) | async-done | bytes 262160 | tf_op jit(solution)/shard_map/reduce_scatter | solution.py:126
  490.1 66.8 %all-reduce.4.cloned.1.call-done = (f32[256,1024]{1,0:T(8,128)}, f32[32,2048]{0,1:T(8,128)}, f32[64,1024]{1,0:T(8,128)}) async-done(((f32[256,1024]{1,0:T(8,128)}, f32[32,2048]{0,1:T(8,128)}, f32[64,1024]{1,0:T(8,128)}), (f32[256,1024]{1,0:T(8,128)}, f32[32,2048]{0,1:T(8,128)}, f32[64,1024]{1,0:T(8,128)})) %all-reduce.4.cloned.1.call-update) | async-done | bytes 1572880 | tf_op jit(solution)/shard_map/psum | solution.py:119
  556.9 2.2 copy.26
  559.1 3.4 divide_subtract_fusion
  (63 shorter events, 9.6 us)
Async XLA Ops:
  7.2 8.9 %copy-start.13 = (s32[8]{0:T(128)S(1)}, s32[8]{0:T(128)}, u32[]{:S(2)}) copy-start(s32[8]{0:T(128)} %param.12) | copy-start | bytes 100
  7.2 4.3 copy-start.10
  7.2 53.2 %copy-start.9 = (bf16[8,32,1024]{2,1,0:T(8,128)(2,1)S(1)}, bf16[8,32,1024]{2,1,0:T(8,128)(2,1)}, u32[]{:S(2)}) copy-start(bf16[8,32,1024]{2,1,0:T(8,128)(2,1)} %param.11) | copy-start | bytes 1572868
  7.2 53.1 %all-gather.3.cloned.1.call-start = ((), (), s32[]{:S(2)}) async-start(), calls=%async_computation.3 | async-start | bytes 4325376 | tf_op jit(solution)/shard_map/all_gather | solution.py:76
  7.9 100.4 %all-gather.5.cloned.1.call-start = ((), (), s32[]{:S(2)}) async-start(), calls=%async_computation.4 | async-start | bytes 4325376 | tf_op jit(solution)/shard_map/all_gather | solution.py:77
  8.7 271.2 %reduce-scatter.6.cloned.1.call-start = ((), (), s32[]{:S(2)}) async-start(), calls=%async_computation.5 | async-start | bytes 1081344 | tf_op jit(solution)/shard_map/reduce_scatter | solution.py:112
  11.5 125.3 %copy-start.5 = (f32[256,256]{0,1:T(8,128)}, f32[256,256]{0,1:T(8,128)S(1)}, u32[]{:S(2)}) copy-start(f32[256,256]{0,1:T(8,128)S(1)} %reshape.130) | copy-start | bytes 786436
  63.8 48.5 %copy-start.12 = (f32[1024]{0:T(1024)S(1)}, f32[1024]{0:T(1024)}, u32[]{:S(2)}) copy-start(f32[1024]{0:T(1024)} %param.15) | copy-start | bytes 12292
  112.0 24.9 %copy-start = (f32[256,1024]{1,0:T(8,128)S(1)}, f32[256,1024]{1,0:T(8,128)}, u32[]{:S(2)}) copy-start(f32[256,1024]{1,0:T(8,128)} %param.16) | copy-start | bytes 3145732
  112.0 24.9 %copy-start.6 = (f32[256,256]{0,1:T(8,128)S(1)}, f32[256,256]{0,1:T(8,128)}, u32[]{:S(2)}) copy-start(f32[256,256]{0,1:T(8,128)} %reshape.127) | copy-start | bytes 786436
  136.9 1.4 copy-start.3
  204.8 189.0 %reduce-scatter.10.cloned.1.call-start = ((), (), s32[]{:S(2)}) async-start(), calls=%async_computation.7 | async-start | bytes 8650752
  301.6 1.0 copy-start.2
  301.6 187.8 %reduce-scatter.8.cloned.1.call-start = ((), (), s32[]{:S(2)}) async-start(), calls=%async_computation.6 | async-start | bytes 8650752 | tf_op jit(solution)/shard_map/reduce_scatter | solution.py:126
  307.2 1.0 copy-start.4
  307.2 249.6 %all-reduce.4.cloned.1.call-start = ((), (), s32[]{:S(2)}) async-start(), calls=%async_computation.8 | async-start | bytes 4718592 | tf_op jit(solution)/shard_map/psum | solution.py:119
  396.0 163.1 %copy-start.1 = (f32[256,1024]{1,0:T(8,128)S(1)}, f32[256,1024]{1,0:T(8,128)}, u32[]{:S(2)}) copy-start(f32[256,1024]{1,0:T(8,128)} %param.16) | copy-start | bytes 3145732
  396.0 163.1 %copy-start.7 = (f32[256,1024]{1,0:T(8,128)S(1)}, f32[256,1024]{1,0:T(8,128)}, u32[]{:S(2)}) copy-start(f32[256,1024]{1,0:T(8,128)} %param.17) | copy-start | bytes 3145732
  396.0 163.1 %copy-start.8 = (f32[256,1024]{1,0:T(8,128)S(1)}, f32[256,1024]{1,0:T(8,128)}, u32[]{:S(2)}) copy-start(f32[256,1024]{1,0:T(8,128)} %param.18) | copy-start | bytes 3145732
  559.1 3.4 copy-start.11
Sparse Core Ops, SparseCore 0:
  10.3 50.0 all-gather.2
  62.6 45.6 all-gather.4
  204.9 74.9 reduce-scatter.5
  301.8 91.9 reduce-scatter.9
  397.3 92.0 reduce-scatter.7
  492.6 64.2 all-reduce.3
where the time goes:
time: 571 us; the launch traced here: 570 us
  waiting for transfers between devices  409 us (72%)
  blocking collectives  86.4 us (15%)
  matrix products  26.2 us (5%)
  local copies, waits for them, and re-layouts  18.2 us (3%)
  other arithmetic  15.4 us (3%)
  between operations  14.3 us (3%)
    reduce_scatter x1, waiting for transfers between devices, on_device(): lax.psum_scatter(full_out, 'clu', scatter_dimension=0, tiled=True)  93.4 us
    unnamed x7, waiting for transfers between devices  85.5 us
    reduce_scatter x1, waiting for transfers between devices, on_device(): lax.psum_scatter(jnp.dot(logit_grad, label_tiles, precision=lax.Precision...  74.8 us
    psum x1, waiting for transfers between devices, on_device(): panel_derivative = lax.psum(local_tile_grad, 'enc')  66.8 us
    psum x1, blocking collectives, on_device(): expsum, possum = lax.psum((jnp.sum(weighted, axis=1), picked), 'clu')  62.2 us
    all_gather x1, waiting for transfers between devices, on_device(): lax.all_gather(w_out, 'clu', axis=0, tiled=True)  44.5 us
    all_gather x1, waiting for transfers between devices, on_device(): lax.all_gather(w_in, 'clu', axis=0, tiled=True)  44.2 us
    all_gather x1, blocking collectives, on_device(): group_emb = lax.all_gather(embedded_tokens, 'clu', axis=0, tiled=True)  24.2 us
  transfers between devices with their start and end apart: 6, of which 6 were waited for; matrix products, arithmetic and copies ran while one was open for 3% of the time, Pallas kernels for 0%

commit v1 on v0

v1 whole, which is shorter than its diff:
```python
import jax
import jax.numpy as jnp
from jax import lax
from jax.experimental import pallas as pl
from jax.experimental.pallas import tpu as pltpu
from jax.sharding import Mesh, PartitionSpec as P

LPC = 4
POS = 4

NORM_EPS = 1e-05
INV_ROOT_TWO = 0.7071067811865476
INV_ROOT_TWO_PI = 0.3989422804014327
CORR_ONE = 1.000026562104397
CORR_TWO = 10.50333528

F32 = jnp.float32
BF16 = jnp.bfloat16
CHIPS = ("x", "z")
FIRST = (((0,), (0,)), ((), ()))
LAST = (((1,), (1,)), ((), ()))


def swap_core(a):
    return lax.ppermute(a, "c", [(0, 1), (1, 0)])


def swap_near(a):
    return lax.ppermute(a, "l", [(0, 1), (1, 0)])


def swap_diag(a):
    return lax.ppermute(a, ("l", "c"), [(0, 3), (3, 0), (1, 2), (2, 1)])


def swap_wrap(a):
    return lax.ppermute(a, ("h", "l"), [(0, 3), (3, 0), (1, 2), (2, 1)])


def gather_chips(a):
    return lax.all_to_all(a, CHIPS, 0, 0, tiled=True)


WHOLE = pl.BlockSpec(memory_space=pltpu.VMEM)
SCALARS = pl.BlockSpec(memory_space=pltpu.SMEM)
ANYWHERE = pl.BlockSpec(memory_space=pl.ANY)
LIMIT = pltpu.CompilerParams(vmem_limit_bytes=40 * 1024 * 1024)


def shape(dims, dtype):
    return jax.ShapeDtypeStruct(dims, dtype)


def cost(flops, data, special=0):
    return pl.CostEstimate(flops=flops, bytes_accessed=data, transcendentals=special)


def iota(dims, axis):
    return lax.broadcasted_iota(jnp.int32, dims, axis)


def pick_kernel(meta, w_in, mine, theirs):
    core, role = meta[0], meta[1]
    part = jnp.where(iota((512, 256), 1) < 128, core * 2 + role, 2 - core * 2 + role)
    at = iota((512, 256), 1) % 128
    spread = (iota((512, 256), 0) == at // 32 * 128 + part * 32 + at % 32).astype(BF16)
    for i in range(4):
        got = jnp.dot(w_in[:, i * 512 : i * 512 + 512], spread, preferred_element_type=F32).astype(BF16)
        mine[:, i * 128 : i * 128 + 128] = got[:, :128]
        theirs[:, i * 128 : i * 128 + 128] = got[:, 128:]


def lay_kernel(meta, mine, theirs, w_out, out):
    core, role = meta[0], meta[1]
    top = jnp.where(role == 0, w_out[:32], w_out[32:])
    first = jnp.where(core == 0, mine[...], theirs[...])
    second = jnp.where(core == 0, theirs[...], mine[...])
    for i in range(out.shape[0]):
        out[i, :32] = top
        out[i, 32:, :512] = first
        out[i, 32:, 512:] = second


def forward_kernel(tok_a, tok_b, weights, part_a, part_b, hidden, slope, w_in, w_out, sems):
    copies = [
        pltpu.make_async_copy(
            weights.at[:, 32:64, k * 512 : k * 512 + 512], w_in.at[:, k * 32 : k * 32 + 32], sems.at[k]
        )
        for k in range(2)
    ]
    copies.append(pltpu.make_async_copy(weights.at[:, 0:32], w_out, sems.at[2]))
    for copy in copies:
        copy.start()
    copies[0].wait()
    copies[1].wait()
    for k, (tok, part) in enumerate(((tok_a, part_a), (tok_b, part_b))):
        pre_act = jnp.dot(tok[...], w_in[...].reshape(1024, 512), preferred_element_type=F32)
        normal_cdf = 0.5 * (1.0 + lax.erf(pre_act * INV_ROOT_TWO))
        act = (pre_act * normal_cdf).astype(BF16)
        hidden[k * 256 : k * 256 + 256] = act
        slope[k * 256 : k * 256 + 256] = (
            normal_cdf + pre_act * jnp.exp(-0.5 * pre_act * pre_act) * INV_ROOT_TWO_PI
        )
        if k == 0:
            copies[2].wait()
        part[...] = jnp.dot(
            act, w_out[...].reshape(512, 1024), preferred_element_type=F32
        ).astype(part.dtype)


def forward(tok_a, tok_b, weights):
    return pl.pallas_call(
        forward_kernel,
        out_shape=(
            shape((256, 1024), BF16),
            shape((256, 1024), F32),
            shape((512, 512), BF16),
            shape((512, 512), F32),
        ),
        in_specs=[WHOLE, WHOLE, ANYWHERE],
        out_specs=(WHOLE,) * 4,
        scratch_shapes=[
            pltpu.VMEM((16, 64, 512), BF16),
            pltpu.VMEM((16, 32, 1024), BF16),
            pltpu.SemaphoreType.DMA((3,)),
        ],
        compiler_params=LIMIT,
        cost_estimate=cost(2**30, 6 * 2**20, 2**19),
    )(tok_a, tok_b, weights)


def norm_kernel(lengths, tok, part, from_core, from_near, gain, rows, emb):
    embs = []
    for d in range(8):
        at = pl.ds(d * 32, 32)
        summed = tok[at].astype(F32) + (
            part[at] + from_core[at].astype(F32) + from_near[at].astype(F32)
        )
        centred = summed - jnp.mean(summed, axis=-1, keepdims=True)
        inv = lax.rsqrt(jnp.mean(centred * centred, axis=-1, keepdims=True) + NORM_EPS)
        normed = centred * inv
        count = jnp.full((32, 1), lengths[d], jnp.int32).astype(F32)
        share = jnp.where(iota((32, 1), 0).astype(F32) < count, 1.0, 0.0) / count
        embs.append(jnp.sum(normed * gain[...] * share, axis=0, keepdims=True))
        high = inv.astype(BF16).astype(F32)
        lane = iota((32, 128), 1)
        extra = jnp.where(lane == 0, high, jnp.where(lane == 1, inv - high, jnp.where(lane == 2, count, 0.0)))
        rows[at, :1024] = normed.astype(BF16)
        rows[at, 1024:] = extra.astype(BF16)
    docs = jnp.concatenate(embs, axis=0)
    emb[...] = jnp.concatenate([docs] * 16, axis=0).astype(BF16)


def score_kernel(emb, own_tiles, oth_tiles, live, packed, weighted):
    docs = emb[...].astype(F32)
    for k, tiles in enumerate((own_tiles, oth_tiles)):
        at = pl.ds(k * 256, 256)
        scores = lax.dot_general(
            docs, tiles[...], LAST, precision=lax.Precision.HIGHEST, preferred_element_type=F32
        )
        weighted[:, at] = live[:, at] * jnp.exp(scores)
    value = weighted[...]
    part_emb = jnp.dot(
        value[:, :256], own_tiles[...], precision=lax.Precision.HIGHEST, preferred_element_type=F32
    ) + jnp.dot(
        value[:, 256:], oth_tiles[...], precision=lax.Precision.HIGHEST, preferred_element_type=F32
    )
    sums = jnp.sum(value, axis=1, keepdims=True) * 0.5
    high = sums.astype(BF16).astype(F32)
    row, lane = iota((128, 128), 0), iota((128, 128), 1)
    chosen = row // 8 == lane
    same = (row % 8 == lane % 8).astype(BF16)
    for k, part in enumerate((high, sums - high)):
        table = jnp.where(chosen, part, 0.0).astype(BF16)
        packed[:, 1024 + k * 128 : 1152 + k * 128] = jnp.dot(
            same, table, preferred_element_type=F32
        ).astype(BF16)
    packed[:, :1024] = part_emb.astype(BF16)


def settle_kernel(meta, got, pos, emb, grad, loss, sums):
    total = got[0].astype(F32)
    for i in range(1, 16):
        total = total + got[i].astype(F32)
    every = (total[:, 1024:1152] + total[:, 1152:1280]) * 2.0
    sums[...] = every
    expsum = jnp.sum(jnp.where(iota((8, 128), 1) == meta[2], every, 0.0), axis=1, keepdims=True)
    pos_mean = jnp.sum(pos[...], axis=0)
    grad[...] = total[:, :1024] / expsum - pos_mean
    picked = jnp.sum(emb[...].astype(F32)[:8] * pos_mean, axis=1, keepdims=True)
    loss[...] = jnp.broadcast_to(jnp.log(expsum) - picked, (8, 128))


def backward_kernel(*refs):
    grads, gain = refs[:4], refs[4]
    rows, toks = refs[5:9], refs[9:13]
    hiddens, slopes, weights, out = refs[13:15], refs[15:17], refs[17], refs[18]
    row_buf, tok_buf, hid_buf, slope_buf, w_out, sum_grad, act_grad, sems = refs[19:]
    first = pltpu.make_async_copy(weights.at[:, 0:32], w_out, sems.at[0])
    first.start()
    row_copies, tok_copies, hid_copies, slope_copies = [], [], [], []
    for k in range(4):
        at = pl.ds(k * 256, 256)
        row_copies.append(pltpu.make_async_copy(rows[k], row_buf.at[at], sems.at[1 + k]))
        row_copies[k].start()
    for k in range(2):
        at = pl.ds(k * 512, 512)
        slope_copies.append(pltpu.make_async_copy(slopes[k], slope_buf.at[at], sems.at[5 + k]))
        slope_copies[k].start()
    for k in range(2):
        at = pl.ds(k * 512, 512)
        hid_copies.append(pltpu.make_async_copy(hiddens[k], hid_buf.at[at], sems.at[7 + k]))
        hid_copies[k].start()
    for k in range(4):
        at = pl.ds(k * 256, 256)
        tok_copies.append(pltpu.make_async_copy(toks[k], tok_buf.at[at], sems.at[9 + k]))
        tok_copies[k].start()
    for k in range(4):
        row_copies[k].wait()
        scaled_grad = grads[k][...] * gain[...]
        grad_mean = jnp.mean(scaled_grad, axis=-1, keepdims=True)
        for d in range(8):
            at = pl.ds(k * 256 + d * 32, 32)
            norm = row_buf[at, :1024].astype(F32)
            extra = row_buf[at, 1024:].astype(F32)
            lane = iota((32, 128), 1)
            scale = jnp.sum(jnp.where(lane < 2, extra, 0.0), axis=1, keepdims=True)
            count = jnp.sum(jnp.where(lane == 2, extra, 0.0), axis=1, keepdims=True)
            share = jnp.where(iota((32, 1), 0).astype(F32) < count, 1.0, 0.0) / count
            grad = scaled_grad[d : d + 1]
            along = jnp.mean(grad * norm, axis=-1, keepdims=True)
            sum_grad[at] = (
                (grad - grad_mean[d : d + 1] - norm * along) * (share * scale)
            ).astype(BF16)
        if k == 0:
            first.wait()
        if k % 2 == 0:
            slope_copies[k // 2].wait()
        at = pl.ds(k * 256, 256)
        back = lax.dot_general(
            sum_grad[at], w_out[...].reshape(512, 1024), LAST, preferred_element_type=F32
        )
        act_grad[at] = (back * slope_buf[at]).astype(BF16)
    for copy in hid_copies:
        copy.wait()
    for i in range(4):
        part = lax.dot_general(
            hid_buf[:, i * 128 : i * 128 + 128], sum_grad[...], FIRST, preferred_element_type=F32
        )
        out[i * 4 : i * 4 + 4, :32] = part.astype(BF16).reshape(4, 32, 1024)
    for copy in tok_copies:
        copy.wait()
    for i in range(4):
        part = lax.dot_general(
            tok_buf[:, i * 256 : i * 256 + 256], act_grad[...], FIRST, preferred_element_type=F32
        ).astype(BF16).reshape(4, 2, 32, 512)
        out[i * 4 : i * 4 + 4, 32:, :512] = part[:, 0]
        out[i * 4 : i * 4 + 4, 32:, 512:] = part[:, 1]


def backward(grads, gain, rows, toks, hiddens, slopes, weights):
    return pl.pallas_call(
        backward_kernel,
        out_shape=shape((16, 64, 1024), BF16),
        in_specs=[WHOLE] * 5 + [ANYWHERE] * 13,
        out_specs=WHOLE,
        scratch_shapes=[
            pltpu.VMEM((1024, 1152), BF16),
            pltpu.VMEM((1024, 1024), BF16),
            pltpu.VMEM((1024, 512), BF16),
            pltpu.VMEM((1024, 512), F32),
            pltpu.VMEM((16, 32, 1024), BF16),
            pltpu.VMEM((1024, 1024), BF16),
            pltpu.VMEM((1024, 512), BF16),
            pltpu.SemaphoreType.DMA((13,)),
        ],
        compiler_params=LIMIT,
        cost_estimate=cost(3 * 2**30, 10 * 2**20),
    )(*grads, gain, *rows, *toks, *hiddens, *slopes, weights)


def total_kernel(got, out):
    total = got[0].astype(F32)
    for i in range(1, 16):
        total = total + got[i].astype(F32)
    out[...] = total.astype(BF16)


def place_kernel(meta, own, near, core_part, diag_part, grad_in, grad_out):
    core, role = meta[0], meta[1]
    mine, theirs = own[:32].astype(F32), near[:32].astype(F32)
    grad_out[:32] = jnp.where(role == 0, mine, theirs)
    grad_out[32:] = jnp.where(role == 0, theirs, mine)
    pieces = (
        jnp.where(core == 0, own[32:, :512], own[32:, 512:]),
        core_part[...],
        jnp.where(core == 0, near[32:, :512], near[32:, 512:]),
        diag_part[...],
    )
    row, lane = iota((512, 512), 0), iota((512, 512), 1)
    piece, at = row // 128, row % 128
    swapped = piece % 2
    part = (core + swapped - 2 * core * swapped) * 2
    flipped = piece // 2
    part = part + role + flipped - 2 * role * flipped
    spread = (lane == at // 32 * 128 + part * 32 + at % 32).astype(BF16)
    for i in range(4):
        block = jnp.concatenate([a[:, i * 128 : i * 128 + 128] for a in pieces], axis=1)
        grad_in[:, i * 512 : i * 512 + 512] = jnp.dot(block, spread, preferred_element_type=F32)


def on_device(
    states,
    lengths,
    w_in,
    w_out,
    norm_gain,
    label_tiles,
    tile_mean,
    tile_var,
    shortlist,
    positives,
    owner_map,
):
    docs, length, width = states.shape
    core = lax.axis_index("c")
    high, low = lax.axis_index("h"), lax.axis_index("l")
    role = high + low - 2 * high * low
    chip = lax.axis_index("x") * 4 + lax.axis_index("z")
    meta = jnp.stack([core, role, chip]).astype(jnp.int32)
    gain = norm_gain.reshape(1, width)
    own_tok = states.reshape(docs * length, width)

    mine, theirs = pl.pallas_call(
        pick_kernel,
        out_shape=(shape((32, 512), BF16),) * 2,
        in_specs=[SCALARS, WHOLE],
        out_specs=(WHOLE, WHOLE),
        cost_estimate=cost(2**25, 2**18),
    )(meta, w_in)
    weights = gather_chips(
        pl.pallas_call(
            lay_kernel,
            out_shape=shape((16, 64, width), BF16),
            grid=(4,),
            in_specs=[SCALARS, WHOLE, WHOLE, WHOLE],
            out_specs=pl.BlockSpec((4, 64, width), lambda i: (i, 0, 0)),
            cost_estimate=cost(0, 2**21),
        )(meta, mine, swap_core(theirs), w_out)
    )

    core_tok, near_tok, diag_tok = swap_core(own_tok), swap_near(own_tok), swap_diag(own_tok)

    oth_tiles = swap_core(label_tiles)
    slots = jnp.concatenate(
        [(chip * 2 + core) * 64 + jnp.arange(64), (chip * 2 + 1 - core) * 64 + jnp.arange(64)]
    ).astype(jnp.int32)
    all_clusters = jnp.arange(owner_map.shape[0], dtype=jnp.int32)
    owner_match = owner_map[:, None] == slots[None, :]
    cluster_ids = jnp.sum(jnp.where(owner_match, all_clusters[:, None], 0), axis=0)
    pick = lambda a: lax.dynamic_index_in_dim(a.reshape(16, 2, 8, -1), core, 1, False).reshape(128, -1)
    short, posit = pick(shortlist), pick(positives)
    cluster_live = jnp.max(
        (short[:, :, None] == cluster_ids[None, None, :]).astype(F32), axis=1
    )
    live = jnp.repeat(cluster_live, LPC, axis=1)
    cluster_hit = (posit[:, :, None] // LPC == cluster_ids[None, None, :]).astype(F32)
    offset_hit = (
        posit[:, :, None] % LPC == jnp.arange(LPC, dtype=jnp.int32)[None, None, :]
    ).astype(F32)
    hits = jnp.sum(cluster_hit[:, :, :, None] * offset_hit[:, :, None, :], axis=1).reshape(128, 512)
    share_hit = hits / POS
    pos_part = (
        jnp.dot(share_hit[:, :256], label_tiles, precision=lax.Precision.HIGH)
        + jnp.dot(share_hit[:, 256:], oth_tiles, precision=lax.Precision.HIGH)
    )
    weights, live, share_hit, pos_part = lax.optimization_barrier(
        (weights, live, share_hit, pos_part)
    )

    near_a, near_b, near_hidden, near_slope = forward(diag_tok, near_tok, weights)
    near_sum = (near_b + swap_core(near_a).astype(F32)).astype(BF16)
    near_sum, pos_part = lax.optimization_barrier((near_sum, pos_part))
    from_near = swap_near(near_sum)
    pos_got = gather_chips(pos_part.reshape(16, docs, width))
    own_a, own_b, own_hidden, own_slope = forward(core_tok, own_tok, weights)
    from_near, pos_got = lax.optimization_barrier((from_near, pos_got))
    own_rows, emb = pl.pallas_call(
        norm_kernel,
        out_shape=(shape((256, 1152), BF16), shape((128, width), BF16)),
        in_specs=[SCALARS] + [WHOLE] * 5,
        out_specs=(WHOLE, WHOLE),
        compiler_params=LIMIT,
        cost_estimate=cost(2**22, 4 * 2**20),
    )(lengths, own_tok, own_b, swap_core(own_a), from_near, gain)

    plane_emb = gather_chips(emb.reshape(16, docs, width)).reshape(128, width)
    core_rows, near_rows, diag_rows = swap_core(own_rows), swap_near(own_rows), swap_diag(own_rows)
    packed, weighted = pl.pallas_call(
        score_kernel,
        out_shape=(shape((128, 1280), BF16), shape((128, 512), F32)),
        in_specs=[WHOLE] * 4,
        out_specs=(WHOLE, WHOLE),
        compiler_params=LIMIT,
        cost_estimate=cost(2**30, 5 * 2**20, 2**16),
    )(plane_emb, label_tiles, oth_tiles, live)
    got = lax.all_to_all(packed.reshape(16, docs, 1280), CHIPS, 0, 0, tiled=True)
    emb_grad, loss, sums = pl.pallas_call(
        settle_kernel,
        out_shape=(shape((docs, width), F32), shape((docs, 128), F32), shape((docs, 128), F32)),
        in_specs=[SCALARS, WHOLE, WHOLE, WHOLE],
        out_specs=(WHOLE,) * 3,
        compiler_params=LIMIT,
        cost_estimate=cost(2**20, 2**20),
    )(meta, got, pos_got, emb)
    loss = loss[:, 0]

    grads = (swap_diag(emb_grad), swap_near(emb_grad), swap_core(emb_grad), emb_grad)
    send = backward(
        grads,
        gain,
        (diag_rows, near_rows, core_rows, own_rows),
        (diag_tok, near_tok, core_tok, own_tok),
        (near_hidden, own_hidden),
        (near_slope, own_slope),
        weights,
    )
    got = lax.all_to_all(send, CHIPS, 0, 0, tiled=True)
    part = pl.pallas_call(
        total_kernel,
        out_shape=shape((64, width), BF16),
        grid=(4,),
        in_specs=[pl.BlockSpec((16, 16, width), lambda i: (0, i, 0))],
        out_specs=pl.BlockSpec((16, width), lambda i: (i, 0)),
        compiler_params=LIMIT,
        cost_estimate=cost(2**20, 2**21),
    )(got)
    both = (part.astype(F32) + swap_wrap(part).astype(F32)).astype(BF16)
    give = jnp.where(core == 0, both[32:, 512:], both[32:, :512])
    grad_in, grad_out = pl.pallas_call(
        place_kernel,
        out_shape=(shape((32, 2048), F32), shape((64, width), F32)),
        in_specs=[SCALARS] + [WHOLE] * 4,
        out_specs=(WHOLE, WHOLE),
        compiler_params=LIMIT,
        cost_estimate=cost(2**26, 2**20),
    )(meta, both, swap_near(both), swap_core(give), swap_diag(give))

    all_sums = sums[:, :16].T.reshape(128)
    logit_grad = weighted / all_sums[:, None] - share_hit
    tile_part = lax.dot_general(
        logit_grad, plane_emb.astype(F32), FIRST, precision=lax.Precision.HIGH
    )
    tile_chip = (tile_part[:256] + swap_core(tile_part[256:])).astype(BF16)

    def add(a, swap):
        return a.astype(F32) + swap(a).astype(F32)

    tile_grad = jnp.concatenate(
        [
            add(add(tile_chip[:128], swap_near).astype(BF16), swap_wrap),
            add(add(tile_chip[128:], swap_wrap).astype(BF16), swap_near),
        ],
        axis=0,
    )
    new_mean = 0.9 * tile_mean + 0.1 * tile_grad
    new_var = 0.999 * tile_var + 0.001 * tile_grad * tile_grad
    new_tiles = label_tiles - 0.001 * (new_mean * CORR_ONE) / (jnp.sqrt(new_var * CORR_TWO) + 1e-08)
    return (loss, new_tiles, new_mean, new_var, grad_in, grad_out)


def solution(mesh):
    grid = Mesh(mesh.devices.reshape(2, 2, 4, 4, 2), ("h", "l", "x", "z", "c"))
    every, plane, group = ("h", "l", "x", "z", "c"), ("x", "z", "c"), ("h", "l")
    return jax.shard_map(
        on_device,
        mesh=grid,
        in_specs=(
            P(every, None, None),
            P(every),
            P(plane, None),
            P(plane, None),
            P(),
            P(plane, None),
            P(plane, None),
            P(plane, None),
            P(group, None),
            P(group, None),
            P(),
        ),
        out_specs=(
            P(every),
            P(plane, None),
            P(plane, None),
            P(plane, None),
            P(plane, None),
            P(plane, None),
        ),
        check_vma=False,
    )
```

time: 571 us -> 198 us (0.35)
  waiting for transfers between devices: 409 us -> 55.5 us
  blocking collectives: 86.4 us -> 15.1 us
  starting transfers between devices: 0.42 us -> 54.5 us
  Pallas kernels: 0 us -> 25.3 us
  matrix products: 26.2 us -> 4.97 us
  between operations: 14.3 us -> 1.18 us
    reduce_scatter x2 -> x0, waiting for transfers between devices: 168 us -> none  [the longest x1 93.4 us: on_device(): lax.psum_scatter(full_out, 'clu', scatter_dimension=0, tiled=True)]
    all_gather x2 -> x0, waiting for transfers between devices: 88.7 us -> none  [the longest x1 44.5 us: on_device(): lax.all_gather(w_out, 'clu', axis=0, tiled=True)]
    unnamed x7 -> x0, waiting for transfers between devices: 85.5 us -> none
    psum x1 -> x0, waiting for transfers between devices: 66.8 us -> none  [on_device(): panel_derivative = lax.psum(local_tile_grad, 'enc')]
    psum x1 -> x0, blocking collectives: 62.2 us -> none  [on_device(): expsum, possum = lax.psum((jnp.sum(weighted, axis=1), picked), 'clu')]
    ppermute x0 -> x23, waiting for transfers between devices: none -> 33.4 us  [the longest x7 17.7 us: swap_near(): return lax.ppermute(a, 'l', [(0, 1), (1, 0)])]
    ppermute x0 -> x23, starting transfers between devices: none -> 31.7 us  [the longest x9 9.35 us: swap_core(): return lax.ppermute(a, 'c', [(0, 1), (1, 0)])]
    pallas_call x0 -> x10, Pallas kernels: none -> 25.3 us  [the longest x1 6.57 us: backward(): pl.pallas_call(backward_kernel, out_shape=shape((16, 64, 1024), BF16), in...]
  transfers between devices with their start and end apart: 6 -> 27, of which waited for: 6 -> 13; matrix products, arithmetic and copies ran while one was open for 3% -> 18% of each run, Pallas kernels for 0% -> 7%
where the time goes in v1:
time: 198 us; the launch traced here: 197 us
  waiting for transfers between devices  55.5 us (28%)
  starting transfers between devices  54.5 us (28%)
  Pallas kernels  25.3 us (13%)
  local copies, waits for them, and re-layouts  20.5 us (10%)
  other arithmetic  19.9 us (10%)
  blocking collectives  15.1 us (8%)
  matrix products  4.97 us (3%)
    ppermute x7, waiting for transfers between devices, swap_near(): return lax.ppermute(a, 'l', [(0, 1), (1, 0)])  17.7 us
    all_to_all x2, waiting for transfers between devices, gather_chips(): return lax.all_to_all(a, CHIPS, 0, 0, tiled=True)  16 us
    all_to_all x1, blocking collectives, gather_chips(): return lax.all_to_all(a, CHIPS, 0, 0, tiled=True)  15.1 us
    all_to_all x2, starting transfers between devices, gather_chips(): return lax.all_to_all(a, CHIPS, 0, 0, tiled=True)  12.2 us
    unnamed x69, local copies, waits for them, and re-layouts  11 us
    reduce_max x1, other arithmetic, on_device(): jnp.max((short[:, :, None] == cluster_ids[None, None, :]).astype(F32), ax...  9.87 us
    ppermute x3, waiting for transfers between devices, swap_wrap(): return lax.ppermute(a, ('h', 'l'), [(0, 3), (3, 0), (1, 2), (2, 1)])  9.82 us
    ppermute x9, starting transfers between devices, swap_core(): return lax.ppermute(a, 'c', [(0, 1), (1, 0)])  9.35 us
  transfers between devices with their start and end apart: 27, of which 13 were waited for; matrix products, arithmetic and copies ran while one was open for 18% of the time, Pallas kernels for 7%

profile of v1, /device:TPU:1, one launch (start us, length us, event | category | flops | bytes accessed | tf_op | source)
XLA Modules:
  0.0 196.9 jit_solution(9521635252409744089)
XLA Ops:
  0.6 2.2 %collective-permute-start.5 = (bf16[256,1024]{1,0:T(8,128)(2,1)}, bf16[256,1024]{1,0:T(8,128)(2,1)}, u32[]{:S(2)}, u32[]{:S(2)}) collective-permute-start(bf16[256,1024]{1,0:T(8,128)(2,1)} %bitcast.24), channel_id=1, source_target_pairs={{0,32},{32,0},{1,33},{33,1},{2,34},{34,2},{3,35},{35,3},{4,36},{36... | collective-permute-start | bytes 1572872 | tf_op jit(solution)/shard_map/ppermute | solution.py:29
  8.5 2.8 %shard_map.155 = bf16[16,64,1024]{2,1,0:T(8,128)(2,1)} custom-call(s32[3]{0:T(128)} %pad_add_fusion.meta, bf16[32,512]{1,0:T(8,128)(2,1)} %get-tuple-element.33.mine, bf16[32,512]{1,0:T(8,128)(2,1)} %copy-done.32, bf16[64,1024]{1,0:T(8,128)(2,1)} %w_out.1), custom_call_target="tpu_custom_call" | custom-call | bytes 2097152 | tf_op jit(solution)/shard_map/pallas_call | solution.py:342
  11.3 7.8 %all-to-all-start = ((bf16[16,64,1024]{2,1,0:T(8,128)(2,1)}), bf16[16,64,1024]{2,1,0:T(8,128)(2,1)S(1)}, u32[]{:S(2)}, u32[]{:S(2)}) async-start(bf16[16,64,1024]{2,1,0:T(8,128)(2,1)} %shard_map.155), calls=%async_computation | async-start | bytes 4194304 | tf_op jit(solution)/shard_map/all_to_all | solution.py:41
  24.9 9.9 %convert_reduce_fusion = f32[128,128]{1,0:T(8,128)S(1)} fusion(s32[128]{0:T(128)S(1)} %select_reduce_fusion, s32[128,400]{1,0:T(8,128)S(1)} %dynamic-slice_bitcast_fusion), kind=kLoop, calls=%fused_computation | loop fusion | flops 19644416 | bytes 270848 | tf_op jit(solution)/shard_map/reduce_max | solution.py:363
  35.4 2.5 %convolution_add_fusion = f32[128,1024]{1,0:T(8,128)} fusion(f32[128,1024]{1,0:T(8,128)S(1)} %fusion.6, f32[256,1024]{1,0:T(8,128)} %collective-permute-done.2.oth_tiles, f32[128,512]{0,1:T(8,128)S(1)} %bitcast.36), kind=kOutput, calls=%fused_computation.2 | convolution fusion | flops 201457664 | bytes 2228224 | tf_op jit(solution)/shard_map/dot_general | solution.py:375
  37.8 10.5 %all-to-all-done.weights.refs_17_ = bf16[16,64,1024]{2,1,0:T(8,128)(2,1)S(1)} async-done(((bf16[16,64,1024]{2,1,0:T(8,128)(2,1)}), bf16[16,64,1024]{2,1,0:T(8,128)(2,1)S(1)}, u32[]{:S(2)}, u32[]{:S(2)}) %all-to-all-start) | async-done | bytes 2097184 | tf_op jit(solution)/shard_map/all_to_all | solution.py:41
  49.0 3.3 %shard_map.157 = (bf16[256,1024]{1,0:T(8,128)(2,1)S(1)}, f32[256,1024]{1,0:T(8,128)S(1)}, bf16[512,512]{1,0:T(8,128)(2,1)S(1)}, f32[512,512]{1,0:T(8,128)S(1)}) custom-call(bf16[256,1024]{1,0:T(8,128)(2,1)} %collective-permute-done.4.tok_a.refs_9_, bf16[256,1024]{1,0:T(8,128)(2,1)} %collective-permute-done.5.tok_b.refs_10_, ...), custom_call_target="tpu_custom_call" | custom-call | flops 1073741824 | bytes 6291456 | tf_op jit(solution)/shard_map/pallas_call | solution.py:112
  60.8 15.1 %all_to_all.25.pos = f32[16,8,1024]{2,1,0:T(8,128)} all-to-all(f32[16,8,1024]{2,1,0:T(8,128)S(1)} %bitcast.38), channel_id=1, replica_groups=mesh['h'=2,'l'=2,'x'=4,'z'=4,'c'=2] {'x','z'}, dimensions={0} | all-to-all | bytes 1048576 | tf_op jit(solution)/shard_map/all_to_all | solution.py:41
  78.7 4.4 %all-to-all-start.2 = ((bf16[16,8,1024]{2,1,0:T(8,128)(2,1)}), bf16[16,8,1024]{2,1,0:T(8,128)(2,1)S(1)}, u32[]{:S(2)}, u32[]{:S(2)}) async-start(bf16[16,8,1024]{2,1,0:T(8,128)(2,1)} %bitcast.31), calls=%async_computation.2 | async-start | bytes 524288 | tf_op jit(solution)/shard_map/all_to_all | solution.py:41
  84.9 5.6 %all-to-all-done.2 = bf16[16,8,1024]{2,1,0:T(8,128)(2,1)S(1)} async-done(((bf16[16,8,1024]{2,1,0:T(8,128)(2,1)}), bf16[16,8,1024]{2,1,0:T(8,128)(2,1)S(1)}, u32[]{:S(2)}, u32[]{:S(2)}) %all-to-all-start.2) | async-done | bytes 262176 | tf_op jit(solution)/shard_map/all_to_all | solution.py:41
  91.5 4.5 %shard_map.159 = (bf16[128,1280]{1,0:T(8,128)(2,1)S(1)}, f32[128,512]{1,0:T(8,128)S(1)}) custom-call(bf16[128,1024]{1,0:T(8,128)(2,1)S(1)} %bitcast.30, f32[256,1024]{1,0:T(8,128)S(1)} %copy-done.1, f32[256,1024]{1,0:T(8,128)} %collective-permute-done.2.oth_tiles, f32[128,512]{1,0:T(8,128)S(1)} %copy-done.22), custom_call_target="tpu_custom_call" | custom-call | flops 1073741824 | bytes 5242880 | tf_op jit(solution)/shard_map/pallas_call | solution.py:399
  97.4 3.7 %all-to-all-start.3 = ((bf16[16,8,1280]{2,1,0:T(8,128)(2,1)}), bf16[16,8,1280]{2,1,0:T(8,128)(2,1)S(1)}, u32[]{:S(2)}, u32[]{:S(2)}) async-start(bf16[16,8,1280]{2,1,0:T(8,128)(2,1)} %bitcast.32), calls=%async_computation.3 | async-start | bytes 655360 | tf_op jit(solution)/shard_map/all_to_all | solution.py:407
  102.9 2.6 %collective-permute-start.18 = (bf16[256,1152]{1,0:T(8,128)(2,1)}, bf16[256,1152]{1,0:T(8,128)(2,1)}, u32[]{:S(2)}, u32[]{:S(2)}) collective-permute-start(bf16[256,1152]{1,0:T(8,128)(2,1)} %copy-done.12), channel_id=1, source_target_pairs={{0,1},{1,0},{2,3},{3,2},{4,5},{5,4},{6,7},{7,6},{8,9},{9,8},{10,11... | collective-permute-start | bytes 1769480 | tf_op jit(solution)/shard_map/ppermute | solution.py:25
  115.0 3.7 %collective-permute-start.8 = (f32[256,1024]{1,0:T(8,128)}, f32[256,1024]{1,0:T(8,128)}, u32[]{:S(2)}, u32[]{:S(2)}) collective-permute-start(f32[256,1024]{1,0:T(8,128)} %slice.43), channel_id=1, source_target_pairs={{0,1},{1,0},{2,3},{3,2},{4,5},{5,4},{6,7},{7,6},{8,9},{9,8},{10,11... | collective-permute-start | bytes 3145736 | tf_op jit(solution)/shard_map/ppermute | solution.py:25
  118.7 2.2 %collective-permute-done.15.refs_2_ = f32[8,1024]{1,0:T(8,128)S(1)} collective-permute-done((f32[8,1024]{1,0:T(8,128)S(1)}, f32[8,1024]{1,0:T(8,128)S(1)}, u32[]{:S(2)}, u32[]{:S(2)}) %collective-permute-start.15) | collective-permute-done | bytes 32800 | tf_op jit(solution)/shard_map/ppermute | solution.py:25
  121.0 12.6 %collective-permute-done.14.refs_1_ = f32[8,1024]{1,0:T(8,128)S(1)} collective-permute-done((f32[8,1024]{1,0:T(8,128)S(1)}, f32[8,1024]{1,0:T(8,128)S(1)}, u32[]{:S(2)}, u32[]{:S(2)}) %collective-permute-start.14) | collective-permute-done | bytes 32800 | tf_op jit(solution)/shard_map/ppermute | solution.py:29
  137.1 6.6 %shard_map.161 = bf16[16,64,1024]{2,1,0:T(8,128)(2,1)S(1)} custom-call(f32[8,1024]{1,0:T(8,128)S(1)} %collective-permute-done.13.refs_0_, f32[8,1024]{1,0:T(8,128)S(1)} %collective-permute-done.14.refs_1_, f32[8,1024]{1,0:T(8,128)S(1)} %collective-permute-done.15.refs_2_, f32[8,1024]{1,0:T(8,128)S(1)} %get-tuple-element.52.refs_3_, f32[1,1024]{1,0:T(1,128)S(1)} %bitcast.34, ...), custom_call_target="tpu_custom_call" | custom-call | flops 3221225472 | bytes 10485760 | tf_op jit(solution)/shard_map/pallas_call | solution.py:262
  145.0 6.9 %all-to-all-start.4 = ((bf16[16,64,1024]{2,1,0:T(8,128)(2,1)}), bf16[16,64,1024]{2,1,0:T(8,128)(2,1)S(1)}, u32[]{:S(2)}, u32[]{:S(2)}) async-start(bf16[16,64,1024]{2,1,0:T(8,128)(2,1)} %copy-done), calls=%async_computation.4 | async-start | bytes 4194304 | tf_op jit(solution)/shard_map/all_to_all | solution.py:428
  156.7 3.5 %collective-permute-done.9 = bf16[128,1024]{1,0:T(8,128)(2,1)S(1)} collective-permute-done((bf16[128,1024]{1,0:T(8,128)(2,1)S(1)}, bf16[128,1024]{1,0:T(8,128)(2,1)S(1)}, u32[]{:S(2)}, u32[]{:S(2)}) %collective-permute-start.9) | collective-permute-done | bytes 262176 | tf_op jit(solution)/shard_map/ppermute | solution.py:29
  160.2 2.7 %collective-permute-done.11 = bf16[128,1024]{1,0:T(8,128)(2,1)S(1)} collective-permute-done((bf16[128,1024]{1,0:T(8,128)(2,1)S(1)}, bf16[128,1024]{1,0:T(8,128)(2,1)S(1)}, u32[]{:S(2)}, u32[]{:S(2)}) %collective-permute-start.11) | collective-permute-done | bytes 262176 | tf_op jit(solution)/shard_map/ppermute | solution.py:37
  165.6 5.7 %collective-permute-done.10 = bf16[128,1024]{1,0:T(8,128)(2,1)} collective-permute-done((bf16[128,1024]{1,0:T(8,128)(2,1)}, bf16[128,1024]{1,0:T(8,128)(2,1)}, u32[]{:S(2)}, u32[]{:S(2)}) %collective-permute-start.10) | collective-permute-done | bytes 262176 | tf_op jit(solution)/shard_map/ppermute | solution.py:37
  173.2 4.3 %all-to-all-done.4.got = bf16[16,64,1024]{2,1,0:T(8,128)(2,1)S(1)} async-done(((bf16[16,64,1024]{2,1,0:T(8,128)(2,1)}), bf16[16,64,1024]{2,1,0:T(8,128)(2,1)S(1)}, u32[]{:S(2)}, u32[]{:S(2)}) %all-to-all-start.4) | async-done | bytes 2097184 | tf_op jit(solution)/shard_map/all_to_all | solution.py:428
  178.1 5.5 %collective-permute-start.19 = (bf16[64,1024]{1,0:T(8,128)(2,1)S(1)}, bf16[64,1024]{1,0:T(8,128)(2,1)S(1)}, u32[]{:S(2)}, u32[]{:S(2)}) collective-permute-start(bf16[64,1024]{1,0:T(8,128)(2,1)S(1)} %shard_map.162), channel_id=1, source_target_pairs={{0,96},{96,0},{32,64},{64,32},{1,97},{97,1},{33,65},{65,33},{2,98}... | collective-permute-start | bytes 393224 | tf_op jit(solution)/shard_map/ppermute | solution.py:37
  186.0 4.5 %collective-permute-start.22 = (bf16[32,512]{1,0:T(8,128)(2,1)S(1)}, bf16[32,512]{1,0:T(8,128)(2,1)S(1)}, u32[]{:S(2)}, u32[]{:S(2)}) collective-permute-start(bf16[32,512]{1,0:T(8,128)(2,1)S(1)} %slice_select_fusion), channel_id=1, source_target_pairs={{0,33},{33,0},{1,32},{32,1},{2,35},{35,2},{3,34},{34,3},{4,37},{37... | collective-permute-start | bytes 98312 | tf_op jit(solution)/shard_map/ppermute | solution.py:33
  (146 shorter events, 62.8 us)
Async XLA Ops:
  0.6 48.4 %collective-permute-start.5 = (bf16[256,1024]{1,0:T(8,128)(2,1)}, bf16[256,1024]{1,0:T(8,128)(2,1)}, u32[]{:S(2)}, u32[]{:S(2)}) collective-permute-start(bf16[256,1024]{1,0:T(8,128)(2,1)} %bitcast.24), channel_id=1, source_target_pairs={{0,32},{32,0},{1,33},{33,1},{2,34},{34,2},{3,35},{35,3},{4,36},{36... | collective-permute-start | bytes 1572872 | tf_op jit(solution)/shard_map/ppermute | solution.py:29
  2.8 46.2 %collective-permute-start.4 = (bf16[256,1024]{1,0:T(8,128)(2,1)}, bf16[256,1024]{1,0:T(8,128)(2,1)}, u32[]{:S(2)}, u32[]{:S(2)}) collective-permute-start(bf16[256,1024]{1,0:T(8,128)(2,1)} %bitcast.25), channel_id=1, source_target_pairs={{0,33},{33,0},{1,32},{32,1},{2,35},{35,2},{3,34},{34,3},{4,37},{37... | collective-permute-start | bytes 1572872 | tf_op jit(solution)/shard_map/ppermute | solution.py:33
  6.2 29.1 %collective-permute-start.2 = (f32[256,1024]{1,0:T(8,128)}, f32[256,1024]{1,0:T(8,128)}, u32[]{:S(2)}, u32[]{:S(2)}) collective-permute-start(f32[256,1024]{1,0:T(8,128)} %own_tiles.1), channel_id=1, source_target_pairs={{0,1},{1,0},{2,3},{3,2},{4,5},{5,4},{6,7},{7,6},{8,9},{9,8},{10,11... | collective-permute-start | bytes 3145736 | tf_op jit(solution)/shard_map/ppermute | solution.py:25
  11.3 36.9 %all-to-all-start = ((bf16[16,64,1024]{2,1,0:T(8,128)(2,1)}), bf16[16,64,1024]{2,1,0:T(8,128)(2,1)S(1)}, u32[]{:S(2)}, u32[]{:S(2)}) async-start(bf16[16,64,1024]{2,1,0:T(8,128)(2,1)} %shard_map.155), calls=%async_computation | async-start | bytes 4194304 | tf_op jit(solution)/shard_map/all_to_all | solution.py:41
  52.3 3.4 %collective-permute-start.6 = (bf16[256,1024]{1,0:T(8,128)(2,1)S(1)}, bf16[256,1024]{1,0:T(8,128)(2,1)S(1)}, u32[]{:S(2)}, u32[]{:S(2)}) collective-permute-start(bf16[256,1024]{1,0:T(8,128)(2,1)S(1)} %get-tuple-element.39), channel_id=1, source_target_pairs={{0,1},{1,0},{2,3},{3,2},{4,5},{5,4},{6,7},{7,6},{8,9},{9,8},{10,11... | collective-permute-start | bytes 1572872 | tf_op jit(solution)/shard_map/ppermute | solution.py:25
  54.2 3.1 %collective-permute-start = (bf16[256,1024]{1,0:T(8,128)(2,1)S(1)}, bf16[256,1024]{1,0:T(8,128)(2,1)S(1)}, u32[]{:S(2)}, u32[]{:S(2)}) collective-permute-start(bf16[256,1024]{1,0:T(8,128)(2,1)S(1)} %bitcast.26), channel_id=1, source_target_pairs={{0,1},{1,0},{2,3},{3,2},{4,5},{5,4},{6,7},{7,6},{8,9},{9,8},{10,11... | collective-permute-start | bytes 1572872 | tf_op jit(solution)/shard_map/ppermute | solution.py:25
  55.9 20.0 %collective-permute-start.7 = (bf16[256,1024]{1,0:T(8,128)(2,1)S(1)}, bf16[256,1024]{1,0:T(8,128)(2,1)S(1)}, u32[]{:S(2)}, u32[]{:S(2)}) collective-permute-start(bf16[256,1024]{1,0:T(8,128)(2,1)S(1)} %add_convert_fusion), channel_id=1, source_target_pairs={{0,32},{32,0},{1,33},{33,1},{2,34},{34,2},{3,35},{35,3},{4,36},{36... | collective-permute-start | bytes 1572872 | tf_op jit(solution)/shard_map/ppermute | solution.py:29
  60.1 15.8 %collective-permute-start.3 = (bf16[256,1024]{1,0:T(8,128)(2,1)S(1)}, bf16[256,1024]{1,0:T(8,128)(2,1)S(1)}, u32[]{:S(2)}, u32[]{:S(2)}) collective-permute-start(bf16[256,1024]{1,0:T(8,128)(2,1)S(1)} %get-tuple-element.37), channel_id=1, source_target_pairs={{0,1},{1,0},{2,3},{3,2},{4,5},{5,4},{6,7},{7,6},{8,9},{9,8},{10,11... | collective-permute-start | bytes 1572872 | tf_op jit(solution)/shard_map/ppermute | solution.py:25
  78.7 11.7 %all-to-all-start.2 = ((bf16[16,8,1024]{2,1,0:T(8,128)(2,1)}), bf16[16,8,1024]{2,1,0:T(8,128)(2,1)S(1)}, u32[]{:S(2)}, u32[]{:S(2)}) async-start(bf16[16,8,1024]{2,1,0:T(8,128)(2,1)} %bitcast.31), calls=%async_computation.2 | async-start | bytes 524288 | tf_op jit(solution)/shard_map/all_to_all | solution.py:41
  97.4 11.4 %all-to-all-start.3 = ((bf16[16,8,1280]{2,1,0:T(8,128)(2,1)}), bf16[16,8,1280]{2,1,0:T(8,128)(2,1)S(1)}, u32[]{:S(2)}, u32[]{:S(2)}) async-start(bf16[16,8,1280]{2,1,0:T(8,128)(2,1)} %bitcast.32), calls=%async_computation.3 | async-start | bytes 655360 | tf_op jit(solution)/shard_map/all_to_all | solution.py:407
  102.9 34.1 %collective-permute-start.18 = (bf16[256,1152]{1,0:T(8,128)(2,1)}, bf16[256,1152]{1,0:T(8,128)(2,1)}, u32[]{:S(2)}, u32[]{:S(2)}) collective-permute-start(bf16[256,1152]{1,0:T(8,128)(2,1)} %copy-done.12), channel_id=1, source_target_pairs={{0,1},{1,0},{2,3},{3,2},{4,5},{5,4},{6,7},{7,6},{8,9},{9,8},{10,11... | collective-permute-start | bytes 1769480 | tf_op jit(solution)/shard_map/ppermute | solution.py:25
  105.4 31.6 %collective-permute-start.17 = (bf16[256,1152]{1,0:T(8,128)(2,1)}, bf16[256,1152]{1,0:T(8,128)(2,1)}, u32[]{:S(2)}, u32[]{:S(2)}) collective-permute-start(bf16[256,1152]{1,0:T(8,128)(2,1)} %copy-done.12), channel_id=1, source_target_pairs={{0,32},{32,0},{1,33},{33,1},{2,34},{34,2},{3,35},{35,3},{4,36},{36... | collective-permute-start | bytes 1769480 | tf_op jit(solution)/shard_map/ppermute | solution.py:29
  105.6 31.4 %collective-permute-start.16 = (bf16[256,1152]{1,0:T(8,128)(2,1)}, bf16[256,1152]{1,0:T(8,128)(2,1)}, u32[]{:S(2)}, u32[]{:S(2)}) collective-permute-start(bf16[256,1152]{1,0:T(8,128)(2,1)} %copy-done.12), channel_id=1, source_target_pairs={{0,33},{33,0},{1,32},{32,1},{2,35},{35,2},{3,34},{34,3},{4,37},{37... | collective-permute-start | bytes 1769480 | tf_op jit(solution)/shard_map/ppermute | solution.py:33
  115.0 37.0 %collective-permute-start.8 = (f32[256,1024]{1,0:T(8,128)}, f32[256,1024]{1,0:T(8,128)}, u32[]{:S(2)}, u32[]{:S(2)}) collective-permute-start(f32[256,1024]{1,0:T(8,128)} %slice.43), channel_id=1, source_target_pairs={{0,1},{1,0},{2,3},{3,2},{4,5},{5,4},{6,7},{7,6},{8,9},{9,8},{10,11... | collective-permute-start | bytes 3145736 | tf_op jit(solution)/shard_map/ppermute | solution.py:25
  120.9 12.8 %collective-permute-start.14 = (f32[8,1024]{1,0:T(8,128)S(1)}, f32[8,1024]{1,0:T(8,128)S(1)}, u32[]{:S(2)}, u32[]{:S(2)}) collective-permute-start(f32[8,1024]{1,0:T(8,128)S(1)} %get-tuple-element.52.refs_3_), channel_id=1, source_target_pairs={{0,32},{32,0},{1,33},{33,1},{2,34},{34,2},{3,35},{35,3},{4,36},{36... | collective-permute-start | bytes 98312 | tf_op jit(solution)/shard_map/ppermute | solution.py:29
  133.7 3.3 %collective-permute-start.13 = (f32[8,1024]{1,0:T(8,128)S(1)}, f32[8,1024]{1,0:T(8,128)S(1)}, u32[]{:S(2)}, u32[]{:S(2)}) collective-permute-start(f32[8,1024]{1,0:T(8,128)S(1)} %get-tuple-element.52.refs_3_), channel_id=1, source_target_pairs={{0,33},{33,0},{1,32},{32,1},{2,35},{35,2},{3,34},{34,3},{4,37},{37... | collective-permute-start | bytes 98312 | tf_op jit(solution)/shard_map/ppermute | solution.py:33
  145.0 32.6 %all-to-all-start.4 = ((bf16[16,64,1024]{2,1,0:T(8,128)(2,1)}), bf16[16,64,1024]{2,1,0:T(8,128)(2,1)S(1)}, u32[]{:S(2)}, u32[]{:S(2)}) async-start(bf16[16,64,1024]{2,1,0:T(8,128)(2,1)} %copy-done), calls=%async_computation.4 | async-start | bytes 4194304 | tf_op jit(solution)/shard_map/all_to_all | solution.py:428
  153.7 6.5 %collective-permute-start.9 = (bf16[128,1024]{1,0:T(8,128)(2,1)S(1)}, bf16[128,1024]{1,0:T(8,128)(2,1)S(1)}, u32[]{:S(2)}, u32[]{:S(2)}) collective-permute-start(bf16[128,1024]{1,0:T(8,128)(2,1)S(1)} %get-tuple-element.65), channel_id=1, source_target_pairs={{0,32},{32,0},{1,33},{33,1},{2,34},{34,2},{3,35},{35,3},{4,36},{36... | collective-permute-start | bytes 786440 | tf_op jit(solution)/shard_map/ppermute | solution.py:29
  154.9 8.1 %collective-permute-start.11 = (bf16[128,1024]{1,0:T(8,128)(2,1)S(1)}, bf16[128,1024]{1,0:T(8,128)(2,1)S(1)}, u32[]{:S(2)}, u32[]{:S(2)}) collective-permute-start(bf16[128,1024]{1,0:T(8,128)(2,1)S(1)} %get-tuple-element.66), channel_id=1, source_target_pairs={{0,96},{96,0},{32,64},{64,32},{1,97},{97,1},{33,65},{65,33},{2,98}... | collective-permute-start | bytes 786440 | tf_op jit(solution)/shard_map/ppermute | solution.py:37
  163.9 7.5 %collective-permute-start.10 = (bf16[128,1024]{1,0:T(8,128)(2,1)}, bf16[128,1024]{1,0:T(8,128)(2,1)}, u32[]{:S(2)}, u32[]{:S(2)}) collective-permute-start(bf16[128,1024]{1,0:T(8,128)(2,1)} %get-tuple-element.63), channel_id=1, source_target_pairs={{0,96},{96,0},{32,64},{64,32},{1,97},{97,1},{33,65},{65,33},{2,98}... | collective-permute-start | bytes 786440 | tf_op jit(solution)/shard_map/ppermute | solution.py:37
  165.0 18.6 %collective-permute-start.12 = (bf16[128,1024]{1,0:T(8,128)(2,1)S(1)}, bf16[128,1024]{1,0:T(8,128)(2,1)}, u32[]{:S(2)}, u32[]{:S(2)}) collective-permute-start(bf16[128,1024]{1,0:T(8,128)(2,1)S(1)} %get-tuple-element.64), channel_id=1, source_target_pairs={{0,32},{32,0},{1,33},{33,1},{2,34},{34,2},{3,35},{35,3},{4,36},{36... | collective-permute-start | bytes 786440 | tf_op jit(solution)/shard_map/ppermute | solution.py:29
  178.1 7.8 %collective-permute-start.19 = (bf16[64,1024]{1,0:T(8,128)(2,1)S(1)}, bf16[64,1024]{1,0:T(8,128)(2,1)S(1)}, u32[]{:S(2)}, u32[]{:S(2)}) collective-permute-start(bf16[64,1024]{1,0:T(8,128)(2,1)S(1)} %shard_map.162), channel_id=1, source_target_pairs={{0,96},{96,0},{32,64},{64,32},{1,97},{97,1},{33,65},{65,33},{2,98}... | collective-permute-start | bytes 393224 | tf_op jit(solution)/shard_map/ppermute | solution.py:37
  186.0 7.4 %collective-permute-start.22 = (bf16[32,512]{1,0:T(8,128)(2,1)S(1)}, bf16[32,512]{1,0:T(8,128)(2,1)S(1)}, u32[]{:S(2)}, u32[]{:S(2)}) collective-permute-start(bf16[32,512]{1,0:T(8,128)(2,1)S(1)} %slice_select_fusion), channel_id=1, source_target_pairs={{0,33},{33,0},{1,32},{32,1},{2,35},{35,2},{3,34},{34,3},{4,37},{37... | collective-permute-start | bytes 98312 | tf_op jit(solution)/shard_map/ppermute | solution.py:33
  190.5 4.6 %collective-permute-start.20 = (bf16[64,1024]{1,0:T(8,128)(2,1)S(1)}, bf16[64,1024]{1,0:T(8,128)(2,1)S(1)}, u32[]{:S(2)}, u32[]{:S(2)}) collective-permute-start(bf16[64,1024]{1,0:T(8,128)(2,1)S(1)} %add_convert_fusion.3.own), channel_id=1, source_target_pairs={{0,32},{32,0},{1,33},{33,1},{2,34},{34,2},{3,35},{35,3},{4,36},{36... | collective-permute-start | bytes 393224 | tf_op jit(solution)/shard_map/ppermute | solution.py:29
  (37 other events, 419.0 us)

commit v2 on v1

--- a/solution.py
+++ b/solution.py
@@ -33,8 +33,16 @@
     return lax.ppermute(a, ("l", "c"), [(0, 3), (3, 0), (1, 2), (2, 1)])
 
 
+def swap_far(a):
+    return lax.ppermute(a, "h", [(0, 1), (1, 0)])
+
+
 def swap_wrap(a):
     return lax.ppermute(a, ("h", "l"), [(0, 3), (3, 0), (1, 2), (2, 1)])
+
+
+def round_bf16(a):
+    return lax.reduce_precision(a, 8, 7)
 
 
 def gather_chips(a):
@@ -70,15 +78,16 @@
         theirs[:, i * 128 : i * 128 + 128] = got[:, 128:]
 
 
-def lay_kernel(meta, mine, theirs, w_out, out):
+def lay_kernel(meta, mine, theirs, w_out, out, block, sems):
     core, role = meta[0], meta[1]
-    top = jnp.where(role == 0, w_out[:32], w_out[32:])
-    first = jnp.where(core == 0, mine[...], theirs[...])
-    second = jnp.where(core == 0, theirs[...], mine[...])
-    for i in range(out.shape[0]):
-        out[i, :32] = top
-        out[i, 32:, :512] = first
-        out[i, 32:, 512:] = second
+    block[:32] = jnp.where(role == 0, w_out[:32], w_out[32:])
+    block[32:, :512] = jnp.where(core == 0, mine[...], theirs[...])
+    block[32:, 512:] = jnp.where(core == 0, theirs[...], mine[...])
+    copies = [pltpu.make_async_copy(block, out.at[i], sems.at[i]) for i in range(16)]
+    for copy in copies:
+        copy.start()
+    for copy in copies:
+        copy.wait()
 
 
 def forward_kernel(tok_a, tok_b, weights, part_a, part_b, hidden, slope, w_in, w_out, sems):
@@ -151,20 +160,22 @@
     emb[...] = jnp.concatenate([docs] * 16, axis=0).astype(BF16)
 
 
-def score_kernel(emb, own_tiles, oth_tiles, live, packed, weighted):
-    docs = emb[...].astype(F32)
-    for k, tiles in enumerate((own_tiles, oth_tiles)):
-        at = pl.ds(k * 256, 256)
-        scores = lax.dot_general(
-            docs, tiles[...], LAST, precision=lax.Precision.HIGHEST, preferred_element_type=F32
-        )
-        weighted[:, at] = live[:, at] * jnp.exp(scores)
-    value = weighted[...]
-    part_emb = jnp.dot(
-        value[:, :256], own_tiles[...], precision=lax.Precision.HIGHEST, preferred_element_type=F32
-    ) + jnp.dot(
-        value[:, 256:], oth_tiles[...], precision=lax.Precision.HIGHEST, preferred_element_type=F32
-    )
+def score_kernel(emb, tiles_hi, tiles_lo, live, packed, weighted, emb_buf, sem):
+    copy = pltpu.make_async_copy(emb, emb_buf, sem)
+    copy.start()
+    grow = (iota((128, 512), 0) == iota((128, 512), 1) // LPC).astype(BF16)
+    mask = jnp.dot(live[...], grow, preferred_element_type=F32)
+    copy.wait()
+    docs = emb_buf[...]
+    scores = lax.dot_general(docs, tiles_hi[...], LAST, preferred_element_type=F32)
+    scores = scores + lax.dot_general(docs, tiles_lo[...], LAST, preferred_element_type=F32)
+    value = mask * jnp.exp(scores)
+    weighted[...] = value
+    value_hi = value.astype(BF16)
+    value_lo = (value - value_hi.astype(F32)).astype(BF16)
+    part_emb = jnp.dot(value_hi, tiles_hi[...], preferred_element_type=F32)
+    part_emb = part_emb + jnp.dot(value_hi, tiles_lo[...], preferred_element_type=F32)
+    part_emb = part_emb + jnp.dot(value_lo, tiles_hi[...], preferred_element_type=F32)
     sums = jnp.sum(value, axis=1, keepdims=True) * 0.5
     high = sums.astype(BF16).astype(F32)
     row, lane = iota((128, 128), 0), iota((128, 128), 1)
@@ -178,7 +189,15 @@
     packed[:, :1024] = part_emb.astype(BF16)
 
 
-def settle_kernel(meta, got, pos, emb, grad, loss, sums):
+def settle_kernel(meta, got_hbm, pos_hbm, emb, grad, loss, sums, got, pos, sems):
+    copies = [
+        pltpu.make_async_copy(got_hbm, got, sems.at[0]),
+        pltpu.make_async_copy(pos_hbm, pos, sems.at[1]),
+    ]
+    for copy in copies:
+        copy.start()
+    for copy in copies:
+        copy.wait()
     total = got[0].astype(F32)
     for i in range(1, 16):
         total = total + got[i].astype(F32)
@@ -195,7 +214,8 @@
     grads, gain = refs[:4], refs[4]
     rows, toks = refs[5:9], refs[9:13]
     hiddens, slopes, weights, out = refs[13:15], refs[15:17], refs[17], refs[18]
-    row_buf, tok_buf, hid_buf, slope_buf, w_out, sum_grad, act_grad, sems = refs[19:]
+    row_buf, tok_buf, hid_buf, slope_buf, w_out, sum_grad, act_grad, result, sems = refs[19:]
+    sent = []
     first = pltpu.make_async_copy(weights.at[:, 0:32], w_out, sems.at[0])
     first.start()
     row_copies, tok_copies, hid_copies, slope_copies = [], [], [], []
@@ -247,15 +267,23 @@
         part = lax.dot_general(
             hid_buf[:, i * 128 : i * 128 + 128], sum_grad[...], FIRST, preferred_element_type=F32
         )
-        out[i * 4 : i * 4 + 4, :32] = part.astype(BF16).reshape(4, 32, 1024)
+        at = pl.ds(i * 4, 4)
+        result[at, :32] = part.astype(BF16).reshape(4, 32, 1024)
+        sent.append(pltpu.make_async_copy(result.at[at, 0:32], out.at[at, 0:32], sems.at[13 + i]))
+        sent[-1].start()
     for copy in tok_copies:
         copy.wait()
     for i in range(4):
         part = lax.dot_general(
             tok_buf[:, i * 256 : i * 256 + 256], act_grad[...], FIRST, preferred_element_type=F32
         ).astype(BF16).reshape(4, 2, 32, 512)
-        out[i * 4 : i * 4 + 4, 32:, :512] = part[:, 0]
-        out[i * 4 : i * 4 + 4, 32:, 512:] = part[:, 1]
+        at = pl.ds(i * 4, 4)
+        result[at, 32:, :512] = part[:, 0]
+        result[at, 32:, 512:] = part[:, 1]
+        sent.append(pltpu.make_async_copy(result.at[at, 32:64], out.at[at, 32:64], sems.at[17 + i]))
+        sent[-1].start()
+    for copy in sent:
+        copy.wait()
 
 
 def backward(grads, gain, rows, toks, hiddens, slopes, weights):
@@ -263,7 +291,7 @@
         backward_kernel,
         out_shape=shape((16, 64, 1024), BF16),
         in_specs=[WHOLE] * 5 + [ANYWHERE] * 13,
-        out_specs=WHOLE,
+        out_specs=ANYWHERE,
         scratch_shapes=[
             pltpu.VMEM((1024, 1152), BF16),
             pltpu.VMEM((1024, 1024), BF16),
@@ -272,40 +300,51 @@
             pltpu.VMEM((16, 32, 1024), BF16),
             pltpu.VMEM((1024, 1024), BF16),
             pltpu.VMEM((1024, 512), BF16),
-            pltpu.SemaphoreType.DMA((13,)),
+            pltpu.VMEM((16, 64, 1024), BF16),
+            pltpu.SemaphoreType.DMA((21,)),
         ],
         compiler_params=LIMIT,
         cost_estimate=cost(3 * 2**30, 10 * 2**20),
     )(*grads, gain, *rows, *toks, *hiddens, *slopes, weights)
 
 
-def total_kernel(got, out):
+def total_kernel(meta, got, out, keep, give):
     total = got[0].astype(F32)
     for i in range(1, 16):
         total = total + got[i].astype(F32)
-    out[...] = total.astype(BF16)
-
-
-def place_kernel(meta, own, near, core_part, diag_part, grad_in, grad_out):
+    total = total.astype(BF16)
+    core, step = meta[0], pl.program_id(0)
+
+    @pl.when(step < 2)
+    def _():
+        out[...] = total
+
+    @pl.when(step >= 2)
+    def _():
+        keep[...] = jnp.where(core == 0, total[:, :512], total[:, 512:])
+        give[...] = jnp.where(core == 0, total[:, 512:], total[:, :512])
+
+
+def place_kernel(meta, own, near, wrap, far, grad_in, grad_out):
     core, role = meta[0], meta[1]
-    mine, theirs = own[:32].astype(F32), near[:32].astype(F32)
+    mine = own[:32].astype(F32) + wrap[:32].astype(F32)
+    theirs = near[:32].astype(F32) + far[:32].astype(F32)
     grad_out[:32] = jnp.where(role == 0, mine, theirs)
     grad_out[32:] = jnp.where(role == 0, theirs, mine)
-    pieces = (
-        jnp.where(core == 0, own[32:, :512], own[32:, 512:]),
-        core_part[...],
-        jnp.where(core == 0, near[32:, :512], near[32:, 512:]),
-        diag_part[...],
-    )
-    row, lane = iota((512, 512), 0), iota((512, 512), 1)
+    row, lane = iota((1024, 512), 0), iota((1024, 512), 1)
     piece, at = row // 128, row % 128
-    swapped = piece % 2
-    part = (core + swapped - 2 * core * swapped) * 2
-    flipped = piece // 2
-    part = part + role + flipped - 2 * role * flipped
+    swapped, flipped = piece % 2, piece // 4
+    part = (core + swapped - 2 * core * swapped) * 2 + (role + flipped - 2 * role * flipped)
     spread = (lane == at // 32 * 128 + part * 32 + at % 32).astype(BF16)
     for i in range(4):
-        block = jnp.concatenate([a[:, i * 128 : i * 128 + 128] for a in pieces], axis=1)
+        block = jnp.concatenate(
+            [
+                a[32:, k * 512 + i * 128 : k * 512 + i * 128 + 128]
+                for a in (own, wrap, near, far)
+                for k in range(2)
+            ],
+            axis=1,
+        )
         grad_in[:, i * 512 : i * 512 + 512] = jnp.dot(block, spread, preferred_element_type=F32)
 
 
@@ -342,9 +381,9 @@
         pl.pallas_call(
             lay_kernel,
             out_shape=shape((16, 64, width), BF16),
-            grid=(4,),
             in_specs=[SCALARS, WHOLE, WHOLE, WHOLE],
-            out_specs=pl.BlockSpec((4, 64, width), lambda i: (i, 0, 0)),
+            out_specs=ANYWHERE,
+            scratch_shapes=[pltpu.VMEM((64, width), BF16), pltpu.SemaphoreType.DMA((16,))],
             cost_estimate=cost(0, 2**21),
         )(meta, mine, swap_core(theirs), w_out)
     )
@@ -362,20 +401,22 @@
     short, posit = pick(shortlist), pick(positives)
     cluster_live = jnp.max(
         (short[:, :, None] == cluster_ids[None, None, :]).astype(F32), axis=1
-    )
-    live = jnp.repeat(cluster_live, LPC, axis=1)
+    ).astype(BF16)
+    tiles = jnp.concatenate([label_tiles, oth_tiles], axis=0)
+    tiles_top = round_bf16(tiles)
+    tiles_hi, tiles_lo = tiles_top.astype(BF16), (tiles - tiles_top).astype(BF16)
     cluster_hit = (posit[:, :, None] // LPC == cluster_ids[None, None, :]).astype(F32)
     offset_hit = (
         posit[:, :, None] % LPC == jnp.arange(LPC, dtype=jnp.int32)[None, None, :]
     ).astype(F32)
     hits = jnp.sum(cluster_hit[:, :, :, None] * offset_hit[:, :, None, :], axis=1).reshape(128, 512)
     share_hit = hits / POS
-    pos_part = (
-        jnp.dot(share_hit[:, :256], label_tiles, precision=lax.Precision.HIGH)
-        + jnp.dot(share_hit[:, 256:], oth_tiles, precision=lax.Precision.HIGH)
-    )
-    weights, live, share_hit, pos_part = lax.optimization_barrier(
-        (weights, live, share_hit, pos_part)
+    hit = share_hit.astype(BF16)
+    pos_part = jnp.dot(hit, tiles_hi, preferred_element_type=F32) + jnp.dot(
+        hit, tiles_lo, preferred_element_type=F32
+    )
+    weights, cluster_live, share_hit, pos_part, tiles_hi, tiles_lo = lax.optimization_barrier(
+        (weights, cluster_live, share_hit, pos_part, tiles_hi, tiles_lo)
     )
 
     near_a, near_b, near_hidden, near_slope = forward(diag_tok, near_tok, weights)
@@ -395,21 +436,29 @@
     )(lengths, own_tok, own_b, swap_core(own_a), from_near, gain)
 
     plane_emb = gather_chips(emb.reshape(16, docs, width)).reshape(128, width)
-    core_rows, near_rows, diag_rows = swap_core(own_rows), swap_near(own_rows), swap_diag(own_rows)
+    near_rows = swap_near(own_rows)
     packed, weighted = pl.pallas_call(
         score_kernel,
         out_shape=(shape((128, 1280), BF16), shape((128, 512), F32)),
-        in_specs=[WHOLE] * 4,
+        in_specs=[ANYWHERE] + [WHOLE] * 3,
         out_specs=(WHOLE, WHOLE),
-        compiler_params=LIMIT,
-        cost_estimate=cost(2**30, 5 * 2**20, 2**16),
-    )(plane_emb, label_tiles, oth_tiles, live)
+        scratch_shapes=[pltpu.VMEM((128, width), BF16), pltpu.SemaphoreType.DMA],
+        compiler_params=LIMIT,
+        cost_estimate=cost(2**29, 3 * 2**20, 2**16),
+    )(plane_emb, tiles_hi, tiles_lo, cluster_live)
+    packed, near_rows = lax.optimization_barrier((packed, near_rows))
+    core_rows, diag_rows = swap_core(own_rows), swap_core(near_rows)
     got = lax.all_to_all(packed.reshape(16, docs, 1280), CHIPS, 0, 0, tiled=True)
     emb_grad, loss, sums = pl.pallas_call(
         settle_kernel,
         out_shape=(shape((docs, width), F32), shape((docs, 128), F32), shape((docs, 128), F32)),
-        in_specs=[SCALARS, WHOLE, WHOLE, WHOLE],
+        in_specs=[SCALARS, ANYWHERE, ANYWHERE, WHOLE],
         out_specs=(WHOLE,) * 3,
+        scratch_shapes=[
+            pltpu.VMEM((16, docs, 1280), BF16),
+            pltpu.VMEM((16, docs, width), F32),
+            pltpu.SemaphoreType.DMA((2,)),
+        ],
         compiler_params=LIMIT,
         cost_estimate=cost(2**20, 2**20),
     )(meta, got, pos_got, emb)
@@ -425,18 +474,22 @@
         (near_slope, own_slope),
         weights,
     )
+    send, weighted = lax.optimization_barrier((send, weighted))
     got = lax.all_to_all(send, CHIPS, 0, 0, tiled=True)
-    part = pl.pallas_call(
+    part, keep, give = pl.pallas_call(
         total_kernel,
-        out_shape=shape((64, width), BF16),
+        out_shape=(shape((32, width), BF16), shape((32, 512), BF16), shape((32, 512), BF16)),
         grid=(4,),
-        in_specs=[pl.BlockSpec((16, 16, width), lambda i: (0, i, 0))],
-        out_specs=pl.BlockSpec((16, width), lambda i: (i, 0)),
+        in_specs=[SCALARS, pl.BlockSpec((16, 16, width), lambda i: (0, i, 0))],
+        out_specs=(
+            pl.BlockSpec((16, width), lambda i: (jnp.minimum(i, 1), 0)),
+            pl.BlockSpec((16, 512), lambda i: (jnp.maximum(i - 2, 0), 0)),
+            pl.BlockSpec((16, 512), lambda i: (jnp.maximum(i - 2, 0), 0)),
+        ),
         compiler_params=LIMIT,
         cost_estimate=cost(2**20, 2**21),
-    )(got)
-    both = (part.astype(F32) + swap_wrap(part).astype(F32)).astype(BF16)
-    give = jnp.where(core == 0, both[32:, 512:], both[32:, :512])
+    )(meta, got)
+    both = jnp.concatenate([part, jnp.concatenate([keep, swap_core(give)], axis=1)], axis=0)
     grad_in, grad_out = pl.pallas_call(
         place_kernel,
         out_shape=(shape((32, 2048), F32), shape((64, width), F32)),
@@ -444,7 +497,7 @@
         out_specs=(WHOLE, WHOLE),
         compiler_params=LIMIT,
         cost_estimate=cost(2**26, 2**20),
-    )(meta, both, swap_near(both), swap_core(give), swap_diag(give))
+    )(meta, both, swap_near(both), swap_wrap(both), swap_far(both))
 
     all_sums = sums[:, :16].T.reshape(128)
     logit_grad = weighted / all_sums[:, None] - share_hit

time: 198 us -> 189 us (0.955)
  starting transfers between devices: 54.5 us -> 47 us
  Pallas kernels: 25.3 us -> 27.7 us
    ppermute x7, waiting for transfers between devices: 17.7 us -> 5.74 us  [swap_near(): return lax.ppermute(a, 'l', [(0, 1), (1, 0)])]
    ppermute x4 -> x2, starting transfers between devices: 7.99 us -> 1.35 us  [swap_diag(): return lax.ppermute(a, ('l', 'c'), [(0, 3), (3, 0), (1, 2), (2, 1)])]
    all_to_all x1, waiting for transfers between devices: 4.34 us -> 9.52 us  [on_device(): got = lax.all_to_all(send, CHIPS, 0, 0, tiled=True)]
    all_to_all x1, waiting for transfers between devices: 1.74 us -> 5.79 us  [on_device(): lax.all_to_all(packed.reshape(16, docs, 1280), CHIPS, 0, 0, tiled=True)]
    all_to_all x2, waiting for transfers between devices: 16 us -> 20 us  [gather_chips(): return lax.all_to_all(a, CHIPS, 0, 0, tiled=True)]
    all_to_all x1, starting transfers between devices: 6.94 us -> 3.72 us  [on_device(): got = lax.all_to_all(send, CHIPS, 0, 0, tiled=True)]
    ppermute x9 -> x10, starting transfers between devices: 9.35 us -> 12.6 us  [swap_core(): return lax.ppermute(a, 'c', [(0, 1), (1, 0)])]
    ppermute x3, starting transfers between devices: 8.37 us -> 5.19 us  [swap_wrap(): return lax.ppermute(a, ('h', 'l'), [(0, 3), (3, 0), (1, 2), (2, 1)])]
  transfers between devices with their start and end apart: 27 -> 27, of which waited for: 13 -> 12; matrix products, arithmetic and copies ran while one was open for 18% -> 14% of each run, Pallas kernels for 7% -> 6%
where the time goes in v2:
time: 189 us; the launch traced here: 188 us
  waiting for transfers between devices  54.7 us (29%)
  starting transfers between devices  47 us (25%)
  Pallas kernels  27.7 us (15%)
  local copies, waits for them, and re-layouts  20.1 us (11%)
  other arithmetic  18.6 us (10%)
  blocking collectives  15 us (8%)
  matrix products  3.67 us (2%)
    all_to_all x2, waiting for transfers between devices, gather_chips(): return lax.all_to_all(a, CHIPS, 0, 0, tiled=True)  20 us
    all_to_all x1, blocking collectives, gather_chips(): return lax.all_to_all(a, CHIPS, 0, 0, tiled=True)  15 us
    unnamed x70, local copies, waits for them, and re-layouts  12.7 us
    ppermute x10, starting transfers between devices, swap_core(): return lax.ppermute(a, 'c', [(0, 1), (1, 0)])  12.6 us
    all_to_all x2, starting transfers between devices, gather_chips(): return lax.all_to_all(a, CHIPS, 0, 0, tiled=True)  12 us
    reduce_max x1, other arithmetic, on_device(): jnp.max((short[:, :, None] == cluster_ids[None, None, :]).astype(F32), ax...  9.89 us
    all_to_all x1, waiting for transfers between devices, on_device(): got = lax.all_to_all(send, CHIPS, 0, 0, tiled=True)  9.52 us
    ppermute x3, waiting for transfers between devices, swap_wrap(): return lax.ppermute(a, ('h', 'l'), [(0, 3), (3, 0), (1, 2), (2, 1)])  9.01 us
  transfers between devices with their start and end apart: 27, of which 12 were waited for; matrix products, arithmetic and copies ran while one was open for 14% of the time, Pallas kernels for 6%

profile of v2, /device:TPU:1, one launch (start us, length us, event | category | flops | bytes accessed | tf_op | source)
XLA Modules:
  0.0 187.9 jit_solution(7181348131939613736)
XLA Ops:
  10.1 2.5 %shard_map.155 = bf16[16,64,1024]{2,1,0:T(8,128)(2,1)} custom-call(s32[3]{0:T(128)} %pad_add_fusion.meta, bf16[32,512]{1,0:T(8,128)(2,1)} %get-tuple-element.42.mine, bf16[32,512]{1,0:T(8,128)(2,1)} %copy-done.33, bf16[64,1024]{1,0:T(8,128)(2,1)} %w_out.1), custom_call_target="tpu_custom_call" | custom-call | bytes 2097152 | tf_op jit(solution)/shard_map/pallas_call | solution.py:381
  12.6 7.9 %all-to-all-start = ((bf16[16,64,1024]{2,1,0:T(8,128)(2,1)}), bf16[16,64,1024]{2,1,0:T(8,128)(2,1)}, u32[]{:S(2)}, u32[]{:S(2)}) async-start(bf16[16,64,1024]{2,1,0:T(8,128)(2,1)} %shard_map.155), calls=%async_computation | async-start | bytes 4194304 | tf_op jit(solution)/shard_map/all_to_all | solution.py:49
  21.8 9.9 %convert_reduce_fusion.live = bf16[128,128]{1,0:T(8,128)(2,1)S(1)} fusion(s32[128]{0:T(128)S(1)} %select_reduce_fusion, s32[128,400]{1,0:T(8,128)S(1)} %dynamic-slice_bitcast_fusion), kind=kLoop, calls=%fused_computation | loop fusion | flops 19644416 | bytes 238080 | tf_op jit(solution)/shard_map/reduce_max | solution.py:402
  35.0 14.6 %all-to-all-done.weights.refs_17_ = bf16[16,64,1024]{2,1,0:T(8,128)(2,1)} async-done(((bf16[16,64,1024]{2,1,0:T(8,128)(2,1)}), bf16[16,64,1024]{2,1,0:T(8,128)(2,1)}, u32[]{:S(2)}, u32[]{:S(2)}) %all-to-all-start) | async-done | bytes 2097184 | tf_op jit(solution)/shard_map/all_to_all | solution.py:49
  49.6 4.3 %shard_map.157 = (bf16[256,1024]{1,0:T(8,128)(2,1)S(1)}, f32[256,1024]{1,0:T(8,128)S(1)}, bf16[512,512]{1,0:T(8,128)(2,1)S(1)}, f32[512,512]{1,0:T(8,128)S(1)}) custom-call(bf16[256,1024]{1,0:T(8,128)(2,1)} %collective-permute-done.4.tok_a.refs_9_, bf16[256,1024]{1,0:T(8,128)(2,1)S(1)} %collective-permute-done.5.tok_b.refs_10_, ...), custom_call_target="tpu_custom_call" | custom-call | flops 1073741824 | bytes 6291456 | tf_op jit(solution)/shard_map/pallas_call | solution.py:121
  58.9 3.2 %shard_map.156 = (bf16[256,1024]{1,0:T(8,128)(2,1)S(1)}, f32[256,1024]{1,0:T(8,128)S(1)}, bf16[512,512]{1,0:T(8,128)(2,1)S(1)}, f32[512,512]{1,0:T(8,128)S(1)}) custom-call(bf16[256,1024]{1,0:T(8,128)(2,1)S(1)} %collective-permute-done.tok_a.refs_11_, bf16[256,1024]{1,0:T(8,128)(2,1)S(1)} %bitcast.27, bf16[16,64,1024]{2,1,0:T(8,128)(2,1)} %all-to-all-done.weights.refs_17_), custom_call_target="tpu_custom_call" | custom-call | flops 1073741824 | bytes 6291456 | tf_op jit(solution)/shard_map/pallas_call | solution.py:121
  62.9 15.0 %all_to_all.25.pos_hbm = f32[16,8,1024]{2,1,0:T(8,128)S(1)} all-to-all(f32[16,8,1024]{2,1,0:T(8,128)S(1)} %bitcast.37), channel_id=1, replica_groups=mesh['h'=2,'l'=2,'x'=4,'z'=4,'c'=2] {'x','z'}, dimensions={0} | all-to-all | bytes 1048576 | tf_op jit(solution)/shard_map/all_to_all | solution.py:49
  80.9 4.2 %all-to-all-start.2 = ((bf16[16,8,1024]{2,1,0:T(8,128)(2,1)}), bf16[16,8,1024]{2,1,0:T(8,128)(2,1)S(1)}, u32[]{:S(2)}, u32[]{:S(2)}) async-start(bf16[16,8,1024]{2,1,0:T(8,128)(2,1)} %bitcast.30), calls=%async_computation.2 | async-start | bytes 524288 | tf_op jit(solution)/shard_map/all_to_all | solution.py:49
  87.1 5.3 %all-to-all-done.2 = bf16[16,8,1024]{2,1,0:T(8,128)(2,1)S(1)} async-done(((bf16[16,8,1024]{2,1,0:T(8,128)(2,1)}), bf16[16,8,1024]{2,1,0:T(8,128)(2,1)S(1)}, u32[]{:S(2)}, u32[]{:S(2)}) %all-to-all-start.2) | async-done | bytes 262176 | tf_op jit(solution)/shard_map/all_to_all | solution.py:49
  94.7 3.0 %collective-permute-start.12 = (bf16[256,1152]{1,0:T(8,128)(2,1)}, bf16[256,1152]{1,0:T(8,128)(2,1)S(1)}, u32[]{:S(2)}, u32[]{:S(2)}) collective-permute-start(bf16[256,1152]{1,0:T(8,128)(2,1)} %collective-permute-done.8.refs_6_), channel_id=1, source_target_pairs={{0,1},{1,0},{2,3},{3,2},{4,5},{5,4},{6,7},{7,6},{8,9},{9,8},{10,11... | collective-permute-start | bytes 1769480 | tf_op jit(solution)/shard_map/ppermute | solution.py:25
  97.8 3.7 %all-to-all-start.3 = ((bf16[16,8,1280]{2,1,0:T(8,128)(2,1)}), bf16[16,8,1280]{2,1,0:T(8,128)(2,1)S(1)}, u32[]{:S(2)}, u32[]{:S(2)}) async-start(bf16[16,8,1280]{2,1,0:T(8,128)(2,1)} %bitcast.31), calls=%async_computation.3 | async-start | bytes 655360 | tf_op jit(solution)/shard_map/all_to_all | solution.py:451
  103.3 5.8 %all-to-all-done.3.got_hbm = bf16[16,8,1280]{2,1,0:T(8,128)(2,1)S(1)} async-done(((bf16[16,8,1280]{2,1,0:T(8,128)(2,1)}), bf16[16,8,1280]{2,1,0:T(8,128)(2,1)S(1)}, u32[]{:S(2)}, u32[]{:S(2)}) %all-to-all-start.3) | async-done | bytes 327712 | tf_op jit(solution)/shard_map/all_to_all | solution.py:451
  110.8 2.4 %collective-permute-start.11 = (f32[8,1024]{1,0:T(8,128)S(1)}, f32[8,1024]{1,0:T(8,128)S(1)}, u32[]{:S(2)}, u32[]{:S(2)}) collective-permute-start(f32[8,1024]{1,0:T(8,128)S(1)} %get-tuple-element.62.refs_3_), channel_id=1, source_target_pairs={{0,1},{1,0},{2,3},{3,2},{4,5},{5,4},{6,7},{7,6},{8,9},{9,8},{10,11... | collective-permute-start | bytes 98312 | tf_op jit(solution)/shard_map/ppermute | solution.py:25
  126.4 7.9 %shard_map.161 = bf16[16,64,1024]{2,1,0:T(8,128)(2,1)S(1)} custom-call(f32[8,1024]{1,0:T(8,128)S(1)} %collective-permute-done.9.refs_0_, f32[8,1024]{1,0:T(8,128)S(1)} %collective-permute-done.10.refs_1_, f32[8,1024]{1,0:T(8,128)S(1)} %collective-permute-done.11.refs_2_, f32[8,1024]{1,0:T(8,128)S(1)} %get-tuple-element.62.refs_3_, f32[1,1024]{1,0:T(1,128)S(1)} %bitcast.33, ...), custom_call_target="tpu_custom_call" | custom-call | flops 3221225472 | bytes 10485760 | tf_op jit(solution)/shard_map/pallas_call | solution.py:290
  136.6 2.3 %slice.25 = f32[256,1024]{1,0:T(8,128)} slice(f32[512,1024]{1,0:T(8,128)} %fusion.3), slice={[256:512], [0:1024]} | slice | bytes 2097152 | tf_op jit(solution)/shard_map/slice | solution.py:507
  139.3 3.7 %all-to-all-start.4 = ((bf16[16,64,1024]{2,1,0:T(8,128)(2,1)}), bf16[16,64,1024]{2,1,0:T(8,128)(2,1)S(1)}, u32[]{:S(2)}, u32[]{:S(2)}) async-start(bf16[16,64,1024]{2,1,0:T(8,128)(2,1)} %copy-done), calls=%async_computation.4 | async-start | bytes 4194304 | tf_op jit(solution)/shard_map/all_to_all | solution.py:478
  145.3 2.4 %collective-permute-start.17 = (bf16[128,1024]{1,0:T(8,128)(2,1)S(1)}, bf16[128,1024]{1,0:T(8,128)(2,1)S(1)}, u32[]{:S(2)}, u32[]{:S(2)}) collective-permute-start(bf16[128,1024]{1,0:T(8,128)(2,1)S(1)} %get-tuple-element.86), channel_id=1, source_target_pairs={{0,96},{96,0},{32,64},{64,32},{1,97},{97,1},{33,65},{65,33},{2,98}... | collective-permute-start | bytes 786440 | tf_op jit(solution)/shard_map/ppermute | solution.py:41
  147.7 4.9 %collective-permute-done.15 = bf16[128,1024]{1,0:T(8,128)(2,1)S(1)} collective-permute-done((bf16[128,1024]{1,0:T(8,128)(2,1)S(1)}, bf16[128,1024]{1,0:T(8,128)(2,1)S(1)}, u32[]{:S(2)}, u32[]{:S(2)}) %collective-permute-start.15) | collective-permute-done | bytes 262176 | tf_op jit(solution)/shard_map/ppermute | solution.py:29
  154.1 2.5 %collective-permute-start.16 = (bf16[128,1024]{1,0:T(8,128)(2,1)S(1)}, bf16[128,1024]{1,0:T(8,128)(2,1)S(1)}, u32[]{:S(2)}, u32[]{:S(2)}) collective-permute-start(bf16[128,1024]{1,0:T(8,128)(2,1)S(1)} %get-tuple-element.83), channel_id=1, source_target_pairs={{0,96},{96,0},{32,64},{64,32},{1,97},{97,1},{33,65},{65,33},{2,98}... | collective-permute-start | bytes 786440 | tf_op jit(solution)/shard_map/ppermute | solution.py:41
  157.3 4.7 %collective-permute-done.16 = bf16[128,1024]{1,0:T(8,128)(2,1)S(1)} collective-permute-done((bf16[128,1024]{1,0:T(8,128)(2,1)S(1)}, bf16[128,1024]{1,0:T(8,128)(2,1)S(1)}, u32[]{:S(2)}, u32[]{:S(2)}) %collective-permute-start.16) | collective-permute-done | bytes 262176 | tf_op jit(solution)/shard_map/ppermute | solution.py:41
  162.8 9.5 %all-to-all-done.4.got = bf16[16,64,1024]{2,1,0:T(8,128)(2,1)S(1)} async-done(((bf16[16,64,1024]{2,1,0:T(8,128)(2,1)}), bf16[16,64,1024]{2,1,0:T(8,128)(2,1)S(1)}, u32[]{:S(2)}, u32[]{:S(2)}) %all-to-all-start.4) | async-done | bytes 2097184 | tf_op jit(solution)/shard_map/all_to_all | solution.py:478
  176.0 2.7 %collective-permute-start.22 = (bf16[64,1024]{1,0:T(8,128)(2,1)S(1)}, bf16[64,1024]{1,0:T(8,128)(2,1)S(1)}, u32[]{:S(2)}, u32[]{:S(2)}) collective-permute-start(bf16[64,1024]{1,0:T(8,128)(2,1)S(1)} %maximum_maximum_fusion.own), channel_id=1, source_target_pairs={{0,64},{64,0},{1,65},{65,1},{2,66},{66,2},{3,67},{67,3},{4,68},{68... | collective-permute-start | bytes 393224 | tf_op jit(solution)/shard_map/ppermute | solution.py:37
  182.5 3.0 %collective-permute-done.21.wrap = bf16[64,1024]{1,0:T(8,128)(2,1)S(1)} collective-permute-done((bf16[64,1024]{1,0:T(8,128)(2,1)S(1)}, bf16[64,1024]{1,0:T(8,128)(2,1)S(1)}, u32[]{:S(2)}, u32[]{:S(2)}) %collective-permute-start.21) | collective-permute-done | bytes 131104 | tf_op jit(solution)/shard_map/ppermute | solution.py:41
  185.5 2.4 %shard_map.163 = (f32[32,2048]{1,0:T(8,128)}, f32[64,1024]{1,0:T(8,128)}) custom-call(s32[3]{0:T(128)S(1)} %copy-done.21, bf16[64,1024]{1,0:T(8,128)(2,1)S(1)} %maximum_maximum_fusion.own, bf16[64,1024]{1,0:T(8,128)(2,1)S(1)} %collective-permute-done.20.near, bf16[64,1024]{1,0:T(8,128)(2,1)S(1)} %collective-permute-done.21.wrap, ...), custom_call_target="tpu_custom_call" | custom-call | flops 67108864 | bytes 1048576 | tf_op jit(solution)/shard_map/pallas_call | solution.py:493
  (145 shorter events, 58.9 us)
Async XLA Ops:
  0.6 49.0 %collective-permute-start.5 = (bf16[256,1024]{1,0:T(8,128)(2,1)}, bf16[256,1024]{1,0:T(8,128)(2,1)S(1)}, u32[]{:S(2)}, u32[]{:S(2)}) collective-permute-start(bf16[256,1024]{1,0:T(8,128)(2,1)} %bitcast.24), channel_id=1, source_target_pairs={{0,32},{32,0},{1,33},{33,1},{2,34},{34,2},{3,35},{35,3},{4,36},{36... | collective-permute-start | bytes 1572872 | tf_op jit(solution)/shard_map/ppermute | solution.py:29
  2.8 46.8 %collective-permute-start.4 = (bf16[256,1024]{1,0:T(8,128)(2,1)}, bf16[256,1024]{1,0:T(8,128)(2,1)}, u32[]{:S(2)}, u32[]{:S(2)}) collective-permute-start(bf16[256,1024]{1,0:T(8,128)(2,1)} %bitcast.25), channel_id=1, source_target_pairs={{0,33},{33,0},{1,32},{32,1},{2,35},{35,2},{3,34},{34,3},{4,37},{37... | collective-permute-start | bytes 1572872 | tf_op jit(solution)/shard_map/ppermute | solution.py:33
  6.3 3.2 %collective-permute-start.1 = (bf16[32,512]{1,0:T(8,128)(2,1)}, bf16[32,512]{1,0:T(8,128)(2,1)S(1)}, u32[]{:S(2)}, u32[]{:S(2)}) collective-permute-start(bf16[32,512]{1,0:T(8,128)(2,1)} %get-tuple-element.43), channel_id=1, source_target_pairs={{0,1},{1,0},{2,3},{3,2},{4,5},{5,4},{6,7},{7,6},{8,9},{9,8},{10,11... | collective-permute-start | bytes 98312 | tf_op jit(solution)/shard_map/ppermute | solution.py:25
  6.3 25.5 %collective-permute-start.2 = (f32[256,1024]{1,0:T(8,128)}, f32[256,1024]{1,0:T(8,128)}, u32[]{:S(2)}, u32[]{:S(2)}) collective-permute-start(f32[256,1024]{1,0:T(8,128)} %param.16), channel_id=1, source_target_pairs={{0,1},{1,0},{2,3},{3,2},{4,5},{5,4},{6,7},{7,6},{8,9},{9,8},{10,11... | collective-permute-start | bytes 3145736 | tf_op jit(solution)/shard_map/ppermute | solution.py:25
  12.6 37.1 %all-to-all-start = ((bf16[16,64,1024]{2,1,0:T(8,128)(2,1)}), bf16[16,64,1024]{2,1,0:T(8,128)(2,1)}, u32[]{:S(2)}, u32[]{:S(2)}) async-start(bf16[16,64,1024]{2,1,0:T(8,128)(2,1)} %shard_map.155), calls=%async_computation | async-start | bytes 4194304 | tf_op jit(solution)/shard_map/all_to_all | solution.py:49
  53.9 3.4 %collective-permute-start.6 = (bf16[256,1024]{1,0:T(8,128)(2,1)S(1)}, bf16[256,1024]{1,0:T(8,128)(2,1)S(1)}, u32[]{:S(2)}, u32[]{:S(2)}) collective-permute-start(bf16[256,1024]{1,0:T(8,128)(2,1)S(1)} %get-tuple-element.48), channel_id=1, source_target_pairs={{0,1},{1,0},{2,3},{3,2},{4,5},{5,4},{6,7},{7,6},{8,9},{9,8},{10,11... | collective-permute-start | bytes 1572872 | tf_op jit(solution)/shard_map/ppermute | solution.py:25
  57.5 20.4 %collective-permute-start.7 = (bf16[256,1024]{1,0:T(8,128)(2,1)S(1)}, bf16[256,1024]{1,0:T(8,128)(2,1)S(1)}, u32[]{:S(2)}, u32[]{:S(2)}) collective-permute-start(bf16[256,1024]{1,0:T(8,128)(2,1)S(1)} %add_convert_fusion), channel_id=1, source_target_pairs={{0,32},{32,0},{1,33},{33,1},{2,34},{34,2},{3,35},{35,3},{4,36},{36... | collective-permute-start | bytes 1572872 | tf_op jit(solution)/shard_map/ppermute | solution.py:29
  62.2 15.8 %collective-permute-start.3 = (bf16[256,1024]{1,0:T(8,128)(2,1)S(1)}, bf16[256,1024]{1,0:T(8,128)(2,1)S(1)}, u32[]{:S(2)}, u32[]{:S(2)}) collective-permute-start(bf16[256,1024]{1,0:T(8,128)(2,1)S(1)} %get-tuple-element.46), channel_id=1, source_target_pairs={{0,1},{1,0},{2,3},{3,2},{4,5},{5,4},{6,7},{7,6},{8,9},{9,8},{10,11... | collective-permute-start | bytes 1572872 | tf_op jit(solution)/shard_map/ppermute | solution.py:25
  80.7 14.0 %collective-permute-start.8 = (bf16[256,1152]{1,0:T(8,128)(2,1)}, bf16[256,1152]{1,0:T(8,128)(2,1)}, u32[]{:S(2)}, u32[]{:S(2)}) collective-permute-start(bf16[256,1152]{1,0:T(8,128)(2,1)} %get-tuple-element.58.refs_8_), channel_id=1, source_target_pairs={{0,32},{32,0},{1,33},{33,1},{2,34},{34,2},{3,35},{35,3},{4,36},{36... | collective-permute-start | bytes 1769480 | tf_op jit(solution)/shard_map/ppermute | solution.py:29
  80.9 11.5 %all-to-all-start.2 = ((bf16[16,8,1024]{2,1,0:T(8,128)(2,1)}), bf16[16,8,1024]{2,1,0:T(8,128)(2,1)S(1)}, u32[]{:S(2)}, u32[]{:S(2)}) async-start(bf16[16,8,1024]{2,1,0:T(8,128)(2,1)} %bitcast.30), calls=%async_computation.2 | async-start | bytes 524288 | tf_op jit(solution)/shard_map/all_to_all | solution.py:49
  85.1 30.0 %collective-permute-start.13 = (bf16[256,1152]{1,0:T(8,128)(2,1)}, bf16[256,1152]{1,0:T(8,128)(2,1)}, u32[]{:S(2)}, u32[]{:S(2)}) collective-permute-start(bf16[256,1152]{1,0:T(8,128)(2,1)} %get-tuple-element.58.refs_8_), channel_id=1, source_target_pairs={{0,1},{1,0},{2,3},{3,2},{4,5},{5,4},{6,7},{7,6},{8,9},{9,8},{10,11... | collective-permute-start | bytes 1769480 | tf_op jit(solution)/shard_map/ppermute | solution.py:25
  94.7 23.2 %collective-permute-start.12 = (bf16[256,1152]{1,0:T(8,128)(2,1)}, bf16[256,1152]{1,0:T(8,128)(2,1)S(1)}, u32[]{:S(2)}, u32[]{:S(2)}) collective-permute-start(bf16[256,1152]{1,0:T(8,128)(2,1)} %collective-permute-done.8.refs_6_), channel_id=1, source_target_pairs={{0,1},{1,0},{2,3},{3,2},{4,5},{5,4},{6,7},{7,6},{8,9},{9,8},{10,11... | collective-permute-start | bytes 1769480 | tf_op jit(solution)/shard_map/ppermute | solution.py:25
  97.8 11.3 %all-to-all-start.3 = ((bf16[16,8,1280]{2,1,0:T(8,128)(2,1)}), bf16[16,8,1280]{2,1,0:T(8,128)(2,1)S(1)}, u32[]{:S(2)}, u32[]{:S(2)}) async-start(bf16[16,8,1280]{2,1,0:T(8,128)(2,1)} %bitcast.31), calls=%async_computation.3 | async-start | bytes 655360 | tf_op jit(solution)/shard_map/all_to_all | solution.py:451
  110.8 4.3 %collective-permute-start.11 = (f32[8,1024]{1,0:T(8,128)S(1)}, f32[8,1024]{1,0:T(8,128)S(1)}, u32[]{:S(2)}, u32[]{:S(2)}) collective-permute-start(f32[8,1024]{1,0:T(8,128)S(1)} %get-tuple-element.62.refs_3_), channel_id=1, source_target_pairs={{0,1},{1,0},{2,3},{3,2},{4,5},{5,4},{6,7},{7,6},{8,9},{9,8},{10,11... | collective-permute-start | bytes 98312 | tf_op jit(solution)/shard_map/ppermute | solution.py:25
  114.5 3.4 %collective-permute-start.9 = (f32[8,1024]{1,0:T(8,128)S(1)}, f32[8,1024]{1,0:T(8,128)S(1)}, u32[]{:S(2)}, u32[]{:S(2)}) collective-permute-start(f32[8,1024]{1,0:T(8,128)S(1)} %get-tuple-element.62.refs_3_), channel_id=1, source_target_pairs={{0,33},{33,0},{1,32},{32,1},{2,35},{35,2},{3,34},{34,3},{4,37},{37... | collective-permute-start | bytes 98312 | tf_op jit(solution)/shard_map/ppermute | solution.py:33
  138.9 4.1 %collective-permute-start.14 = (f32[256,1024]{1,0:T(8,128)}, f32[256,1024]{1,0:T(8,128)}, u32[]{:S(2)}, u32[]{:S(2)}) collective-permute-start(f32[256,1024]{1,0:T(8,128)} %slice.25), channel_id=1, source_target_pairs={{0,1},{1,0},{2,3},{3,2},{4,5},{5,4},{6,7},{7,6},{8,9},{9,8},{10,11... | collective-permute-start | bytes 3145736 | tf_op jit(solution)/shard_map/ppermute | solution.py:25
  139.3 33.1 %all-to-all-start.4 = ((bf16[16,64,1024]{2,1,0:T(8,128)(2,1)}), bf16[16,64,1024]{2,1,0:T(8,128)(2,1)S(1)}, u32[]{:S(2)}, u32[]{:S(2)}) async-start(bf16[16,64,1024]{2,1,0:T(8,128)(2,1)} %copy-done), calls=%async_computation.4 | async-start | bytes 4194304 | tf_op jit(solution)/shard_map/all_to_all | solution.py:478
  144.7 7.8 %collective-permute-start.15 = (bf16[128,1024]{1,0:T(8,128)(2,1)S(1)}, bf16[128,1024]{1,0:T(8,128)(2,1)S(1)}, u32[]{:S(2)}, u32[]{:S(2)}) collective-permute-start(bf16[128,1024]{1,0:T(8,128)(2,1)S(1)} %get-tuple-element.85), channel_id=1, source_target_pairs={{0,32},{32,0},{1,33},{33,1},{2,34},{34,2},{3,35},{35,3},{4,36},{36... | collective-permute-start | bytes 786440 | tf_op jit(solution)/shard_map/ppermute | solution.py:29
  145.3 8.6 %collective-permute-start.17 = (bf16[128,1024]{1,0:T(8,128)(2,1)S(1)}, bf16[128,1024]{1,0:T(8,128)(2,1)S(1)}, u32[]{:S(2)}, u32[]{:S(2)}) collective-permute-start(bf16[128,1024]{1,0:T(8,128)(2,1)S(1)} %get-tuple-element.86), channel_id=1, source_target_pairs={{0,96},{96,0},{32,64},{64,32},{1,97},{97,1},{33,65},{65,33},{2,98}... | collective-permute-start | bytes 786440 | tf_op jit(solution)/shard_map/ppermute | solution.py:41
  154.1 7.8 %collective-permute-start.16 = (bf16[128,1024]{1,0:T(8,128)(2,1)S(1)}, bf16[128,1024]{1,0:T(8,128)(2,1)S(1)}, u32[]{:S(2)}, u32[]{:S(2)}) collective-permute-start(bf16[128,1024]{1,0:T(8,128)(2,1)S(1)} %get-tuple-element.83), channel_id=1, source_target_pairs={{0,96},{96,0},{32,64},{64,32},{1,97},{97,1},{33,65},{65,33},{2,98}... | collective-permute-start | bytes 786440 | tf_op jit(solution)/shard_map/ppermute | solution.py:41
  156.6 18.3 %collective-permute-start.18 = (bf16[128,1024]{1,0:T(8,128)(2,1)S(1)}, bf16[128,1024]{1,0:T(8,128)(2,1)}, u32[]{:S(2)}, u32[]{:S(2)}) collective-permute-start(bf16[128,1024]{1,0:T(8,128)(2,1)S(1)} %get-tuple-element.84), channel_id=1, source_target_pairs={{0,32},{32,0},{1,33},{33,1},{2,34},{34,2},{3,35},{35,3},{4,36},{36... | collective-permute-start | bytes 786440 | tf_op jit(solution)/shard_map/ppermute | solution.py:29
  176.0 6.5 %collective-permute-start.22 = (bf16[64,1024]{1,0:T(8,128)(2,1)S(1)}, bf16[64,1024]{1,0:T(8,128)(2,1)S(1)}, u32[]{:S(2)}, u32[]{:S(2)}) collective-permute-start(bf16[64,1024]{1,0:T(8,128)(2,1)S(1)} %maximum_maximum_fusion.own), channel_id=1, source_target_pairs={{0,64},{64,0},{1,65},{65,1},{2,66},{66,2},{3,67},{67,3},{4,68},{68... | collective-permute-start | bytes 393224 | tf_op jit(solution)/shard_map/ppermute | solution.py:37
  178.7 6.8 %collective-permute-start.21 = (bf16[64,1024]{1,0:T(8,128)(2,1)S(1)}, bf16[64,1024]{1,0:T(8,128)(2,1)S(1)}, u32[]{:S(2)}, u32[]{:S(2)}) collective-permute-start(bf16[64,1024]{1,0:T(8,128)(2,1)S(1)} %maximum_maximum_fusion.own), channel_id=1, source_target_pairs={{0,96},{96,0},{32,64},{64,32},{1,97},{97,1},{33,65},{65,33},{2,98}... | collective-permute-start | bytes 393224 | tf_op jit(solution)/shard_map/ppermute | solution.py:41
  179.0 6.5 %collective-permute-start.20 = (bf16[64,1024]{1,0:T(8,128)(2,1)S(1)}, bf16[64,1024]{1,0:T(8,128)(2,1)S(1)}, u32[]{:S(2)}, u32[]{:S(2)}) collective-permute-start(bf16[64,1024]{1,0:T(8,128)(2,1)S(1)} %maximum_maximum_fusion.own), channel_id=1, source_target_pairs={{0,32},{32,0},{1,33},{33,1},{2,34},{34,2},{3,35},{35,3},{4,36},{36... | collective-permute-start | bytes 393224 | tf_op jit(solution)/shard_map/ppermute | solution.py:29
  (37 other events, 276.7 us)

commit v3 on v2

--- a/solution.py
+++ b/solution.py
@@ -7,6 +7,7 @@
 
 LPC = 4
 POS = 4
+POS_SCALE = 32768.0
 
 NORM_EPS = 1e-05
 INV_ROOT_TWO = 0.7071067811865476
@@ -52,7 +53,8 @@
 WHOLE = pl.BlockSpec(memory_space=pltpu.VMEM)
 SCALARS = pl.BlockSpec(memory_space=pltpu.SMEM)
 ANYWHERE = pl.BlockSpec(memory_space=pl.ANY)
-LIMIT = pltpu.CompilerParams(vmem_limit_bytes=40 * 1024 * 1024)
+LIMIT = pltpu.CompilerParams(vmem_limit_bytes=20 * 1024 * 1024)
+MOST = pltpu.CompilerParams(vmem_limit_bytes=60 * 1024 * 1024)
 
 
 def shape(dims, dtype):
@@ -138,7 +140,7 @@
     )(tok_a, tok_b, weights)
 
 
-def norm_kernel(lengths, tok, part, from_core, from_near, gain, rows, emb):
+def norm_kernel(lengths, tok, part, from_core, from_near, gain, rows, emb_hbm, emb, sem):
     embs = []
     for d in range(8):
         at = pl.ds(d * 32, 32)
@@ -158,9 +160,12 @@
         rows[at, 1024:] = extra.astype(BF16)
     docs = jnp.concatenate(embs, axis=0)
     emb[...] = jnp.concatenate([docs] * 16, axis=0).astype(BF16)
-
-
-def score_kernel(emb, tiles_hi, tiles_lo, live, packed, weighted, emb_buf, sem):
+    copy = pltpu.make_async_copy(emb, emb_hbm, sem)
+    copy.start()
+    copy.wait()
+
+
+def score_kernel(emb, tiles_hi, tiles_lo, live, packed_hbm, weighted, emb_buf, packed, sem):
     copy = pltpu.make_async_copy(emb, emb_buf, sem)
     copy.start()
     grow = (iota((128, 512), 0) == iota((128, 512), 1) // LPC).astype(BF16)
@@ -187,27 +192,39 @@
             same, table, preferred_element_type=F32
         ).astype(BF16)
     packed[:, :1024] = part_emb.astype(BF16)
-
-
-def settle_kernel(meta, got_hbm, pos_hbm, emb, grad, loss, sums, got, pos, sems):
-    copies = [
-        pltpu.make_async_copy(got_hbm, got, sems.at[0]),
-        pltpu.make_async_copy(pos_hbm, pos, sems.at[1]),
-    ]
-    for copy in copies:
-        copy.start()
-    for copy in copies:
-        copy.wait()
+    copy = pltpu.make_async_copy(packed, packed_hbm, sem)
+    copy.start()
+    copy.wait()
+
+
+def settle_kernel(meta, got_hbm, pos, emb, grad, loss, sums, got, sem):
+    copy = pltpu.make_async_copy(got_hbm, got, sem)
+    copy.start()
+    copy.wait()
     total = got[0].astype(F32)
     for i in range(1, 16):
         total = total + got[i].astype(F32)
     every = (total[:, 1024:1152] + total[:, 1152:1280]) * 2.0
     sums[...] = every
     expsum = jnp.sum(jnp.where(iota((8, 128), 1) == meta[2], every, 0.0), axis=1, keepdims=True)
-    pos_mean = jnp.sum(pos[...], axis=0)
+    pos_mean = pos[...]
     grad[...] = total[:, :1024] / expsum - pos_mean
     picked = jnp.sum(emb[...].astype(F32)[:8] * pos_mean, axis=1, keepdims=True)
     loss[...] = jnp.broadcast_to(jnp.log(expsum) - picked, (8, 128))
+
+
+def tile_kernel(sums, weighted, share_hit, emb, own, other):
+    rows = jnp.concatenate([sums[...]] * 16, axis=0)
+    chosen = iota((128, 128), 0) // 8 == iota((128, 128), 1)
+    column = jnp.sum(jnp.where(chosen, rows, 0.0), axis=1, keepdims=True)
+    grad = weighted[...] / column - share_hit[...]
+    grad_hi = grad.astype(BF16)
+    grad_lo = (grad - grad_hi.astype(F32)).astype(BF16)
+    for k, out in enumerate((own, other)):
+        at = slice(k * 256, k * 256 + 256)
+        part = lax.dot_general(grad_hi[:, at], emb[...], FIRST, preferred_element_type=F32)
+        part = part + lax.dot_general(grad_lo[:, at], emb[...], FIRST, preferred_element_type=F32)
+        out[...] = part.astype(out.dtype)
 
 
 def backward_kernel(*refs):
@@ -303,7 +320,7 @@
             pltpu.VMEM((16, 64, 1024), BF16),
             pltpu.SemaphoreType.DMA((21,)),
         ],
-        compiler_params=LIMIT,
+        compiler_params=MOST,
         cost_estimate=cost(3 * 2**30, 10 * 2**20),
     )(*grads, gain, *rows, *toks, *hiddens, *slopes, weights)
 
@@ -336,8 +353,8 @@
     swapped, flipped = piece % 2, piece // 4
     part = (core + swapped - 2 * core * swapped) * 2 + (role + flipped - 2 * role * flipped)
     spread = (lane == at // 32 * 128 + part * 32 + at % 32).astype(BF16)
-    for i in range(4):
-        block = jnp.concatenate(
+    blocks = [
+        jnp.concatenate(
             [
                 a[32:, k * 512 + i * 128 : k * 512 + i * 128 + 128]
                 for a in (own, wrap, near, far)
@@ -345,7 +362,11 @@
             ],
             axis=1,
         )
-        grad_in[:, i * 512 : i * 512 + 512] = jnp.dot(block, spread, preferred_element_type=F32)
+        for i in range(4)
+    ]
+    placed = jnp.dot(jnp.concatenate(blocks, axis=0), spread, preferred_element_type=F32)
+    for i in range(4):
+        grad_in[:, i * 512 : i * 512 + 512] = placed[i * 32 : i * 32 + 32]
 
 
 def on_device(
@@ -415,6 +436,7 @@
     pos_part = jnp.dot(hit, tiles_hi, preferred_element_type=F32) + jnp.dot(
         hit, tiles_lo, preferred_element_type=F32
     )
+    pos_part = (pos_part * POS_SCALE).astype(jnp.float16)
     weights, cluster_live, share_hit, pos_part, tiles_hi, tiles_lo = lax.optimization_barrier(
         (weights, cluster_live, share_hit, pos_part, tiles_hi, tiles_lo)
     )
@@ -426,11 +448,13 @@
     pos_got = gather_chips(pos_part.reshape(16, docs, width))
     own_a, own_b, own_hidden, own_slope = forward(core_tok, own_tok, weights)
     from_near, pos_got = lax.optimization_barrier((from_near, pos_got))
+    pos_mean = jnp.sum(pos_got.astype(F32), axis=0) * (1.0 / POS_SCALE)
     own_rows, emb = pl.pallas_call(
         norm_kernel,
         out_shape=(shape((256, 1152), BF16), shape((128, width), BF16)),
         in_specs=[SCALARS] + [WHOLE] * 5,
-        out_specs=(WHOLE, WHOLE),
+        out_specs=(WHOLE, ANYWHERE),
+        scratch_shapes=[pltpu.VMEM((128, width), BF16), pltpu.SemaphoreType.DMA],
         compiler_params=LIMIT,
         cost_estimate=cost(2**22, 4 * 2**20),
     )(lengths, own_tok, own_b, swap_core(own_a), from_near, gain)
@@ -441,8 +465,12 @@
         score_kernel,
         out_shape=(shape((128, 1280), BF16), shape((128, 512), F32)),
         in_specs=[ANYWHERE] + [WHOLE] * 3,
-        out_specs=(WHOLE, WHOLE),
-        scratch_shapes=[pltpu.VMEM((128, width), BF16), pltpu.SemaphoreType.DMA],
+        out_specs=(ANYWHERE, WHOLE),
+        scratch_shapes=[
+            pltpu.VMEM((128, width), BF16),
+            pltpu.VMEM((128, 1280), BF16),
+            pltpu.SemaphoreType.DMA,
+        ],
         compiler_params=LIMIT,
         cost_estimate=cost(2**29, 3 * 2**20, 2**16),
     )(plane_emb, tiles_hi, tiles_lo, cluster_live)
@@ -452,16 +480,15 @@
     emb_grad, loss, sums = pl.pallas_call(
         settle_kernel,
         out_shape=(shape((docs, width), F32), shape((docs, 128), F32), shape((docs, 128), F32)),
-        in_specs=[SCALARS, ANYWHERE, ANYWHERE, WHOLE],
+        in_specs=[SCALARS, ANYWHERE, WHOLE, WHOLE],
         out_specs=(WHOLE,) * 3,
         scratch_shapes=[
             pltpu.VMEM((16, docs, 1280), BF16),
-            pltpu.VMEM((16, docs, width), F32),
-            pltpu.SemaphoreType.DMA((2,)),
+            pltpu.SemaphoreType.DMA,
         ],
         compiler_params=LIMIT,
         cost_estimate=cost(2**20, 2**20),
-    )(meta, got, pos_got, emb)
+    )(meta, got, pos_mean, emb)
     loss = loss[:, 0]
 
     grads = (swap_diag(emb_grad), swap_near(emb_grad), swap_core(emb_grad), emb_grad)
@@ -474,7 +501,6 @@
         (near_slope, own_slope),
         weights,
     )
-    send, weighted = lax.optimization_barrier((send, weighted))
     got = lax.all_to_all(send, CHIPS, 0, 0, tiled=True)
     part, keep, give = pl.pallas_call(
         total_kernel,
@@ -499,12 +525,15 @@
         cost_estimate=cost(2**26, 2**20),
     )(meta, both, swap_near(both), swap_wrap(both), swap_far(both))
 
-    all_sums = sums[:, :16].T.reshape(128)
-    logit_grad = weighted / all_sums[:, None] - share_hit
-    tile_part = lax.dot_general(
-        logit_grad, plane_emb.astype(F32), FIRST, precision=lax.Precision.HIGH
-    )
-    tile_chip = (tile_part[:256] + swap_core(tile_part[256:])).astype(BF16)
+    tile_own, tile_other = pl.pallas_call(
+        tile_kernel,
+        out_shape=(shape((256, width), F32), shape((256, width), BF16)),
+        in_specs=[WHOLE] * 4,
+        out_specs=(WHOLE, WHOLE),
+        compiler_params=LIMIT,
+        cost_estimate=cost(2**28, 2**21),
+    )(sums, weighted, share_hit, plane_emb)
+    tile_chip = (tile_own + swap_core(tile_other).astype(F32)).astype(BF16)
 
     def add(a, swap):
         return a.astype(F32) + swap(a).astype(F32)

time: 189 us -> 174 us (0.921)
  local copies, waits for them, and re-layouts: 20.1 us -> 6.81 us
  Pallas kernels: 27.7 us -> 31.7 us
  matrix products: 3.67 us -> 1.37 us
  blocking collectives: 15 us -> 12.8 us
    unnamed x70 -> x54, local copies, waits for them, and re-layouts: 12.7 us -> 3.53 us
    all_to_all x1, waiting for transfers between devices: 5.79 us -> 8.4 us  [on_device(): lax.all_to_all(packed.reshape(16, docs, 1280), CHIPS, 0, 0, tiled=True)]
    slice x1 -> x0, local copies, waits for them, and re-layouts: 2.31 us -> none  [on_device(): tile_chip = (tile_part[:256] + swap_core(tile_part[256:])).astype(BF16)]
    all_to_all x1, blocking collectives: 15 us -> 12.8 us  [gather_chips(): return lax.all_to_all(a, CHIPS, 0, 0, tiled=True)]
    dot_general x1 -> x0, matrix products: 2.21 us -> none  [on_device(): lax.dot_general(logit_grad, plane_emb.astype(F32), FIRST, precision=lax.P...]
  transfers between devices with their start and end apart: 27 -> 27, of which waited for: 12 -> 11; matrix products, arithmetic and copies ran while one was open for 14% -> 13% of each run, Pallas kernels for 6% -> 13%
where the time goes in v3:
time: 174 us
  waiting for transfers between devices  54.9 us (32%)
  starting transfers between devices  46.4 us (27%)
  Pallas kernels  31.7 us (18%)
  other arithmetic  18.2 us (10%)
  blocking collectives  12.8 us (7%)
  local copies, waits for them, and re-layouts  6.81 us (4%)
    all_to_all x2, waiting for transfers between devices, gather_chips(): return lax.all_to_all(a, CHIPS, 0, 0, tiled=True)  20.2 us
    all_to_all x1, blocking collectives, gather_chips(): return lax.all_to_all(a, CHIPS, 0, 0, tiled=True)  12.8 us
    ppermute x10, starting transfers between devices, swap_core(): return lax.ppermute(a, 'c', [(0, 1), (1, 0)])  12.1 us
    all_to_all x2, starting transfers between devices, gather_chips(): return lax.all_to_all(a, CHIPS, 0, 0, tiled=True)  11.6 us
    ppermute x3, waiting for transfers between devices, swap_wrap(): return lax.ppermute(a, ('h', 'l'), [(0, 3), (3, 0), (1, 2), (2, 1)])  9.93 us
    reduce_max x1, other arithmetic, on_device(): jnp.max((short[:, :, None] == cluster_ids[None, None, :]).astype(F32), ax...  9.89 us
    all_to_all x1, waiting for transfers between devices, on_device(): got = lax.all_to_all(send, CHIPS, 0, 0, tiled=True)  9.48 us
    pallas_call x1, Pallas kernels, backward(): pl.pallas_call(backward_kernel, out_shape=shape((16, 64, 1024), BF16), in...  9.04 us
  transfers between devices with their start and end apart: 27, of which 11 were waited for; matrix products, arithmetic and copies ran while one was open for 13% of the time, Pallas kernels for 13%

profile of v3, /device:TPU:1, one launch (start us, length us, event | category | flops | bytes accessed | tf_op | source)
XLA Modules:
  0.0 173.5 jit_solution(17863439339344092236)
XLA Ops:
  0.6 2.2 %collective-permute-start.5 = (bf16[256,1024]{1,0:T(8,128)(2,1)}, bf16[256,1024]{1,0:T(8,128)(2,1)S(1)}, u32[]{:S(2)}, u32[]{:S(2)}) collective-permute-start(bf16[256,1024]{1,0:T(8,128)(2,1)} %bitcast.19), channel_id=1, source_target_pairs={{0,32},{32,0},{1,33},{33,1},{2,34},{34,2},{3,35},{35,3},{4,36},{36... | collective-permute-start | bytes 1572872 | tf_op jit(solution)/shard_map/ppermute | solution.py:30
  10.1 2.5 %shard_map.155 = bf16[16,64,1024]{2,1,0:T(8,128)(2,1)} custom-call(s32[3]{0:T(128)} %pad_add_fusion.meta, bf16[32,512]{1,0:T(8,128)(2,1)} %get-tuple-element.42.mine, bf16[32,512]{1,0:T(8,128)(2,1)} %copy-done.22, bf16[64,1024]{1,0:T(8,128)(2,1)} %w_out.1), custom_call_target="tpu_custom_call" | custom-call | bytes 2097152 | tf_op jit(solution)/shard_map/pallas_call | solution.py:402
  12.6 7.9 %all-to-all-start = ((bf16[16,64,1024]{2,1,0:T(8,128)(2,1)}), bf16[16,64,1024]{2,1,0:T(8,128)(2,1)}, u32[]{:S(2)}, u32[]{:S(2)}) async-start(bf16[16,64,1024]{2,1,0:T(8,128)(2,1)} %shard_map.155), calls=%async_computation | async-start | bytes 4194304 | tf_op jit(solution)/shard_map/all_to_all | solution.py:50
  21.8 9.9 %convert_reduce_fusion.live = bf16[128,128]{1,0:T(8,128)(2,1)S(1)} fusion(s32[128]{0:T(128)S(1)} %select_reduce_fusion, s32[128,400]{1,0:T(8,128)S(1)} %dynamic-slice_bitcast_fusion), kind=kLoop, calls=%fused_computation | loop fusion | flops 19644416 | bytes 238080 | tf_op jit(solution)/shard_map/reduce_max | solution.py:423
  34.8 14.8 %all-to-all-done.weights.refs_17_ = bf16[16,64,1024]{2,1,0:T(8,128)(2,1)} async-done(((bf16[16,64,1024]{2,1,0:T(8,128)(2,1)}), bf16[16,64,1024]{2,1,0:T(8,128)(2,1)}, u32[]{:S(2)}, u32[]{:S(2)}) %all-to-all-start) | async-done | bytes 2097184 | tf_op jit(solution)/shard_map/all_to_all | solution.py:50
  49.7 4.3 %shard_map.157 = (bf16[256,1024]{1,0:T(8,128)(2,1)S(1)}, f32[256,1024]{1,0:T(8,128)S(1)}, bf16[512,512]{1,0:T(8,128)(2,1)S(1)}, f32[512,512]{1,0:T(8,128)S(1)}) custom-call(bf16[256,1024]{1,0:T(8,128)(2,1)} %collective-permute-done.4.tok_a.refs_9_, bf16[256,1024]{1,0:T(8,128)(2,1)S(1)} %collective-permute-done.5.tok_b.refs_10_, ...), custom_call_target="tpu_custom_call" | custom-call | flops 1073741824 | bytes 6291456 | tf_op jit(solution)/shard_map/pallas_call | solution.py:123
  59.0 3.2 %shard_map.156 = (bf16[256,1024]{1,0:T(8,128)(2,1)S(1)}, f32[256,1024]{1,0:T(8,128)S(1)}, bf16[512,512]{1,0:T(8,128)(2,1)S(1)}, f32[512,512]{1,0:T(8,128)S(1)}) custom-call(bf16[256,1024]{1,0:T(8,128)(2,1)S(1)} %collective-permute-done.tok_a.refs_11_, bf16[256,1024]{1,0:T(8,128)(2,1)S(1)} %bitcast.23, bf16[16,64,1024]{2,1,0:T(8,128)(2,1)} %all-to-all-done.weights.refs_17_), custom_call_target="tpu_custom_call" | custom-call | flops 1073741824 | bytes 6291456 | tf_op jit(solution)/shard_map/pallas_call | solution.py:123
  63.0 12.8 %all_to_all.25 = f16[16,8,1024]{2,1,0:T(8,128)(2,1)} all-to-all(f16[16,8,1024]{2,1,0:T(8,128)(2,1)S(1)} %bitcast.33), channel_id=1, replica_groups=mesh['h'=2,'l'=2,'x'=4,'z'=4,'c'=2] {'x','z'}, dimensions={0} | all-to-all | bytes 524288 | tf_op jit(solution)/shard_map/all_to_all | solution.py:50
  75.8 2.8 %shard_map.158 = (bf16[256,1152]{1,0:T(8,128)(2,1)}, bf16[128,1024]{1,0:T(8,128)(2,1)}) custom-call(s32[8]{0:T(128)S(1)} %copy-done.10, bf16[256,1024]{1,0:T(8,128)(2,1)S(1)} %bitcast.24, f32[256,1024]{1,0:T(8,128)S(1)} %get-tuple-element.45.part, bf16[256,1024]{1,0:T(8,128)(2,1)S(1)} %collective-permute-done.3.from_core, ...), custom_call_target="tpu_custom_call" | custom-call | flops 4194304 | bytes 4194304 | tf_op jit(solution)/shard_map/pallas_call | solution.py:452
  78.8 3.8 %all-to-all-start.2 = ((bf16[16,8,1024]{2,1,0:T(8,128)(2,1)}), bf16[16,8,1024]{2,1,0:T(8,128)(2,1)S(1)}, u32[]{:S(2)}, u32[]{:S(2)}) async-start(bf16[16,8,1024]{2,1,0:T(8,128)(2,1)} %bitcast.9), calls=%async_computation.2 | async-start | bytes 524288 | tf_op jit(solution)/shard_map/all_to_all | solution.py:50
  84.5 5.4 %all-to-all-done.2 = bf16[16,8,1024]{2,1,0:T(8,128)(2,1)S(1)} async-done(((bf16[16,8,1024]{2,1,0:T(8,128)(2,1)}), bf16[16,8,1024]{2,1,0:T(8,128)(2,1)S(1)}, u32[]{:S(2)}, u32[]{:S(2)}) %all-to-all-start.2) | async-done | bytes 262176 | tf_op jit(solution)/shard_map/all_to_all | solution.py:50
  89.9 2.3 %shard_map.159 = (bf16[128,1280]{1,0:T(8,128)(2,1)}, f32[128,512]{1,0:T(8,128)S(1)}) custom-call(bf16[128,1024]{1,0:T(8,128)(2,1)S(1)} %bitcast.25, bf16[512,1024]{1,0:T(8,128)(2,1)S(1)} %get-tuple-element.54.tiles_hi, bf16[512,1024]{1,0:T(8,128)(2,1)S(1)} %get-tuple-element.55.tiles_lo, bf16[128,128]{1,0:T(8,128)(2,1)S(1)} %convert_reduce_fusion.live), custom_call_target="tpu_custom_call" | custom-call | flops 536870912 | bytes 3145728 | tf_op jit(solution)/shard_map/pallas_call | solution.py:464
  92.3 3.1 %collective-permute-start.17 = (bf16[256,1152]{1,0:T(8,128)(2,1)}, bf16[256,1152]{1,0:T(8,128)(2,1)S(1)}, u32[]{:S(2)}, u32[]{:S(2)}) collective-permute-start(bf16[256,1152]{1,0:T(8,128)(2,1)} %collective-permute-done.8.refs_6_), channel_id=1, source_target_pairs={{0,1},{1,0},{2,3},{3,2},{4,5},{5,4},{6,7},{7,6},{8,9},{9,8},{10,11... | collective-permute-start | bytes 1769480 | tf_op jit(solution)/shard_map/ppermute | solution.py:26
  95.3 3.5 %all-to-all-start.3 = ((bf16[16,8,1280]{2,1,0:T(8,128)(2,1)}), bf16[16,8,1280]{2,1,0:T(8,128)(2,1)S(1)}, u32[]{:S(2)}, u32[]{:S(2)}) async-start(bf16[16,8,1280]{2,1,0:T(8,128)(2,1)} %bitcast.11), calls=%async_computation.3 | async-start | bytes 655360 | tf_op jit(solution)/shard_map/all_to_all | solution.py:479
  99.0 8.4 %all-to-all-done.3.got_hbm = bf16[16,8,1280]{2,1,0:T(8,128)(2,1)S(1)} async-done(((bf16[16,8,1280]{2,1,0:T(8,128)(2,1)}), bf16[16,8,1280]{2,1,0:T(8,128)(2,1)S(1)}, u32[]{:S(2)}, u32[]{:S(2)}) %all-to-all-start.3) | async-done | bytes 327712 | tf_op jit(solution)/shard_map/all_to_all | solution.py:479
  115.9 9.0 %shard_map.162 = bf16[16,64,1024]{2,1,0:T(8,128)(2,1)} custom-call(f32[8,1024]{1,0:T(8,128)} %copy-done.25, f32[8,1024]{1,0:T(8,128)} %copy-done.24, f32[8,1024]{1,0:T(8,128)} %copy-done.23, f32[8,1024]{1,0:T(8,128)} %copy-done.7, f32[1,1024]{1,0:T(1,128)} %bitcast.27, bf16[256,1152]{1,0:T(8,128)(2,1)} %copy-done.20, ...), custom_call_target="tpu_custom_call" | custom-call | flops 3221225472 | bytes 10485760 | tf_op jit(solution)/shard_map/pallas_call | solution.py:307
  124.9 3.7 %all-to-all-start.4 = ((bf16[16,64,1024]{2,1,0:T(8,128)(2,1)}), bf16[16,64,1024]{2,1,0:T(8,128)(2,1)S(1)}, u32[]{:S(2)}, u32[]{:S(2)}) async-start(bf16[16,64,1024]{2,1,0:T(8,128)(2,1)} %shard_map.162), calls=%async_computation.4 | async-start | bytes 4194304 | tf_op jit(solution)/shard_map/all_to_all | solution.py:504
  133.2 4.4 %collective-permute-done.10 = bf16[128,1024]{1,0:T(8,128)(2,1)S(1)} collective-permute-done((bf16[128,1024]{1,0:T(8,128)(2,1)S(1)}, bf16[128,1024]{1,0:T(8,128)(2,1)S(1)}, u32[]{:S(2)}, u32[]{:S(2)}) %collective-permute-start.10) | collective-permute-done | bytes 262176 | tf_op jit(solution)/shard_map/ppermute | solution.py:30
  137.6 2.2 %collective-permute-done.12 = bf16[128,1024]{1,0:T(8,128)(2,1)S(1)} collective-permute-done((bf16[128,1024]{1,0:T(8,128)(2,1)S(1)}, bf16[128,1024]{1,0:T(8,128)(2,1)S(1)}, u32[]{:S(2)}, u32[]{:S(2)}) %collective-permute-start.12) | collective-permute-done | bytes 262176 | tf_op jit(solution)/shard_map/ppermute | solution.py:42
  142.5 5.0 %collective-permute-done.11 = bf16[128,1024]{1,0:T(8,128)(2,1)S(1)} collective-permute-done((bf16[128,1024]{1,0:T(8,128)(2,1)S(1)}, bf16[128,1024]{1,0:T(8,128)(2,1)S(1)}, u32[]{:S(2)}, u32[]{:S(2)}) %collective-permute-start.11) | collective-permute-done | bytes 262176 | tf_op jit(solution)/shard_map/ppermute | solution.py:42
  148.4 9.5 %all-to-all-done.4.got = bf16[16,64,1024]{2,1,0:T(8,128)(2,1)S(1)} async-done(((bf16[16,64,1024]{2,1,0:T(8,128)(2,1)}), bf16[16,64,1024]{2,1,0:T(8,128)(2,1)S(1)}, u32[]{:S(2)}, u32[]{:S(2)}) %all-to-all-start.4) | async-done | bytes 2097184 | tf_op jit(solution)/shard_map/all_to_all | solution.py:504
  162.0 2.9 %collective-permute-start.22 = (bf16[64,1024]{1,0:T(8,128)(2,1)S(1)}, bf16[64,1024]{1,0:T(8,128)(2,1)S(1)}, u32[]{:S(2)}, u32[]{:S(2)}) collective-permute-start(bf16[64,1024]{1,0:T(8,128)(2,1)S(1)} %maximum_maximum_fusion.own), channel_id=1, source_target_pairs={{0,64},{64,0},{1,65},{65,1},{2,66},{66,2},{3,67},{67,3},{4,68},{68... | collective-permute-start | bytes 393224 | tf_op jit(solution)/shard_map/ppermute | solution.py:38
  165.7 2.1 %divide_subtract_fusion = (f32[256,1024]{1,0:T(8,128)}, f32[256,1024]{1,0:T(8,128)}, f32[256,1024]{1,0:T(8,128)}) fusion(f32[256,1024]{1,0:T(8,128)S(1)} %copy-done.14, f32[128,1024]{1,0:T(8,128)S(1)} %convert_add_fusion, f32[128,1024]{1,0:T(8,128)S(1)} %copy-done.15, f32[256,1024]{1,0:T(8,128)S(1)} %copy-done.16, f32[256,1024]{1,0:T(8,128)S(1)} %copy-done.17), kind=kLoop, calls=%fused_computation.10 | loop fusion | flops 3407872 | bytes 7340032 | tf_op jit(solution)/shard_map/sub | solution.py:550
  168.5 2.8 %collective-permute-done.21.wrap = bf16[64,1024]{1,0:T(8,128)(2,1)S(1)} collective-permute-done((bf16[64,1024]{1,0:T(8,128)(2,1)S(1)}, bf16[64,1024]{1,0:T(8,128)(2,1)S(1)}, u32[]{:S(2)}, u32[]{:S(2)}) %collective-permute-start.21) | collective-permute-done | bytes 131104 | tf_op jit(solution)/shard_map/ppermute | solution.py:42
  (127 shorter events, 43.8 us)
Async XLA Ops:
  0.6 49.0 %collective-permute-start.5 = (bf16[256,1024]{1,0:T(8,128)(2,1)}, bf16[256,1024]{1,0:T(8,128)(2,1)S(1)}, u32[]{:S(2)}, u32[]{:S(2)}) collective-permute-start(bf16[256,1024]{1,0:T(8,128)(2,1)} %bitcast.19), channel_id=1, source_target_pairs={{0,32},{32,0},{1,33},{33,1},{2,34},{34,2},{3,35},{35,3},{4,36},{36... | collective-permute-start | bytes 1572872 | tf_op jit(solution)/shard_map/ppermute | solution.py:30
  2.8 46.8 %collective-permute-start.4 = (bf16[256,1024]{1,0:T(8,128)(2,1)}, bf16[256,1024]{1,0:T(8,128)(2,1)}, u32[]{:S(2)}, u32[]{:S(2)}) collective-permute-start(bf16[256,1024]{1,0:T(8,128)(2,1)} %bitcast.20), channel_id=1, source_target_pairs={{0,33},{33,0},{1,32},{32,1},{2,35},{35,2},{3,34},{34,3},{4,37},{37... | collective-permute-start | bytes 1572872 | tf_op jit(solution)/shard_map/ppermute | solution.py:34
  6.3 25.4 %collective-permute-start.2 = (f32[256,1024]{1,0:T(8,128)}, f32[256,1024]{1,0:T(8,128)}, u32[]{:S(2)}, u32[]{:S(2)}) collective-permute-start(f32[256,1024]{1,0:T(8,128)} %param.16), channel_id=1, source_target_pairs={{0,1},{1,0},{2,3},{3,2},{4,5},{5,4},{6,7},{7,6},{8,9},{9,8},{10,11... | collective-permute-start | bytes 3145736 | tf_op jit(solution)/shard_map/ppermute | solution.py:26
  12.6 37.0 %all-to-all-start = ((bf16[16,64,1024]{2,1,0:T(8,128)(2,1)}), bf16[16,64,1024]{2,1,0:T(8,128)(2,1)}, u32[]{:S(2)}, u32[]{:S(2)}) async-start(bf16[16,64,1024]{2,1,0:T(8,128)(2,1)} %shard_map.155), calls=%async_computation | async-start | bytes 4194304 | tf_op jit(solution)/shard_map/all_to_all | solution.py:50
  54.0 3.4 %collective-permute-start.6 = (bf16[256,1024]{1,0:T(8,128)(2,1)S(1)}, bf16[256,1024]{1,0:T(8,128)(2,1)S(1)}, u32[]{:S(2)}, u32[]{:S(2)}) collective-permute-start(bf16[256,1024]{1,0:T(8,128)(2,1)S(1)} %get-tuple-element.48), channel_id=1, source_target_pairs={{0,1},{1,0},{2,3},{3,2},{4,5},{5,4},{6,7},{7,6},{8,9},{9,8},{10,11... | collective-permute-start | bytes 1572872 | tf_op jit(solution)/shard_map/ppermute | solution.py:26
  57.6 18.2 %collective-permute-start.7 = (bf16[256,1024]{1,0:T(8,128)(2,1)S(1)}, bf16[256,1024]{1,0:T(8,128)(2,1)S(1)}, u32[]{:S(2)}, u32[]{:S(2)}) collective-permute-start(bf16[256,1024]{1,0:T(8,128)(2,1)S(1)} %add_convert_fusion.1), channel_id=1, source_target_pairs={{0,32},{32,0},{1,33},{33,1},{2,34},{34,2},{3,35},{35,3},{4,36},{36... | collective-permute-start | bytes 1572872 | tf_op jit(solution)/shard_map/ppermute | solution.py:30
  62.2 13.5 %collective-permute-start.3 = (bf16[256,1024]{1,0:T(8,128)(2,1)S(1)}, bf16[256,1024]{1,0:T(8,128)(2,1)S(1)}, u32[]{:S(2)}, u32[]{:S(2)}) collective-permute-start(bf16[256,1024]{1,0:T(8,128)(2,1)S(1)} %get-tuple-element.46), channel_id=1, source_target_pairs={{0,1},{1,0},{2,3},{3,2},{4,5},{5,4},{6,7},{7,6},{8,9},{9,8},{10,11... | collective-permute-start | bytes 1572872 | tf_op jit(solution)/shard_map/ppermute | solution.py:26
  78.6 13.7 %collective-permute-start.8 = (bf16[256,1152]{1,0:T(8,128)(2,1)}, bf16[256,1152]{1,0:T(8,128)(2,1)}, u32[]{:S(2)}, u32[]{:S(2)}) collective-permute-start(bf16[256,1152]{1,0:T(8,128)(2,1)} %get-tuple-element.58.refs_8_), channel_id=1, source_target_pairs={{0,32},{32,0},{1,33},{33,1},{2,34},{34,2},{3,35},{35,3},{4,36},{36... | collective-permute-start | bytes 1769480 | tf_op jit(solution)/shard_map/ppermute | solution.py:30
  78.8 11.1 %all-to-all-start.2 = ((bf16[16,8,1024]{2,1,0:T(8,128)(2,1)}), bf16[16,8,1024]{2,1,0:T(8,128)(2,1)S(1)}, u32[]{:S(2)}, u32[]{:S(2)}) async-start(bf16[16,8,1024]{2,1,0:T(8,128)(2,1)} %bitcast.9), calls=%async_computation.2 | async-start | bytes 524288 | tf_op jit(solution)/shard_map/all_to_all | solution.py:50
  82.6 32.2 %collective-permute-start.18 = (bf16[256,1152]{1,0:T(8,128)(2,1)}, bf16[256,1152]{1,0:T(8,128)(2,1)}, u32[]{:S(2)}, u32[]{:S(2)}) collective-permute-start(bf16[256,1152]{1,0:T(8,128)(2,1)} %get-tuple-element.58.refs_8_), channel_id=1, source_target_pairs={{0,1},{1,0},{2,3},{3,2},{4,5},{5,4},{6,7},{7,6},{8,9},{9,8},{10,11... | collective-permute-start | bytes 1769480 | tf_op jit(solution)/shard_map/ppermute | solution.py:26
  92.3 22.8 %collective-permute-start.17 = (bf16[256,1152]{1,0:T(8,128)(2,1)}, bf16[256,1152]{1,0:T(8,128)(2,1)S(1)}, u32[]{:S(2)}, u32[]{:S(2)}) collective-permute-start(bf16[256,1152]{1,0:T(8,128)(2,1)} %collective-permute-done.8.refs_6_), channel_id=1, source_target_pairs={{0,1},{1,0},{2,3},{3,2},{4,5},{5,4},{6,7},{7,6},{8,9},{9,8},{10,11... | collective-permute-start | bytes 1769480 | tf_op jit(solution)/shard_map/ppermute | solution.py:26
  95.3 12.0 %all-to-all-start.3 = ((bf16[16,8,1280]{2,1,0:T(8,128)(2,1)}), bf16[16,8,1280]{2,1,0:T(8,128)(2,1)S(1)}, u32[]{:S(2)}, u32[]{:S(2)}) async-start(bf16[16,8,1280]{2,1,0:T(8,128)(2,1)} %bitcast.11), calls=%async_computation.3 | async-start | bytes 655360 | tf_op jit(solution)/shard_map/all_to_all | solution.py:479
  108.6 6.4 %collective-permute-start.16 = (f32[8,1024]{1,0:T(8,128)S(1)}, f32[8,1024]{1,0:T(8,128)S(1)}, u32[]{:S(2)}, u32[]{:S(2)}) collective-permute-start(f32[8,1024]{1,0:T(8,128)S(1)} %get-tuple-element.67.refs_3_), channel_id=1, source_target_pairs={{0,1},{1,0},{2,3},{3,2},{4,5},{5,4},{6,7},{7,6},{8,9},{9,8},{10,11... | collective-permute-start | bytes 98312 | tf_op jit(solution)/shard_map/ppermute | solution.py:26
  110.4 4.6 %collective-permute-start.15 = (f32[8,1024]{1,0:T(8,128)S(1)}, f32[8,1024]{1,0:T(8,128)S(1)}, u32[]{:S(2)}, u32[]{:S(2)}) collective-permute-start(f32[8,1024]{1,0:T(8,128)S(1)} %get-tuple-element.67.refs_3_), channel_id=1, source_target_pairs={{0,32},{32,0},{1,33},{33,1},{2,34},{34,2},{3,35},{35,3},{4,36},{36... | collective-permute-start | bytes 98312 | tf_op jit(solution)/shard_map/ppermute | solution.py:30
  111.7 3.4 %collective-permute-start.14 = (f32[8,1024]{1,0:T(8,128)S(1)}, f32[8,1024]{1,0:T(8,128)S(1)}, u32[]{:S(2)}, u32[]{:S(2)}) collective-permute-start(f32[8,1024]{1,0:T(8,128)S(1)} %get-tuple-element.67.refs_3_), channel_id=1, source_target_pairs={{0,33},{33,0},{1,32},{32,1},{2,35},{35,2},{3,34},{34,3},{4,37},{37... | collective-permute-start | bytes 98312 | tf_op jit(solution)/shard_map/ppermute | solution.py:34
  114.8 13.8 %collective-permute-start.9 = (bf16[256,1024]{1,0:T(8,128)(2,1)}, bf16[256,1024]{1,0:T(8,128)(2,1)}, u32[]{:S(2)}, u32[]{:S(2)}) collective-permute-start(bf16[256,1024]{1,0:T(8,128)(2,1)} %get-tuple-element.66), channel_id=1, source_target_pairs={{0,1},{1,0},{2,3},{3,2},{4,5},{5,4},{6,7},{7,6},{8,9},{9,8},{10,11... | collective-permute-start | bytes 1572872 | tf_op jit(solution)/shard_map/ppermute | solution.py:26
  124.9 32.9 %all-to-all-start.4 = ((bf16[16,64,1024]{2,1,0:T(8,128)(2,1)}), bf16[16,64,1024]{2,1,0:T(8,128)(2,1)S(1)}, u32[]{:S(2)}, u32[]{:S(2)}) async-start(bf16[16,64,1024]{2,1,0:T(8,128)(2,1)} %shard_map.162), calls=%async_computation.4 | async-start | bytes 4194304 | tf_op jit(solution)/shard_map/all_to_all | solution.py:504
  130.0 7.6 %collective-permute-start.10 = (bf16[128,1024]{1,0:T(8,128)(2,1)S(1)}, bf16[128,1024]{1,0:T(8,128)(2,1)S(1)}, u32[]{:S(2)}, u32[]{:S(2)}) collective-permute-start(bf16[128,1024]{1,0:T(8,128)(2,1)S(1)} %get-tuple-element.85), channel_id=1, source_target_pairs={{0,32},{32,0},{1,33},{33,1},{2,34},{34,2},{3,35},{35,3},{4,36},{36... | collective-permute-start | bytes 786440 | tf_op jit(solution)/shard_map/ppermute | solution.py:30
  131.3 8.4 %collective-permute-start.12 = (bf16[128,1024]{1,0:T(8,128)(2,1)S(1)}, bf16[128,1024]{1,0:T(8,128)(2,1)S(1)}, u32[]{:S(2)}, u32[]{:S(2)}) collective-permute-start(bf16[128,1024]{1,0:T(8,128)(2,1)S(1)} %get-tuple-element.86), channel_id=1, source_target_pairs={{0,96},{96,0},{32,64},{64,32},{1,97},{97,1},{33,65},{65,33},{2,98}... | collective-permute-start | bytes 786440 | tf_op jit(solution)/shard_map/ppermute | solution.py:42
  139.9 7.6 %collective-permute-start.11 = (bf16[128,1024]{1,0:T(8,128)(2,1)S(1)}, bf16[128,1024]{1,0:T(8,128)(2,1)S(1)}, u32[]{:S(2)}, u32[]{:S(2)}) collective-permute-start(bf16[128,1024]{1,0:T(8,128)(2,1)S(1)} %get-tuple-element.83), channel_id=1, source_target_pairs={{0,96},{96,0},{32,64},{64,32},{1,97},{97,1},{33,65},{65,33},{2,98}... | collective-permute-start | bytes 786440 | tf_op jit(solution)/shard_map/ppermute | solution.py:42
  141.9 19.1 %collective-permute-start.13 = (bf16[128,1024]{1,0:T(8,128)(2,1)S(1)}, bf16[128,1024]{1,0:T(8,128)(2,1)}, u32[]{:S(2)}, u32[]{:S(2)}) collective-permute-start(bf16[128,1024]{1,0:T(8,128)(2,1)S(1)} %get-tuple-element.84), channel_id=1, source_target_pairs={{0,32},{32,0},{1,33},{33,1},{2,34},{34,2},{3,35},{35,3},{4,36},{36... | collective-permute-start | bytes 786440 | tf_op jit(solution)/shard_map/ppermute | solution.py:30
  162.0 6.5 %collective-permute-start.22 = (bf16[64,1024]{1,0:T(8,128)(2,1)S(1)}, bf16[64,1024]{1,0:T(8,128)(2,1)S(1)}, u32[]{:S(2)}, u32[]{:S(2)}) collective-permute-start(bf16[64,1024]{1,0:T(8,128)(2,1)S(1)} %maximum_maximum_fusion.own), channel_id=1, source_target_pairs={{0,64},{64,0},{1,65},{65,1},{2,66},{66,2},{3,67},{67,3},{4,68},{68... | collective-permute-start | bytes 393224 | tf_op jit(solution)/shard_map/ppermute | solution.py:38
  164.9 6.4 %collective-permute-start.21 = (bf16[64,1024]{1,0:T(8,128)(2,1)S(1)}, bf16[64,1024]{1,0:T(8,128)(2,1)S(1)}, u32[]{:S(2)}, u32[]{:S(2)}) collective-permute-start(bf16[64,1024]{1,0:T(8,128)(2,1)S(1)} %maximum_maximum_fusion.own), channel_id=1, source_target_pairs={{0,96},{96,0},{32,64},{64,32},{1,97},{97,1},{33,65},{65,33},{2,98}... | collective-permute-start | bytes 393224 | tf_op jit(solution)/shard_map/ppermute | solution.py:42
  165.7 5.9 %collective-permute-start.20 = (bf16[64,1024]{1,0:T(8,128)(2,1)S(1)}, bf16[64,1024]{1,0:T(8,128)(2,1)S(1)}, u32[]{:S(2)}, u32[]{:S(2)}) collective-permute-start(bf16[64,1024]{1,0:T(8,128)(2,1)S(1)} %maximum_maximum_fusion.own), channel_id=1, source_target_pairs={{0,32},{32,0},{1,33},{33,1},{2,34},{34,2},{3,35},{35,3},{4,36},{36... | collective-permute-start | bytes 393224 | tf_op jit(solution)/shard_map/ppermute | solution.py:30
  (29 other events, 275.5 us)

commit v4 on v3

--- a/solution.py
+++ b/solution.py
@@ -119,7 +119,7 @@
         ).astype(part.dtype)
 
 
-def forward(tok_a, tok_b, weights):
+def forward(tok_a, tok_b, weights, flops):
     return pl.pallas_call(
         forward_kernel,
         out_shape=(
@@ -136,7 +136,7 @@
             pltpu.SemaphoreType.DMA((3,)),
         ],
         compiler_params=LIMIT,
-        cost_estimate=cost(2**30, 6 * 2**20, 2**19),
+        cost_estimate=cost(flops, 6 * 2**20, 2**19),
     )(tok_a, tok_b, weights)
 
 
@@ -398,16 +398,18 @@
         out_specs=(WHOLE, WHOLE),
         cost_estimate=cost(2**25, 2**18),
     )(meta, w_in)
-    weights = gather_chips(
-        pl.pallas_call(
-            lay_kernel,
-            out_shape=shape((16, 64, width), BF16),
-            in_specs=[SCALARS, WHOLE, WHOLE, WHOLE],
-            out_specs=ANYWHERE,
-            scratch_shapes=[pltpu.VMEM((64, width), BF16), pltpu.SemaphoreType.DMA((16,))],
-            cost_estimate=cost(0, 2**21),
-        )(meta, mine, swap_core(theirs), w_out)
+    block = pl.pallas_call(
+        lay_kernel,
+        out_shape=shape((16, 64, width), BF16),
+        in_specs=[SCALARS, WHOLE, WHOLE, WHOLE],
+        out_specs=ANYWHERE,
+        scratch_shapes=[pltpu.VMEM((64, width), BF16), pltpu.SemaphoreType.DMA((16,))],
+        cost_estimate=cost(0, 2**21),
+    )(meta, mine, swap_core(theirs), w_out)
+    block, own_tok, label_tiles, shortlist, positives, owner_map = lax.optimization_barrier(
+        (block, own_tok, label_tiles, shortlist, positives, owner_map)
     )
+    weights = gather_chips(block)
 
     core_tok, near_tok, diag_tok = swap_core(own_tok), swap_near(own_tok), swap_diag(own_tok)
 
@@ -441,12 +443,12 @@
         (weights, cluster_live, share_hit, pos_part, tiles_hi, tiles_lo)
     )
 
-    near_a, near_b, near_hidden, near_slope = forward(diag_tok, near_tok, weights)
+    near_a, near_b, near_hidden, near_slope = forward(diag_tok, near_tok, weights, 2**30)
     near_sum = (near_b + swap_core(near_a).astype(F32)).astype(BF16)
     near_sum, pos_part = lax.optimization_barrier((near_sum, pos_part))
     from_near = swap_near(near_sum)
     pos_got = gather_chips(pos_part.reshape(16, docs, width))
-    own_a, own_b, own_hidden, own_slope = forward(core_tok, own_tok, weights)
+    own_a, own_b, own_hidden, own_slope = forward(core_tok, own_tok, weights, 2**36)
     from_near, pos_got = lax.optimization_barrier((from_near, pos_got))
     pos_mean = jnp.sum(pos_got.astype(F32), axis=0) * (1.0 / POS_SCALE)
     own_rows, emb = pl.pallas_call(

time: 174 us -> 173 us (level)
    unnamed x54 -> x59, local copies, waits for them, and re-layouts: 3.53 us -> 2.58 us
  transfers between devices with their start and end apart: 27 -> 27, of which waited for: 11 -> 13; matrix products, arithmetic and copies ran while one was open for 13% -> 13% of each run, Pallas kernels for 13% -> 11%
where the time goes in v4:
time: 173 us; the launch traced here: 172 us
  waiting for transfers between devices  54.8 us (32%)
  starting transfers between devices  46.2 us (27%)
  Pallas kernels  31.7 us (18%)
  other arithmetic  18.2 us (11%)
  blocking collectives  12.9 us (7%)
  local copies, waits for them, and re-layouts  5.37 us (3%)
    all_to_all x2, waiting for transfers between devices, gather_chips(): return lax.all_to_all(a, CHIPS, 0, 0, tiled=True)  19.6 us
    ppermute x10, starting transfers between devices, swap_core(): return lax.ppermute(a, 'c', [(0, 1), (1, 0)])  13.2 us
    all_to_all x1, blocking collectives, gather_chips(): return lax.all_to_all(a, CHIPS, 0, 0, tiled=True)  12.9 us
    all_to_all x2, starting transfers between devices, gather_chips(): return lax.all_to_all(a, CHIPS, 0, 0, tiled=True)  11.5 us
    ppermute x3, waiting for transfers between devices, swap_wrap(): return lax.ppermute(a, ('h', 'l'), [(0, 3), (3, 0), (1, 2), (2, 1)])  9.92 us
    reduce_max x1, other arithmetic, on_device(): jnp.max((short[:, :, None] == cluster_ids[None, None, :]).astype(F32), ax...  9.89 us
    pallas_call x1, Pallas kernels, backward(): pl.pallas_call(backward_kernel, out_shape=shape((16, 64, 1024), BF16), in...  9 us
    all_to_all x1, waiting for transfers between devices, on_device(): got = lax.all_to_all(send, CHIPS, 0, 0, tiled=True)  8.92 us
  transfers between devices with their start and end apart: 27, of which 13 were waited for; matrix products, arithmetic and copies ran while one was open for 13% of the time, Pallas kernels for 11%

profile of v4, /device:TPU:1, one launch (start us, length us, event | category | flops | bytes accessed | tf_op | source)
XLA Modules:
  0.0 171.8 jit_solution(17032734253648534323)
XLA Ops:
  6.2 2.5 %shard_map.155 = bf16[16,64,1024]{2,1,0:T(8,128)(2,1)} custom-call(s32[3]{0:T(128)} %pad_add_fusion.meta, bf16[32,512]{1,0:T(8,128)(2,1)} %get-tuple-element.48.mine, bf16[32,512]{1,0:T(8,128)(2,1)} %copy-done.26, bf16[64,1024]{1,0:T(8,128)(2,1)} %w_out.1), custom_call_target="tpu_custom_call" | custom-call | bytes 2097152 | tf_op jit(solution)/shard_map/pallas_call | solution.py:401
  10.8 7.7 %all-to-all-start = ((bf16[16,64,1024]{2,1,0:T(8,128)(2,1)}), bf16[16,64,1024]{2,1,0:T(8,128)(2,1)}, u32[]{:S(2)}, u32[]{:S(2)}) async-start(bf16[16,64,1024]{2,1,0:T(8,128)(2,1)} %shard_map.155), calls=%async_computation | async-start | bytes 4194304 | tf_op jit(solution)/shard_map/all_to_all | solution.py:50
  20.6 9.9 %convert_reduce_fusion.live = bf16[128,128]{1,0:T(8,128)(2,1)S(1)} fusion(s32[128]{0:T(128)S(1)} %select_reduce_fusion, s32[128,400]{1,0:T(8,128)S(1)} %dynamic-slice_bitcast_fusion), kind=kLoop, calls=%fused_computation | loop fusion | flops 19644416 | bytes 238080 | tf_op jit(solution)/shard_map/reduce_max | solution.py:425
  33.7 14.2 %all-to-all-done.weights.refs_17_ = bf16[16,64,1024]{2,1,0:T(8,128)(2,1)} async-done(((bf16[16,64,1024]{2,1,0:T(8,128)(2,1)}), bf16[16,64,1024]{2,1,0:T(8,128)(2,1)}, u32[]{:S(2)}, u32[]{:S(2)}) %all-to-all-start) | async-done | bytes 2097184 | tf_op jit(solution)/shard_map/all_to_all | solution.py:50
  47.8 4.3 %shard_map.157 = (bf16[256,1024]{1,0:T(8,128)(2,1)S(1)}, f32[256,1024]{1,0:T(8,128)S(1)}, bf16[512,512]{1,0:T(8,128)(2,1)S(1)}, f32[512,512]{1,0:T(8,128)S(1)}) custom-call(bf16[256,1024]{1,0:T(8,128)(2,1)} %collective-permute-done.4.tok_a.refs_9_, bf16[256,1024]{1,0:T(8,128)(2,1)S(1)} %collective-permute-done.5.tok_b.refs_10_, ...), custom_call_target="tpu_custom_call" | custom-call | flops 1073741824 | bytes 6291456 | tf_op jit(solution)/shard_map/pallas_call | solution.py:123
  57.0 3.2 %shard_map.156 = (bf16[256,1024]{1,0:T(8,128)(2,1)S(1)}, f32[256,1024]{1,0:T(8,128)S(1)}, bf16[512,512]{1,0:T(8,128)(2,1)S(1)}, f32[512,512]{1,0:T(8,128)S(1)}) custom-call(bf16[256,1024]{1,0:T(8,128)(2,1)S(1)} %collective-permute-done.1.tok_a.refs_11_, bf16[256,1024]{1,0:T(8,128)(2,1)S(1)} %bitcast.23, bf16[16,64,1024]{2,1,0:T(8,128)(2,1)} %all-to-all-done.weights.refs_17_), custom_call_target="tpu_custom_call" | custom-call | flops 68719476736 | bytes 6291456 | tf_op jit(solution)/shard_map/pallas_call | solution.py:123
  61.0 12.9 %all_to_all.25 = f16[16,8,1024]{2,1,0:T(8,128)(2,1)S(1)} all-to-all(f16[16,8,1024]{2,1,0:T(8,128)(2,1)S(1)} %bitcast.33), channel_id=1, replica_groups=mesh['h'=2,'l'=2,'x'=4,'z'=4,'c'=2] {'x','z'}, dimensions={0} | all-to-all | bytes 524288 | tf_op jit(solution)/shard_map/all_to_all | solution.py:50
  73.9 2.7 %shard_map.158 = (bf16[256,1152]{1,0:T(8,128)(2,1)}, bf16[128,1024]{1,0:T(8,128)(2,1)}) custom-call(s32[8]{0:T(128)S(1)} %copy-done.10, bf16[256,1024]{1,0:T(8,128)(2,1)S(1)} %bitcast.24, f32[256,1024]{1,0:T(8,128)S(1)} %get-tuple-element.57.part, bf16[256,1024]{1,0:T(8,128)(2,1)S(1)} %collective-permute-done.3.from_core, ...), custom_call_target="tpu_custom_call" | custom-call | flops 4194304 | bytes 4194304 | tf_op jit(solution)/shard_map/pallas_call | solution.py:454
  76.9 3.8 %all-to-all-start.2 = ((bf16[16,8,1024]{2,1,0:T(8,128)(2,1)}), bf16[16,8,1024]{2,1,0:T(8,128)(2,1)S(1)}, u32[]{:S(2)}, u32[]{:S(2)}) async-start(bf16[16,8,1024]{2,1,0:T(8,128)(2,1)} %bitcast.9), calls=%async_computation.2 | async-start | bytes 524288 | tf_op jit(solution)/shard_map/all_to_all | solution.py:50
  82.6 5.4 %all-to-all-done.2 = bf16[16,8,1024]{2,1,0:T(8,128)(2,1)S(1)} async-done(((bf16[16,8,1024]{2,1,0:T(8,128)(2,1)}), bf16[16,8,1024]{2,1,0:T(8,128)(2,1)S(1)}, u32[]{:S(2)}, u32[]{:S(2)}) %all-to-all-start.2) | async-done | bytes 262176 | tf_op jit(solution)/shard_map/all_to_all | solution.py:50
  88.0 2.3 %shard_map.159 = (bf16[128,1280]{1,0:T(8,128)(2,1)}, f32[128,512]{1,0:T(8,128)S(1)}) custom-call(bf16[128,1024]{1,0:T(8,128)(2,1)S(1)} %bitcast.25, bf16[512,1024]{1,0:T(8,128)(2,1)S(1)} %get-tuple-element.66.tiles_hi, bf16[512,1024]{1,0:T(8,128)(2,1)S(1)} %get-tuple-element.67.tiles_lo, bf16[128,128]{1,0:T(8,128)(2,1)S(1)} %convert_reduce_fusion.live), custom_call_target="tpu_custom_call" | custom-call | flops 536870912 | bytes 3145728 | tf_op jit(solution)/shard_map/pallas_call | solution.py:466
  90.4 3.1 %collective-permute-start.17 = (bf16[256,1152]{1,0:T(8,128)(2,1)}, bf16[256,1152]{1,0:T(8,128)(2,1)S(1)}, u32[]{:S(2)}, u32[]{:S(2)}) collective-permute-start(bf16[256,1152]{1,0:T(8,128)(2,1)} %collective-permute-done.8.refs_6_), channel_id=1, source_target_pairs={{0,1},{1,0},{2,3},{3,2},{4,5},{5,4},{6,7},{7,6},{8,9},{9,8},{10,11... | collective-permute-start | bytes 1769480 | tf_op jit(solution)/shard_map/ppermute | solution.py:26
  93.5 3.5 %all-to-all-start.3 = ((bf16[16,8,1280]{2,1,0:T(8,128)(2,1)}), bf16[16,8,1280]{2,1,0:T(8,128)(2,1)S(1)}, u32[]{:S(2)}, u32[]{:S(2)}) async-start(bf16[16,8,1280]{2,1,0:T(8,128)(2,1)} %bitcast.11), calls=%async_computation.3 | async-start | bytes 655360 | tf_op jit(solution)/shard_map/all_to_all | solution.py:481
  97.1 8.4 %all-to-all-done.3.got_hbm = bf16[16,8,1280]{2,1,0:T(8,128)(2,1)S(1)} async-done(((bf16[16,8,1280]{2,1,0:T(8,128)(2,1)}), bf16[16,8,1280]{2,1,0:T(8,128)(2,1)S(1)}, u32[]{:S(2)}, u32[]{:S(2)}) %all-to-all-start.3) | async-done | bytes 327712 | tf_op jit(solution)/shard_map/all_to_all | solution.py:481
  114.0 9.0 %shard_map.162 = bf16[16,64,1024]{2,1,0:T(8,128)(2,1)} custom-call(f32[8,1024]{1,0:T(8,128)} %copy-done.25, f32[8,1024]{1,0:T(8,128)} %copy-done.24, f32[8,1024]{1,0:T(8,128)} %copy-done.23, f32[8,1024]{1,0:T(8,128)} %copy-done.7, f32[1,1024]{1,0:T(1,128)} %bitcast.27, bf16[256,1152]{1,0:T(8,128)(2,1)} %copy-done.21, ...), custom_call_target="tpu_custom_call" | custom-call | flops 3221225472 | bytes 10485760 | tf_op jit(solution)/shard_map/pallas_call | solution.py:307
  123.0 3.7 %all-to-all-start.4 = ((bf16[16,64,1024]{2,1,0:T(8,128)(2,1)}), bf16[16,64,1024]{2,1,0:T(8,128)(2,1)S(1)}, u32[]{:S(2)}, u32[]{:S(2)}) async-start(bf16[16,64,1024]{2,1,0:T(8,128)(2,1)} %shard_map.162), calls=%async_computation.4 | async-start | bytes 4194304 | tf_op jit(solution)/shard_map/all_to_all | solution.py:506
  131.3 4.4 %collective-permute-done.10 = bf16[128,1024]{1,0:T(8,128)(2,1)S(1)} collective-permute-done((bf16[128,1024]{1,0:T(8,128)(2,1)S(1)}, bf16[128,1024]{1,0:T(8,128)(2,1)S(1)}, u32[]{:S(2)}, u32[]{:S(2)}) %collective-permute-start.10) | collective-permute-done | bytes 262176 | tf_op jit(solution)/shard_map/ppermute | solution.py:30
  135.6 2.2 %collective-permute-done.12 = bf16[128,1024]{1,0:T(8,128)(2,1)S(1)} collective-permute-done((bf16[128,1024]{1,0:T(8,128)(2,1)S(1)}, bf16[128,1024]{1,0:T(8,128)(2,1)S(1)}, u32[]{:S(2)}, u32[]{:S(2)}) %collective-permute-start.12) | collective-permute-done | bytes 262176 | tf_op jit(solution)/shard_map/ppermute | solution.py:42
  141.2 5.0 %collective-permute-done.11 = bf16[128,1024]{1,0:T(8,128)(2,1)S(1)} collective-permute-done((bf16[128,1024]{1,0:T(8,128)(2,1)S(1)}, bf16[128,1024]{1,0:T(8,128)(2,1)S(1)}, u32[]{:S(2)}, u32[]{:S(2)}) %collective-permute-start.11) | collective-permute-done | bytes 262176 | tf_op jit(solution)/shard_map/ppermute | solution.py:42
  147.0 8.9 %all-to-all-done.4.got = bf16[16,64,1024]{2,1,0:T(8,128)(2,1)S(1)} async-done(((bf16[16,64,1024]{2,1,0:T(8,128)(2,1)}), bf16[16,64,1024]{2,1,0:T(8,128)(2,1)S(1)}, u32[]{:S(2)}, u32[]{:S(2)}) %all-to-all-start.4) | async-done | bytes 2097184 | tf_op jit(solution)/shard_map/all_to_all | solution.py:506
  157.0 2.0 %collective-permute-start.19 = (bf16[32,512]{1,0:T(8,128)(2,1)S(1)}, bf16[32,512]{1,0:T(8,128)(2,1)S(1)}, u32[]{:S(2)}, u32[]{:S(2)}) collective-permute-start(bf16[32,512]{1,0:T(8,128)(2,1)S(1)} %get-tuple-element.87), channel_id=1, source_target_pairs={{0,1},{1,0},{2,3},{3,2},{4,5},{5,4},{6,7},{7,6},{8,9},{9,8},{10,11... | collective-permute-start | bytes 98312 | tf_op jit(solution)/shard_map/ppermute | solution.py:26
  160.2 2.9 %collective-permute-start.22 = (bf16[64,1024]{1,0:T(8,128)(2,1)S(1)}, bf16[64,1024]{1,0:T(8,128)(2,1)S(1)}, u32[]{:S(2)}, u32[]{:S(2)}) collective-permute-start(bf16[64,1024]{1,0:T(8,128)(2,1)S(1)} %maximum_maximum_fusion.own), channel_id=1, source_target_pairs={{0,64},{64,0},{1,65},{65,1},{2,66},{66,2},{3,67},{67,3},{4,68},{68... | collective-permute-start | bytes 393224 | tf_op jit(solution)/shard_map/ppermute | solution.py:38
  163.9 2.1 %divide_subtract_fusion = (f32[256,1024]{1,0:T(8,128)}, f32[256,1024]{1,0:T(8,128)}, f32[256,1024]{1,0:T(8,128)}) fusion(f32[256,1024]{1,0:T(8,128)S(1)} %copy-done.14, f32[128,1024]{1,0:T(8,128)S(1)} %convert_add_fusion, f32[128,1024]{1,0:T(8,128)S(1)} %copy-done.17, f32[256,1024]{1,0:T(8,128)S(1)} %copy-done.18, f32[256,1024]{1,0:T(8,128)S(1)} %copy-done.19), kind=kLoop, calls=%fused_computation.10 | loop fusion | flops 3407872 | bytes 7340032 | tf_op jit(solution)/shard_map/sub | solution.py:552
  166.8 2.8 %collective-permute-done.21.wrap = bf16[64,1024]{1,0:T(8,128)(2,1)S(1)} collective-permute-done((bf16[64,1024]{1,0:T(8,128)(2,1)S(1)}, bf16[64,1024]{1,0:T(8,128)(2,1)S(1)}, u32[]{:S(2)}, u32[]{:S(2)}) %collective-permute-start.21) | collective-permute-done | bytes 131104 | tf_op jit(solution)/shard_map/ppermute | solution.py:42
  (133 shorter events, 43.6 us)
Async XLA Ops:
  8.8 39.1 %collective-permute-start.5 = (bf16[256,1024]{1,0:T(8,128)(2,1)S(1)}, bf16[256,1024]{1,0:T(8,128)(2,1)S(1)}, u32[]{:S(2)}, u32[]{:S(2)}) collective-permute-start(bf16[256,1024]{1,0:T(8,128)(2,1)S(1)} %bitcast.20), channel_id=1, source_target_pairs={{0,32},{32,0},{1,33},{33,1},{2,34},{34,2},{3,35},{35,3},{4,36},{36... | collective-permute-start | bytes 1572872 | tf_op jit(solution)/shard_map/ppermute | solution.py:30
  10.2 37.6 %collective-permute-start.4 = (bf16[256,1024]{1,0:T(8,128)(2,1)S(1)}, bf16[256,1024]{1,0:T(8,128)(2,1)}, u32[]{:S(2)}, u32[]{:S(2)}) collective-permute-start(bf16[256,1024]{1,0:T(8,128)(2,1)S(1)} %bitcast.21), channel_id=1, source_target_pairs={{0,33},{33,0},{1,32},{32,1},{2,35},{35,2},{3,34},{34,3},{4,37},{37... | collective-permute-start | bytes 1572872 | tf_op jit(solution)/shard_map/ppermute | solution.py:34
  10.8 37.0 %all-to-all-start = ((bf16[16,64,1024]{2,1,0:T(8,128)(2,1)}), bf16[16,64,1024]{2,1,0:T(8,128)(2,1)}, u32[]{:S(2)}, u32[]{:S(2)}) async-start(bf16[16,64,1024]{2,1,0:T(8,128)(2,1)} %shard_map.155), calls=%async_computation | async-start | bytes 4194304 | tf_op jit(solution)/shard_map/all_to_all | solution.py:50
  19.0 11.6 %collective-permute-start.2 = (f32[256,1024]{1,0:T(8,128)S(1)}, f32[256,1024]{1,0:T(8,128)}, u32[]{:S(2)}, u32[]{:S(2)}) collective-permute-start(f32[256,1024]{1,0:T(8,128)S(1)} %copy-done.13), channel_id=1, source_target_pairs={{0,1},{1,0},{2,3},{3,2},{4,5},{5,4},{6,7},{7,6},{8,9},{9,8},{10,11... | collective-permute-start | bytes 3145736 | tf_op jit(solution)/shard_map/ppermute | solution.py:26
  52.2 3.2 %collective-permute-start.6 = (bf16[256,1024]{1,0:T(8,128)(2,1)S(1)}, bf16[256,1024]{1,0:T(8,128)(2,1)S(1)}, u32[]{:S(2)}, u32[]{:S(2)}) collective-permute-start(bf16[256,1024]{1,0:T(8,128)(2,1)S(1)} %get-tuple-element.60), channel_id=1, source_target_pairs={{0,1},{1,0},{2,3},{3,2},{4,5},{5,4},{6,7},{7,6},{8,9},{9,8},{10,11... | collective-permute-start | bytes 1572872 | tf_op jit(solution)/shard_map/ppermute | solution.py:26
  55.6 18.3 %collective-permute-start.7 = (bf16[256,1024]{1,0:T(8,128)(2,1)S(1)}, bf16[256,1024]{1,0:T(8,128)(2,1)S(1)}, u32[]{:S(2)}, u32[]{:S(2)}) collective-permute-start(bf16[256,1024]{1,0:T(8,128)(2,1)S(1)} %add_convert_fusion.1), channel_id=1, source_target_pairs={{0,32},{32,0},{1,33},{33,1},{2,34},{34,2},{3,35},{35,3},{4,36},{36... | collective-permute-start | bytes 1572872 | tf_op jit(solution)/shard_map/ppermute | solution.py:30
  60.2 13.7 %collective-permute-start.3 = (bf16[256,1024]{1,0:T(8,128)(2,1)S(1)}, bf16[256,1024]{1,0:T(8,128)(2,1)S(1)}, u32[]{:S(2)}, u32[]{:S(2)}) collective-permute-start(bf16[256,1024]{1,0:T(8,128)(2,1)S(1)} %get-tuple-element.58), channel_id=1, source_target_pairs={{0,1},{1,0},{2,3},{3,2},{4,5},{5,4},{6,7},{7,6},{8,9},{9,8},{10,11... | collective-permute-start | bytes 1572872 | tf_op jit(solution)/shard_map/ppermute | solution.py:26
  76.7 13.7 %collective-permute-start.8 = (bf16[256,1152]{1,0:T(8,128)(2,1)}, bf16[256,1152]{1,0:T(8,128)(2,1)}, u32[]{:S(2)}, u32[]{:S(2)}) collective-permute-start(bf16[256,1152]{1,0:T(8,128)(2,1)} %get-tuple-element.70.refs_8_), channel_id=1, source_target_pairs={{0,32},{32,0},{1,33},{33,1},{2,34},{34,2},{3,35},{35,3},{4,36},{36... | collective-permute-start | bytes 1769480 | tf_op jit(solution)/shard_map/ppermute | solution.py:30
  76.9 11.1 %all-to-all-start.2 = ((bf16[16,8,1024]{2,1,0:T(8,128)(2,1)}), bf16[16,8,1024]{2,1,0:T(8,128)(2,1)S(1)}, u32[]{:S(2)}, u32[]{:S(2)}) async-start(bf16[16,8,1024]{2,1,0:T(8,128)(2,1)} %bitcast.9), calls=%async_computation.2 | async-start | bytes 524288 | tf_op jit(solution)/shard_map/all_to_all | solution.py:50
  80.7 32.2 %collective-permute-start.18 = (bf16[256,1152]{1,0:T(8,128)(2,1)}, bf16[256,1152]{1,0:T(8,128)(2,1)}, u32[]{:S(2)}, u32[]{:S(2)}) collective-permute-start(bf16[256,1152]{1,0:T(8,128)(2,1)} %get-tuple-element.70.refs_8_), channel_id=1, source_target_pairs={{0,1},{1,0},{2,3},{3,2},{4,5},{5,4},{6,7},{7,6},{8,9},{9,8},{10,11... | collective-permute-start | bytes 1769480 | tf_op jit(solution)/shard_map/ppermute | solution.py:26
  90.4 22.8 %collective-permute-start.17 = (bf16[256,1152]{1,0:T(8,128)(2,1)}, bf16[256,1152]{1,0:T(8,128)(2,1)S(1)}, u32[]{:S(2)}, u32[]{:S(2)}) collective-permute-start(bf16[256,1152]{1,0:T(8,128)(2,1)} %collective-permute-done.8.refs_6_), channel_id=1, source_target_pairs={{0,1},{1,0},{2,3},{3,2},{4,5},{5,4},{6,7},{7,6},{8,9},{9,8},{10,11... | collective-permute-start | bytes 1769480 | tf_op jit(solution)/shard_map/ppermute | solution.py:26
  93.5 12.0 %all-to-all-start.3 = ((bf16[16,8,1280]{2,1,0:T(8,128)(2,1)}), bf16[16,8,1280]{2,1,0:T(8,128)(2,1)S(1)}, u32[]{:S(2)}, u32[]{:S(2)}) async-start(bf16[16,8,1280]{2,1,0:T(8,128)(2,1)} %bitcast.11), calls=%async_computation.3 | async-start | bytes 655360 | tf_op jit(solution)/shard_map/all_to_all | solution.py:481
  106.7 6.4 %collective-permute-start.16 = (f32[8,1024]{1,0:T(8,128)S(1)}, f32[8,1024]{1,0:T(8,128)S(1)}, u32[]{:S(2)}, u32[]{:S(2)}) collective-permute-start(f32[8,1024]{1,0:T(8,128)S(1)} %get-tuple-element.79.refs_3_), channel_id=1, source_target_pairs={{0,1},{1,0},{2,3},{3,2},{4,5},{5,4},{6,7},{7,6},{8,9},{9,8},{10,11... | collective-permute-start | bytes 98312 | tf_op jit(solution)/shard_map/ppermute | solution.py:26
  108.5 4.6 %collective-permute-start.15 = (f32[8,1024]{1,0:T(8,128)S(1)}, f32[8,1024]{1,0:T(8,128)S(1)}, u32[]{:S(2)}, u32[]{:S(2)}) collective-permute-start(f32[8,1024]{1,0:T(8,128)S(1)} %get-tuple-element.79.refs_3_), channel_id=1, source_target_pairs={{0,32},{32,0},{1,33},{33,1},{2,34},{34,2},{3,35},{35,3},{4,36},{36... | collective-permute-start | bytes 98312 | tf_op jit(solution)/shard_map/ppermute | solution.py:30
  109.8 3.4 %collective-permute-start.14 = (f32[8,1024]{1,0:T(8,128)S(1)}, f32[8,1024]{1,0:T(8,128)S(1)}, u32[]{:S(2)}, u32[]{:S(2)}) collective-permute-start(f32[8,1024]{1,0:T(8,128)S(1)} %get-tuple-element.79.refs_3_), channel_id=1, source_target_pairs={{0,33},{33,0},{1,32},{32,1},{2,35},{35,2},{3,34},{34,3},{4,37},{37... | collective-permute-start | bytes 98312 | tf_op jit(solution)/shard_map/ppermute | solution.py:34
  113.0 13.8 %collective-permute-start.9 = (bf16[256,1024]{1,0:T(8,128)(2,1)}, bf16[256,1024]{1,0:T(8,128)(2,1)}, u32[]{:S(2)}, u32[]{:S(2)}) collective-permute-start(bf16[256,1024]{1,0:T(8,128)(2,1)} %get-tuple-element.78), channel_id=1, source_target_pairs={{0,1},{1,0},{2,3},{3,2},{4,5},{5,4},{6,7},{7,6},{8,9},{9,8},{10,11... | collective-permute-start | bytes 1572872 | tf_op jit(solution)/shard_map/ppermute | solution.py:26
  123.0 32.9 %all-to-all-start.4 = ((bf16[16,64,1024]{2,1,0:T(8,128)(2,1)}), bf16[16,64,1024]{2,1,0:T(8,128)(2,1)S(1)}, u32[]{:S(2)}, u32[]{:S(2)}) async-start(bf16[16,64,1024]{2,1,0:T(8,128)(2,1)} %shard_map.162), calls=%async_computation.4 | async-start | bytes 4194304 | tf_op jit(solution)/shard_map/all_to_all | solution.py:506
  128.0 7.6 %collective-permute-start.10 = (bf16[128,1024]{1,0:T(8,128)(2,1)S(1)}, bf16[128,1024]{1,0:T(8,128)(2,1)S(1)}, u32[]{:S(2)}, u32[]{:S(2)}) collective-permute-start(bf16[128,1024]{1,0:T(8,128)(2,1)S(1)} %get-tuple-element.97), channel_id=1, source_target_pairs={{0,32},{32,0},{1,33},{33,1},{2,34},{34,2},{3,35},{35,3},{4,36},{36... | collective-permute-start | bytes 786440 | tf_op jit(solution)/shard_map/ppermute | solution.py:30
  129.4 8.4 %collective-permute-start.12 = (bf16[128,1024]{1,0:T(8,128)(2,1)S(1)}, bf16[128,1024]{1,0:T(8,128)(2,1)S(1)}, u32[]{:S(2)}, u32[]{:S(2)}) collective-permute-start(bf16[128,1024]{1,0:T(8,128)(2,1)S(1)} %get-tuple-element.98), channel_id=1, source_target_pairs={{0,96},{96,0},{32,64},{64,32},{1,97},{97,1},{33,65},{65,33},{2,98}... | collective-permute-start | bytes 786440 | tf_op jit(solution)/shard_map/ppermute | solution.py:42
  138.7 7.5 %collective-permute-start.11 = (bf16[128,1024]{1,0:T(8,128)(2,1)S(1)}, bf16[128,1024]{1,0:T(8,128)(2,1)S(1)}, u32[]{:S(2)}, u32[]{:S(2)}) collective-permute-start(bf16[128,1024]{1,0:T(8,128)(2,1)S(1)} %get-tuple-element.95), channel_id=1, source_target_pairs={{0,96},{96,0},{32,64},{64,32},{1,97},{97,1},{33,65},{65,33},{2,98}... | collective-permute-start | bytes 786440 | tf_op jit(solution)/shard_map/ppermute | solution.py:42
  140.6 18.5 %collective-permute-start.13 = (bf16[128,1024]{1,0:T(8,128)(2,1)}, bf16[128,1024]{1,0:T(8,128)(2,1)}, u32[]{:S(2)}, u32[]{:S(2)}) collective-permute-start(bf16[128,1024]{1,0:T(8,128)(2,1)} %get-tuple-element.96), channel_id=1, source_target_pairs={{0,32},{32,0},{1,33},{33,1},{2,34},{34,2},{3,35},{35,3},{4,36},{36... | collective-permute-start | bytes 786440 | tf_op jit(solution)/shard_map/ppermute | solution.py:30
  160.2 6.6 %collective-permute-start.22 = (bf16[64,1024]{1,0:T(8,128)(2,1)S(1)}, bf16[64,1024]{1,0:T(8,128)(2,1)S(1)}, u32[]{:S(2)}, u32[]{:S(2)}) collective-permute-start(bf16[64,1024]{1,0:T(8,128)(2,1)S(1)} %maximum_maximum_fusion.own), channel_id=1, source_target_pairs={{0,64},{64,0},{1,65},{65,1},{2,66},{66,2},{3,67},{67,3},{4,68},{68... | collective-permute-start | bytes 393224 | tf_op jit(solution)/shard_map/ppermute | solution.py:38
  163.1 6.5 %collective-permute-start.21 = (bf16[64,1024]{1,0:T(8,128)(2,1)S(1)}, bf16[64,1024]{1,0:T(8,128)(2,1)S(1)}, u32[]{:S(2)}, u32[]{:S(2)}) collective-permute-start(bf16[64,1024]{1,0:T(8,128)(2,1)S(1)} %maximum_maximum_fusion.own), channel_id=1, source_target_pairs={{0,96},{96,0},{32,64},{64,32},{1,97},{97,1},{33,65},{65,33},{2,98}... | collective-permute-start | bytes 393224 | tf_op jit(solution)/shard_map/ppermute | solution.py:42
  163.9 6.0 %collective-permute-start.20 = (bf16[64,1024]{1,0:T(8,128)(2,1)S(1)}, bf16[64,1024]{1,0:T(8,128)(2,1)S(1)}, u32[]{:S(2)}, u32[]{:S(2)}) collective-permute-start(bf16[64,1024]{1,0:T(8,128)(2,1)S(1)} %maximum_maximum_fusion.own), channel_id=1, source_target_pairs={{0,32},{32,0},{1,33},{33,1},{2,34},{34,2},{3,35},{35,3},{4,36},{36... | collective-permute-start | bytes 393224 | tf_op jit(solution)/shard_map/ppermute | solution.py:30
  (32 other events, 302.4 us)

commit v5 on v4

--- a/solution.py
+++ b/solution.py
@@ -69,8 +69,13 @@
     return lax.broadcasted_iota(jnp.int32, dims, axis)
 
 
-def pick_kernel(meta, w_in, mine, theirs):
-    core, role = meta[0], meta[1]
+def place_of():
+    core, high, low = (lax.axis_index(axis) for axis in ("c", "h", "l"))
+    return core, high + low - 2 * high * low
+
+
+def pick_kernel(w_in, mine, theirs):
+    core, role = place_of()
     part = jnp.where(iota((512, 256), 1) < 128, core * 2 + role, 2 - core * 2 + role)
     at = iota((512, 256), 1) % 128
     spread = (iota((512, 256), 0) == at // 32 * 128 + part * 32 + at % 32).astype(BF16)
@@ -80,11 +85,15 @@
         theirs[:, i * 128 : i * 128 + 128] = got[:, 128:]
 
 
-def lay_kernel(meta, mine, theirs, w_out, out, block, sems):
-    core, role = meta[0], meta[1]
-    block[:32] = jnp.where(role == 0, w_out[:32], w_out[32:])
+def lay_kernel(mine, theirs, w_out, out, block, sems):
+    core, role = place_of()
+    top = pltpu.make_async_copy(
+        w_out.at[pl.ds(pl.multiple_of(role * 32, 32), 32)], block.at[0:32], sems.at[16]
+    )
+    top.start()
     block[32:, :512] = jnp.where(core == 0, mine[...], theirs[...])
     block[32:, 512:] = jnp.where(core == 0, theirs[...], mine[...])
+    top.wait()
     copies = [pltpu.make_async_copy(block, out.at[i], sems.at[i]) for i in range(16)]
     for copy in copies:
         copy.start()
@@ -92,7 +101,7 @@
         copy.wait()
 
 
-def forward_kernel(tok_a, tok_b, weights, part_a, part_b, hidden, slope, w_in, w_out, sems):
+def forward_kernel(tok, weights, part, hidden, slope, w_in, w_out, sems):
     copies = [
         pltpu.make_async_copy(
             weights.at[:, 32:64, k * 512 : k * 512 + 512], w_in.at[:, k * 32 : k * 32 + 32], sems.at[k]
@@ -104,40 +113,31 @@
         copy.start()
     copies[0].wait()
     copies[1].wait()
-    for k, (tok, part) in enumerate(((tok_a, part_a), (tok_b, part_b))):
-        pre_act = jnp.dot(tok[...], w_in[...].reshape(1024, 512), preferred_element_type=F32)
-        normal_cdf = 0.5 * (1.0 + lax.erf(pre_act * INV_ROOT_TWO))
-        act = (pre_act * normal_cdf).astype(BF16)
-        hidden[k * 256 : k * 256 + 256] = act
-        slope[k * 256 : k * 256 + 256] = (
-            normal_cdf + pre_act * jnp.exp(-0.5 * pre_act * pre_act) * INV_ROOT_TWO_PI
-        )
-        if k == 0:
-            copies[2].wait()
-        part[...] = jnp.dot(
-            act, w_out[...].reshape(512, 1024), preferred_element_type=F32
-        ).astype(part.dtype)
-
-
-def forward(tok_a, tok_b, weights, flops):
+    pre_act = jnp.dot(tok[...], w_in[...].reshape(1024, 512), preferred_element_type=F32)
+    normal_cdf = 0.5 * (1.0 + lax.erf(pre_act * INV_ROOT_TWO))
+    act = (pre_act * normal_cdf).astype(BF16)
+    copies[2].wait()
+    part[...] = jnp.dot(
+        act, w_out[...].reshape(512, 1024), preferred_element_type=F32
+    ).astype(part.dtype)
+    hidden[...] = act
+    slope[...] = normal_cdf + pre_act * jnp.exp(-0.5 * pre_act * pre_act) * INV_ROOT_TWO_PI
+
+
+def forward(tok, weights, dtype):
     return pl.pallas_call(
         forward_kernel,
-        out_shape=(
-            shape((256, 1024), BF16),
-            shape((256, 1024), F32),
-            shape((512, 512), BF16),
-            shape((512, 512), F32),
-        ),
-        in_specs=[WHOLE, WHOLE, ANYWHERE],
-        out_specs=(WHOLE,) * 4,
+        out_shape=(shape((256, 1024), dtype), shape((256, 512), BF16), shape((256, 512), F32)),
+        in_specs=[WHOLE, ANYWHERE],
+        out_specs=(WHOLE,) * 3,
         scratch_shapes=[
             pltpu.VMEM((16, 64, 512), BF16),
             pltpu.VMEM((16, 32, 1024), BF16),
             pltpu.SemaphoreType.DMA((3,)),
         ],
         compiler_params=LIMIT,
-        cost_estimate=cost(flops, 6 * 2**20, 2**19),
-    )(tok_a, tok_b, weights)
+        cost_estimate=cost(2**32, 6 * 2**20, 2**18),
+    )(tok, weights)
 
 
 def norm_kernel(lengths, tok, part, from_core, from_near, gain, rows, emb_hbm, emb, sem):
@@ -230,8 +230,8 @@
 def backward_kernel(*refs):
     grads, gain = refs[:4], refs[4]
     rows, toks = refs[5:9], refs[9:13]
-    hiddens, slopes, weights, out = refs[13:15], refs[15:17], refs[17], refs[18]
-    row_buf, tok_buf, hid_buf, slope_buf, w_out, sum_grad, act_grad, result, sems = refs[19:]
+    hiddens, slopes, weights, out = refs[13:17], refs[17:21], refs[21], refs[22]
+    row_buf, tok_buf, hid_buf, slope_buf, w_out, sum_grad, act_grad, result, sems = refs[23:]
     sent = []
     first = pltpu.make_async_copy(weights.at[:, 0:32], w_out, sems.at[0])
     first.start()
@@ -240,13 +240,13 @@
         at = pl.ds(k * 256, 256)
         row_copies.append(pltpu.make_async_copy(rows[k], row_buf.at[at], sems.at[1 + k]))
         row_copies[k].start()
-    for k in range(2):
-        at = pl.ds(k * 512, 512)
-        slope_copies.append(pltpu.make_async_copy(slopes[k], slope_buf.at[at], sems.at[5 + k]))
+    for k in range(4):
+        at = pl.ds(k * 256, 256)
+        slope_copies.append(pltpu.make_async_copy(slopes[k], slope_buf.at[at], sems.at[21 + k]))
         slope_copies[k].start()
-    for k in range(2):
-        at = pl.ds(k * 512, 512)
-        hid_copies.append(pltpu.make_async_copy(hiddens[k], hid_buf.at[at], sems.at[7 + k]))
+    for k in range(4):
+        at = pl.ds(k * 256, 256)
+        hid_copies.append(pltpu.make_async_copy(hiddens[k], hid_buf.at[at], sems.at[5 + k]))
         hid_copies[k].start()
     for k in range(4):
         at = pl.ds(k * 256, 256)
@@ -271,8 +271,7 @@
             ).astype(BF16)
         if k == 0:
             first.wait()
-        if k % 2 == 0:
-            slope_copies[k // 2].wait()
+        slope_copies[k].wait()
         at = pl.ds(k * 256, 256)
         back = lax.dot_general(
             sum_grad[at], w_out[...].reshape(512, 1024), LAST, preferred_element_type=F32
@@ -307,7 +306,7 @@
     return pl.pallas_call(
         backward_kernel,
         out_shape=shape((16, 64, 1024), BF16),
-        in_specs=[WHOLE] * 5 + [ANYWHERE] * 13,
+        in_specs=[WHOLE] * 5 + [ANYWHERE] * 17,
         out_specs=ANYWHERE,
         scratch_shapes=[
             pltpu.VMEM((1024, 1152), BF16),
@@ -318,7 +317,7 @@
             pltpu.VMEM((1024, 1024), BF16),
             pltpu.VMEM((1024, 512), BF16),
             pltpu.VMEM((16, 64, 1024), BF16),
-            pltpu.SemaphoreType.DMA((21,)),
+            pltpu.SemaphoreType.DMA((25,)),
         ],
         compiler_params=MOST,
         cost_estimate=cost(3 * 2**30, 10 * 2**20),
@@ -394,24 +393,22 @@
     mine, theirs = pl.pallas_call(
         pick_kernel,
         out_shape=(shape((32, 512), BF16),) * 2,
-        in_specs=[SCALARS, WHOLE],
+        in_specs=[WHOLE],
         out_specs=(WHOLE, WHOLE),
         cost_estimate=cost(2**25, 2**18),
-    )(meta, w_in)
+    )(w_in)
     block = pl.pallas_call(
         lay_kernel,
         out_shape=shape((16, 64, width), BF16),
-        in_specs=[SCALARS, WHOLE, WHOLE, WHOLE],
+        in_specs=[WHOLE, WHOLE, ANYWHERE],
         out_specs=ANYWHERE,
-        scratch_shapes=[pltpu.VMEM((64, width), BF16), pltpu.SemaphoreType.DMA((16,))],
+        scratch_shapes=[pltpu.VMEM((64, width), BF16), pltpu.SemaphoreType.DMA((17,))],
         cost_estimate=cost(0, 2**21),
-    )(meta, mine, swap_core(theirs), w_out)
+    )(mine, swap_core(theirs), w_out)
     block, own_tok, label_tiles, shortlist, positives, owner_map = lax.optimization_barrier(
         (block, own_tok, label_tiles, shortlist, positives, owner_map)
     )
     weights = gather_chips(block)
-
-    core_tok, near_tok, diag_tok = swap_core(own_tok), swap_near(own_tok), swap_diag(own_tok)
 
     oth_tiles = swap_core(label_tiles)
     slots = jnp.concatenate(
@@ -420,6 +417,10 @@
     all_clusters = jnp.arange(owner_map.shape[0], dtype=jnp.int32)
     owner_match = owner_map[:, None] == slots[None, :]
     cluster_ids = jnp.sum(jnp.where(owner_match, all_clusters[:, None], 0), axis=0)
+    own_tok, cluster_ids = lax.optimization_barrier((own_tok, cluster_ids))
+
+    core_tok, near_tok, diag_tok = swap_core(own_tok), swap_near(own_tok), swap_diag(own_tok)
+
     pick = lambda a: lax.dynamic_index_in_dim(a.reshape(16, 2, 8, -1), core, 1, False).reshape(128, -1)
     short, posit = pick(shortlist), pick(positives)
     cluster_live = jnp.max(
@@ -443,12 +444,16 @@
         (weights, cluster_live, share_hit, pos_part, tiles_hi, tiles_lo)
     )
 
-    near_a, near_b, near_hidden, near_slope = forward(diag_tok, near_tok, weights, 2**30)
+    near_a, diag_hidden, diag_slope = forward(diag_tok, weights, BF16)
+    near_a, near_tok = lax.optimization_barrier((near_a, near_tok))
+    near_b, near_hidden, near_slope = forward(near_tok, weights, F32)
     near_sum = (near_b + swap_core(near_a).astype(F32)).astype(BF16)
-    near_sum, pos_part = lax.optimization_barrier((near_sum, pos_part))
+    near_sum, pos_part, core_tok = lax.optimization_barrier((near_sum, pos_part, core_tok))
     from_near = swap_near(near_sum)
     pos_got = gather_chips(pos_part.reshape(16, docs, width))
-    own_a, own_b, own_hidden, own_slope = forward(core_tok, own_tok, weights, 2**36)
+    own_a, core_hidden, core_slope = forward(core_tok, weights, BF16)
+    own_a, own_tok = lax.optimization_barrier((own_a, own_tok))
+    own_b, own_hidden, own_slope = forward(own_tok, weights, F32)
     from_near, pos_got = lax.optimization_barrier((from_near, pos_got))
     pos_mean = jnp.sum(pos_got.astype(F32), axis=0) * (1.0 / POS_SCALE)
     own_rows, emb = pl.pallas_call(
@@ -499,8 +504,8 @@
         gain,
         (diag_rows, near_rows, core_rows, own_rows),
         (diag_tok, near_tok, core_tok, own_tok),
-        (near_hidden, own_hidden),
-        (near_slope, own_slope),
+        (diag_hidden, near_hidden, core_hidden, own_hidden),
+        (diag_slope, near_slope, core_slope, own_slope),
         weights,
     )
     got = lax.all_to_all(send, CHIPS, 0, 0, tiled=True)

time: 173 us -> 179 us (1.035)
  blocking collectives: 12.9 us -> 0 us
  local copies, waits for them, and re-layouts: 5.37 us -> 12.1 us
  Pallas kernels: 31.7 us -> 36.8 us
  starting transfers between devices: 46.2 us -> 51.2 us
    all_to_all x1 -> x0, blocking collectives: 12.9 us -> none  [gather_chips(): return lax.all_to_all(a, CHIPS, 0, 0, tiled=True)]
    unnamed x59 -> x63, local copies, waits for them, and re-layouts: 2.58 us -> 9.27 us
    all_to_all x2 -> x3, starting transfers between devices: 11.5 us -> 17 us  [gather_chips(): return lax.all_to_all(a, CHIPS, 0, 0, tiled=True)]
    pallas_call x2 -> x4, Pallas kernels: 7.53 us -> 11.3 us  [forward(): pl.pallas_call(forward_kernel, out_shape=(shape((256, 1024), dtype), shap...]
    all_to_all x2 -> x3, waiting for transfers between devices: 19.6 us -> 23.1 us  [gather_chips(): return lax.all_to_all(a, CHIPS, 0, 0, tiled=True)]
  transfers between devices with their start and end apart: 27 -> 28, of which waited for: 13 -> 13; matrix products, arithmetic and copies ran while one was open for 13% -> 13% of each run, Pallas kernels for 11% -> 15%
where the time goes in v5:
time: 179 us; the launch traced here: 178 us
  waiting for transfers between devices  56.1 us (31%)
  starting transfers between devices  51.2 us (29%)
  Pallas kernels  36.8 us (21%)
  other arithmetic  19.5 us (11%)
  local copies, waits for them, and re-layouts  12.1 us (7%)
    all_to_all x3, waiting for transfers between devices, gather_chips(): return lax.all_to_all(a, CHIPS, 0, 0, tiled=True)  23.1 us
    all_to_all x3, starting transfers between devices, gather_chips(): return lax.all_to_all(a, CHIPS, 0, 0, tiled=True)  17 us
    ppermute x10, starting transfers between devices, swap_core(): return lax.ppermute(a, 'c', [(0, 1), (1, 0)])  12.8 us
    pallas_call x4, Pallas kernels, forward(): pl.pallas_call(forward_kernel, out_shape=(shape((256, 1024), dtype), shap...  11.3 us
    reduce_max x1, other arithmetic, on_device(): jnp.max((short[:, :, None] == cluster_ids[None, None, :]).astype(F32), ax...  9.89 us
    ppermute x3, waiting for transfers between devices, swap_wrap(): return lax.ppermute(a, ('h', 'l'), [(0, 3), (3, 0), (1, 2), (2, 1)])  9.86 us
    unnamed x63, local copies, waits for them, and re-layouts  9.27 us
    pallas_call x1, Pallas kernels, backward(): pl.pallas_call(backward_kernel, out_shape=shape((16, 64, 1024), BF16), in...  9.15 us
  transfers between devices with their start and end apart: 28, of which 13 were waited for; matrix products, arithmetic and copies ran while one was open for 13% of the time, Pallas kernels for 15%

profile of v5, /device:TPU:1, one launch (start us, length us, event | category | flops | bytes accessed | tf_op | source)
XLA Modules:
  0.0 178.3 jit_solution(9386911560001336171)
XLA Ops:
  5.7 3.1 %shard_map.155 = bf16[16,64,1024]{2,1,0:T(8,128)(2,1)} custom-call(bf16[32,512]{1,0:T(8,128)(2,1)} %get-tuple-element.59.mine, bf16[32,512]{1,0:T(8,128)(2,1)} %copy-done.27, bf16[64,1024]{1,0:T(8,128)(2,1)} %w_out.1), custom_call_target="tpu_custom_call" | custom-call | bytes 2097152 | tf_op jit(solution)/shard_map/pallas_call | solution.py:400
  11.3 7.7 %all-to-all-start = ((bf16[16,64,1024]{2,1,0:T(8,128)(2,1)}), bf16[16,64,1024]{2,1,0:T(8,128)(2,1)}, u32[]{:S(2)}, u32[]{:S(2)}) async-start(bf16[16,64,1024]{2,1,0:T(8,128)(2,1)} %shard_map.155), calls=%async_computation | async-start | bytes 4194304 | tf_op jit(solution)/shard_map/all_to_all | solution.py:50
  20.7 9.9 %convert_reduce_fusion.live = bf16[128,128]{1,0:T(8,128)(2,1)S(1)} fusion(s32[128]{0:T(128)S(1)} %select_reduce_fusion, s32[128,400]{1,0:T(8,128)S(1)} %dynamic-slice_bitcast_fusion), kind=kLoop, calls=%fused_computation | loop fusion | flops 19644416 | bytes 238080 | tf_op jit(solution)/shard_map/reduce_max | solution.py:426
  33.8 14.5 %all-to-all-done.weights.refs_21_ = bf16[16,64,1024]{2,1,0:T(8,128)(2,1)} async-done(((bf16[16,64,1024]{2,1,0:T(8,128)(2,1)}), bf16[16,64,1024]{2,1,0:T(8,128)(2,1)}, u32[]{:S(2)}, u32[]{:S(2)}) %all-to-all-start) | async-done | bytes 2097184 | tf_op jit(solution)/shard_map/all_to_all | solution.py:50
  48.3 3.4 %shard_map.156 = (bf16[256,1024]{1,0:T(8,128)(2,1)S(1)}, bf16[256,512]{1,0:T(8,128)(2,1)S(1)}, f32[256,512]{1,0:T(8,128)S(1)}) custom-call(bf16[256,1024]{1,0:T(8,128)(2,1)} %collective-permute-done.1.tok.refs_9_, bf16[16,64,1024]{2,1,0:T(8,128)(2,1)} %all-to-all-done.weights.refs_21_), custom_call_target="tpu_custom_call" | custom-call | flops 4294967296 | bytes 6291456 | tf_op jit(solution)/shard_map/pallas_call | solution.py:128
  55.0 2.4 %shard_map.157 = (f32[256,1024]{1,0:T(8,128)S(1)}, bf16[256,512]{1,0:T(8,128)(2,1)S(1)}, f32[256,512]{1,0:T(8,128)S(1)}) custom-call(bf16[256,1024]{1,0:T(8,128)(2,1)S(1)} %collective-permute-done.3.tok.refs_10_, bf16[16,64,1024]{2,1,0:T(8,128)(2,1)} %all-to-all-done.weights.refs_21_), custom_call_target="tpu_custom_call" | custom-call | flops 4294967296 | bytes 6291456 | tf_op jit(solution)/shard_map/pallas_call | solution.py:128
  59.8 3.2 %shard_map.158 = (bf16[256,1024]{1,0:T(8,128)(2,1)}, bf16[256,512]{1,0:T(8,128)(2,1)S(1)}, f32[256,512]{1,0:T(8,128)S(1)}) custom-call(bf16[256,1024]{1,0:T(8,128)(2,1)S(1)} %collective-permute-done.5.tok.refs_11_, bf16[16,64,1024]{2,1,0:T(8,128)(2,1)} %all-to-all-done.weights.refs_21_), custom_call_target="tpu_custom_call" | custom-call | flops 4294967296 | bytes 6291456 | tf_op jit(solution)/shard_map/pallas_call | solution.py:128
  65.2 5.4 %all-to-all-start.1 = ((f16[16,8,1024]{2,1,0:T(8,128)(2,1)}), f16[16,8,1024]{2,1,0:T(8,128)(2,1)}, u32[]{:S(2)}, u32[]{:S(2)}) async-start(f16[16,8,1024]{2,1,0:T(8,128)(2,1)} %bitcast.33), calls=%async_computation.1 | async-start | bytes 524288 | tf_op jit(solution)/shard_map/all_to_all | solution.py:50
  70.6 2.4 %shard_map.159 = (f32[256,1024]{1,0:T(8,128)S(1)}, bf16[256,512]{1,0:T(8,128)(2,1)S(1)}, f32[256,512]{1,0:T(8,128)S(1)}) custom-call(bf16[256,1024]{1,0:T(8,128)(2,1)S(1)} %bitcast.23, bf16[16,64,1024]{2,1,0:T(8,128)(2,1)} %all-to-all-done.weights.refs_21_), custom_call_target="tpu_custom_call" | custom-call | flops 4294967296 | bytes 6291456 | tf_op jit(solution)/shard_map/pallas_call | solution.py:128
  75.5 3.0 %all-to-all-done.1 = f16[16,8,1024]{2,1,0:T(8,128)(2,1)} async-done(((f16[16,8,1024]{2,1,0:T(8,128)(2,1)}), f16[16,8,1024]{2,1,0:T(8,128)(2,1)}, u32[]{:S(2)}, u32[]{:S(2)}) %all-to-all-start.1) | async-done | bytes 262176 | tf_op jit(solution)/shard_map/all_to_all | solution.py:50
  79.8 3.2 %shard_map.160 = (bf16[256,1152]{1,0:T(8,128)(2,1)}, bf16[128,1024]{1,0:T(8,128)(2,1)}) custom-call(s32[8]{0:T(128)S(1)} %copy-done.15, bf16[256,1024]{1,0:T(8,128)(2,1)S(1)} %bitcast.24, f32[256,1024]{1,0:T(8,128)S(1)} %copy-done.2, bf16[256,1024]{1,0:T(8,128)(2,1)} %collective-permute-done.6.from_core, ...), custom_call_target="tpu_custom_call" | custom-call | flops 4194304 | bytes 4194304 | tf_op jit(solution)/shard_map/pallas_call | solution.py:459
  83.1 3.9 %all-to-all-start.2 = ((bf16[16,8,1024]{2,1,0:T(8,128)(2,1)}), bf16[16,8,1024]{2,1,0:T(8,128)(2,1)S(1)}, u32[]{:S(2)}, u32[]{:S(2)}) async-start(bf16[16,8,1024]{2,1,0:T(8,128)(2,1)} %bitcast.9), calls=%async_computation.2 | async-start | bytes 524288 | tf_op jit(solution)/shard_map/all_to_all | solution.py:50
  88.7 5.6 %all-to-all-done.2 = bf16[16,8,1024]{2,1,0:T(8,128)(2,1)S(1)} async-done(((bf16[16,8,1024]{2,1,0:T(8,128)(2,1)}), bf16[16,8,1024]{2,1,0:T(8,128)(2,1)S(1)}, u32[]{:S(2)}, u32[]{:S(2)}) %all-to-all-start.2) | async-done | bytes 262176 | tf_op jit(solution)/shard_map/all_to_all | solution.py:50
  94.3 2.3 %shard_map.161 = (bf16[128,1280]{1,0:T(8,128)(2,1)}, f32[128,512]{1,0:T(8,128)S(1)}) custom-call(bf16[128,1024]{1,0:T(8,128)(2,1)S(1)} %bitcast.25, bf16[512,1024]{1,0:T(8,128)(2,1)S(1)} %get-tuple-element.84.tiles_hi, bf16[512,1024]{1,0:T(8,128)(2,1)S(1)} %get-tuple-element.85.tiles_lo, bf16[128,128]{1,0:T(8,128)(2,1)S(1)} %convert_reduce_fusion.live), custom_call_target="tpu_custom_call" | custom-call | flops 536870912 | bytes 3145728 | tf_op jit(solution)/shard_map/pallas_call | solution.py:471
  96.7 3.1 %collective-permute-start.17 = (bf16[256,1152]{1,0:T(8,128)(2,1)}, bf16[256,1152]{1,0:T(8,128)(2,1)S(1)}, u32[]{:S(2)}, u32[]{:S(2)}) collective-permute-start(bf16[256,1152]{1,0:T(8,128)(2,1)} %collective-permute-done.8.refs_6_), channel_id=1, source_target_pairs={{0,1},{1,0},{2,3},{3,2},{4,5},{5,4},{6,7},{7,6},{8,9},{9,8},{10,11... | collective-permute-start | bytes 1769480 | tf_op jit(solution)/shard_map/ppermute | solution.py:26
  99.8 3.5 %all-to-all-start.3 = ((bf16[16,8,1280]{2,1,0:T(8,128)(2,1)}), bf16[16,8,1280]{2,1,0:T(8,128)(2,1)S(1)}, u32[]{:S(2)}, u32[]{:S(2)}) async-start(bf16[16,8,1280]{2,1,0:T(8,128)(2,1)} %bitcast.11), calls=%async_computation.3 | async-start | bytes 655360 | tf_op jit(solution)/shard_map/all_to_all | solution.py:486
  104.4 7.5 %all-to-all-done.3.got_hbm = bf16[16,8,1280]{2,1,0:T(8,128)(2,1)S(1)} async-done(((bf16[16,8,1280]{2,1,0:T(8,128)(2,1)}), bf16[16,8,1280]{2,1,0:T(8,128)(2,1)S(1)}, u32[]{:S(2)}, u32[]{:S(2)}) %all-to-all-start.3) | async-done | bytes 327712 | tf_op jit(solution)/shard_map/all_to_all | solution.py:486
  120.3 9.2 %shard_map.164 = bf16[16,64,1024]{2,1,0:T(8,128)(2,1)} custom-call(f32[8,1024]{1,0:T(8,128)} %copy-done.28, f32[8,1024]{1,0:T(8,128)} %copy-done.26, f32[8,1024]{1,0:T(8,128)} %copy-done.25, f32[8,1024]{1,0:T(8,128)} %copy-done.13, f32[1,1024]{1,0:T(1,128)} %bitcast.27, bf16[256,1152]{1,0:T(8,128)(2,1)} %copy-done.23, ...), custom_call_target="tpu_custom_call" | custom-call | flops 3221225472 | bytes 10485760 | tf_op jit(solution)/shard_map/pallas_call | solution.py:306
  129.5 3.7 %all-to-all-start.4 = ((bf16[16,64,1024]{2,1,0:T(8,128)(2,1)}), bf16[16,64,1024]{2,1,0:T(8,128)(2,1)S(1)}, u32[]{:S(2)}, u32[]{:S(2)}) async-start(bf16[16,64,1024]{2,1,0:T(8,128)(2,1)} %shard_map.164), calls=%async_computation.4 | async-start | bytes 4194304 | tf_op jit(solution)/shard_map/all_to_all | solution.py:511
  137.7 4.4 %collective-permute-done.10 = bf16[128,1024]{1,0:T(8,128)(2,1)S(1)} collective-permute-done((bf16[128,1024]{1,0:T(8,128)(2,1)S(1)}, bf16[128,1024]{1,0:T(8,128)(2,1)S(1)}, u32[]{:S(2)}, u32[]{:S(2)}) %collective-permute-start.10) | collective-permute-done | bytes 262176 | tf_op jit(solution)/shard_map/ppermute | solution.py:30
  147.7 5.0 %collective-permute-done.11 = bf16[128,1024]{1,0:T(8,128)(2,1)S(1)} collective-permute-done((bf16[128,1024]{1,0:T(8,128)(2,1)S(1)}, bf16[128,1024]{1,0:T(8,128)(2,1)S(1)}, u32[]{:S(2)}, u32[]{:S(2)}) %collective-permute-start.11) | collective-permute-done | bytes 262176 | tf_op jit(solution)/shard_map/ppermute | solution.py:42
  153.5 8.9 %all-to-all-done.4.got = bf16[16,64,1024]{2,1,0:T(8,128)(2,1)S(1)} async-done(((bf16[16,64,1024]{2,1,0:T(8,128)(2,1)}), bf16[16,64,1024]{2,1,0:T(8,128)(2,1)S(1)}, u32[]{:S(2)}, u32[]{:S(2)}) %all-to-all-start.4) | async-done | bytes 2097184 | tf_op jit(solution)/shard_map/all_to_all | solution.py:511
  166.6 3.0 %collective-permute-start.22 = (bf16[64,1024]{1,0:T(8,128)(2,1)S(1)}, bf16[64,1024]{1,0:T(8,128)(2,1)S(1)}, u32[]{:S(2)}, u32[]{:S(2)}) collective-permute-start(bf16[64,1024]{1,0:T(8,128)(2,1)S(1)} %maximum_maximum_fusion.own), channel_id=1, source_target_pairs={{0,64},{64,0},{1,65},{65,1},{2,66},{66,2},{3,67},{67,3},{4,68},{68... | collective-permute-start | bytes 393224 | tf_op jit(solution)/shard_map/ppermute | solution.py:38
  173.3 2.7 %collective-permute-done.21.wrap = bf16[64,1024]{1,0:T(8,128)(2,1)S(1)} collective-permute-done((bf16[64,1024]{1,0:T(8,128)(2,1)S(1)}, bf16[64,1024]{1,0:T(8,128)(2,1)S(1)}, u32[]{:S(2)}, u32[]{:S(2)}) %collective-permute-start.21) | collective-permute-done | bytes 131104 | tf_op jit(solution)/shard_map/ppermute | solution.py:42
  (140 shorter events, 56.2 us)
Async XLA Ops:
  9.2 44.0 %collective-permute-start.3 = (bf16[256,1024]{1,0:T(8,128)(2,1)S(1)}, bf16[256,1024]{1,0:T(8,128)(2,1)S(1)}, u32[]{:S(2)}, u32[]{:S(2)}) collective-permute-start(bf16[256,1024]{1,0:T(8,128)(2,1)S(1)} %bitcast.20), channel_id=1, source_target_pairs={{0,32},{32,0},{1,33},{33,1},{2,34},{34,2},{3,35},{35,3},{4,36},{36... | collective-permute-start | bytes 1572872 | tf_op jit(solution)/shard_map/ppermute | solution.py:30
  10.7 37.6 %collective-permute-start.1 = (bf16[256,1024]{1,0:T(8,128)(2,1)S(1)}, bf16[256,1024]{1,0:T(8,128)(2,1)}, u32[]{:S(2)}, u32[]{:S(2)}) collective-permute-start(bf16[256,1024]{1,0:T(8,128)(2,1)S(1)} %bitcast.21), channel_id=1, source_target_pairs={{0,33},{33,0},{1,32},{32,1},{2,35},{35,2},{3,34},{34,3},{4,37},{37... | collective-permute-start | bytes 1572872 | tf_op jit(solution)/shard_map/ppermute | solution.py:34
  11.3 37.0 %all-to-all-start = ((bf16[16,64,1024]{2,1,0:T(8,128)(2,1)}), bf16[16,64,1024]{2,1,0:T(8,128)(2,1)}, u32[]{:S(2)}, u32[]{:S(2)}) async-start(bf16[16,64,1024]{2,1,0:T(8,128)(2,1)} %shard_map.155), calls=%async_computation | async-start | bytes 4194304 | tf_op jit(solution)/shard_map/all_to_all | solution.py:50
  19.4 11.2 %collective-permute-start.2 = (f32[256,1024]{1,0:T(8,128)S(1)}, f32[256,1024]{1,0:T(8,128)}, u32[]{:S(2)}, u32[]{:S(2)}) collective-permute-start(f32[256,1024]{1,0:T(8,128)S(1)} %copy-done.18), channel_id=1, source_target_pairs={{0,1},{1,0},{2,3},{3,2},{4,5},{5,4},{6,7},{7,6},{8,9},{9,8},{10,11... | collective-permute-start | bytes 3145736 | tf_op jit(solution)/shard_map/ppermute | solution.py:26
  53.3 4.1 %collective-permute-start.4 = (bf16[256,1024]{1,0:T(8,128)(2,1)S(1)}, bf16[256,1024]{1,0:T(8,128)(2,1)S(1)}, u32[]{:S(2)}, u32[]{:S(2)}) collective-permute-start(bf16[256,1024]{1,0:T(8,128)(2,1)S(1)} %get-tuple-element.73), channel_id=1, source_target_pairs={{0,1},{1,0},{2,3},{3,2},{4,5},{5,4},{6,7},{7,6},{8,9},{9,8},{10,11... | collective-permute-start | bytes 1572872 | tf_op jit(solution)/shard_map/ppermute | solution.py:26
  58.4 20.1 %collective-permute-start.7 = (bf16[256,1024]{1,0:T(8,128)(2,1)}, bf16[256,1024]{1,0:T(8,128)(2,1)S(1)}, u32[]{:S(2)}, u32[]{:S(2)}) collective-permute-start(bf16[256,1024]{1,0:T(8,128)(2,1)} %add_convert_fusion.1), channel_id=1, source_target_pairs={{0,32},{32,0},{1,33},{33,1},{2,34},{34,2},{3,35},{35,3},{4,36},{36... | collective-permute-start | bytes 1572872 | tf_op jit(solution)/shard_map/ppermute | solution.py:30
  64.5 14.0 %collective-permute-start.6 = (bf16[256,1024]{1,0:T(8,128)(2,1)}, bf16[256,1024]{1,0:T(8,128)(2,1)}, u32[]{:S(2)}, u32[]{:S(2)}) collective-permute-start(bf16[256,1024]{1,0:T(8,128)(2,1)} %get-tuple-element.79), channel_id=1, source_target_pairs={{0,1},{1,0},{2,3},{3,2},{4,5},{5,4},{6,7},{7,6},{8,9},{9,8},{10,11... | collective-permute-start | bytes 1572872 | tf_op jit(solution)/shard_map/ppermute | solution.py:26
  65.2 13.3 %all-to-all-start.1 = ((f16[16,8,1024]{2,1,0:T(8,128)(2,1)}), f16[16,8,1024]{2,1,0:T(8,128)(2,1)}, u32[]{:S(2)}, u32[]{:S(2)}) async-start(f16[16,8,1024]{2,1,0:T(8,128)(2,1)} %bitcast.33), calls=%async_computation.1 | async-start | bytes 524288 | tf_op jit(solution)/shard_map/all_to_all | solution.py:50
  83.0 13.7 %collective-permute-start.8 = (bf16[256,1152]{1,0:T(8,128)(2,1)}, bf16[256,1152]{1,0:T(8,128)(2,1)}, u32[]{:S(2)}, u32[]{:S(2)}) collective-permute-start(bf16[256,1152]{1,0:T(8,128)(2,1)} %get-tuple-element.88.refs_8_), channel_id=1, source_target_pairs={{0,32},{32,0},{1,33},{33,1},{2,34},{34,2},{3,35},{35,3},{4,36},{36... | collective-permute-start | bytes 1769480 | tf_op jit(solution)/shard_map/ppermute | solution.py:30
  83.1 11.2 %all-to-all-start.2 = ((bf16[16,8,1024]{2,1,0:T(8,128)(2,1)}), bf16[16,8,1024]{2,1,0:T(8,128)(2,1)S(1)}, u32[]{:S(2)}, u32[]{:S(2)}) async-start(bf16[16,8,1024]{2,1,0:T(8,128)(2,1)} %bitcast.9), calls=%async_computation.2 | async-start | bytes 524288 | tf_op jit(solution)/shard_map/all_to_all | solution.py:50
  87.0 32.1 %collective-permute-start.18 = (bf16[256,1152]{1,0:T(8,128)(2,1)}, bf16[256,1152]{1,0:T(8,128)(2,1)}, u32[]{:S(2)}, u32[]{:S(2)}) collective-permute-start(bf16[256,1152]{1,0:T(8,128)(2,1)} %get-tuple-element.88.refs_8_), channel_id=1, source_target_pairs={{0,1},{1,0},{2,3},{3,2},{4,5},{5,4},{6,7},{7,6},{8,9},{9,8},{10,11... | collective-permute-start | bytes 1769480 | tf_op jit(solution)/shard_map/ppermute | solution.py:26
  96.7 22.8 %collective-permute-start.17 = (bf16[256,1152]{1,0:T(8,128)(2,1)}, bf16[256,1152]{1,0:T(8,128)(2,1)S(1)}, u32[]{:S(2)}, u32[]{:S(2)}) collective-permute-start(bf16[256,1152]{1,0:T(8,128)(2,1)} %collective-permute-done.8.refs_6_), channel_id=1, source_target_pairs={{0,1},{1,0},{2,3},{3,2},{4,5},{5,4},{6,7},{7,6},{8,9},{9,8},{10,11... | collective-permute-start | bytes 1769480 | tf_op jit(solution)/shard_map/ppermute | solution.py:26
  99.8 12.0 %all-to-all-start.3 = ((bf16[16,8,1280]{2,1,0:T(8,128)(2,1)}), bf16[16,8,1280]{2,1,0:T(8,128)(2,1)S(1)}, u32[]{:S(2)}, u32[]{:S(2)}) async-start(bf16[16,8,1280]{2,1,0:T(8,128)(2,1)} %bitcast.11), calls=%async_computation.3 | async-start | bytes 655360 | tf_op jit(solution)/shard_map/all_to_all | solution.py:486
  113.0 6.3 %collective-permute-start.16 = (f32[8,1024]{1,0:T(8,128)S(1)}, f32[8,1024]{1,0:T(8,128)S(1)}, u32[]{:S(2)}, u32[]{:S(2)}) collective-permute-start(f32[8,1024]{1,0:T(8,128)S(1)} %get-tuple-element.97.refs_3_), channel_id=1, source_target_pairs={{0,1},{1,0},{2,3},{3,2},{4,5},{5,4},{6,7},{7,6},{8,9},{9,8},{10,11... | collective-permute-start | bytes 98312 | tf_op jit(solution)/shard_map/ppermute | solution.py:26
  114.7 4.6 %collective-permute-start.15 = (f32[8,1024]{1,0:T(8,128)S(1)}, f32[8,1024]{1,0:T(8,128)S(1)}, u32[]{:S(2)}, u32[]{:S(2)}) collective-permute-start(f32[8,1024]{1,0:T(8,128)S(1)} %get-tuple-element.97.refs_3_), channel_id=1, source_target_pairs={{0,32},{32,0},{1,33},{33,1},{2,34},{34,2},{3,35},{35,3},{4,36},{36... | collective-permute-start | bytes 98312 | tf_op jit(solution)/shard_map/ppermute | solution.py:30
  119.1 14.1 %collective-permute-start.9 = (bf16[256,1024]{1,0:T(8,128)(2,1)}, bf16[256,1024]{1,0:T(8,128)(2,1)}, u32[]{:S(2)}, u32[]{:S(2)}) collective-permute-start(bf16[256,1024]{1,0:T(8,128)(2,1)} %get-tuple-element.96), channel_id=1, source_target_pairs={{0,1},{1,0},{2,3},{3,2},{4,5},{5,4},{6,7},{7,6},{8,9},{9,8},{10,11... | collective-permute-start | bytes 1572872 | tf_op jit(solution)/shard_map/ppermute | solution.py:26
  129.5 32.9 %all-to-all-start.4 = ((bf16[16,64,1024]{2,1,0:T(8,128)(2,1)}), bf16[16,64,1024]{2,1,0:T(8,128)(2,1)S(1)}, u32[]{:S(2)}, u32[]{:S(2)}) async-start(bf16[16,64,1024]{2,1,0:T(8,128)(2,1)} %shard_map.164), calls=%async_computation.4 | async-start | bytes 4194304 | tf_op jit(solution)/shard_map/all_to_all | solution.py:511
  134.5 7.6 %collective-permute-start.10 = (bf16[128,1024]{1,0:T(8,128)(2,1)S(1)}, bf16[128,1024]{1,0:T(8,128)(2,1)S(1)}, u32[]{:S(2)}, u32[]{:S(2)}) collective-permute-start(bf16[128,1024]{1,0:T(8,128)(2,1)S(1)} %get-tuple-element.119), channel_id=1, source_target_pairs={{0,32},{32,0},{1,33},{33,1},{2,34},{34,2},{3,35},{35,3},{4,36},{36... | collective-permute-start | bytes 786440 | tf_op jit(solution)/shard_map/ppermute | solution.py:30
  135.8 8.4 %collective-permute-start.12 = (bf16[128,1024]{1,0:T(8,128)(2,1)S(1)}, bf16[128,1024]{1,0:T(8,128)(2,1)S(1)}, u32[]{:S(2)}, u32[]{:S(2)}) collective-permute-start(bf16[128,1024]{1,0:T(8,128)(2,1)S(1)} %get-tuple-element.120), channel_id=1, source_target_pairs={{0,96},{96,0},{32,64},{64,32},{1,97},{97,1},{33,65},{65,33},{2,98}... | collective-permute-start | bytes 786440 | tf_op jit(solution)/shard_map/ppermute | solution.py:42
  145.2 7.5 %collective-permute-start.11 = (bf16[128,1024]{1,0:T(8,128)(2,1)S(1)}, bf16[128,1024]{1,0:T(8,128)(2,1)S(1)}, u32[]{:S(2)}, u32[]{:S(2)}) collective-permute-start(bf16[128,1024]{1,0:T(8,128)(2,1)S(1)} %get-tuple-element.117), channel_id=1, source_target_pairs={{0,96},{96,0},{32,64},{64,32},{1,97},{97,1},{33,65},{65,33},{2,98}... | collective-permute-start | bytes 786440 | tf_op jit(solution)/shard_map/ppermute | solution.py:42
  147.0 18.5 %collective-permute-start.13 = (bf16[128,1024]{1,0:T(8,128)(2,1)}, bf16[128,1024]{1,0:T(8,128)(2,1)}, u32[]{:S(2)}, u32[]{:S(2)}) collective-permute-start(bf16[128,1024]{1,0:T(8,128)(2,1)} %get-tuple-element.118), channel_id=1, source_target_pairs={{0,32},{32,0},{1,33},{33,1},{2,34},{34,2},{3,35},{35,3},{4,36},{36... | collective-permute-start | bytes 786440 | tf_op jit(solution)/shard_map/ppermute | solution.py:30
  166.6 6.6 %collective-permute-start.22 = (bf16[64,1024]{1,0:T(8,128)(2,1)S(1)}, bf16[64,1024]{1,0:T(8,128)(2,1)S(1)}, u32[]{:S(2)}, u32[]{:S(2)}) collective-permute-start(bf16[64,1024]{1,0:T(8,128)(2,1)S(1)} %maximum_maximum_fusion.own), channel_id=1, source_target_pairs={{0,64},{64,0},{1,65},{65,1},{2,66},{66,2},{3,67},{67,3},{4,68},{68... | collective-permute-start | bytes 393224 | tf_op jit(solution)/shard_map/ppermute | solution.py:38
  169.6 6.4 %collective-permute-start.21 = (bf16[64,1024]{1,0:T(8,128)(2,1)S(1)}, bf16[64,1024]{1,0:T(8,128)(2,1)S(1)}, u32[]{:S(2)}, u32[]{:S(2)}) collective-permute-start(bf16[64,1024]{1,0:T(8,128)(2,1)S(1)} %maximum_maximum_fusion.own), channel_id=1, source_target_pairs={{0,96},{96,0},{32,64},{64,32},{1,97},{97,1},{33,65},{65,33},{2,98}... | collective-permute-start | bytes 393224 | tf_op jit(solution)/shard_map/ppermute | solution.py:42
  170.4 6.0 %collective-permute-start.20 = (bf16[64,1024]{1,0:T(8,128)(2,1)S(1)}, bf16[64,1024]{1,0:T(8,128)(2,1)S(1)}, u32[]{:S(2)}, u32[]{:S(2)}) collective-permute-start(bf16[64,1024]{1,0:T(8,128)(2,1)S(1)} %maximum_maximum_fusion.own), channel_id=1, source_target_pairs={{0,32},{32,0},{1,33},{33,1},{2,34},{34,2},{3,35},{35,3},{4,36},{36... | collective-permute-start | bytes 393224 | tf_op jit(solution)/shard_map/ppermute | solution.py:30
  (35 other events, 175.6 us)

commit v6 on v5

--- a/solution.py
+++ b/solution.py
@@ -1,3 +1,5 @@
+import functools
+
 import jax
 import jax.numpy as jnp
 from jax import lax
@@ -87,13 +89,9 @@
 
 def lay_kernel(mine, theirs, w_out, out, block, sems):
     core, role = place_of()
-    top = pltpu.make_async_copy(
-        w_out.at[pl.ds(pl.multiple_of(role * 32, 32), 32)], block.at[0:32], sems.at[16]
-    )
-    top.start()
+    block[:32] = jnp.where(role == 0, w_out[:32], w_out[32:])
     block[32:, :512] = jnp.where(core == 0, mine[...], theirs[...])
     block[32:, 512:] = jnp.where(core == 0, theirs[...], mine[...])
-    top.wait()
     copies = [pltpu.make_async_copy(block, out.at[i], sems.at[i]) for i in range(16)]
     for copy in copies:
         copy.start()
@@ -101,7 +99,9 @@
         copy.wait()
 
 
-def forward_kernel(tok, weights, part, hidden, slope, w_in, w_out, sems):
+def forward_kernel(count, *refs):
+    toks, weights, parts = refs[:count], refs[count], refs[count + 1 : 2 * count + 1]
+    hidden_hbm, slope_hbm, w_in, w_out, hidden, slope, sems = refs[2 * count + 1 :]
     copies = [
         pltpu.make_async_copy(
             weights.at[:, 32:64, k * 512 : k * 512 + 512], w_in.at[:, k * 32 : k * 32 + 32], sems.at[k]
@@ -113,31 +113,46 @@
         copy.start()
     copies[0].wait()
     copies[1].wait()
-    pre_act = jnp.dot(tok[...], w_in[...].reshape(1024, 512), preferred_element_type=F32)
-    normal_cdf = 0.5 * (1.0 + lax.erf(pre_act * INV_ROOT_TWO))
-    act = (pre_act * normal_cdf).astype(BF16)
-    copies[2].wait()
-    part[...] = jnp.dot(
-        act, w_out[...].reshape(512, 1024), preferred_element_type=F32
-    ).astype(part.dtype)
-    hidden[...] = act
-    slope[...] = normal_cdf + pre_act * jnp.exp(-0.5 * pre_act * pre_act) * INV_ROOT_TWO_PI
-
-
-def forward(tok, weights, dtype):
-    return pl.pallas_call(
-        forward_kernel,
-        out_shape=(shape((256, 1024), dtype), shape((256, 512), BF16), shape((256, 512), F32)),
-        in_specs=[WHOLE, ANYWHERE],
-        out_specs=(WHOLE,) * 3,
+    sent = []
+    for k, (tok, part) in enumerate(zip(toks, parts)):
+        at = pl.ds(k * 256, 256)
+        pre_act = jnp.dot(tok[...], w_in[...].reshape(1024, 512), preferred_element_type=F32)
+        normal_cdf = 0.5 * (1.0 + lax.erf(pre_act * INV_ROOT_TWO))
+        act = (pre_act * normal_cdf).astype(BF16)
+        hidden[at] = act
+        slope[at] = normal_cdf + pre_act * jnp.exp(-0.5 * pre_act * pre_act) * INV_ROOT_TWO_PI
+        sent.append(pltpu.make_async_copy(hidden.at[at], hidden_hbm.at[at], sems.at[3 + 2 * k]))
+        sent.append(pltpu.make_async_copy(slope.at[at], slope_hbm.at[at], sems.at[4 + 2 * k]))
+        sent[-2].start()
+        sent[-1].start()
+        if k == 0:
+            copies[2].wait()
+        part[...] = jnp.dot(
+            act, w_out[...].reshape(512, 1024), preferred_element_type=F32
+        ).astype(part.dtype)
+    for copy in sent:
+        copy.wait()
+
+
+def forward(toks, weights, dtypes):
+    count = len(toks)
+    *parts, hidden, slope = pl.pallas_call(
+        functools.partial(forward_kernel, count),
+        out_shape=[shape((256, 1024), dtype) for dtype in dtypes]
+        + [shape((256 * count, 512), BF16), shape((256 * count, 512), F32)],
+        in_specs=[WHOLE] * count + [ANYWHERE],
+        out_specs=[WHOLE] * count + [ANYWHERE] * 2,
         scratch_shapes=[
             pltpu.VMEM((16, 64, 512), BF16),
             pltpu.VMEM((16, 32, 1024), BF16),
-            pltpu.SemaphoreType.DMA((3,)),
+            pltpu.VMEM((256 * count, 512), BF16),
+            pltpu.VMEM((256 * count, 512), F32),
+            pltpu.SemaphoreType.DMA((7,)),
         ],
         compiler_params=LIMIT,
         cost_estimate=cost(2**32, 6 * 2**20, 2**18),
-    )(tok, weights)
+    )(*toks, weights)
+    return (*parts, (hidden, slope))
 
 
 def norm_kernel(lengths, tok, part, from_core, from_near, gain, rows, emb_hbm, emb, sem):
@@ -230,8 +245,8 @@
 def backward_kernel(*refs):
     grads, gain = refs[:4], refs[4]
     rows, toks = refs[5:9], refs[9:13]
-    hiddens, slopes, weights, out = refs[13:17], refs[17:21], refs[21], refs[22]
-    row_buf, tok_buf, hid_buf, slope_buf, w_out, sum_grad, act_grad, result, sems = refs[23:]
+    hiddens, slopes, weights, out = refs[13:16], refs[16:19], refs[19], refs[20]
+    row_buf, tok_buf, hid_buf, slope_buf, w_out, sum_grad, act_grad, result, sems = refs[21:]
     sent = []
     first = pltpu.make_async_copy(weights.at[:, 0:32], w_out, sems.at[0])
     first.start()
@@ -240,12 +255,11 @@
         at = pl.ds(k * 256, 256)
         row_copies.append(pltpu.make_async_copy(rows[k], row_buf.at[at], sems.at[1 + k]))
         row_copies[k].start()
-    for k in range(4):
-        at = pl.ds(k * 256, 256)
+    spans = (pl.ds(0, 512), pl.ds(512, 256), pl.ds(768, 256))
+    for k, at in enumerate(spans):
         slope_copies.append(pltpu.make_async_copy(slopes[k], slope_buf.at[at], sems.at[21 + k]))
         slope_copies[k].start()
-    for k in range(4):
-        at = pl.ds(k * 256, 256)
+    for k, at in enumerate(spans):
         hid_copies.append(pltpu.make_async_copy(hiddens[k], hid_buf.at[at], sems.at[5 + k]))
         hid_copies[k].start()
     for k in range(4):
@@ -271,7 +285,8 @@
             ).astype(BF16)
         if k == 0:
             first.wait()
-        slope_copies[k].wait()
+        if k != 1:
+            slope_copies[max(k - 1, 0)].wait()
         at = pl.ds(k * 256, 256)
         back = lax.dot_general(
             sum_grad[at], w_out[...].reshape(512, 1024), LAST, preferred_element_type=F32
@@ -306,7 +321,7 @@
     return pl.pallas_call(
         backward_kernel,
         out_shape=shape((16, 64, 1024), BF16),
-        in_specs=[WHOLE] * 5 + [ANYWHERE] * 17,
+        in_specs=[WHOLE] * 5 + [ANYWHERE] * 15,
         out_specs=ANYWHERE,
         scratch_shapes=[
             pltpu.VMEM((1024, 1152), BF16),
@@ -317,7 +332,7 @@
             pltpu.VMEM((1024, 1024), BF16),
             pltpu.VMEM((1024, 512), BF16),
             pltpu.VMEM((16, 64, 1024), BF16),
-            pltpu.SemaphoreType.DMA((25,)),
+            pltpu.SemaphoreType.DMA((24,)),
         ],
         compiler_params=MOST,
         cost_estimate=cost(3 * 2**30, 10 * 2**20),
@@ -400,15 +415,17 @@
     block = pl.pallas_call(
         lay_kernel,
         out_shape=shape((16, 64, width), BF16),
-        in_specs=[WHOLE, WHOLE, ANYWHERE],
+        in_specs=[WHOLE, WHOLE, WHOLE],
         out_specs=ANYWHERE,
-        scratch_shapes=[pltpu.VMEM((64, width), BF16), pltpu.SemaphoreType.DMA((17,))],
+        scratch_shapes=[pltpu.VMEM((64, width), BF16), pltpu.SemaphoreType.DMA((16,))],
         cost_estimate=cost(0, 2**21),
     )(mine, swap_core(theirs), w_out)
     block, own_tok, label_tiles, shortlist, positives, owner_map = lax.optimization_barrier(
         (block, own_tok, label_tiles, shortlist, positives, owner_map)
     )
     weights = gather_chips(block)
+
+    core_tok, near_tok, diag_tok = swap_core(own_tok), swap_near(own_tok), swap_diag(own_tok)
 
     oth_tiles = swap_core(label_tiles)
     slots = jnp.concatenate(
@@ -417,10 +434,6 @@
     all_clusters = jnp.arange(owner_map.shape[0], dtype=jnp.int32)
     owner_match = owner_map[:, None] == slots[None, :]
     cluster_ids = jnp.sum(jnp.where(owner_match, all_clusters[:, None], 0), axis=0)
-    own_tok, cluster_ids = lax.optimization_barrier((own_tok, cluster_ids))
-
-    core_tok, near_tok, diag_tok = swap_core(own_tok), swap_near(own_tok), swap_diag(own_tok)
-
     pick = lambda a: lax.dynamic_index_in_dim(a.reshape(16, 2, 8, -1), core, 1, False).reshape(128, -1)
     short, posit = pick(shortlist), pick(positives)
     cluster_live = jnp.max(
@@ -444,16 +457,14 @@
         (weights, cluster_live, share_hit, pos_part, tiles_hi, tiles_lo)
     )
 
-    near_a, diag_hidden, diag_slope = forward(diag_tok, weights, BF16)
-    near_a, near_tok = lax.optimization_barrier((near_a, near_tok))
-    near_b, near_hidden, near_slope = forward(near_tok, weights, F32)
+    near_a, near_b, near_kept = forward((diag_tok, near_tok), weights, (BF16, F32))
     near_sum = (near_b + swap_core(near_a).astype(F32)).astype(BF16)
     near_sum, pos_part, core_tok = lax.optimization_barrier((near_sum, pos_part, core_tok))
     from_near = swap_near(near_sum)
     pos_got = gather_chips(pos_part.reshape(16, docs, width))
-    own_a, core_hidden, core_slope = forward(core_tok, weights, BF16)
+    own_a, core_kept = forward((core_tok,), weights, (BF16,))
     own_a, own_tok = lax.optimization_barrier((own_a, own_tok))
-    own_b, own_hidden, own_slope = forward(own_tok, weights, F32)
+    own_b, own_kept = forward((own_tok,), weights, (F32,))
     from_near, pos_got = lax.optimization_barrier((from_near, pos_got))
     pos_mean = jnp.sum(pos_got.astype(F32), axis=0) * (1.0 / POS_SCALE)
     own_rows, emb = pl.pallas_call(
@@ -504,8 +515,8 @@
         gain,
         (diag_rows, near_rows, core_rows, own_rows),
         (diag_tok, near_tok, core_tok, own_tok),
-        (diag_hidden, near_hidden, core_hidden, own_hidden),
-        (diag_slope, near_slope, core_slope, own_slope),
+        (near_kept[0], core_kept[0], own_kept[0]),
+        (near_kept[1], core_kept[1], own_kept[1]),
         weights,
     )
     got = lax.all_to_all(send, CHIPS, 0, 0, tiled=True)

time: 179 us -> 176 us (0.983)
  Pallas kernels: 36.8 us -> 34.9 us
  local copies, waits for them, and re-layouts: 12.1 us -> 10.3 us
    unnamed x63 -> x57, local copies, waits for them, and re-layouts: 9.27 us -> 7.52 us
    pallas_call x4 -> x3, Pallas kernels: 11.3 us -> 10.1 us  [forward(): pl.pallas_call(functools.partial(forward_kernel, count), out_shape=[shape...]
  transfers between devices with their start and end apart: 28 -> 28, of which waited for: 13 -> 14; matrix products, arithmetic and copies ran while one was open for 13% -> 13% of each run, Pallas kernels for 15% -> 12%
where the time goes in v6:
time: 176 us; the launch traced here: 175 us
  waiting for transfers between devices  57.6 us (33%)
  starting transfers between devices  51.3 us (29%)
  Pallas kernels  34.9 us (20%)
  other arithmetic  18.7 us (11%)
  local copies, waits for them, and re-layouts  10.3 us (6%)
    all_to_all x3, waiting for transfers between devices, gather_chips(): return lax.all_to_all(a, CHIPS, 0, 0, tiled=True)  22.8 us
    all_to_all x3, starting transfers between devices, gather_chips(): return lax.all_to_all(a, CHIPS, 0, 0, tiled=True)  17 us
    ppermute x10, starting transfers between devices, swap_core(): return lax.ppermute(a, 'c', [(0, 1), (1, 0)])  12.8 us
    pallas_call x3, Pallas kernels, forward(): pl.pallas_call(functools.partial(forward_kernel, count), out_shape=[shape...  10.1 us
    reduce_max x1, other arithmetic, on_device(): jnp.max((short[:, :, None] == cluster_ids[None, None, :]).astype(F32), ax...  9.89 us
    ppermute x3, waiting for transfers between devices, swap_wrap(): return lax.ppermute(a, ('h', 'l'), [(0, 3), (3, 0), (1, 2), (2, 1)])  9.75 us
    all_to_all x1, waiting for transfers between devices, on_device(): got = lax.all_to_all(send, CHIPS, 0, 0, tiled=True)  9.55 us
    pallas_call x1, Pallas kernels, backward(): pl.pallas_call(backward_kernel, out_shape=shape((16, 64, 1024), BF16), in...  9.19 us
  transfers between devices with their start and end apart: 28, of which 14 were waited for; matrix products, arithmetic and copies ran while one was open for 13% of the time, Pallas kernels for 12%

profile of v6, /device:TPU:1, one launch (start us, length us, event | category | flops | bytes accessed | tf_op | source)
XLA Modules:
  0.0 175.4 jit_solution(13529398945885448603)
XLA Ops:
  5.7 2.5 %shard_map.155 = bf16[16,64,1024]{2,1,0:T(8,128)(2,1)} custom-call(bf16[32,512]{1,0:T(8,128)(2,1)} %get-tuple-element.53.mine, bf16[32,512]{1,0:T(8,128)(2,1)} %copy-done.23, bf16[64,1024]{1,0:T(8,128)(2,1)} %w_out.1), custom_call_target="tpu_custom_call" | custom-call | bytes 2097152 | tf_op jit(solution)/shard_map/pallas_call | solution.py:415
  10.3 7.7 %all-to-all-start = ((bf16[16,64,1024]{2,1,0:T(8,128)(2,1)}), bf16[16,64,1024]{2,1,0:T(8,128)(2,1)}, u32[]{:S(2)}, u32[]{:S(2)}) async-start(bf16[16,64,1024]{2,1,0:T(8,128)(2,1)} %shard_map.155), calls=%async_computation | async-start | bytes 4194304 | tf_op jit(solution)/shard_map/all_to_all | solution.py:52
  20.1 9.9 %convert_reduce_fusion.live = bf16[128,128]{1,0:T(8,128)(2,1)S(1)} fusion(s32[128]{0:T(128)S(1)} %select_reduce_fusion, s32[128,400]{1,0:T(8,128)S(1)} %dynamic-slice_bitcast_fusion), kind=kLoop, calls=%fused_computation | loop fusion | flops 19644416 | bytes 238080 | tf_op jit(solution)/shard_map/reduce_max | solution.py:439
  33.1 14.2 %all-to-all-done.refs_2_.refs_1_.refs_19_ = bf16[16,64,1024]{2,1,0:T(8,128)(2,1)} async-done(((bf16[16,64,1024]{2,1,0:T(8,128)(2,1)}), bf16[16,64,1024]{2,1,0:T(8,128)(2,1)}, u32[]{:S(2)}, u32[]{:S(2)}) %all-to-all-start) | async-done | bytes 2097184 | tf_op jit(solution)/shard_map/all_to_all | solution.py:52
  47.3 4.5 %shard_map.156 = (bf16[256,1024]{1,0:T(8,128)(2,1)S(1)}, f32[256,1024]{1,0:T(8,128)S(1)}, bf16[512,512]{1,0:T(8,128)(2,1)S(1)}, f32[512,512]{1,0:T(8,128)S(1)}) custom-call(bf16[256,1024]{1,0:T(8,128)(2,1)} %collective-permute-done.1.refs_0_.refs_9_, bf16[256,1024]{1,0:T(8,128)(2,1)S(1)} %collective-permute-done.2.refs_1_.refs_10_, ...), custom_call_target="tpu_custom_call" | custom-call | flops 4294967296 | bytes 6291456 | tf_op jit(solution)/shard_map/pallas_call | solution.py:139
  57.4 3.2 %shard_map.157 = (bf16[256,1024]{1,0:T(8,128)(2,1)}, bf16[256,512]{1,0:T(8,128)(2,1)S(1)}, f32[256,512]{1,0:T(8,128)S(1)}) custom-call(bf16[256,1024]{1,0:T(8,128)(2,1)S(1)} %collective-permute-done.5.refs_0_.refs_11_, bf16[16,64,1024]{2,1,0:T(8,128)(2,1)} %all-to-all-done.refs_2_.refs_1_.refs_19_), custom_call_target="tpu_custom_call" | custom-call | flops 4294967296 | bytes 6291456 | tf_op jit(solution)/shard_map/pallas_call | solution.py:139
  62.8 5.4 %all-to-all-start.1 = ((f16[16,8,1024]{2,1,0:T(8,128)(2,1)}), f16[16,8,1024]{2,1,0:T(8,128)(2,1)}, u32[]{:S(2)}, u32[]{:S(2)}) async-start(f16[16,8,1024]{2,1,0:T(8,128)(2,1)} %bitcast.33), calls=%async_computation.1 | async-start | bytes 524288 | tf_op jit(solution)/shard_map/all_to_all | solution.py:52
  68.2 2.4 %shard_map.158 = (f32[256,1024]{1,0:T(8,128)S(1)}, bf16[256,512]{1,0:T(8,128)(2,1)S(1)}, f32[256,512]{1,0:T(8,128)S(1)}) custom-call(bf16[256,1024]{1,0:T(8,128)(2,1)S(1)} %bitcast.23, bf16[16,64,1024]{2,1,0:T(8,128)(2,1)} %all-to-all-done.refs_2_.refs_1_.refs_19_), custom_call_target="tpu_custom_call" | custom-call | flops 4294967296 | bytes 6291456 | tf_op jit(solution)/shard_map/pallas_call | solution.py:139
  73.0 3.0 %all-to-all-done.1 = f16[16,8,1024]{2,1,0:T(8,128)(2,1)} async-done(((f16[16,8,1024]{2,1,0:T(8,128)(2,1)}), f16[16,8,1024]{2,1,0:T(8,128)(2,1)}, u32[]{:S(2)}, u32[]{:S(2)}) %all-to-all-start.1) | async-done | bytes 262176 | tf_op jit(solution)/shard_map/all_to_all | solution.py:52
  77.3 3.2 %shard_map.159 = (bf16[256,1152]{1,0:T(8,128)(2,1)}, bf16[128,1024]{1,0:T(8,128)(2,1)}) custom-call(s32[8]{0:T(128)S(1)} %copy-done.13, bf16[256,1024]{1,0:T(8,128)(2,1)S(1)} %bitcast.24, f32[256,1024]{1,0:T(8,128)S(1)} %copy-done.2, bf16[256,1024]{1,0:T(8,128)(2,1)} %collective-permute-done.6.from_core, ...), custom_call_target="tpu_custom_call" | custom-call | flops 4194304 | bytes 4194304 | tf_op jit(solution)/shard_map/pallas_call | solution.py:470
  80.7 3.9 %all-to-all-start.2 = ((bf16[16,8,1024]{2,1,0:T(8,128)(2,1)}), bf16[16,8,1024]{2,1,0:T(8,128)(2,1)S(1)}, u32[]{:S(2)}, u32[]{:S(2)}) async-start(bf16[16,8,1024]{2,1,0:T(8,128)(2,1)} %bitcast.9), calls=%async_computation.2 | async-start | bytes 524288 | tf_op jit(solution)/shard_map/all_to_all | solution.py:52
  86.3 5.6 %all-to-all-done.2 = bf16[16,8,1024]{2,1,0:T(8,128)(2,1)S(1)} async-done(((bf16[16,8,1024]{2,1,0:T(8,128)(2,1)}), bf16[16,8,1024]{2,1,0:T(8,128)(2,1)S(1)}, u32[]{:S(2)}, u32[]{:S(2)}) %all-to-all-start.2) | async-done | bytes 262176 | tf_op jit(solution)/shard_map/all_to_all | solution.py:52
  91.9 2.3 %shard_map.160 = (bf16[128,1280]{1,0:T(8,128)(2,1)}, f32[128,512]{1,0:T(8,128)S(1)}) custom-call(bf16[128,1024]{1,0:T(8,128)(2,1)S(1)} %bitcast.25, bf16[512,1024]{1,0:T(8,128)(2,1)S(1)} %get-tuple-element.74.tiles_hi, bf16[512,1024]{1,0:T(8,128)(2,1)S(1)} %get-tuple-element.75.tiles_lo, bf16[128,128]{1,0:T(8,128)(2,1)S(1)} %convert_reduce_fusion.live), custom_call_target="tpu_custom_call" | custom-call | flops 536870912 | bytes 3145728 | tf_op jit(solution)/shard_map/pallas_call | solution.py:482
  94.2 3.1 %collective-permute-start.17 = (bf16[256,1152]{1,0:T(8,128)(2,1)}, bf16[256,1152]{1,0:T(8,128)(2,1)}, u32[]{:S(2)}, u32[]{:S(2)}) collective-permute-start(bf16[256,1152]{1,0:T(8,128)(2,1)} %collective-permute-done.8.refs_6_), channel_id=1, source_target_pairs={{0,1},{1,0},{2,3},{3,2},{4,5},{5,4},{6,7},{7,6},{8,9},{9,8},{10,11... | collective-permute-start | bytes 1769480 | tf_op jit(solution)/shard_map/ppermute | solution.py:28
  97.4 3.5 %all-to-all-start.3 = ((bf16[16,8,1280]{2,1,0:T(8,128)(2,1)}), bf16[16,8,1280]{2,1,0:T(8,128)(2,1)S(1)}, u32[]{:S(2)}, u32[]{:S(2)}) async-start(bf16[16,8,1280]{2,1,0:T(8,128)(2,1)} %bitcast.11), calls=%async_computation.3 | async-start | bytes 655360 | tf_op jit(solution)/shard_map/all_to_all | solution.py:497
  101.9 7.5 %all-to-all-done.3.got_hbm = bf16[16,8,1280]{2,1,0:T(8,128)(2,1)S(1)} async-done(((bf16[16,8,1280]{2,1,0:T(8,128)(2,1)}), bf16[16,8,1280]{2,1,0:T(8,128)(2,1)S(1)}, u32[]{:S(2)}, u32[]{:S(2)}) %all-to-all-start.3) | async-done | bytes 327712 | tf_op jit(solution)/shard_map/all_to_all | solution.py:497
  117.7 9.2 %shard_map.163 = bf16[16,64,1024]{2,1,0:T(8,128)(2,1)} custom-call(f32[8,1024]{1,0:T(8,128)} %copy-done.25, f32[8,1024]{1,0:T(8,128)} %copy-done.24, f32[8,1024]{1,0:T(8,128)} %copy-done.22, f32[8,1024]{1,0:T(8,128)} %copy-done.11, f32[1,1024]{1,0:T(1,128)} %bitcast.27, bf16[256,1152]{1,0:T(8,128)(2,1)} %collective-permute-done.17.refs_5_, ...), custom_call_target="tpu_custom_call" | custom-call | flops 3221225472 | bytes 10485760 | tf_op jit(solution)/shard_map/pallas_call | solution.py:321
  126.9 3.7 %all-to-all-start.4 = ((bf16[16,64,1024]{2,1,0:T(8,128)(2,1)}), bf16[16,64,1024]{2,1,0:T(8,128)(2,1)S(1)}, u32[]{:S(2)}, u32[]{:S(2)}) async-start(bf16[16,64,1024]{2,1,0:T(8,128)(2,1)} %shard_map.163), calls=%async_computation.4 | async-start | bytes 4194304 | tf_op jit(solution)/shard_map/all_to_all | solution.py:522
  135.1 4.4 %collective-permute-done.10 = bf16[128,1024]{1,0:T(8,128)(2,1)S(1)} collective-permute-done((bf16[128,1024]{1,0:T(8,128)(2,1)S(1)}, bf16[128,1024]{1,0:T(8,128)(2,1)S(1)}, u32[]{:S(2)}, u32[]{:S(2)}) %collective-permute-start.10) | collective-permute-done | bytes 262176 | tf_op jit(solution)/shard_map/ppermute | solution.py:32
  144.4 5.0 %collective-permute-done.11 = bf16[128,1024]{1,0:T(8,128)(2,1)S(1)} collective-permute-done((bf16[128,1024]{1,0:T(8,128)(2,1)S(1)}, bf16[128,1024]{1,0:T(8,128)(2,1)S(1)}, u32[]{:S(2)}, u32[]{:S(2)}) %collective-permute-start.11) | collective-permute-done | bytes 262176 | tf_op jit(solution)/shard_map/ppermute | solution.py:44
  150.2 9.6 %all-to-all-done.4.got = bf16[16,64,1024]{2,1,0:T(8,128)(2,1)S(1)} async-done(((bf16[16,64,1024]{2,1,0:T(8,128)(2,1)}), bf16[16,64,1024]{2,1,0:T(8,128)(2,1)S(1)}, u32[]{:S(2)}, u32[]{:S(2)}) %all-to-all-start.4) | async-done | bytes 2097184 | tf_op jit(solution)/shard_map/all_to_all | solution.py:522
  163.9 3.0 %collective-permute-start.22 = (bf16[64,1024]{1,0:T(8,128)(2,1)S(1)}, bf16[64,1024]{1,0:T(8,128)(2,1)S(1)}, u32[]{:S(2)}, u32[]{:S(2)}) collective-permute-start(bf16[64,1024]{1,0:T(8,128)(2,1)S(1)} %maximum_maximum_fusion.own), channel_id=1, source_target_pairs={{0,64},{64,0},{1,65},{65,1},{2,66},{66,2},{3,67},{67,3},{4,68},{68... | collective-permute-start | bytes 393224 | tf_op jit(solution)/shard_map/ppermute | solution.py:40
  167.7 2.1 %divide_subtract_fusion = (f32[256,1024]{1,0:T(8,128)}, f32[256,1024]{1,0:T(8,128)}, f32[256,1024]{1,0:T(8,128)}) fusion(f32[256,1024]{1,0:T(8,128)S(1)} %copy-done.17, f32[128,1024]{1,0:T(8,128)S(1)} %convert_add_fusion, f32[128,1024]{1,0:T(8,128)S(1)} %copy-done.18, f32[256,1024]{1,0:T(8,128)S(1)} %copy-done.19, f32[256,1024]{1,0:T(8,128)S(1)} %copy-done.20), kind=kLoop, calls=%fused_computation.10 | loop fusion | flops 3407872 | bytes 7340032 | tf_op jit(solution)/shard_map/sub | solution.py:568
  170.4 2.7 %collective-permute-done.21.wrap = bf16[64,1024]{1,0:T(8,128)(2,1)S(1)} collective-permute-done((bf16[64,1024]{1,0:T(8,128)(2,1)S(1)}, bf16[64,1024]{1,0:T(8,128)(2,1)S(1)}, u32[]{:S(2)}, u32[]{:S(2)}) %collective-permute-start.21) | collective-permute-done | bytes 131104 | tf_op jit(solution)/shard_map/ppermute | solution.py:44
  (133 shorter events, 52.8 us)
Async XLA Ops:
  8.2 39.1 %collective-permute-start.2 = (bf16[256,1024]{1,0:T(8,128)(2,1)S(1)}, bf16[256,1024]{1,0:T(8,128)(2,1)S(1)}, u32[]{:S(2)}, u32[]{:S(2)}) collective-permute-start(bf16[256,1024]{1,0:T(8,128)(2,1)S(1)} %bitcast.20), channel_id=1, source_target_pairs={{0,32},{32,0},{1,33},{33,1},{2,34},{34,2},{3,35},{35,3},{4,36},{36... | collective-permute-start | bytes 1572872 | tf_op jit(solution)/shard_map/ppermute | solution.py:32
  9.7 37.6 %collective-permute-start.1 = (bf16[256,1024]{1,0:T(8,128)(2,1)S(1)}, bf16[256,1024]{1,0:T(8,128)(2,1)}, u32[]{:S(2)}, u32[]{:S(2)}) collective-permute-start(bf16[256,1024]{1,0:T(8,128)(2,1)S(1)} %bitcast.21), channel_id=1, source_target_pairs={{0,33},{33,0},{1,32},{32,1},{2,35},{35,2},{3,34},{34,3},{4,37},{37... | collective-permute-start | bytes 1572872 | tf_op jit(solution)/shard_map/ppermute | solution.py:36
  10.3 37.0 %all-to-all-start = ((bf16[16,64,1024]{2,1,0:T(8,128)(2,1)}), bf16[16,64,1024]{2,1,0:T(8,128)(2,1)}, u32[]{:S(2)}, u32[]{:S(2)}) async-start(bf16[16,64,1024]{2,1,0:T(8,128)(2,1)} %shard_map.155), calls=%async_computation | async-start | bytes 4194304 | tf_op jit(solution)/shard_map/all_to_all | solution.py:52
  18.4 11.6 %collective-permute-start.3 = (f32[256,1024]{1,0:T(8,128)S(1)}, f32[256,1024]{1,0:T(8,128)}, u32[]{:S(2)}, u32[]{:S(2)}) collective-permute-start(f32[256,1024]{1,0:T(8,128)S(1)} %copy-done.16), channel_id=1, source_target_pairs={{0,1},{1,0},{2,3},{3,2},{4,5},{5,4},{6,7},{7,6},{8,9},{9,8},{10,11... | collective-permute-start | bytes 3145736 | tf_op jit(solution)/shard_map/ppermute | solution.py:28
  56.0 20.0 %collective-permute-start.7 = (bf16[256,1024]{1,0:T(8,128)(2,1)}, bf16[256,1024]{1,0:T(8,128)(2,1)S(1)}, u32[]{:S(2)}, u32[]{:S(2)}) collective-permute-start(bf16[256,1024]{1,0:T(8,128)(2,1)} %add_convert_fusion.1), channel_id=1, source_target_pairs={{0,32},{32,0},{1,33},{33,1},{2,34},{34,2},{3,35},{35,3},{4,36},{36... | collective-permute-start | bytes 1572872 | tf_op jit(solution)/shard_map/ppermute | solution.py:32
  62.1 14.0 %collective-permute-start.6 = (bf16[256,1024]{1,0:T(8,128)(2,1)}, bf16[256,1024]{1,0:T(8,128)(2,1)}, u32[]{:S(2)}, u32[]{:S(2)}) collective-permute-start(bf16[256,1024]{1,0:T(8,128)(2,1)} %get-tuple-element.69), channel_id=1, source_target_pairs={{0,1},{1,0},{2,3},{3,2},{4,5},{5,4},{6,7},{7,6},{8,9},{9,8},{10,11... | collective-permute-start | bytes 1572872 | tf_op jit(solution)/shard_map/ppermute | solution.py:28
  62.8 13.3 %all-to-all-start.1 = ((f16[16,8,1024]{2,1,0:T(8,128)(2,1)}), f16[16,8,1024]{2,1,0:T(8,128)(2,1)}, u32[]{:S(2)}, u32[]{:S(2)}) async-start(f16[16,8,1024]{2,1,0:T(8,128)(2,1)} %bitcast.33), calls=%async_computation.1 | async-start | bytes 524288 | tf_op jit(solution)/shard_map/all_to_all | solution.py:52
  80.5 13.7 %collective-permute-start.8 = (bf16[256,1152]{1,0:T(8,128)(2,1)}, bf16[256,1152]{1,0:T(8,128)(2,1)}, u32[]{:S(2)}, u32[]{:S(2)}) collective-permute-start(bf16[256,1152]{1,0:T(8,128)(2,1)} %get-tuple-element.78.refs_8_), channel_id=1, source_target_pairs={{0,32},{32,0},{1,33},{33,1},{2,34},{34,2},{3,35},{35,3},{4,36},{36... | collective-permute-start | bytes 1769480 | tf_op jit(solution)/shard_map/ppermute | solution.py:32
  80.7 11.2 %all-to-all-start.2 = ((bf16[16,8,1024]{2,1,0:T(8,128)(2,1)}), bf16[16,8,1024]{2,1,0:T(8,128)(2,1)S(1)}, u32[]{:S(2)}, u32[]{:S(2)}) async-start(bf16[16,8,1024]{2,1,0:T(8,128)(2,1)} %bitcast.9), calls=%async_computation.2 | async-start | bytes 524288 | tf_op jit(solution)/shard_map/all_to_all | solution.py:52
  84.6 32.1 %collective-permute-start.18 = (bf16[256,1152]{1,0:T(8,128)(2,1)}, bf16[256,1152]{1,0:T(8,128)(2,1)}, u32[]{:S(2)}, u32[]{:S(2)}) collective-permute-start(bf16[256,1152]{1,0:T(8,128)(2,1)} %get-tuple-element.78.refs_8_), channel_id=1, source_target_pairs={{0,1},{1,0},{2,3},{3,2},{4,5},{5,4},{6,7},{7,6},{8,9},{9,8},{10,11... | collective-permute-start | bytes 1769480 | tf_op jit(solution)/shard_map/ppermute | solution.py:28
  94.2 22.8 %collective-permute-start.17 = (bf16[256,1152]{1,0:T(8,128)(2,1)}, bf16[256,1152]{1,0:T(8,128)(2,1)}, u32[]{:S(2)}, u32[]{:S(2)}) collective-permute-start(bf16[256,1152]{1,0:T(8,128)(2,1)} %collective-permute-done.8.refs_6_), channel_id=1, source_target_pairs={{0,1},{1,0},{2,3},{3,2},{4,5},{5,4},{6,7},{7,6},{8,9},{9,8},{10,11... | collective-permute-start | bytes 1769480 | tf_op jit(solution)/shard_map/ppermute | solution.py:28
  97.4 12.0 %all-to-all-start.3 = ((bf16[16,8,1280]{2,1,0:T(8,128)(2,1)}), bf16[16,8,1280]{2,1,0:T(8,128)(2,1)S(1)}, u32[]{:S(2)}, u32[]{:S(2)}) async-start(bf16[16,8,1280]{2,1,0:T(8,128)(2,1)} %bitcast.11), calls=%async_computation.3 | async-start | bytes 655360 | tf_op jit(solution)/shard_map/all_to_all | solution.py:497
  110.6 6.3 %collective-permute-start.16 = (f32[8,1024]{1,0:T(8,128)S(1)}, f32[8,1024]{1,0:T(8,128)S(1)}, u32[]{:S(2)}, u32[]{:S(2)}) collective-permute-start(f32[8,1024]{1,0:T(8,128)S(1)} %get-tuple-element.87.refs_3_), channel_id=1, source_target_pairs={{0,1},{1,0},{2,3},{3,2},{4,5},{5,4},{6,7},{7,6},{8,9},{9,8},{10,11... | collective-permute-start | bytes 98312 | tf_op jit(solution)/shard_map/ppermute | solution.py:28
  112.2 4.6 %collective-permute-start.15 = (f32[8,1024]{1,0:T(8,128)S(1)}, f32[8,1024]{1,0:T(8,128)S(1)}, u32[]{:S(2)}, u32[]{:S(2)}) collective-permute-start(f32[8,1024]{1,0:T(8,128)S(1)} %get-tuple-element.87.refs_3_), channel_id=1, source_target_pairs={{0,32},{32,0},{1,33},{33,1},{2,34},{34,2},{3,35},{35,3},{4,36},{36... | collective-permute-start | bytes 98312 | tf_op jit(solution)/shard_map/ppermute | solution.py:32
  113.7 3.4 %collective-permute-start.14 = (f32[8,1024]{1,0:T(8,128)S(1)}, f32[8,1024]{1,0:T(8,128)S(1)}, u32[]{:S(2)}, u32[]{:S(2)}) collective-permute-start(f32[8,1024]{1,0:T(8,128)S(1)} %get-tuple-element.87.refs_3_), channel_id=1, source_target_pairs={{0,33},{33,0},{1,32},{32,1},{2,35},{35,2},{3,34},{34,3},{4,37},{37... | collective-permute-start | bytes 98312 | tf_op jit(solution)/shard_map/ppermute | solution.py:36
  116.7 13.9 %collective-permute-start.9 = (bf16[256,1024]{1,0:T(8,128)(2,1)}, bf16[256,1024]{1,0:T(8,128)(2,1)}, u32[]{:S(2)}, u32[]{:S(2)}) collective-permute-start(bf16[256,1024]{1,0:T(8,128)(2,1)} %get-tuple-element.86), channel_id=1, source_target_pairs={{0,1},{1,0},{2,3},{3,2},{4,5},{5,4},{6,7},{7,6},{8,9},{9,8},{10,11... | collective-permute-start | bytes 1572872 | tf_op jit(solution)/shard_map/ppermute | solution.py:28
  126.9 32.9 %all-to-all-start.4 = ((bf16[16,64,1024]{2,1,0:T(8,128)(2,1)}), bf16[16,64,1024]{2,1,0:T(8,128)(2,1)S(1)}, u32[]{:S(2)}, u32[]{:S(2)}) async-start(bf16[16,64,1024]{2,1,0:T(8,128)(2,1)} %shard_map.163), calls=%async_computation.4 | async-start | bytes 4194304 | tf_op jit(solution)/shard_map/all_to_all | solution.py:522
  131.9 7.6 %collective-permute-start.10 = (bf16[128,1024]{1,0:T(8,128)(2,1)S(1)}, bf16[128,1024]{1,0:T(8,128)(2,1)S(1)}, u32[]{:S(2)}, u32[]{:S(2)}) collective-permute-start(bf16[128,1024]{1,0:T(8,128)(2,1)S(1)} %get-tuple-element.107), channel_id=1, source_target_pairs={{0,32},{32,0},{1,33},{33,1},{2,34},{34,2},{3,35},{35,3},{4,36},{36... | collective-permute-start | bytes 786440 | tf_op jit(solution)/shard_map/ppermute | solution.py:32
  133.2 8.4 %collective-permute-start.12 = (bf16[128,1024]{1,0:T(8,128)(2,1)S(1)}, bf16[128,1024]{1,0:T(8,128)(2,1)S(1)}, u32[]{:S(2)}, u32[]{:S(2)}) collective-permute-start(bf16[128,1024]{1,0:T(8,128)(2,1)S(1)} %get-tuple-element.108), channel_id=1, source_target_pairs={{0,96},{96,0},{32,64},{64,32},{1,97},{97,1},{33,65},{65,33},{2,98}... | collective-permute-start | bytes 786440 | tf_op jit(solution)/shard_map/ppermute | solution.py:44
  141.8 7.6 %collective-permute-start.11 = (bf16[128,1024]{1,0:T(8,128)(2,1)S(1)}, bf16[128,1024]{1,0:T(8,128)(2,1)S(1)}, u32[]{:S(2)}, u32[]{:S(2)}) collective-permute-start(bf16[128,1024]{1,0:T(8,128)(2,1)S(1)} %get-tuple-element.105), channel_id=1, source_target_pairs={{0,96},{96,0},{32,64},{64,32},{1,97},{97,1},{33,65},{65,33},{2,98}... | collective-permute-start | bytes 786440 | tf_op jit(solution)/shard_map/ppermute | solution.py:44
  143.8 19.1 %collective-permute-start.13 = (bf16[128,1024]{1,0:T(8,128)(2,1)S(1)}, bf16[128,1024]{1,0:T(8,128)(2,1)}, u32[]{:S(2)}, u32[]{:S(2)}) collective-permute-start(bf16[128,1024]{1,0:T(8,128)(2,1)S(1)} %get-tuple-element.106), channel_id=1, source_target_pairs={{0,32},{32,0},{1,33},{33,1},{2,34},{34,2},{3,35},{35,3},{4,36},{36... | collective-permute-start | bytes 786440 | tf_op jit(solution)/shard_map/ppermute | solution.py:32
  163.9 6.5 %collective-permute-start.22 = (bf16[64,1024]{1,0:T(8,128)(2,1)S(1)}, bf16[64,1024]{1,0:T(8,128)(2,1)S(1)}, u32[]{:S(2)}, u32[]{:S(2)}) collective-permute-start(bf16[64,1024]{1,0:T(8,128)(2,1)S(1)} %maximum_maximum_fusion.own), channel_id=1, source_target_pairs={{0,64},{64,0},{1,65},{65,1},{2,66},{66,2},{3,67},{67,3},{4,68},{68... | collective-permute-start | bytes 393224 | tf_op jit(solution)/shard_map/ppermute | solution.py:40
  166.9 6.2 %collective-permute-start.21 = (bf16[64,1024]{1,0:T(8,128)(2,1)S(1)}, bf16[64,1024]{1,0:T(8,128)(2,1)S(1)}, u32[]{:S(2)}, u32[]{:S(2)}) collective-permute-start(bf16[64,1024]{1,0:T(8,128)(2,1)S(1)} %maximum_maximum_fusion.own), channel_id=1, source_target_pairs={{0,96},{96,0},{32,64},{64,32},{1,97},{97,1},{33,65},{65,33},{2,98}... | collective-permute-start | bytes 393224 | tf_op jit(solution)/shard_map/ppermute | solution.py:44
  167.7 5.9 %collective-permute-start.20 = (bf16[64,1024]{1,0:T(8,128)(2,1)S(1)}, bf16[64,1024]{1,0:T(8,128)(2,1)S(1)}, u32[]{:S(2)}, u32[]{:S(2)}) collective-permute-start(bf16[64,1024]{1,0:T(8,128)(2,1)S(1)} %maximum_maximum_fusion.own), channel_id=1, source_target_pairs={{0,32},{32,0},{1,33},{33,1},{2,34},{34,2},{3,35},{35,3},{4,36},{36... | collective-permute-start | bytes 393224 | tf_op jit(solution)/shard_map/ppermute | solution.py:32
  (32 other events, 180.6 us)

commit v7 on v4

--- a/solution.py
+++ b/solution.py
@@ -69,8 +69,13 @@
     return lax.broadcasted_iota(jnp.int32, dims, axis)
 
 
-def pick_kernel(meta, w_in, mine, theirs):
-    core, role = meta[0], meta[1]
+def place_of():
+    core, high, low = (lax.axis_index(axis) for axis in ("c", "h", "l"))
+    return core, high + low - 2 * high * low
+
+
+def pick_kernel(w_in, mine, theirs):
+    core, role = place_of()
     part = jnp.where(iota((512, 256), 1) < 128, core * 2 + role, 2 - core * 2 + role)
     at = iota((512, 256), 1) % 128
     spread = (iota((512, 256), 0) == at // 32 * 128 + part * 32 + at % 32).astype(BF16)
@@ -80,8 +85,8 @@
         theirs[:, i * 128 : i * 128 + 128] = got[:, 128:]
 
 
-def lay_kernel(meta, mine, theirs, w_out, out, block, sems):
-    core, role = meta[0], meta[1]
+def lay_kernel(mine, theirs, w_out, out, block, sems):
+    core, role = place_of()
     block[:32] = jnp.where(role == 0, w_out[:32], w_out[32:])
     block[32:, :512] = jnp.where(core == 0, mine[...], theirs[...])
     block[32:, 512:] = jnp.where(core == 0, theirs[...], mine[...])
@@ -252,23 +257,40 @@
         at = pl.ds(k * 256, 256)
         tok_copies.append(pltpu.make_async_copy(toks[k], tok_buf.at[at], sems.at[9 + k]))
         tok_copies[k].start()
+    spread = (iota((128, 256), 0) // 2 == iota((128, 256), 1) // 128).astype(BF16)
+    spread = jnp.where((iota((128, 256), 0) < 3), spread, jnp.zeros_like(spread))
+    ones = jnp.ones((32, 128), BF16)
+    own_doc = iota((256, 16), 0) // 32 == iota((256, 16), 1) % 8
+    place = (iota((256, 128), 0) % 32).astype(F32)
     for k in range(4):
         row_copies[k].wait()
-        scaled_grad = grads[k][...] * gain[...]
-        grad_mean = jnp.mean(scaled_grad, axis=-1, keepdims=True)
+        grad = grads[k][...] * gain[...]
+        grad_dev = grad - jnp.mean(grad, axis=-1, keepdims=True)
+        grad_hi = grad.astype(BF16)
+        grad_lo = (grad - grad_hi.astype(F32)).astype(BF16)
+        rows_at = pl.ds(k * 256, 256)
+        factors = jnp.dot(row_buf[rows_at, 1024:], spread, preferred_element_type=F32)
+        count = factors[:, 128:]
+        factor = jnp.where(place < count, 1.0, 0.0) / count * factors[:, :128]
+        along = lax.dot_general(
+            row_buf[rows_at, :1024],
+            jnp.concatenate([grad_hi, grad_lo], axis=0),
+            LAST,
+            preferred_element_type=F32,
+        )
+        along = jnp.where(own_doc, along, 0.0) * (1.0 / 1024.0)
+        along_hi = along.astype(BF16)
+        along_lo = (along - along_hi.astype(F32)).astype(BF16)
+        along = jnp.dot(
+            jnp.concatenate([along_hi, along_lo], axis=1), ones, preferred_element_type=F32
+        )
         for d in range(8):
             at = pl.ds(k * 256 + d * 32, 32)
+            here = slice(d * 32, d * 32 + 32)
             norm = row_buf[at, :1024].astype(F32)
-            extra = row_buf[at, 1024:].astype(F32)
-            lane = iota((32, 128), 1)
-            scale = jnp.sum(jnp.where(lane < 2, extra, 0.0), axis=1, keepdims=True)
-            count = jnp.sum(jnp.where(lane == 2, extra, 0.0), axis=1, keepdims=True)
-            share = jnp.where(iota((32, 1), 0).astype(F32) < count, 1.0, 0.0) / count
-            grad = scaled_grad[d : d + 1]
-            along = jnp.mean(grad * norm, axis=-1, keepdims=True)
-            sum_grad[at] = (
-                (grad - grad_mean[d : d + 1] - norm * along) * (share * scale)
-            ).astype(BF16)
+            wide = jnp.concatenate([along[here]] * 8, axis=1)
+            scale = jnp.concatenate([factor[here]] * 8, axis=1)
+            sum_grad[at] = ((grad_dev[d : d + 1] - norm * wide) * scale).astype(BF16)
         if k == 0:
             first.wait()
         if k % 2 == 0:
@@ -394,18 +416,20 @@
     mine, theirs = pl.pallas_call(
         pick_kernel,
         out_shape=(shape((32, 512), BF16),) * 2,
-        in_specs=[SCALARS, WHOLE],
+        in_specs=[WHOLE],
         out_specs=(WHOLE, WHOLE),
+        compiler_params=LIMIT,
         cost_estimate=cost(2**25, 2**18),
-    )(meta, w_in)
+    )(w_in)
     block = pl.pallas_call(
         lay_kernel,
         out_shape=shape((16, 64, width), BF16),
-        in_specs=[SCALARS, WHOLE, WHOLE, WHOLE],
+        in_specs=[WHOLE, WHOLE, WHOLE],
         out_specs=ANYWHERE,
         scratch_shapes=[pltpu.VMEM((64, width), BF16), pltpu.SemaphoreType.DMA((16,))],
+        compiler_params=LIMIT,
         cost_estimate=cost(0, 2**21),
-    )(meta, mine, swap_core(theirs), w_out)
+    )(mine, swap_core(theirs), w_out)
     block, own_tok, label_tiles, shortlist, positives, owner_map = lax.optimization_barrier(
         (block, own_tok, label_tiles, shortlist, positives, owner_map)
     )
@@ -444,11 +468,13 @@
     )
 
     near_a, near_b, near_hidden, near_slope = forward(diag_tok, near_tok, weights, 2**30)
-    near_sum = (near_b + swap_core(near_a).astype(F32)).astype(BF16)
+    near_a, core_tok = lax.optimization_barrier((near_a, core_tok))
+    own_a, own_b, own_hidden, own_slope = forward(core_tok, own_tok, weights, 2**30)
+    near_a, own_a, own_b = lax.optimization_barrier((swap_core(near_a), own_a, own_b))
+    near_sum = (near_b + near_a.astype(F32)).astype(BF16)
     near_sum, pos_part = lax.optimization_barrier((near_sum, pos_part))
     from_near = swap_near(near_sum)
     pos_got = gather_chips(pos_part.reshape(16, docs, width))
-    own_a, own_b, own_hidden, own_slope = forward(core_tok, own_tok, weights, 2**36)
     from_near, pos_got = lax.optimization_barrier((from_near, pos_got))
     pos_mean = jnp.sum(pos_got.astype(F32), axis=0) * (1.0 / POS_SCALE)
     own_rows, emb = pl.pallas_call(

time: 173 us -> 172 us (level)
  local copies, waits for them, and re-layouts: 5.37 us -> 8.17 us
  waiting for transfers between devices: 54.8 us -> 53 us
    unnamed x59 -> x51, local copies, waits for them, and re-layouts: 2.58 us -> 5.37 us
    ppermute x7, starting transfers between devices: 5.68 us -> 3.89 us  [swap_near(): return lax.ppermute(a, 'l', [(0, 1), (1, 0)])]
  transfers between devices with their start and end apart: 27 -> 27, of which waited for: 13 -> 10; matrix products, arithmetic and copies ran while one was open for 13% -> 13% of each run, Pallas kernels for 11% -> 14%
where the time goes in v7:
time: 172 us; the launch traced here: 171 us
  waiting for transfers between devices  53 us (31%)
  starting transfers between devices  46.8 us (27%)
  Pallas kernels  30.4 us (18%)
  other arithmetic  17.9 us (10%)
  blocking collectives  12.6 us (7%)
  local copies, waits for them, and re-layouts  8.17 us (5%)
    all_to_all x2, waiting for transfers between devices, gather_chips(): return lax.all_to_all(a, CHIPS, 0, 0, tiled=True)  19.6 us
    ppermute x10, starting transfers between devices, swap_core(): return lax.ppermute(a, 'c', [(0, 1), (1, 0)])  13.2 us
    all_to_all x1, blocking collectives, gather_chips(): return lax.all_to_all(a, CHIPS, 0, 0, tiled=True)  12.6 us
    all_to_all x2, starting transfers between devices, gather_chips(): return lax.all_to_all(a, CHIPS, 0, 0, tiled=True)  12.5 us
    all_to_all x1, waiting for transfers between devices, on_device(): got = lax.all_to_all(send, CHIPS, 0, 0, tiled=True)  10.5 us
    pallas_call x1, Pallas kernels, backward(): pl.pallas_call(backward_kernel, out_shape=shape((16, 64, 1024), BF16), in...  10.5 us
    reduce_max x1, other arithmetic, on_device(): jnp.max((short[:, :, None] == cluster_ids[None, None, :]).astype(F32), ax...  9.87 us
    ppermute x3, waiting for transfers between devices, swap_wrap(): return lax.ppermute(a, ('h', 'l'), [(0, 3), (3, 0), (1, 2), (2, 1)])  8.47 us
  transfers between devices with their start and end apart: 27, of which 10 were waited for; matrix products, arithmetic and copies ran while one was open for 13% of the time, Pallas kernels for 14%

profile of v7, /device:TPU:1, one launch (start us, length us, event | category | flops | bytes accessed | tf_op | source)
XLA Modules:
  0.0 171.5 jit_solution(18080249199698363487)
XLA Ops:
  8.9 7.7 %all-to-all-start = ((bf16[16,64,1024]{2,1,0:T(8,128)(2,1)}), bf16[16,64,1024]{2,1,0:T(8,128)(2,1)}, u32[]{:S(2)}, u32[]{:S(2)}) async-start(bf16[16,64,1024]{2,1,0:T(8,128)(2,1)} %shard_map.155), calls=%async_computation | async-start | bytes 4194304 | tf_op jit(solution)/shard_map/all_to_all | solution.py:50
  18.8 9.9 %convert_reduce_fusion.live = bf16[128,128]{1,0:T(8,128)(2,1)S(1)} fusion(s32[128]{0:T(128)S(1)} %select_reduce_fusion, s32[128,400]{1,0:T(8,128)S(1)} %dynamic-slice_bitcast_fusion), kind=kLoop, calls=%fused_computation | loop fusion | flops 19644416 | bytes 238080 | tf_op jit(solution)/shard_map/reduce_max | solution.py:449
  31.9 13.9 %all-to-all-done.weights.refs_17_ = bf16[16,64,1024]{2,1,0:T(8,128)(2,1)} async-done(((bf16[16,64,1024]{2,1,0:T(8,128)(2,1)}), bf16[16,64,1024]{2,1,0:T(8,128)(2,1)}, u32[]{:S(2)}, u32[]{:S(2)}) %all-to-all-start) | async-done | bytes 2097184 | tf_op jit(solution)/shard_map/all_to_all | solution.py:50
  45.8 4.3 %shard_map.156 = (bf16[256,1024]{1,0:T(8,128)(2,1)S(1)}, f32[256,1024]{1,0:T(8,128)S(1)}, bf16[512,512]{1,0:T(8,128)(2,1)S(1)}, f32[512,512]{1,0:T(8,128)S(1)}) custom-call(bf16[256,1024]{1,0:T(8,128)(2,1)} %collective-permute-done.1.tok_a.refs_9_, bf16[256,1024]{1,0:T(8,128)(2,1)} %collective-permute-done.2.tok_b.refs_10_, ...), custom_call_target="tpu_custom_call" | custom-call | flops 1073741824 | bytes 6291456 | tf_op jit(solution)/shard_map/pallas_call | solution.py:128
  53.8 3.1 %shard_map.157 = (bf16[256,1024]{1,0:T(8,128)(2,1)S(1)}, f32[256,1024]{1,0:T(8,128)S(1)}, bf16[512,512]{1,0:T(8,128)(2,1)S(1)}, f32[512,512]{1,0:T(8,128)S(1)}) custom-call(bf16[256,1024]{1,0:T(8,128)(2,1)S(1)} %collective-permute-done.4.tok_a.refs_11_, bf16[256,1024]{1,0:T(8,128)(2,1)S(1)} %bitcast.23, bf16[16,64,1024]{2,1,0:T(8,128)(2,1)} %all-to-all-done.weights.refs_17_), custom_call_target="tpu_custom_call" | custom-call | flops 1073741824 | bytes 6291456 | tf_op jit(solution)/shard_map/pallas_call | solution.py:128
  58.9 12.6 %all_to_all.25 = f16[16,8,1024]{2,1,0:T(8,128)(2,1)} all-to-all(f16[16,8,1024]{2,1,0:T(8,128)(2,1)S(1)} %bitcast.33), channel_id=1, replica_groups=mesh['h'=2,'l'=2,'x'=4,'z'=4,'c'=2] {'x','z'}, dimensions={0} | all-to-all | bytes 524288 | tf_op jit(solution)/shard_map/all_to_all | solution.py:50
  71.6 2.7 %shard_map.158 = (bf16[256,1152]{1,0:T(8,128)(2,1)}, bf16[128,1024]{1,0:T(8,128)(2,1)}) custom-call(s32[8]{0:T(128)S(1)} %copy-done.10, bf16[256,1024]{1,0:T(8,128)(2,1)S(1)} %bitcast.24, f32[256,1024]{1,0:T(8,128)S(1)} %get-tuple-element.67.part, bf16[256,1024]{1,0:T(8,128)(2,1)S(1)} %collective-permute-done.6.from_core, ...), custom_call_target="tpu_custom_call" | custom-call | flops 4194304 | bytes 4194304 | tf_op jit(solution)/shard_map/pallas_call | solution.py:480
  74.7 4.8 %all-to-all-start.2 = ((bf16[16,8,1024]{2,1,0:T(8,128)(2,1)}), bf16[16,8,1024]{2,1,0:T(8,128)(2,1)S(1)}, u32[]{:S(2)}, u32[]{:S(2)}) async-start(bf16[16,8,1024]{2,1,0:T(8,128)(2,1)} %bitcast.9), calls=%async_computation.2 | async-start | bytes 524288 | tf_op jit(solution)/shard_map/all_to_all | solution.py:50
  81.2 5.7 %all-to-all-done.2 = bf16[16,8,1024]{2,1,0:T(8,128)(2,1)S(1)} async-done(((bf16[16,8,1024]{2,1,0:T(8,128)(2,1)}), bf16[16,8,1024]{2,1,0:T(8,128)(2,1)S(1)}, u32[]{:S(2)}, u32[]{:S(2)}) %all-to-all-start.2) | async-done | bytes 262176 | tf_op jit(solution)/shard_map/all_to_all | solution.py:50
  86.9 2.3 %shard_map.159 = (bf16[128,1280]{1,0:T(8,128)(2,1)}, f32[128,512]{1,0:T(8,128)S(1)}) custom-call(bf16[128,1024]{1,0:T(8,128)(2,1)S(1)} %bitcast.25, bf16[512,1024]{1,0:T(8,128)(2,1)S(1)} %get-tuple-element.76.tiles_hi, bf16[512,1024]{1,0:T(8,128)(2,1)S(1)} %get-tuple-element.77.tiles_lo, bf16[128,128]{1,0:T(8,128)(2,1)S(1)} %convert_reduce_fusion.live), custom_call_target="tpu_custom_call" | custom-call | flops 536870912 | bytes 3145728 | tf_op jit(solution)/shard_map/pallas_call | solution.py:492
  89.2 2.9 %collective-permute-start.17 = (bf16[256,1152]{1,0:T(8,128)(2,1)}, bf16[256,1152]{1,0:T(8,128)(2,1)}, u32[]{:S(2)}, u32[]{:S(2)}) collective-permute-start(bf16[256,1152]{1,0:T(8,128)(2,1)} %collective-permute-done.8.refs_6_), channel_id=1, source_target_pairs={{0,1},{1,0},{2,3},{3,2},{4,5},{5,4},{6,7},{7,6},{8,9},{9,8},{10,11... | collective-permute-start | bytes 1769480 | tf_op jit(solution)/shard_map/ppermute | solution.py:26
  92.2 3.5 %all-to-all-start.3 = ((bf16[16,8,1280]{2,1,0:T(8,128)(2,1)}), bf16[16,8,1280]{2,1,0:T(8,128)(2,1)S(1)}, u32[]{:S(2)}, u32[]{:S(2)}) async-start(bf16[16,8,1280]{2,1,0:T(8,128)(2,1)} %bitcast.11), calls=%async_computation.3 | async-start | bytes 655360 | tf_op jit(solution)/shard_map/all_to_all | solution.py:507
  96.7 7.5 %all-to-all-done.3.got_hbm = bf16[16,8,1280]{2,1,0:T(8,128)(2,1)S(1)} async-done(((bf16[16,8,1280]{2,1,0:T(8,128)(2,1)}), bf16[16,8,1280]{2,1,0:T(8,128)(2,1)S(1)}, u32[]{:S(2)}, u32[]{:S(2)}) %all-to-all-start.3) | async-done | bytes 327712 | tf_op jit(solution)/shard_map/all_to_all | solution.py:507
  112.5 10.5 %shard_map.162 = bf16[16,64,1024]{2,1,0:T(8,128)(2,1)} custom-call(f32[8,1024]{1,0:T(8,128)} %copy-done.22, f32[8,1024]{1,0:T(8,128)} %copy-done.21, f32[8,1024]{1,0:T(8,128)} %copy-done.20, f32[8,1024]{1,0:T(8,128)} %copy-done.8, f32[1,1024]{1,0:T(1,128)} %bitcast.27, bf16[256,1152]{1,0:T(8,128)(2,1)} %collective-permute-done.17.refs_5_, ...), custom_call_target="tpu_custom_call" | custom-call | flops 3221225472 | bytes 10485760 | tf_op jit(solution)/shard_map/pallas_call | solution.py:329
  122.9 3.7 %all-to-all-start.4 = ((bf16[16,64,1024]{2,1,0:T(8,128)(2,1)}), bf16[16,64,1024]{2,1,0:T(8,128)(2,1)S(1)}, u32[]{:S(2)}, u32[]{:S(2)}) async-start(bf16[16,64,1024]{2,1,0:T(8,128)(2,1)} %shard_map.162), calls=%async_computation.4 | async-start | bytes 4194304 | tf_op jit(solution)/shard_map/all_to_all | solution.py:532
  128.3 2.6 %collective-permute-start.12 = (bf16[128,1024]{1,0:T(8,128)(2,1)S(1)}, bf16[128,1024]{1,0:T(8,128)(2,1)S(1)}, u32[]{:S(2)}, u32[]{:S(2)}) collective-permute-start(bf16[128,1024]{1,0:T(8,128)(2,1)S(1)} %get-tuple-element.108), channel_id=1, source_target_pairs={{0,96},{96,0},{32,64},{64,32},{1,97},{97,1},{33,65},{65,33},{2,98}... | collective-permute-start | bytes 786440 | tf_op jit(solution)/shard_map/ppermute | solution.py:42
  130.9 4.6 %collective-permute-done.10 = bf16[128,1024]{1,0:T(8,128)(2,1)S(1)} collective-permute-done((bf16[128,1024]{1,0:T(8,128)(2,1)S(1)}, bf16[128,1024]{1,0:T(8,128)(2,1)S(1)}, u32[]{:S(2)}, u32[]{:S(2)}) %collective-permute-start.10) | collective-permute-done | bytes 262176 | tf_op jit(solution)/shard_map/ppermute | solution.py:30
  136.9 2.6 %collective-permute-start.11 = (bf16[128,1024]{1,0:T(8,128)(2,1)S(1)}, bf16[128,1024]{1,0:T(8,128)(2,1)S(1)}, u32[]{:S(2)}, u32[]{:S(2)}) collective-permute-start(bf16[128,1024]{1,0:T(8,128)(2,1)S(1)} %get-tuple-element.105), channel_id=1, source_target_pairs={{0,96},{96,0},{32,64},{64,32},{1,97},{97,1},{33,65},{65,33},{2,98}... | collective-permute-start | bytes 786440 | tf_op jit(solution)/shard_map/ppermute | solution.py:42
  140.2 4.3 %collective-permute-done.11 = bf16[128,1024]{1,0:T(8,128)(2,1)S(1)} collective-permute-done((bf16[128,1024]{1,0:T(8,128)(2,1)S(1)}, bf16[128,1024]{1,0:T(8,128)(2,1)S(1)}, u32[]{:S(2)}, u32[]{:S(2)}) %collective-permute-start.11) | collective-permute-done | bytes 262176 | tf_op jit(solution)/shard_map/ppermute | solution.py:42
  145.3 10.5 %all-to-all-done.4.got = bf16[16,64,1024]{2,1,0:T(8,128)(2,1)S(1)} async-done(((bf16[16,64,1024]{2,1,0:T(8,128)(2,1)}), bf16[16,64,1024]{2,1,0:T(8,128)(2,1)S(1)}, u32[]{:S(2)}, u32[]{:S(2)}) %all-to-all-start.4) | async-done | bytes 2097184 | tf_op jit(solution)/shard_map/all_to_all | solution.py:532
  156.9 2.1 %collective-permute-start.19 = (bf16[32,512]{1,0:T(8,128)(2,1)S(1)}, bf16[32,512]{1,0:T(8,128)(2,1)S(1)}, u32[]{:S(2)}, u32[]{:S(2)}) collective-permute-start(bf16[32,512]{1,0:T(8,128)(2,1)S(1)} %get-tuple-element.97), channel_id=1, source_target_pairs={{0,1},{1,0},{2,3},{3,2},{4,5},{5,4},{6,7},{7,6},{8,9},{9,8},{10,11... | collective-permute-start | bytes 98312 | tf_op jit(solution)/shard_map/ppermute | solution.py:26
  160.1 2.7 %collective-permute-start.22 = (bf16[64,1024]{1,0:T(8,128)(2,1)S(1)}, bf16[64,1024]{1,0:T(8,128)(2,1)S(1)}, u32[]{:S(2)}, u32[]{:S(2)}) collective-permute-start(bf16[64,1024]{1,0:T(8,128)(2,1)S(1)} %maximum_maximum_fusion.own), channel_id=1, source_target_pairs={{0,64},{64,0},{1,65},{65,1},{2,66},{66,2},{3,67},{67,3},{4,68},{68... | collective-permute-start | bytes 393224 | tf_op jit(solution)/shard_map/ppermute | solution.py:38
  162.9 2.1 %divide_subtract_fusion = (f32[256,1024]{1,0:T(8,128)}, f32[256,1024]{1,0:T(8,128)}, f32[256,1024]{1,0:T(8,128)}) fusion(f32[256,1024]{1,0:T(8,128)S(1)} %copy-done.14, f32[128,1024]{1,0:T(8,128)S(1)} %convert_add_fusion, f32[128,1024]{1,0:T(8,128)S(1)} %copy-done.15, f32[256,1024]{1,0:T(8,128)S(1)} %copy-done.16, f32[256,1024]{1,0:T(8,128)S(1)} %copy-done.17), kind=kLoop, calls=%fused_computation.10 | loop fusion | flops 3407872 | bytes 7340032 | tf_op jit(solution)/shard_map/sub | solution.py:578
  166.6 3.0 %collective-permute-done.21.wrap = bf16[64,1024]{1,0:T(8,128)(2,1)S(1)} collective-permute-done((bf16[64,1024]{1,0:T(8,128)(2,1)S(1)}, bf16[64,1024]{1,0:T(8,128)(2,1)S(1)}, u32[]{:S(2)}, u32[]{:S(2)}) %collective-permute-start.21) | collective-permute-done | bytes 131104 | tf_op jit(solution)/shard_map/ppermute | solution.py:42
  (125 shorter events, 40.6 us)
Async XLA Ops:
  6.7 45.2 %collective-permute-start.4 = (bf16[256,1024]{1,0:T(8,128)(2,1)S(1)}, bf16[256,1024]{1,0:T(8,128)(2,1)S(1)}, u32[]{:S(2)}, u32[]{:S(2)}) collective-permute-start(bf16[256,1024]{1,0:T(8,128)(2,1)S(1)} %bitcast.20), channel_id=1, source_target_pairs={{0,1},{1,0},{2,3},{3,2},{4,5},{5,4},{6,7},{7,6},{8,9},{9,8},{10,11... | collective-permute-start | bytes 1572872 | tf_op jit(solution)/shard_map/ppermute | solution.py:26
  7.1 38.7 %collective-permute-start.2 = (bf16[256,1024]{1,0:T(8,128)(2,1)S(1)}, bf16[256,1024]{1,0:T(8,128)(2,1)}, u32[]{:S(2)}, u32[]{:S(2)}) collective-permute-start(bf16[256,1024]{1,0:T(8,128)(2,1)S(1)} %bitcast.21), channel_id=1, source_target_pairs={{0,32},{32,0},{1,33},{33,1},{2,34},{34,2},{3,35},{35,3},{4,36},{36... | collective-permute-start | bytes 1572872 | tf_op jit(solution)/shard_map/ppermute | solution.py:30
  8.5 37.3 %collective-permute-start.1 = (bf16[256,1024]{1,0:T(8,128)(2,1)S(1)}, bf16[256,1024]{1,0:T(8,128)(2,1)}, u32[]{:S(2)}, u32[]{:S(2)}) collective-permute-start(bf16[256,1024]{1,0:T(8,128)(2,1)S(1)} %bitcast.22), channel_id=1, source_target_pairs={{0,33},{33,0},{1,32},{32,1},{2,35},{35,2},{3,34},{34,3},{4,37},{37... | collective-permute-start | bytes 1572872 | tf_op jit(solution)/shard_map/ppermute | solution.py:34
  8.9 36.9 %all-to-all-start = ((bf16[16,64,1024]{2,1,0:T(8,128)(2,1)}), bf16[16,64,1024]{2,1,0:T(8,128)(2,1)}, u32[]{:S(2)}, u32[]{:S(2)}) async-start(bf16[16,64,1024]{2,1,0:T(8,128)(2,1)} %shard_map.155), calls=%async_computation | async-start | bytes 4194304 | tf_op jit(solution)/shard_map/all_to_all | solution.py:50
  17.1 11.7 %collective-permute-start.3 = (f32[256,1024]{1,0:T(8,128)S(1)}, f32[256,1024]{1,0:T(8,128)}, u32[]{:S(2)}, u32[]{:S(2)}) collective-permute-start(f32[256,1024]{1,0:T(8,128)S(1)} %copy-done.13), channel_id=1, source_target_pairs={{0,1},{1,0},{2,3},{3,2},{4,5},{5,4},{6,7},{7,6},{8,9},{9,8},{10,11... | collective-permute-start | bytes 3145736 | tf_op jit(solution)/shard_map/ppermute | solution.py:26
  51.9 5.0 %collective-permute-start.5 = (bf16[256,1024]{1,0:T(8,128)(2,1)S(1)}, bf16[256,1024]{1,0:T(8,128)(2,1)S(1)}, u32[]{:S(2)}, u32[]{:S(2)}) collective-permute-start(bf16[256,1024]{1,0:T(8,128)(2,1)S(1)} %get-tuple-element.63), channel_id=1, source_target_pairs={{0,1},{1,0},{2,3},{3,2},{4,5},{5,4},{6,7},{7,6},{8,9},{9,8},{10,11... | collective-permute-start | bytes 1572872 | tf_op jit(solution)/shard_map/ppermute | solution.py:26
  57.1 14.5 %collective-permute-start.7 = (bf16[256,1024]{1,0:T(8,128)(2,1)S(1)}, bf16[256,1024]{1,0:T(8,128)(2,1)S(1)}, u32[]{:S(2)}, u32[]{:S(2)}) collective-permute-start(bf16[256,1024]{1,0:T(8,128)(2,1)S(1)} %add_convert_fusion.1), channel_id=1, source_target_pairs={{0,32},{32,0},{1,33},{33,1},{2,34},{34,2},{3,35},{35,3},{4,36},{36... | collective-permute-start | bytes 1572872 | tf_op jit(solution)/shard_map/ppermute | solution.py:30
  58.4 13.1 %collective-permute-start.6 = (bf16[256,1024]{1,0:T(8,128)(2,1)S(1)}, bf16[256,1024]{1,0:T(8,128)(2,1)S(1)}, u32[]{:S(2)}, u32[]{:S(2)}) collective-permute-start(bf16[256,1024]{1,0:T(8,128)(2,1)S(1)} %get-tuple-element.68), channel_id=1, source_target_pairs={{0,1},{1,0},{2,3},{3,2},{4,5},{5,4},{6,7},{7,6},{8,9},{9,8},{10,11... | collective-permute-start | bytes 1572872 | tf_op jit(solution)/shard_map/ppermute | solution.py:26
  74.4 14.9 %collective-permute-start.8 = (bf16[256,1152]{1,0:T(8,128)(2,1)}, bf16[256,1152]{1,0:T(8,128)(2,1)}, u32[]{:S(2)}, u32[]{:S(2)}) collective-permute-start(bf16[256,1152]{1,0:T(8,128)(2,1)} %get-tuple-element.80.refs_8_), channel_id=1, source_target_pairs={{0,32},{32,0},{1,33},{33,1},{2,34},{34,2},{3,35},{35,3},{4,36},{36... | collective-permute-start | bytes 1769480 | tf_op jit(solution)/shard_map/ppermute | solution.py:30
  74.7 12.1 %all-to-all-start.2 = ((bf16[16,8,1024]{2,1,0:T(8,128)(2,1)}), bf16[16,8,1024]{2,1,0:T(8,128)(2,1)S(1)}, u32[]{:S(2)}, u32[]{:S(2)}) async-start(bf16[16,8,1024]{2,1,0:T(8,128)(2,1)} %bitcast.9), calls=%async_computation.2 | async-start | bytes 524288 | tf_op jit(solution)/shard_map/all_to_all | solution.py:50
  79.6 32.1 %collective-permute-start.18 = (bf16[256,1152]{1,0:T(8,128)(2,1)}, bf16[256,1152]{1,0:T(8,128)(2,1)}, u32[]{:S(2)}, u32[]{:S(2)}) collective-permute-start(bf16[256,1152]{1,0:T(8,128)(2,1)} %get-tuple-element.80.refs_8_), channel_id=1, source_target_pairs={{0,1},{1,0},{2,3},{3,2},{4,5},{5,4},{6,7},{7,6},{8,9},{9,8},{10,11... | collective-permute-start | bytes 1769480 | tf_op jit(solution)/shard_map/ppermute | solution.py:26
  89.2 22.6 %collective-permute-start.17 = (bf16[256,1152]{1,0:T(8,128)(2,1)}, bf16[256,1152]{1,0:T(8,128)(2,1)}, u32[]{:S(2)}, u32[]{:S(2)}) collective-permute-start(bf16[256,1152]{1,0:T(8,128)(2,1)} %collective-permute-done.8.refs_6_), channel_id=1, source_target_pairs={{0,1},{1,0},{2,3},{3,2},{4,5},{5,4},{6,7},{7,6},{8,9},{9,8},{10,11... | collective-permute-start | bytes 1769480 | tf_op jit(solution)/shard_map/ppermute | solution.py:26
  92.2 12.0 %all-to-all-start.3 = ((bf16[16,8,1280]{2,1,0:T(8,128)(2,1)}), bf16[16,8,1280]{2,1,0:T(8,128)(2,1)S(1)}, u32[]{:S(2)}, u32[]{:S(2)}) async-start(bf16[16,8,1280]{2,1,0:T(8,128)(2,1)} %bitcast.11), calls=%async_computation.3 | async-start | bytes 655360 | tf_op jit(solution)/shard_map/all_to_all | solution.py:507
  105.4 6.4 %collective-permute-start.16 = (f32[8,1024]{1,0:T(8,128)S(1)}, f32[8,1024]{1,0:T(8,128)S(1)}, u32[]{:S(2)}, u32[]{:S(2)}) collective-permute-start(f32[8,1024]{1,0:T(8,128)S(1)} %get-tuple-element.89.refs_3_), channel_id=1, source_target_pairs={{0,1},{1,0},{2,3},{3,2},{4,5},{5,4},{6,7},{7,6},{8,9},{9,8},{10,11... | collective-permute-start | bytes 98312 | tf_op jit(solution)/shard_map/ppermute | solution.py:26
  107.2 4.6 %collective-permute-start.15 = (f32[8,1024]{1,0:T(8,128)S(1)}, f32[8,1024]{1,0:T(8,128)S(1)}, u32[]{:S(2)}, u32[]{:S(2)}) collective-permute-start(f32[8,1024]{1,0:T(8,128)S(1)} %get-tuple-element.89.refs_3_), channel_id=1, source_target_pairs={{0,32},{32,0},{1,33},{33,1},{2,34},{34,2},{3,35},{35,3},{4,36},{36... | collective-permute-start | bytes 98312 | tf_op jit(solution)/shard_map/ppermute | solution.py:30
  111.7 15.0 %collective-permute-start.9 = (bf16[256,1024]{1,0:T(8,128)(2,1)}, bf16[256,1024]{1,0:T(8,128)(2,1)}, u32[]{:S(2)}, u32[]{:S(2)}) collective-permute-start(bf16[256,1024]{1,0:T(8,128)(2,1)} %get-tuple-element.88), channel_id=1, source_target_pairs={{0,1},{1,0},{2,3},{3,2},{4,5},{5,4},{6,7},{7,6},{8,9},{9,8},{10,11... | collective-permute-start | bytes 1572872 | tf_op jit(solution)/shard_map/ppermute | solution.py:26
  122.9 32.9 %all-to-all-start.4 = ((bf16[16,64,1024]{2,1,0:T(8,128)(2,1)}), bf16[16,64,1024]{2,1,0:T(8,128)(2,1)S(1)}, u32[]{:S(2)}, u32[]{:S(2)}) async-start(bf16[16,64,1024]{2,1,0:T(8,128)(2,1)} %shard_map.162), calls=%async_computation.4 | async-start | bytes 4194304 | tf_op jit(solution)/shard_map/all_to_all | solution.py:532
  127.9 7.6 %collective-permute-start.10 = (bf16[128,1024]{1,0:T(8,128)(2,1)S(1)}, bf16[128,1024]{1,0:T(8,128)(2,1)S(1)}, u32[]{:S(2)}, u32[]{:S(2)}) collective-permute-start(bf16[128,1024]{1,0:T(8,128)(2,1)S(1)} %get-tuple-element.107), channel_id=1, source_target_pairs={{0,32},{32,0},{1,33},{33,1},{2,34},{34,2},{3,35},{35,3},{4,36},{36... | collective-permute-start | bytes 786440 | tf_op jit(solution)/shard_map/ppermute | solution.py:30
  128.3 8.4 %collective-permute-start.12 = (bf16[128,1024]{1,0:T(8,128)(2,1)S(1)}, bf16[128,1024]{1,0:T(8,128)(2,1)S(1)}, u32[]{:S(2)}, u32[]{:S(2)}) collective-permute-start(bf16[128,1024]{1,0:T(8,128)(2,1)S(1)} %get-tuple-element.108), channel_id=1, source_target_pairs={{0,96},{96,0},{32,64},{64,32},{1,97},{97,1},{33,65},{65,33},{2,98}... | collective-permute-start | bytes 786440 | tf_op jit(solution)/shard_map/ppermute | solution.py:42
  136.9 7.6 %collective-permute-start.11 = (bf16[128,1024]{1,0:T(8,128)(2,1)S(1)}, bf16[128,1024]{1,0:T(8,128)(2,1)S(1)}, u32[]{:S(2)}, u32[]{:S(2)}) collective-permute-start(bf16[128,1024]{1,0:T(8,128)(2,1)S(1)} %get-tuple-element.105), channel_id=1, source_target_pairs={{0,96},{96,0},{32,64},{64,32},{1,97},{97,1},{33,65},{65,33},{2,98}... | collective-permute-start | bytes 786440 | tf_op jit(solution)/shard_map/ppermute | solution.py:42
  139.6 19.4 %collective-permute-start.13 = (bf16[128,1024]{1,0:T(8,128)(2,1)S(1)}, bf16[128,1024]{1,0:T(8,128)(2,1)}, u32[]{:S(2)}, u32[]{:S(2)}) collective-permute-start(bf16[128,1024]{1,0:T(8,128)(2,1)S(1)} %get-tuple-element.106), channel_id=1, source_target_pairs={{0,32},{32,0},{1,33},{33,1},{2,34},{34,2},{3,35},{35,3},{4,36},{36... | collective-permute-start | bytes 786440 | tf_op jit(solution)/shard_map/ppermute | solution.py:30
  160.1 6.5 %collective-permute-start.22 = (bf16[64,1024]{1,0:T(8,128)(2,1)S(1)}, bf16[64,1024]{1,0:T(8,128)(2,1)S(1)}, u32[]{:S(2)}, u32[]{:S(2)}) collective-permute-start(bf16[64,1024]{1,0:T(8,128)(2,1)S(1)} %maximum_maximum_fusion.own), channel_id=1, source_target_pairs={{0,64},{64,0},{1,65},{65,1},{2,66},{66,2},{3,67},{67,3},{4,68},{68... | collective-permute-start | bytes 393224 | tf_op jit(solution)/shard_map/ppermute | solution.py:38
  162.8 6.8 %collective-permute-start.21 = (bf16[64,1024]{1,0:T(8,128)(2,1)S(1)}, bf16[64,1024]{1,0:T(8,128)(2,1)S(1)}, u32[]{:S(2)}, u32[]{:S(2)}) collective-permute-start(bf16[64,1024]{1,0:T(8,128)(2,1)S(1)} %maximum_maximum_fusion.own), channel_id=1, source_target_pairs={{0,96},{96,0},{32,64},{64,32},{1,97},{97,1},{33,65},{65,33},{2,98}... | collective-permute-start | bytes 393224 | tf_op jit(solution)/shard_map/ppermute | solution.py:42
  162.9 6.7 %collective-permute-start.20 = (bf16[64,1024]{1,0:T(8,128)(2,1)S(1)}, bf16[64,1024]{1,0:T(8,128)(2,1)S(1)}, u32[]{:S(2)}, u32[]{:S(2)}) collective-permute-start(bf16[64,1024]{1,0:T(8,128)(2,1)S(1)} %maximum_maximum_fusion.own), channel_id=1, source_target_pairs={{0,32},{32,0},{1,33},{33,1},{2,34},{34,2},{3,35},{35,3},{4,36},{36... | collective-permute-start | bytes 393224 | tf_op jit(solution)/shard_map/ppermute | solution.py:30
  (28 other events, 211.9 us)

commit v8 on v4

--- a/solution.py
+++ b/solution.py
@@ -69,8 +69,13 @@
     return lax.broadcasted_iota(jnp.int32, dims, axis)
 
 
-def pick_kernel(meta, w_in, mine, theirs):
-    core, role = meta[0], meta[1]
+def place_of():
+    core, high, low = (lax.axis_index(axis) for axis in ("c", "h", "l"))
+    return core, high + low - 2 * high * low
+
+
+def pick_kernel(w_in, mine, theirs):
+    core, role = place_of()
     part = jnp.where(iota((512, 256), 1) < 128, core * 2 + role, 2 - core * 2 + role)
     at = iota((512, 256), 1) % 128
     spread = (iota((512, 256), 0) == at // 32 * 128 + part * 32 + at % 32).astype(BF16)
@@ -80,8 +85,8 @@
         theirs[:, i * 128 : i * 128 + 128] = got[:, 128:]
 
 
-def lay_kernel(meta, mine, theirs, w_out, out, block, sems):
-    core, role = meta[0], meta[1]
+def lay_kernel(mine, theirs, w_out, out, block, sems):
+    core, role = place_of()
     block[:32] = jnp.where(role == 0, w_out[:32], w_out[32:])
     block[32:, :512] = jnp.where(core == 0, mine[...], theirs[...])
     block[32:, 512:] = jnp.where(core == 0, theirs[...], mine[...])
@@ -227,15 +232,34 @@
         out[...] = part.astype(out.dtype)
 
 
+def turn_kernel(*refs):
+    at = 0
+    for part in refs[:-1]:
+        refs[-1][:, at : at + part.shape[0]] = part[...].T
+        at += part.shape[0]
+
+
+def turn(*parts):
+    dims = (parts[0].shape[1], sum(part.shape[0] for part in parts))
+    return pl.pallas_call(
+        turn_kernel,
+        out_shape=shape(dims, BF16),
+        in_specs=[WHOLE] * len(parts),
+        out_specs=WHOLE,
+        compiler_params=LIMIT,
+        cost_estimate=cost(2**20, 2**22),
+    )(*parts)
+
+
 def backward_kernel(*refs):
     grads, gain = refs[:4], refs[4]
-    rows, toks = refs[5:9], refs[9:13]
-    hiddens, slopes, weights, out = refs[13:15], refs[15:17], refs[17], refs[18]
-    row_buf, tok_buf, hid_buf, slope_buf, w_out, sum_grad, act_grad, result, sems = refs[19:]
+    rows, toks, hiddens = refs[5:9], refs[9], refs[10]
+    slopes, weights, out = refs[11:13], refs[13], refs[14]
+    row_buf, tok_buf, hid_buf, slope_buf, w_out, sum_grad, act_grad, result, sems = refs[15:]
     sent = []
     first = pltpu.make_async_copy(weights.at[:, 0:32], w_out, sems.at[0])
     first.start()
-    row_copies, tok_copies, hid_copies, slope_copies = [], [], [], []
+    row_copies, slope_copies = [], []
     for k in range(4):
         at = pl.ds(k * 256, 256)
         row_copies.append(pltpu.make_async_copy(rows[k], row_buf.at[at], sems.at[1 + k]))
@@ -244,14 +268,10 @@
         at = pl.ds(k * 512, 512)
         slope_copies.append(pltpu.make_async_copy(slopes[k], slope_buf.at[at], sems.at[5 + k]))
         slope_copies[k].start()
-    for k in range(2):
-        at = pl.ds(k * 512, 512)
-        hid_copies.append(pltpu.make_async_copy(hiddens[k], hid_buf.at[at], sems.at[7 + k]))
-        hid_copies[k].start()
-    for k in range(4):
-        at = pl.ds(k * 256, 256)
-        tok_copies.append(pltpu.make_async_copy(toks[k], tok_buf.at[at], sems.at[9 + k]))
-        tok_copies[k].start()
+    hid_copy = pltpu.make_async_copy(hiddens, hid_buf, sems.at[7])
+    hid_copy.start()
+    tok_copy = pltpu.make_async_copy(toks, tok_buf, sems.at[8])
+    tok_copy.start()
     for k in range(4):
         row_copies[k].wait()
         scaled_grad = grads[k][...] * gain[...]
@@ -278,26 +298,24 @@
             sum_grad[at], w_out[...].reshape(512, 1024), LAST, preferred_element_type=F32
         )
         act_grad[at] = (back * slope_buf[at]).astype(BF16)
-    for copy in hid_copies:
-        copy.wait()
+    hid_copy.wait()
+    for i in range(2):
+        part = jnp.dot(
+            hid_buf[i * 256 : i * 256 + 256], sum_grad[...], preferred_element_type=F32
+        )
+        at = pl.ds(i * 8, 8)
+        result[at, :32] = part.astype(BF16).reshape(8, 32, 1024)
+        sent.append(pltpu.make_async_copy(result.at[at, 0:32], out.at[at, 0:32], sems.at[9 + i]))
+        sent[-1].start()
+    tok_copy.wait()
     for i in range(4):
-        part = lax.dot_general(
-            hid_buf[:, i * 128 : i * 128 + 128], sum_grad[...], FIRST, preferred_element_type=F32
-        )
-        at = pl.ds(i * 4, 4)
-        result[at, :32] = part.astype(BF16).reshape(4, 32, 1024)
-        sent.append(pltpu.make_async_copy(result.at[at, 0:32], out.at[at, 0:32], sems.at[13 + i]))
-        sent[-1].start()
-    for copy in tok_copies:
-        copy.wait()
-    for i in range(4):
-        part = lax.dot_general(
-            tok_buf[:, i * 256 : i * 256 + 256], act_grad[...], FIRST, preferred_element_type=F32
+        part = jnp.dot(
+            tok_buf[i * 256 : i * 256 + 256], act_grad[...], preferred_element_type=F32
         ).astype(BF16).reshape(4, 2, 32, 512)
         at = pl.ds(i * 4, 4)
         result[at, 32:, :512] = part[:, 0]
         result[at, 32:, 512:] = part[:, 1]
-        sent.append(pltpu.make_async_copy(result.at[at, 32:64], out.at[at, 32:64], sems.at[17 + i]))
+        sent.append(pltpu.make_async_copy(result.at[at, 32:64], out.at[at, 32:64], sems.at[11 + i]))
         sent[-1].start()
     for copy in sent:
         copy.wait()
@@ -307,22 +325,22 @@
     return pl.pallas_call(
         backward_kernel,
         out_shape=shape((16, 64, 1024), BF16),
-        in_specs=[WHOLE] * 5 + [ANYWHERE] * 13,
+        in_specs=[WHOLE] * 5 + [ANYWHERE] * 9,
         out_specs=ANYWHERE,
         scratch_shapes=[
             pltpu.VMEM((1024, 1152), BF16),
             pltpu.VMEM((1024, 1024), BF16),
-            pltpu.VMEM((1024, 512), BF16),
+            pltpu.VMEM((512, 1024), BF16),
             pltpu.VMEM((1024, 512), F32),
             pltpu.VMEM((16, 32, 1024), BF16),
             pltpu.VMEM((1024, 1024), BF16),
             pltpu.VMEM((1024, 512), BF16),
             pltpu.VMEM((16, 64, 1024), BF16),
-            pltpu.SemaphoreType.DMA((21,)),
+            pltpu.SemaphoreType.DMA((15,)),
         ],
         compiler_params=MOST,
         cost_estimate=cost(3 * 2**30, 10 * 2**20),
-    )(*grads, gain, *rows, *toks, *hiddens, *slopes, weights)
+    )(*grads, gain, *rows, toks, hiddens, *slopes, weights)
 
 
 def total_kernel(meta, got, out, keep, give):
@@ -394,18 +412,20 @@
     mine, theirs = pl.pallas_call(
         pick_kernel,
         out_shape=(shape((32, 512), BF16),) * 2,
-        in_specs=[SCALARS, WHOLE],
+        in_specs=[WHOLE],
         out_specs=(WHOLE, WHOLE),
+        compiler_params=LIMIT,
         cost_estimate=cost(2**25, 2**18),
-    )(meta, w_in)
+    )(w_in)
     block = pl.pallas_call(
         lay_kernel,
         out_shape=shape((16, 64, width), BF16),
-        in_specs=[SCALARS, WHOLE, WHOLE, WHOLE],
+        in_specs=[WHOLE, WHOLE, WHOLE],
         out_specs=ANYWHERE,
         scratch_shapes=[pltpu.VMEM((64, width), BF16), pltpu.SemaphoreType.DMA((16,))],
+        compiler_params=LIMIT,
         cost_estimate=cost(0, 2**21),
-    )(meta, mine, swap_core(theirs), w_out)
+    )(mine, swap_core(theirs), w_out)
     block, own_tok, label_tiles, shortlist, positives, owner_map = lax.optimization_barrier(
         (block, own_tok, label_tiles, shortlist, positives, owner_map)
     )
@@ -439,16 +459,21 @@
         hit, tiles_lo, preferred_element_type=F32
     )
     pos_part = (pos_part * POS_SCALE).astype(jnp.float16)
-    weights, cluster_live, share_hit, pos_part, tiles_hi, tiles_lo = lax.optimization_barrier(
-        (weights, cluster_live, share_hit, pos_part, tiles_hi, tiles_lo)
+    turned_tok = turn(diag_tok, near_tok, core_tok, own_tok)
+    weights, cluster_live, share_hit, pos_part, tiles_hi, tiles_lo, turned_tok = (
+        lax.optimization_barrier(
+            (weights, cluster_live, share_hit, pos_part, tiles_hi, tiles_lo, turned_tok)
+        )
     )
 
     near_a, near_b, near_hidden, near_slope = forward(diag_tok, near_tok, weights, 2**30)
-    near_sum = (near_b + swap_core(near_a).astype(F32)).astype(BF16)
+    near_a, core_tok = lax.optimization_barrier((near_a, core_tok))
+    own_a, own_b, own_hidden, own_slope = forward(core_tok, own_tok, weights, 2**30)
+    near_a, own_a, own_b = lax.optimization_barrier((swap_core(near_a), own_a, own_b))
+    near_sum = (near_b + near_a.astype(F32)).astype(BF16)
     near_sum, pos_part = lax.optimization_barrier((near_sum, pos_part))
     from_near = swap_near(near_sum)
     pos_got = gather_chips(pos_part.reshape(16, docs, width))
-    own_a, own_b, own_hidden, own_slope = forward(core_tok, own_tok, weights, 2**36)
     from_near, pos_got = lax.optimization_barrier((from_near, pos_got))
     pos_mean = jnp.sum(pos_got.astype(F32), axis=0) * (1.0 / POS_SCALE)
     own_rows, emb = pl.pallas_call(
@@ -462,6 +487,8 @@
     )(lengths, own_tok, own_b, swap_core(own_a), from_near, gain)
 
     plane_emb = gather_chips(emb.reshape(16, docs, width)).reshape(128, width)
+    turned_hidden = turn(near_hidden, own_hidden)
+    plane_emb, turned_hidden = lax.optimization_barrier((plane_emb, turned_hidden))
     near_rows = swap_near(own_rows)
     packed, weighted = pl.pallas_call(
         score_kernel,
@@ -498,8 +525,8 @@
         grads,
         gain,
         (diag_rows, near_rows, core_rows, own_rows),
-        (diag_tok, near_tok, core_tok, own_tok),
-        (near_hidden, own_hidden),
+        turned_tok,
+        turned_hidden,
         (near_slope, own_slope),
         weights,
     )

time: 173 us -> 171 us (0.988)
  local copies, waits for them, and re-layouts: 5.37 us -> 16.6 us
  waiting for transfers between devices: 54.8 us -> 45.7 us
  Pallas kernels: 31.7 us -> 28.6 us
    all_to_all x2, waiting for transfers between devices: 19.6 us -> 11.2 us  [gather_chips(): return lax.all_to_all(a, CHIPS, 0, 0, tiled=True)]
    unnamed x59 -> x71, local copies, waits for them, and re-layouts: 2.58 us -> 10.3 us
    optimization_barrier x1, local copies, waits for them, and re-layouts: 0.2 us -> 2 us  [on_device(): lax.optimization_barrier((block, own_tok, label_tiles, shortlist, positiv...]
  transfers between devices with their start and end apart: 27 -> 27, of which waited for: 13 -> 10; matrix products, arithmetic and copies ran while one was open for 13% -> 15% of each run, Pallas kernels for 11% -> 11%
where the time goes in v8:
time: 171 us; the launch traced here: 170 us
  starting transfers between devices  46.3 us (27%)
  waiting for transfers between devices  45.7 us (27%)
  Pallas kernels  28.6 us (17%)
  other arithmetic  17.7 us (10%)
  local copies, waits for them, and re-layouts  16.6 us (10%)
  blocking collectives  12.6 us (7%)
    all_to_all x1, blocking collectives, gather_chips(): return lax.all_to_all(a, CHIPS, 0, 0, tiled=True)  12.6 us
    all_to_all x2, starting transfers between devices, gather_chips(): return lax.all_to_all(a, CHIPS, 0, 0, tiled=True)  12.5 us
    ppermute x10, starting transfers between devices, swap_core(): return lax.ppermute(a, 'c', [(0, 1), (1, 0)])  12.4 us
    all_to_all x2, waiting for transfers between devices, gather_chips(): return lax.all_to_all(a, CHIPS, 0, 0, tiled=True)  11.2 us
    all_to_all x1, waiting for transfers between devices, on_device(): got = lax.all_to_all(send, CHIPS, 0, 0, tiled=True)  10.6 us
    unnamed x71, local copies, waits for them, and re-layouts  10.3 us
    reduce_max x1, other arithmetic, on_device(): jnp.max((short[:, :, None] == cluster_ids[None, None, :]).astype(F32), ax...  9.87 us
    pallas_call x1, Pallas kernels, backward(): pl.pallas_call(backward_kernel, out_shape=shape((16, 64, 1024), BF16), in...  8.82 us
  transfers between devices with their start and end apart: 27, of which 10 were waited for; matrix products, arithmetic and copies ran while one was open for 15% of the time, Pallas kernels for 11%

profile of v8, /device:TPU:1, one launch (start us, length us, event | category | flops | bytes accessed | tf_op | source)
XLA Modules:
  0.0 170.1 jit_solution(4389856202608480197)
XLA Ops:
  8.9 7.7 %all-to-all-start = ((bf16[16,64,1024]{2,1,0:T(8,128)(2,1)}), bf16[16,64,1024]{2,1,0:T(8,128)(2,1)}, u32[]{:S(2)}, u32[]{:S(2)}) async-start(bf16[16,64,1024]{2,1,0:T(8,128)(2,1)} %shard_map.155), calls=%async_computation | async-start | bytes 4194304 | tf_op jit(solution)/shard_map/all_to_all | solution.py:50
  23.2 9.9 %convert_reduce_fusion.live = bf16[128,128]{1,0:T(8,128)(2,1)S(1)} fusion(s32[128]{0:T(128)S(1)} %select_reduce_fusion, s32[128,400]{1,0:T(8,128)S(1)} %dynamic-slice_bitcast_fusion), kind=kLoop, calls=%fused_computation | loop fusion | flops 19644416 | bytes 238080 | tf_op jit(solution)/shard_map/reduce_max | solution.py:445
  38.2 7.6 %all-to-all-done.weights.refs_13_ = bf16[16,64,1024]{2,1,0:T(8,128)(2,1)} async-done(((bf16[16,64,1024]{2,1,0:T(8,128)(2,1)}), bf16[16,64,1024]{2,1,0:T(8,128)(2,1)}, u32[]{:S(2)}, u32[]{:S(2)}) %all-to-all-start) | async-done | bytes 2097184 | tf_op jit(solution)/shard_map/all_to_all | solution.py:50
  47.9 3.1 %shard_map.157 = (bf16[256,1024]{1,0:T(8,128)(2,1)S(1)}, f32[256,1024]{1,0:T(8,128)S(1)}, bf16[512,512]{1,0:T(8,128)(2,1)S(1)}, f32[512,512]{1,0:T(8,128)S(1)}) custom-call(bf16[256,1024]{1,0:T(8,128)(2,1)S(1)} %copy-done.12, bf16[256,1024]{1,0:T(8,128)(2,1)S(1)} %copy-done.10, bf16[16,64,1024]{2,1,0:T(8,128)(2,1)} %all-to-all-done.weights.refs_13_), custom_call_target="tpu_custom_call" | custom-call | flops 1073741824 | bytes 6291456 | tf_op jit(solution)/shard_map/pallas_call | solution.py:128
  53.9 3.0 %shard_map.158 = (bf16[256,1024]{1,0:T(8,128)(2,1)S(1)}, f32[256,1024]{1,0:T(8,128)S(1)}, bf16[512,512]{1,0:T(8,128)(2,1)S(1)}, f32[512,512]{1,0:T(8,128)S(1)}) custom-call(bf16[256,1024]{1,0:T(8,128)(2,1)S(1)} %copy-done.8, bf16[256,1024]{1,0:T(8,128)(2,1)S(1)} %bitcast.23, bf16[16,64,1024]{2,1,0:T(8,128)(2,1)} %all-to-all-done.weights.refs_13_), custom_call_target="tpu_custom_call" | custom-call | flops 1073741824 | bytes 6291456 | tf_op jit(solution)/shard_map/pallas_call | solution.py:128
  58.9 12.6 %all_to_all.25 = f16[16,8,1024]{2,1,0:T(8,128)(2,1)} all-to-all(f16[16,8,1024]{2,1,0:T(8,128)(2,1)S(1)} %bitcast.33), channel_id=1, replica_groups=mesh['h'=2,'l'=2,'x'=4,'z'=4,'c'=2] {'x','z'}, dimensions={0} | all-to-all | bytes 524288 | tf_op jit(solution)/shard_map/all_to_all | solution.py:50
  71.5 2.7 %shard_map.159 = (bf16[256,1152]{1,0:T(8,128)(2,1)}, bf16[128,1024]{1,0:T(8,128)(2,1)}) custom-call(s32[8]{0:T(128)S(1)} %copy-done.17, bf16[256,1024]{1,0:T(8,128)(2,1)S(1)} %bitcast.24, f32[256,1024]{1,0:T(8,128)S(1)} %get-tuple-element.70.part, bf16[256,1024]{1,0:T(8,128)(2,1)S(1)} %collective-permute-done.6.from_core, ...), custom_call_target="tpu_custom_call" | custom-call | flops 4194304 | bytes 4194304 | tf_op jit(solution)/shard_map/pallas_call | solution.py:479
  75.0 4.8 %all-to-all-start.2 = ((bf16[16,8,1024]{2,1,0:T(8,128)(2,1)}), bf16[16,8,1024]{2,1,0:T(8,128)(2,1)S(1)}, u32[]{:S(2)}, u32[]{:S(2)}) async-start(bf16[16,8,1024]{2,1,0:T(8,128)(2,1)} %bitcast.9), calls=%async_computation.2 | async-start | bytes 524288 | tf_op jit(solution)/shard_map/all_to_all | solution.py:50
  83.6 3.6 %all-to-all-done.2 = bf16[16,8,1024]{2,1,0:T(8,128)(2,1)S(1)} async-done(((bf16[16,8,1024]{2,1,0:T(8,128)(2,1)}), bf16[16,8,1024]{2,1,0:T(8,128)(2,1)S(1)}, u32[]{:S(2)}, u32[]{:S(2)}) %all-to-all-start.2) | async-done | bytes 262176 | tf_op jit(solution)/shard_map/all_to_all | solution.py:50
  87.2 2.3 %shard_map.161 = (bf16[128,1280]{1,0:T(8,128)(2,1)}, f32[128,512]{1,0:T(8,128)S(1)}) custom-call(bf16[128,1024]{1,0:T(8,128)(2,1)S(1)} %bitcast.25, bf16[512,1024]{1,0:T(8,128)(2,1)S(1)} %get-tuple-element.82.tiles_hi, bf16[512,1024]{1,0:T(8,128)(2,1)S(1)} %get-tuple-element.83.tiles_lo, bf16[128,128]{1,0:T(8,128)(2,1)S(1)} %convert_reduce_fusion.live), custom_call_target="tpu_custom_call" | custom-call | flops 536870912 | bytes 3145728 | tf_op jit(solution)/shard_map/pallas_call | solution.py:493
  89.5 2.6 %collective-permute-start.17 = (bf16[256,1152]{1,0:T(8,128)(2,1)}, bf16[256,1152]{1,0:T(8,128)(2,1)S(1)}, u32[]{:S(2)}, u32[]{:S(2)}) collective-permute-start(bf16[256,1152]{1,0:T(8,128)(2,1)} %collective-permute-done.8.refs_6_), channel_id=1, source_target_pairs={{0,1},{1,0},{2,3},{3,2},{4,5},{5,4},{6,7},{7,6},{8,9},{9,8},{10,11... | collective-permute-start | bytes 1769480 | tf_op jit(solution)/shard_map/ppermute | solution.py:26
  92.2 3.5 %all-to-all-start.3 = ((bf16[16,8,1280]{2,1,0:T(8,128)(2,1)}), bf16[16,8,1280]{2,1,0:T(8,128)(2,1)S(1)}, u32[]{:S(2)}, u32[]{:S(2)}) async-start(bf16[16,8,1280]{2,1,0:T(8,128)(2,1)} %bitcast.11), calls=%async_computation.3 | async-start | bytes 655360 | tf_op jit(solution)/shard_map/all_to_all | solution.py:508
  95.8 8.4 %all-to-all-done.3.got_hbm = bf16[16,8,1280]{2,1,0:T(8,128)(2,1)S(1)} async-done(((bf16[16,8,1280]{2,1,0:T(8,128)(2,1)}), bf16[16,8,1280]{2,1,0:T(8,128)(2,1)S(1)}, u32[]{:S(2)}, u32[]{:S(2)}) %all-to-all-start.3) | async-done | bytes 327712 | tf_op jit(solution)/shard_map/all_to_all | solution.py:508
  112.6 8.8 %shard_map.164 = bf16[16,64,1024]{2,1,0:T(8,128)(2,1)} custom-call(f32[8,1024]{1,0:T(8,128)} %copy-done.32, f32[8,1024]{1,0:T(8,128)} %copy-done.31, f32[8,1024]{1,0:T(8,128)} %copy-done.30, f32[8,1024]{1,0:T(8,128)} %copy-done.15, f32[1,1024]{1,0:T(1,128)} %bitcast.27, bf16[256,1152]{1,0:T(8,128)(2,1)} %copy-done.29, ...), custom_call_target="tpu_custom_call" | custom-call | flops 3221225472 | bytes 10485760 | tf_op jit(solution)/shard_map/pallas_call | solution.py:325
  121.4 3.7 %all-to-all-start.4 = ((bf16[16,64,1024]{2,1,0:T(8,128)(2,1)}), bf16[16,64,1024]{2,1,0:T(8,128)(2,1)S(1)}, u32[]{:S(2)}, u32[]{:S(2)}) async-start(bf16[16,64,1024]{2,1,0:T(8,128)(2,1)} %shard_map.164), calls=%async_computation.4 | async-start | bytes 4194304 | tf_op jit(solution)/shard_map/all_to_all | solution.py:533
  126.8 2.7 %collective-permute-start.12 = (bf16[128,1024]{1,0:T(8,128)(2,1)S(1)}, bf16[128,1024]{1,0:T(8,128)(2,1)S(1)}, u32[]{:S(2)}, u32[]{:S(2)}) collective-permute-start(bf16[128,1024]{1,0:T(8,128)(2,1)S(1)} %get-tuple-element.114), channel_id=1, source_target_pairs={{0,96},{96,0},{32,64},{64,32},{1,97},{97,1},{33,65},{65,33},{2,98}... | collective-permute-start | bytes 786440 | tf_op jit(solution)/shard_map/ppermute | solution.py:42
  129.4 4.6 %collective-permute-done.10 = bf16[128,1024]{1,0:T(8,128)(2,1)S(1)} collective-permute-done((bf16[128,1024]{1,0:T(8,128)(2,1)S(1)}, bf16[128,1024]{1,0:T(8,128)(2,1)S(1)}, u32[]{:S(2)}, u32[]{:S(2)}) %collective-permute-start.10) | collective-permute-done | bytes 262176 | tf_op jit(solution)/shard_map/ppermute | solution.py:30
  135.3 2.7 %collective-permute-start.11 = (bf16[128,1024]{1,0:T(8,128)(2,1)S(1)}, bf16[128,1024]{1,0:T(8,128)(2,1)S(1)}, u32[]{:S(2)}, u32[]{:S(2)}) collective-permute-start(bf16[128,1024]{1,0:T(8,128)(2,1)S(1)} %get-tuple-element.111), channel_id=1, source_target_pairs={{0,96},{96,0},{32,64},{64,32},{1,97},{97,1},{33,65},{65,33},{2,98}... | collective-permute-start | bytes 786440 | tf_op jit(solution)/shard_map/ppermute | solution.py:42
  138.7 4.2 %collective-permute-done.11 = bf16[128,1024]{1,0:T(8,128)(2,1)S(1)} collective-permute-done((bf16[128,1024]{1,0:T(8,128)(2,1)S(1)}, bf16[128,1024]{1,0:T(8,128)(2,1)S(1)}, u32[]{:S(2)}, u32[]{:S(2)}) %collective-permute-start.11) | collective-permute-done | bytes 262176 | tf_op jit(solution)/shard_map/ppermute | solution.py:42
  143.8 10.6 %all-to-all-done.4.got = bf16[16,64,1024]{2,1,0:T(8,128)(2,1)S(1)} async-done(((bf16[16,64,1024]{2,1,0:T(8,128)(2,1)}), bf16[16,64,1024]{2,1,0:T(8,128)(2,1)S(1)}, u32[]{:S(2)}, u32[]{:S(2)}) %all-to-all-start.4) | async-done | bytes 2097184 | tf_op jit(solution)/shard_map/all_to_all | solution.py:533
  155.4 2.1 %collective-permute-start.19 = (bf16[32,512]{1,0:T(8,128)(2,1)S(1)}, bf16[32,512]{1,0:T(8,128)(2,1)S(1)}, u32[]{:S(2)}, u32[]{:S(2)}) collective-permute-start(bf16[32,512]{1,0:T(8,128)(2,1)S(1)} %get-tuple-element.103), channel_id=1, source_target_pairs={{0,1},{1,0},{2,3},{3,2},{4,5},{5,4},{6,7},{7,6},{8,9},{9,8},{10,11... | collective-permute-start | bytes 98312 | tf_op jit(solution)/shard_map/ppermute | solution.py:26
  158.6 2.7 %collective-permute-start.22 = (bf16[64,1024]{1,0:T(8,128)(2,1)S(1)}, bf16[64,1024]{1,0:T(8,128)(2,1)S(1)}, u32[]{:S(2)}, u32[]{:S(2)}) collective-permute-start(bf16[64,1024]{1,0:T(8,128)(2,1)S(1)} %maximum_maximum_fusion.own), channel_id=1, source_target_pairs={{0,64},{64,0},{1,65},{65,1},{2,66},{66,2},{3,67},{67,3},{4,68},{68... | collective-permute-start | bytes 393224 | tf_op jit(solution)/shard_map/ppermute | solution.py:38
  161.4 2.1 %divide_subtract_fusion = (f32[256,1024]{1,0:T(8,128)}, f32[256,1024]{1,0:T(8,128)}, f32[256,1024]{1,0:T(8,128)}) fusion(f32[256,1024]{1,0:T(8,128)S(1)} %copy-done.21, f32[128,1024]{1,0:T(8,128)S(1)} %convert_add_fusion, f32[128,1024]{1,0:T(8,128)S(1)} %copy-done.22, f32[256,1024]{1,0:T(8,128)S(1)} %copy-done.24, f32[256,1024]{1,0:T(8,128)S(1)} %copy-done.25), kind=kLoop, calls=%fused_computation.10 | loop fusion | flops 3407872 | bytes 7340032 | tf_op jit(solution)/shard_map/sub | solution.py:579
  165.3 2.9 %collective-permute-done.21.wrap = bf16[64,1024]{1,0:T(8,128)(2,1)S(1)} collective-permute-done((bf16[64,1024]{1,0:T(8,128)(2,1)S(1)}, bf16[64,1024]{1,0:T(8,128)(2,1)S(1)}, u32[]{:S(2)}, u32[]{:S(2)}) %collective-permute-start.21) | collective-permute-done | bytes 131104 | tf_op jit(solution)/shard_map/ppermute | solution.py:42
  (147 shorter events, 49.6 us)
Async XLA Ops:
  6.7 26.4 %collective-permute-start.4 = (bf16[256,1024]{1,0:T(8,128)(2,1)S(1)}, bf16[256,1024]{1,0:T(8,128)(2,1)S(1)}, u32[]{:S(2)}, u32[]{:S(2)}) collective-permute-start(bf16[256,1024]{1,0:T(8,128)(2,1)S(1)} %bitcast.19), channel_id=1, source_target_pairs={{0,1},{1,0},{2,3},{3,2},{4,5},{5,4},{6,7},{7,6},{8,9},{9,8},{10,11... | collective-permute-start | bytes 1572872 | tf_op jit(solution)/shard_map/ppermute | solution.py:26
  7.1 26.0 %collective-permute-start.2 = (bf16[256,1024]{1,0:T(8,128)(2,1)S(1)}, bf16[256,1024]{1,0:T(8,128)(2,1)S(1)}, u32[]{:S(2)}, u32[]{:S(2)}) collective-permute-start(bf16[256,1024]{1,0:T(8,128)(2,1)S(1)} %bitcast.20), channel_id=1, source_target_pairs={{0,32},{32,0},{1,33},{33,1},{2,34},{34,2},{3,35},{35,3},{4,36},{36... | collective-permute-start | bytes 1572872 | tf_op jit(solution)/shard_map/ppermute | solution.py:30
  8.5 24.6 %collective-permute-start.1 = (bf16[256,1024]{1,0:T(8,128)(2,1)S(1)}, bf16[256,1024]{1,0:T(8,128)(2,1)S(1)}, u32[]{:S(2)}, u32[]{:S(2)}) collective-permute-start(bf16[256,1024]{1,0:T(8,128)(2,1)S(1)} %bitcast.21), channel_id=1, source_target_pairs={{0,33},{33,0},{1,32},{32,1},{2,35},{35,2},{3,34},{34,3},{4,37},{37... | collective-permute-start | bytes 1572872 | tf_op jit(solution)/shard_map/ppermute | solution.py:34
  8.9 36.9 %all-to-all-start = ((bf16[16,64,1024]{2,1,0:T(8,128)(2,1)}), bf16[16,64,1024]{2,1,0:T(8,128)(2,1)}, u32[]{:S(2)}, u32[]{:S(2)}) async-start(bf16[16,64,1024]{2,1,0:T(8,128)(2,1)} %shard_map.155), calls=%async_computation | async-start | bytes 4194304 | tf_op jit(solution)/shard_map/all_to_all | solution.py:50
  17.1 17.2 %collective-permute-start.3 = (f32[256,1024]{1,0:T(8,128)S(1)}, f32[256,1024]{1,0:T(8,128)}, u32[]{:S(2)}, u32[]{:S(2)}) collective-permute-start(f32[256,1024]{1,0:T(8,128)S(1)} %copy-done.20), channel_id=1, source_target_pairs={{0,1},{1,0},{2,3},{3,2},{4,5},{5,4},{6,7},{7,6},{8,9},{9,8},{10,11... | collective-permute-start | bytes 3145736 | tf_op jit(solution)/shard_map/ppermute | solution.py:26
  52.0 5.0 %collective-permute-start.5 = (bf16[256,1024]{1,0:T(8,128)(2,1)S(1)}, bf16[256,1024]{1,0:T(8,128)(2,1)S(1)}, u32[]{:S(2)}, u32[]{:S(2)}) collective-permute-start(bf16[256,1024]{1,0:T(8,128)(2,1)S(1)} %get-tuple-element.66), channel_id=1, source_target_pairs={{0,1},{1,0},{2,3},{3,2},{4,5},{5,4},{6,7},{7,6},{8,9},{9,8},{10,11... | collective-permute-start | bytes 1572872 | tf_op jit(solution)/shard_map/ppermute | solution.py:26
  57.2 14.3 %collective-permute-start.7 = (bf16[256,1024]{1,0:T(8,128)(2,1)S(1)}, bf16[256,1024]{1,0:T(8,128)(2,1)S(1)}, u32[]{:S(2)}, u32[]{:S(2)}) collective-permute-start(bf16[256,1024]{1,0:T(8,128)(2,1)S(1)} %add_convert_fusion.1), channel_id=1, source_target_pairs={{0,32},{32,0},{1,33},{33,1},{2,34},{34,2},{3,35},{35,3},{4,36},{36... | collective-permute-start | bytes 1572872 | tf_op jit(solution)/shard_map/ppermute | solution.py:30
  58.5 12.9 %collective-permute-start.6 = (bf16[256,1024]{1,0:T(8,128)(2,1)S(1)}, bf16[256,1024]{1,0:T(8,128)(2,1)S(1)}, u32[]{:S(2)}, u32[]{:S(2)}) collective-permute-start(bf16[256,1024]{1,0:T(8,128)(2,1)S(1)} %get-tuple-element.71), channel_id=1, source_target_pairs={{0,1},{1,0},{2,3},{3,2},{4,5},{5,4},{6,7},{7,6},{8,9},{9,8},{10,11... | collective-permute-start | bytes 1572872 | tf_op jit(solution)/shard_map/ppermute | solution.py:26
  74.2 15.3 %collective-permute-start.8 = (bf16[256,1152]{1,0:T(8,128)(2,1)}, bf16[256,1152]{1,0:T(8,128)(2,1)}, u32[]{:S(2)}, u32[]{:S(2)}) collective-permute-start(bf16[256,1152]{1,0:T(8,128)(2,1)} %get-tuple-element.86.refs_8_), channel_id=1, source_target_pairs={{0,32},{32,0},{1,33},{33,1},{2,34},{34,2},{3,35},{35,3},{4,36},{36... | collective-permute-start | bytes 1769480 | tf_op jit(solution)/shard_map/ppermute | solution.py:30
  75.0 12.2 %all-to-all-start.2 = ((bf16[16,8,1024]{2,1,0:T(8,128)(2,1)}), bf16[16,8,1024]{2,1,0:T(8,128)(2,1)S(1)}, u32[]{:S(2)}, u32[]{:S(2)}) async-start(bf16[16,8,1024]{2,1,0:T(8,128)(2,1)} %bitcast.9), calls=%async_computation.2 | async-start | bytes 524288 | tf_op jit(solution)/shard_map/all_to_all | solution.py:50
  82.2 29.4 %collective-permute-start.18 = (bf16[256,1152]{1,0:T(8,128)(2,1)}, bf16[256,1152]{1,0:T(8,128)(2,1)}, u32[]{:S(2)}, u32[]{:S(2)}) collective-permute-start(bf16[256,1152]{1,0:T(8,128)(2,1)} %get-tuple-element.86.refs_8_), channel_id=1, source_target_pairs={{0,1},{1,0},{2,3},{3,2},{4,5},{5,4},{6,7},{7,6},{8,9},{9,8},{10,11... | collective-permute-start | bytes 1769480 | tf_op jit(solution)/shard_map/ppermute | solution.py:26
  89.5 22.2 %collective-permute-start.17 = (bf16[256,1152]{1,0:T(8,128)(2,1)}, bf16[256,1152]{1,0:T(8,128)(2,1)S(1)}, u32[]{:S(2)}, u32[]{:S(2)}) collective-permute-start(bf16[256,1152]{1,0:T(8,128)(2,1)} %collective-permute-done.8.refs_6_), channel_id=1, source_target_pairs={{0,1},{1,0},{2,3},{3,2},{4,5},{5,4},{6,7},{7,6},{8,9},{9,8},{10,11... | collective-permute-start | bytes 1769480 | tf_op jit(solution)/shard_map/ppermute | solution.py:26
  92.2 12.0 %all-to-all-start.3 = ((bf16[16,8,1280]{2,1,0:T(8,128)(2,1)}), bf16[16,8,1280]{2,1,0:T(8,128)(2,1)S(1)}, u32[]{:S(2)}, u32[]{:S(2)}) async-start(bf16[16,8,1280]{2,1,0:T(8,128)(2,1)} %bitcast.11), calls=%async_computation.3 | async-start | bytes 655360 | tf_op jit(solution)/shard_map/all_to_all | solution.py:508
  105.5 6.2 %collective-permute-start.16 = (f32[8,1024]{1,0:T(8,128)S(1)}, f32[8,1024]{1,0:T(8,128)S(1)}, u32[]{:S(2)}, u32[]{:S(2)}) collective-permute-start(f32[8,1024]{1,0:T(8,128)S(1)} %get-tuple-element.95.refs_3_), channel_id=1, source_target_pairs={{0,1},{1,0},{2,3},{3,2},{4,5},{5,4},{6,7},{7,6},{8,9},{9,8},{10,11... | collective-permute-start | bytes 98312 | tf_op jit(solution)/shard_map/ppermute | solution.py:26
  107.1 4.6 %collective-permute-start.15 = (f32[8,1024]{1,0:T(8,128)S(1)}, f32[8,1024]{1,0:T(8,128)S(1)}, u32[]{:S(2)}, u32[]{:S(2)}) collective-permute-start(f32[8,1024]{1,0:T(8,128)S(1)} %get-tuple-element.95.refs_3_), channel_id=1, source_target_pairs={{0,32},{32,0},{1,33},{33,1},{2,34},{34,2},{3,35},{35,3},{4,36},{36... | collective-permute-start | bytes 98312 | tf_op jit(solution)/shard_map/ppermute | solution.py:30
  111.5 13.6 %collective-permute-start.9 = (bf16[256,1024]{1,0:T(8,128)(2,1)}, bf16[256,1024]{1,0:T(8,128)(2,1)}, u32[]{:S(2)}, u32[]{:S(2)}) collective-permute-start(bf16[256,1024]{1,0:T(8,128)(2,1)} %get-tuple-element.94), channel_id=1, source_target_pairs={{0,1},{1,0},{2,3},{3,2},{4,5},{5,4},{6,7},{7,6},{8,9},{9,8},{10,11... | collective-permute-start | bytes 1572872 | tf_op jit(solution)/shard_map/ppermute | solution.py:26
  121.4 33.0 %all-to-all-start.4 = ((bf16[16,64,1024]{2,1,0:T(8,128)(2,1)}), bf16[16,64,1024]{2,1,0:T(8,128)(2,1)S(1)}, u32[]{:S(2)}, u32[]{:S(2)}) async-start(bf16[16,64,1024]{2,1,0:T(8,128)(2,1)} %shard_map.164), calls=%async_computation.4 | async-start | bytes 4194304 | tf_op jit(solution)/shard_map/all_to_all | solution.py:533
  126.4 7.6 %collective-permute-start.10 = (bf16[128,1024]{1,0:T(8,128)(2,1)S(1)}, bf16[128,1024]{1,0:T(8,128)(2,1)S(1)}, u32[]{:S(2)}, u32[]{:S(2)}) collective-permute-start(bf16[128,1024]{1,0:T(8,128)(2,1)S(1)} %get-tuple-element.113), channel_id=1, source_target_pairs={{0,32},{32,0},{1,33},{33,1},{2,34},{34,2},{3,35},{35,3},{4,36},{36... | collective-permute-start | bytes 786440 | tf_op jit(solution)/shard_map/ppermute | solution.py:30
  126.8 8.4 %collective-permute-start.12 = (bf16[128,1024]{1,0:T(8,128)(2,1)S(1)}, bf16[128,1024]{1,0:T(8,128)(2,1)S(1)}, u32[]{:S(2)}, u32[]{:S(2)}) collective-permute-start(bf16[128,1024]{1,0:T(8,128)(2,1)S(1)} %get-tuple-element.114), channel_id=1, source_target_pairs={{0,96},{96,0},{32,64},{64,32},{1,97},{97,1},{33,65},{65,33},{2,98}... | collective-permute-start | bytes 786440 | tf_op jit(solution)/shard_map/ppermute | solution.py:42
  135.3 7.5 %collective-permute-start.11 = (bf16[128,1024]{1,0:T(8,128)(2,1)S(1)}, bf16[128,1024]{1,0:T(8,128)(2,1)S(1)}, u32[]{:S(2)}, u32[]{:S(2)}) collective-permute-start(bf16[128,1024]{1,0:T(8,128)(2,1)S(1)} %get-tuple-element.111), channel_id=1, source_target_pairs={{0,96},{96,0},{32,64},{64,32},{1,97},{97,1},{33,65},{65,33},{2,98}... | collective-permute-start | bytes 786440 | tf_op jit(solution)/shard_map/ppermute | solution.py:42
  138.1 19.4 %collective-permute-start.13 = (bf16[128,1024]{1,0:T(8,128)(2,1)S(1)}, bf16[128,1024]{1,0:T(8,128)(2,1)}, u32[]{:S(2)}, u32[]{:S(2)}) collective-permute-start(bf16[128,1024]{1,0:T(8,128)(2,1)S(1)} %get-tuple-element.112), channel_id=1, source_target_pairs={{0,32},{32,0},{1,33},{33,1},{2,34},{34,2},{3,35},{35,3},{4,36},{36... | collective-permute-start | bytes 786440 | tf_op jit(solution)/shard_map/ppermute | solution.py:30
  158.6 6.6 %collective-permute-start.22 = (bf16[64,1024]{1,0:T(8,128)(2,1)S(1)}, bf16[64,1024]{1,0:T(8,128)(2,1)S(1)}, u32[]{:S(2)}, u32[]{:S(2)}) collective-permute-start(bf16[64,1024]{1,0:T(8,128)(2,1)S(1)} %maximum_maximum_fusion.own), channel_id=1, source_target_pairs={{0,64},{64,0},{1,65},{65,1},{2,66},{66,2},{3,67},{67,3},{4,68},{68... | collective-permute-start | bytes 393224 | tf_op jit(solution)/shard_map/ppermute | solution.py:38
  161.4 6.9 %collective-permute-start.21 = (bf16[64,1024]{1,0:T(8,128)(2,1)S(1)}, bf16[64,1024]{1,0:T(8,128)(2,1)S(1)}, u32[]{:S(2)}, u32[]{:S(2)}) collective-permute-start(bf16[64,1024]{1,0:T(8,128)(2,1)S(1)} %maximum_maximum_fusion.own), channel_id=1, source_target_pairs={{0,96},{96,0},{32,64},{64,32},{1,97},{97,1},{33,65},{65,33},{2,98}... | collective-permute-start | bytes 393224 | tf_op jit(solution)/shard_map/ppermute | solution.py:42
  161.4 6.9 %collective-permute-start.20 = (bf16[64,1024]{1,0:T(8,128)(2,1)S(1)}, bf16[64,1024]{1,0:T(8,128)(2,1)S(1)}, u32[]{:S(2)}, u32[]{:S(2)}) collective-permute-start(bf16[64,1024]{1,0:T(8,128)(2,1)S(1)} %maximum_maximum_fusion.own), channel_id=1, source_target_pairs={{0,32},{32,0},{1,33},{33,1},{2,34},{34,2},{3,35},{35,3},{4,36},{36... | collective-permute-start | bytes 393224 | tf_op jit(solution)/shard_map/ppermute | solution.py:30
  (38 other events, 245.8 us)

commit v9 on v4

--- a/solution.py
+++ b/solution.py
@@ -69,8 +69,14 @@
     return lax.broadcasted_iota(jnp.int32, dims, axis)
 
 
-def pick_kernel(meta, w_in, mine, theirs):
-    core, role = meta[0], meta[1]
+def place_of():
+    core, high, low = (lax.axis_index(axis) for axis in ("c", "h", "l"))
+    return core, high + low - 2 * high * low
+
+
+def pick_kernel(w_in, w_out, mine, theirs, top):
+    core, role = place_of()
+    top[...] = jnp.where(role == 0, w_out[:32], w_out[32:])
     part = jnp.where(iota((512, 256), 1) < 128, core * 2 + role, 2 - core * 2 + role)
     at = iota((512, 256), 1) % 128
     spread = (iota((512, 256), 0) == at // 32 * 128 + part * 32 + at % 32).astype(BF16)
@@ -80,9 +86,9 @@
         theirs[:, i * 128 : i * 128 + 128] = got[:, 128:]
 
 
-def lay_kernel(meta, mine, theirs, w_out, out, block, sems):
-    core, role = meta[0], meta[1]
-    block[:32] = jnp.where(role == 0, w_out[:32], w_out[32:])
+def lay_kernel(mine, theirs, top, out, block, sems):
+    core, role = place_of()
+    block[:32] = top[...]
     block[32:, :512] = jnp.where(core == 0, mine[...], theirs[...])
     block[32:, 512:] = jnp.where(core == 0, theirs[...], mine[...])
     copies = [pltpu.make_async_copy(block, out.at[i], sems.at[i]) for i in range(16)]
@@ -213,27 +219,21 @@
     loss[...] = jnp.broadcast_to(jnp.log(expsum) - picked, (8, 128))
 
 
-def tile_kernel(sums, weighted, share_hit, emb, own, other):
-    rows = jnp.concatenate([sums[...]] * 16, axis=0)
-    chosen = iota((128, 128), 0) // 8 == iota((128, 128), 1)
-    column = jnp.sum(jnp.where(chosen, rows, 0.0), axis=1, keepdims=True)
-    grad = weighted[...] / column - share_hit[...]
-    grad_hi = grad.astype(BF16)
-    grad_lo = (grad - grad_hi.astype(F32)).astype(BF16)
-    for k, out in enumerate((own, other)):
-        at = slice(k * 256, k * 256 + 256)
-        part = lax.dot_general(grad_hi[:, at], emb[...], FIRST, preferred_element_type=F32)
-        part = part + lax.dot_general(grad_lo[:, at], emb[...], FIRST, preferred_element_type=F32)
-        out[...] = part.astype(out.dtype)
-
-
 def backward_kernel(*refs):
-    grads, gain = refs[:4], refs[4]
-    rows, toks = refs[5:9], refs[9:13]
-    hiddens, slopes, weights, out = refs[13:15], refs[15:17], refs[17], refs[18]
-    row_buf, tok_buf, hid_buf, slope_buf, w_out, sum_grad, act_grad, result, sems = refs[19:]
+    grads, gain, sums = refs[:4], refs[4], refs[5]
+    rows, toks = refs[6:10], refs[10:14]
+    hiddens, slopes, weights = refs[14:16], refs[16:18], refs[18]
+    tile_in, out, tile_out = refs[19:22], refs[22], refs[23:25]
+    row_buf, tok_buf, hid_buf, slope_buf, w_out, sum_grad, act_grad, result = refs[25:33]
+    tile_bufs, tile_results, sems = refs[33:36], refs[36:38], refs[38]
     sent = []
     first = pltpu.make_async_copy(weights.at[:, 0:32], w_out, sems.at[0])
+    tile_copies = [
+        pltpu.make_async_copy(part, buf, sems.at[21 + k])
+        for k, (part, buf) in enumerate(zip(tile_in, tile_bufs))
+    ]
+    for copy in tile_copies:
+        copy.start()
     first.start()
     row_copies, tok_copies, hid_copies, slope_copies = [], [], [], []
     for k in range(4):
@@ -252,6 +252,21 @@
         at = pl.ds(k * 256, 256)
         tok_copies.append(pltpu.make_async_copy(toks[k], tok_buf.at[at], sems.at[9 + k]))
         tok_copies[k].start()
+    for copy in tile_copies:
+        copy.wait()
+    weighted, share_hit, emb = tile_bufs
+    chosen = iota((128, 128), 0) // 8 == iota((128, 128), 1)
+    column = jnp.where(chosen, jnp.concatenate([sums[...]] * 16, axis=0), 0.0)
+    logit = weighted[...] / jnp.sum(column, axis=1, keepdims=True) - share_hit[...]
+    logit_hi = logit.astype(BF16)
+    logit_lo = (logit - logit_hi.astype(F32)).astype(BF16)
+    for k, part in enumerate(tile_results):
+        at = slice(k * 256, k * 256 + 256)
+        value = lax.dot_general(logit_hi[:, at], emb[...], FIRST, preferred_element_type=F32)
+        value = value + lax.dot_general(logit_lo[:, at], emb[...], FIRST, preferred_element_type=F32)
+        part[...] = value.astype(part.dtype)
+        sent.append(pltpu.make_async_copy(part, tile_out[k], sems.at[24 + k]))
+        sent[-1].start()
     for k in range(4):
         row_copies[k].wait()
         scaled_grad = grads[k][...] * gain[...]
@@ -280,12 +295,12 @@
         act_grad[at] = (back * slope_buf[at]).astype(BF16)
     for copy in hid_copies:
         copy.wait()
-    for i in range(4):
+    for i in range(2):
         part = lax.dot_general(
-            hid_buf[:, i * 128 : i * 128 + 128], sum_grad[...], FIRST, preferred_element_type=F32
+            hid_buf[:, i * 256 : i * 256 + 256], sum_grad[...], FIRST, preferred_element_type=F32
         )
-        at = pl.ds(i * 4, 4)
-        result[at, :32] = part.astype(BF16).reshape(4, 32, 1024)
+        at = pl.ds(i * 8, 8)
+        result[at, :32] = part.astype(BF16).reshape(8, 32, 1024)
         sent.append(pltpu.make_async_copy(result.at[at, 0:32], out.at[at, 0:32], sems.at[13 + i]))
         sent[-1].start()
     for copy in tok_copies:
@@ -303,12 +318,16 @@
         copy.wait()
 
 
-def backward(grads, gain, rows, toks, hiddens, slopes, weights):
+def backward(grads, gain, sums, rows, toks, hiddens, slopes, weights, tile_in):
     return pl.pallas_call(
         backward_kernel,
-        out_shape=shape((16, 64, 1024), BF16),
-        in_specs=[WHOLE] * 5 + [ANYWHERE] * 13,
-        out_specs=ANYWHERE,
+        out_shape=(
+            shape((16, 64, 1024), BF16),
+            shape((256, 1024), F32),
+            shape((256, 1024), BF16),
+        ),
+        in_specs=[WHOLE] * 6 + [ANYWHERE] * 16,
+        out_specs=(ANYWHERE,) * 3,
         scratch_shapes=[
             pltpu.VMEM((1024, 1152), BF16),
             pltpu.VMEM((1024, 1024), BF16),
@@ -318,11 +337,16 @@
             pltpu.VMEM((1024, 1024), BF16),
             pltpu.VMEM((1024, 512), BF16),
             pltpu.VMEM((16, 64, 1024), BF16),
-            pltpu.SemaphoreType.DMA((21,)),
+            pltpu.VMEM((128, 512), F32),
+            pltpu.VMEM((128, 512), F32),
+            pltpu.VMEM((128, 1024), BF16),
+            pltpu.VMEM((256, 1024), F32),
+            pltpu.VMEM((256, 1024), BF16),
+            pltpu.SemaphoreType.DMA((26,)),
         ],
         compiler_params=MOST,
         cost_estimate=cost(3 * 2**30, 10 * 2**20),
-    )(*grads, gain, *rows, *toks, *hiddens, *slopes, weights)
+    )(*grads, gain, sums, *rows, *toks, *hiddens, *slopes, weights, *tile_in)
 
 
 def total_kernel(meta, got, out, keep, give):
@@ -391,21 +415,23 @@
     gain = norm_gain.reshape(1, width)
     own_tok = states.reshape(docs * length, width)
 
-    mine, theirs = pl.pallas_call(
+    mine, theirs, top = pl.pallas_call(
         pick_kernel,
-        out_shape=(shape((32, 512), BF16),) * 2,
-        in_specs=[SCALARS, WHOLE],
-        out_specs=(WHOLE, WHOLE),
+        out_shape=(shape((32, 512), BF16),) * 2 + (shape((32, width), BF16),),
+        in_specs=[WHOLE, WHOLE],
+        out_specs=(WHOLE,) * 3,
+        compiler_params=LIMIT,
         cost_estimate=cost(2**25, 2**18),
-    )(meta, w_in)
+    )(w_in, w_out)
     block = pl.pallas_call(
         lay_kernel,
         out_shape=shape((16, 64, width), BF16),
-        in_specs=[SCALARS, WHOLE, WHOLE, WHOLE],
+        in_specs=[WHOLE, WHOLE, WHOLE],
         out_specs=ANYWHERE,
         scratch_shapes=[pltpu.VMEM((64, width), BF16), pltpu.SemaphoreType.DMA((16,))],
+        compiler_params=LIMIT,
         cost_estimate=cost(0, 2**21),
-    )(meta, mine, swap_core(theirs), w_out)
+    )(mine, swap_core(theirs), top)
     block, own_tok, label_tiles, shortlist, positives, owner_map = lax.optimization_barrier(
         (block, own_tok, label_tiles, shortlist, positives, owner_map)
     )
@@ -444,11 +470,13 @@
     )
 
     near_a, near_b, near_hidden, near_slope = forward(diag_tok, near_tok, weights, 2**30)
-    near_sum = (near_b + swap_core(near_a).astype(F32)).astype(BF16)
+    near_a, core_tok = lax.optimization_barrier((near_a, core_tok))
+    own_a, own_b, own_hidden, own_slope = forward(core_tok, own_tok, weights, 2**30)
+    near_a, own_a, own_b = lax.optimization_barrier((swap_core(near_a), own_a, own_b))
+    near_sum = (near_b + near_a.astype(F32)).astype(BF16)
     near_sum, pos_part = lax.optimization_barrier((near_sum, pos_part))
     from_near = swap_near(near_sum)
     pos_got = gather_chips(pos_part.reshape(16, docs, width))
-    own_a, own_b, own_hidden, own_slope = forward(core_tok, own_tok, weights, 2**36)
     from_near, pos_got = lax.optimization_barrier((from_near, pos_got))
     pos_mean = jnp.sum(pos_got.astype(F32), axis=0) * (1.0 / POS_SCALE)
     own_rows, emb = pl.pallas_call(
@@ -494,14 +522,16 @@
     loss = loss[:, 0]
 
     grads = (swap_diag(emb_grad), swap_near(emb_grad), swap_core(emb_grad), emb_grad)
-    send = backward(
+    send, tile_own, tile_other = backward(
         grads,
         gain,
+        sums,
         (diag_rows, near_rows, core_rows, own_rows),
         (diag_tok, near_tok, core_tok, own_tok),
         (near_hidden, own_hidden),
         (near_slope, own_slope),
         weights,
+        (weighted, share_hit, plane_emb),
     )
     got = lax.all_to_all(send, CHIPS, 0, 0, tiled=True)
     part, keep, give = pl.pallas_call(
@@ -527,14 +557,6 @@
         cost_estimate=cost(2**26, 2**20),
     )(meta, both, swap_near(both), swap_wrap(both), swap_far(both))
 
-    tile_own, tile_other = pl.pallas_call(
-        tile_kernel,
-        out_shape=(shape((256, width), F32), shape((256, width), BF16)),
-        in_specs=[WHOLE] * 4,
-        out_specs=(WHOLE, WHOLE),
-        compiler_params=LIMIT,
-        cost_estimate=cost(2**28, 2**21),
-    )(sums, weighted, share_hit, plane_emb)
     tile_chip = (tile_own + swap_core(tile_other).astype(F32)).astype(BF16)
 
     def add(a, swap):

time: 173 us -> 172 us (level)
  local copies, waits for them, and re-layouts: 5.37 us -> 10.4 us
  Pallas kernels: 31.7 us -> 26.7 us
    unnamed x59 -> x63, local copies, waits for them, and re-layouts: 2.58 us -> 6.93 us
    pallas_call x3 -> x2, Pallas kernels: 12.5 us -> 9.54 us  [the longest x1 9.22 us: backward(): pl.pallas_call(backward_kernel, out_shape=(shape((16, 64, 1024), BF16), s...]
  transfers between devices with their start and end apart: 27 -> 27, of which waited for: 13 -> 13; matrix products, arithmetic and copies ran while one was open for 13% -> 13% of each run, Pallas kernels for 11% -> 7%
where the time goes in v9:
time: 172 us; the launch traced here: 171 us
  waiting for transfers between devices  53.7 us (31%)
  starting transfers between devices  47.2 us (27%)
  Pallas kernels  26.7 us (16%)
  other arithmetic  17.9 us (10%)
  blocking collectives  12.6 us (7%)
  local copies, waits for them, and re-layouts  10.4 us (6%)
    all_to_all x2, waiting for transfers between devices, gather_chips(): return lax.all_to_all(a, CHIPS, 0, 0, tiled=True)  19.8 us
    all_to_all x1, blocking collectives, gather_chips(): return lax.all_to_all(a, CHIPS, 0, 0, tiled=True)  12.6 us
    all_to_all x2, starting transfers between devices, gather_chips(): return lax.all_to_all(a, CHIPS, 0, 0, tiled=True)  12.5 us
    ppermute x10, starting transfers between devices, swap_core(): return lax.ppermute(a, 'c', [(0, 1), (1, 0)])  12.5 us
    reduce_max x1, other arithmetic, on_device(): jnp.max((short[:, :, None] == cluster_ids[None, None, :]).astype(F32), ax...  9.89 us
    all_to_all x1, waiting for transfers between devices, on_device(): got = lax.all_to_all(send, CHIPS, 0, 0, tiled=True)  9.67 us
    pallas_call x1, Pallas kernels, backward(): pl.pallas_call(backward_kernel, out_shape=(shape((16, 64, 1024), BF16), s...  9.22 us
    ppermute x3, waiting for transfers between devices, swap_wrap(): return lax.ppermute(a, ('h', 'l'), [(0, 3), (3, 0), (1, 2), (2, 1)])  9.13 us
  transfers between devices with their start and end apart: 27, of which 13 were waited for; matrix products, arithmetic and copies ran while one was open for 13% of the time, Pallas kernels for 7%

profile of v9, /device:TPU:1, one launch (start us, length us, event | category | flops | bytes accessed | tf_op | source)
XLA Modules:
  0.0 171.1 jit_solution(12486895500949565779)
XLA Ops:
  8.9 7.7 %all-to-all-start = ((bf16[16,64,1024]{2,1,0:T(8,128)(2,1)}), bf16[16,64,1024]{2,1,0:T(8,128)(2,1)}, u32[]{:S(2)}, u32[]{:S(2)}) async-start(bf16[16,64,1024]{2,1,0:T(8,128)(2,1)} %shard_map.155), calls=%async_computation | async-start | bytes 4194304 | tf_op jit(solution)/shard_map/all_to_all | solution.py:50
  18.9 9.9 %convert_reduce_fusion.live = bf16[128,128]{1,0:T(8,128)(2,1)S(1)} fusion(s32[128]{0:T(128)S(1)} %select_reduce_fusion, s32[128,400]{1,0:T(8,128)S(1)} %dynamic-slice_bitcast_fusion), kind=kLoop, calls=%fused_computation | loop fusion | flops 19644416 | bytes 238080 | tf_op jit(solution)/shard_map/reduce_max | solution.py:451
  31.9 13.9 %all-to-all-done.weights.refs_18_ = bf16[16,64,1024]{2,1,0:T(8,128)(2,1)} async-done(((bf16[16,64,1024]{2,1,0:T(8,128)(2,1)}), bf16[16,64,1024]{2,1,0:T(8,128)(2,1)}, u32[]{:S(2)}, u32[]{:S(2)}) %all-to-all-start) | async-done | bytes 2097184 | tf_op jit(solution)/shard_map/all_to_all | solution.py:50
  45.8 4.3 %shard_map.156 = (bf16[256,1024]{1,0:T(8,128)(2,1)S(1)}, f32[256,1024]{1,0:T(8,128)S(1)}, bf16[512,512]{1,0:T(8,128)(2,1)S(1)}, f32[512,512]{1,0:T(8,128)S(1)}) custom-call(bf16[256,1024]{1,0:T(8,128)(2,1)} %collective-permute-done.1.tok_a.refs_10_, bf16[256,1024]{1,0:T(8,128)(2,1)} %collective-permute-done.2.tok_b.refs_11_, ...), custom_call_target="tpu_custom_call" | custom-call | flops 1073741824 | bytes 6291456 | tf_op jit(solution)/shard_map/pallas_call | solution.py:129
  51.9 1.9 %collective-permute-start.5 = (bf16[256,1024]{1,0:T(8,128)(2,1)S(1)}, bf16[256,1024]{1,0:T(8,128)(2,1)S(1)}, u32[]{:S(2)}, u32[]{:S(2)}) collective-permute-start(bf16[256,1024]{1,0:T(8,128)(2,1)S(1)} %get-tuple-element.66), channel_id=1, source_target_pairs={{0,1},{1,0},{2,3},{3,2},{4,5},{5,4},{6,7},{7,6},{8,9},{9,8},{10,11... | collective-permute-start | bytes 1572872 | tf_op jit(solution)/shard_map/ppermute | solution.py:26
  53.8 3.0 %shard_map.157 = (bf16[256,1024]{1,0:T(8,128)(2,1)S(1)}, f32[256,1024]{1,0:T(8,128)S(1)}, bf16[512,512]{1,0:T(8,128)(2,1)S(1)}, f32[512,512]{1,0:T(8,128)S(1)}) custom-call(bf16[256,1024]{1,0:T(8,128)(2,1)S(1)} %collective-permute-done.4.tok_a.refs_12_, bf16[256,1024]{1,0:T(8,128)(2,1)S(1)} %bitcast.25, bf16[16,64,1024]{2,1,0:T(8,128)(2,1)} %all-to-all-done.weights.refs_18_), custom_call_target="tpu_custom_call" | custom-call | flops 1073741824 | bytes 6291456 | tf_op jit(solution)/shard_map/pallas_call | solution.py:129
  60.4 12.6 %all_to_all.25 = f16[16,8,1024]{2,1,0:T(8,128)(2,1)} all-to-all(f16[16,8,1024]{2,1,0:T(8,128)(2,1)S(1)} %bitcast.33), channel_id=1, replica_groups=mesh['h'=2,'l'=2,'x'=4,'z'=4,'c'=2] {'x','z'}, dimensions={0} | all-to-all | bytes 524288 | tf_op jit(solution)/shard_map/all_to_all | solution.py:50
  73.0 1.9 %shard_map.158 = (bf16[256,1152]{1,0:T(8,128)(2,1)S(1)}, bf16[128,1024]{1,0:T(8,128)(2,1)}) custom-call(s32[8]{0:T(128)S(1)} %copy-done.5, bf16[256,1024]{1,0:T(8,128)(2,1)S(1)} %bitcast.26, f32[256,1024]{1,0:T(8,128)S(1)} %get-tuple-element.70.part, bf16[256,1024]{1,0:T(8,128)(2,1)S(1)} %collective-permute-done.6.from_core, ...), custom_call_target="tpu_custom_call" | custom-call | flops 4194304 | bytes 4194304 | tf_op jit(solution)/shard_map/pallas_call | solution.py:482
  75.7 4.8 %all-to-all-start.2 = ((bf16[16,8,1024]{2,1,0:T(8,128)(2,1)}), bf16[16,8,1024]{2,1,0:T(8,128)(2,1)S(1)}, u32[]{:S(2)}, u32[]{:S(2)}) async-start(bf16[16,8,1024]{2,1,0:T(8,128)(2,1)} %bitcast.9), calls=%async_computation.2 | async-start | bytes 524288 | tf_op jit(solution)/shard_map/all_to_all | solution.py:50
  82.0 5.9 %all-to-all-done.2 = bf16[16,8,1024]{2,1,0:T(8,128)(2,1)S(1)} async-done(((bf16[16,8,1024]{2,1,0:T(8,128)(2,1)}), bf16[16,8,1024]{2,1,0:T(8,128)(2,1)S(1)}, u32[]{:S(2)}, u32[]{:S(2)}) %all-to-all-start.2) | async-done | bytes 262176 | tf_op jit(solution)/shard_map/all_to_all | solution.py:50
  87.8 2.3 %shard_map.159 = (bf16[128,1280]{1,0:T(8,128)(2,1)}, f32[128,512]{1,0:T(8,128)S(1)}) custom-call(bf16[128,1024]{1,0:T(8,128)(2,1)S(1)} %bitcast.19, bf16[512,1024]{1,0:T(8,128)(2,1)S(1)} %get-tuple-element.79.tiles_hi, bf16[512,1024]{1,0:T(8,128)(2,1)S(1)} %get-tuple-element.80.tiles_lo, bf16[128,128]{1,0:T(8,128)(2,1)S(1)} %convert_reduce_fusion.live), custom_call_target="tpu_custom_call" | custom-call | flops 536870912 | bytes 3145728 | tf_op jit(solution)/shard_map/pallas_call | solution.py:494
  90.9 2.6 %collective-permute-start.12 = (bf16[256,1152]{1,0:T(8,128)(2,1)}, bf16[256,1152]{1,0:T(8,128)(2,1)S(1)}, u32[]{:S(2)}, u32[]{:S(2)}) collective-permute-start(bf16[256,1152]{1,0:T(8,128)(2,1)} %collective-permute-done.8.refs_7_), channel_id=1, source_target_pairs={{0,1},{1,0},{2,3},{3,2},{4,5},{5,4},{6,7},{7,6},{8,9},{9,8},{10,11... | collective-permute-start | bytes 1769480 | tf_op jit(solution)/shard_map/ppermute | solution.py:26
  93.5 3.5 %all-to-all-start.3 = ((bf16[16,8,1280]{2,1,0:T(8,128)(2,1)}), bf16[16,8,1280]{2,1,0:T(8,128)(2,1)S(1)}, u32[]{:S(2)}, u32[]{:S(2)}) async-start(bf16[16,8,1280]{2,1,0:T(8,128)(2,1)} %bitcast.11), calls=%async_computation.3 | async-start | bytes 655360 | tf_op jit(solution)/shard_map/all_to_all | solution.py:509
  98.1 7.5 %all-to-all-done.3.got_hbm = bf16[16,8,1280]{2,1,0:T(8,128)(2,1)S(1)} async-done(((bf16[16,8,1280]{2,1,0:T(8,128)(2,1)}), bf16[16,8,1280]{2,1,0:T(8,128)(2,1)S(1)}, u32[]{:S(2)}, u32[]{:S(2)}) %all-to-all-start.3) | async-done | bytes 327712 | tf_op jit(solution)/shard_map/all_to_all | solution.py:509
  113.3 9.2 %shard_map.161 = (bf16[16,64,1024]{2,1,0:T(8,128)(2,1)}, f32[256,1024]{1,0:T(8,128)}, bf16[256,1024]{1,0:T(8,128)(2,1)}) custom-call(f32[8,1024]{1,0:T(8,128)} %copy-done.30, f32[8,1024]{1,0:T(8,128)} %copy-done.29, f32[8,1024]{1,0:T(8,128)} %copy-done.28, f32[8,1024]{1,0:T(8,128)} %copy-done.9, f32[1,1024]{1,0:T(1,128)} %bitcast.27, f32[8,128]{1,0:T(8,128)} %copy-done.10, ...), custom_call_target="tpu_custom_call" | custom-call | flops 3221225472 | bytes 10485760 | tf_op jit(solution)/shard_map/pallas_call | solution.py:322
  123.0 3.8 %all-to-all-start.4 = ((bf16[16,64,1024]{2,1,0:T(8,128)(2,1)}), bf16[16,64,1024]{2,1,0:T(8,128)(2,1)S(1)}, u32[]{:S(2)}, u32[]{:S(2)}) async-start(bf16[16,64,1024]{2,1,0:T(8,128)(2,1)} %get-tuple-element.98), calls=%async_computation.4 | async-start | bytes 4194304 | tf_op jit(solution)/shard_map/all_to_all | solution.py:536
  129.1 2.3 %collective-permute-start.17 = (bf16[128,1024]{1,0:T(8,128)(2,1)S(1)}, bf16[128,1024]{1,0:T(8,128)(2,1)S(1)}, u32[]{:S(2)}, u32[]{:S(2)}) collective-permute-start(bf16[128,1024]{1,0:T(8,128)(2,1)S(1)} %get-tuple-element.112), channel_id=1, source_target_pairs={{0,96},{96,0},{32,64},{64,32},{1,97},{97,1},{33,65},{65,33},{2,98}... | collective-permute-start | bytes 786440 | tf_op jit(solution)/shard_map/ppermute | solution.py:42
  131.4 4.6 %collective-permute-done.15 = bf16[128,1024]{1,0:T(8,128)(2,1)S(1)} collective-permute-done((bf16[128,1024]{1,0:T(8,128)(2,1)S(1)}, bf16[128,1024]{1,0:T(8,128)(2,1)S(1)}, u32[]{:S(2)}, u32[]{:S(2)}) %collective-permute-start.15) | collective-permute-done | bytes 262176 | tf_op jit(solution)/shard_map/ppermute | solution.py:30
  137.9 2.4 %collective-permute-start.16 = (bf16[128,1024]{1,0:T(8,128)(2,1)S(1)}, bf16[128,1024]{1,0:T(8,128)(2,1)S(1)}, u32[]{:S(2)}, u32[]{:S(2)}) collective-permute-start(bf16[128,1024]{1,0:T(8,128)(2,1)S(1)} %get-tuple-element.109), channel_id=1, source_target_pairs={{0,96},{96,0},{32,64},{64,32},{1,97},{97,1},{33,65},{65,33},{2,98}... | collective-permute-start | bytes 786440 | tf_op jit(solution)/shard_map/ppermute | solution.py:42
  140.9 4.7 %collective-permute-done.16 = bf16[128,1024]{1,0:T(8,128)(2,1)S(1)} collective-permute-done((bf16[128,1024]{1,0:T(8,128)(2,1)S(1)}, bf16[128,1024]{1,0:T(8,128)(2,1)S(1)}, u32[]{:S(2)}, u32[]{:S(2)}) %collective-permute-start.16) | collective-permute-done | bytes 262176 | tf_op jit(solution)/shard_map/ppermute | solution.py:42
  146.5 9.7 %all-to-all-done.4.got = bf16[16,64,1024]{2,1,0:T(8,128)(2,1)S(1)} async-done(((bf16[16,64,1024]{2,1,0:T(8,128)(2,1)}), bf16[16,64,1024]{2,1,0:T(8,128)(2,1)S(1)}, u32[]{:S(2)}, u32[]{:S(2)}) %all-to-all-start.4) | async-done | bytes 2097184 | tf_op jit(solution)/shard_map/all_to_all | solution.py:536
  159.9 3.0 %collective-permute-start.22 = (bf16[64,1024]{1,0:T(8,128)(2,1)S(1)}, bf16[64,1024]{1,0:T(8,128)(2,1)S(1)}, u32[]{:S(2)}, u32[]{:S(2)}) collective-permute-start(bf16[64,1024]{1,0:T(8,128)(2,1)S(1)} %maximum_maximum_fusion.own), channel_id=1, source_target_pairs={{0,64},{64,0},{1,65},{65,1},{2,66},{66,2},{3,67},{67,3},{4,68},{68... | collective-permute-start | bytes 393224 | tf_op jit(solution)/shard_map/ppermute | solution.py:38
  163.3 2.1 %divide_subtract_fusion = (f32[256,1024]{1,0:T(8,128)}, f32[256,1024]{1,0:T(8,128)}, f32[256,1024]{1,0:T(8,128)}) fusion(f32[256,1024]{1,0:T(8,128)S(1)} %copy-done.16, f32[128,1024]{1,0:T(8,128)S(1)} %convert_add_fusion, f32[128,1024]{1,0:T(8,128)S(1)} %copy-done.19, f32[256,1024]{1,0:T(8,128)S(1)} %copy-done.20, f32[256,1024]{1,0:T(8,128)S(1)} %copy-done.21), kind=kLoop, calls=%fused_computation.10 | loop fusion | flops 3407872 | bytes 7340032 | tf_op jit(solution)/shard_map/sub | solution.py:574
  166.4 2.7 %collective-permute-done.21.wrap = bf16[64,1024]{1,0:T(8,128)(2,1)S(1)} collective-permute-done((bf16[64,1024]{1,0:T(8,128)(2,1)S(1)}, bf16[64,1024]{1,0:T(8,128)(2,1)S(1)}, u32[]{:S(2)}, u32[]{:S(2)}) %collective-permute-start.21) | collective-permute-done | bytes 131104 | tf_op jit(solution)/shard_map/ppermute | solution.py:42
  (136 shorter events, 43.6 us)
Async XLA Ops:
  6.7 45.2 %collective-permute-start.4 = (bf16[256,1024]{1,0:T(8,128)(2,1)S(1)}, bf16[256,1024]{1,0:T(8,128)(2,1)S(1)}, u32[]{:S(2)}, u32[]{:S(2)}) collective-permute-start(bf16[256,1024]{1,0:T(8,128)(2,1)S(1)} %bitcast.22), channel_id=1, source_target_pairs={{0,1},{1,0},{2,3},{3,2},{4,5},{5,4},{6,7},{7,6},{8,9},{9,8},{10,11... | collective-permute-start | bytes 1572872 | tf_op jit(solution)/shard_map/ppermute | solution.py:26
  7.1 38.7 %collective-permute-start.2 = (bf16[256,1024]{1,0:T(8,128)(2,1)S(1)}, bf16[256,1024]{1,0:T(8,128)(2,1)}, u32[]{:S(2)}, u32[]{:S(2)}) collective-permute-start(bf16[256,1024]{1,0:T(8,128)(2,1)S(1)} %bitcast.23), channel_id=1, source_target_pairs={{0,32},{32,0},{1,33},{33,1},{2,34},{34,2},{3,35},{35,3},{4,36},{36... | collective-permute-start | bytes 1572872 | tf_op jit(solution)/shard_map/ppermute | solution.py:30
  8.5 37.3 %collective-permute-start.1 = (bf16[256,1024]{1,0:T(8,128)(2,1)S(1)}, bf16[256,1024]{1,0:T(8,128)(2,1)}, u32[]{:S(2)}, u32[]{:S(2)}) collective-permute-start(bf16[256,1024]{1,0:T(8,128)(2,1)S(1)} %bitcast.24), channel_id=1, source_target_pairs={{0,33},{33,0},{1,32},{32,1},{2,35},{35,2},{3,34},{34,3},{4,37},{37... | collective-permute-start | bytes 1572872 | tf_op jit(solution)/shard_map/ppermute | solution.py:34
  8.9 36.9 %all-to-all-start = ((bf16[16,64,1024]{2,1,0:T(8,128)(2,1)}), bf16[16,64,1024]{2,1,0:T(8,128)(2,1)}, u32[]{:S(2)}, u32[]{:S(2)}) async-start(bf16[16,64,1024]{2,1,0:T(8,128)(2,1)} %shard_map.155), calls=%async_computation | async-start | bytes 4194304 | tf_op jit(solution)/shard_map/all_to_all | solution.py:50
  17.1 11.7 %collective-permute-start.3 = (f32[256,1024]{1,0:T(8,128)S(1)}, f32[256,1024]{1,0:T(8,128)}, u32[]{:S(2)}, u32[]{:S(2)}) collective-permute-start(f32[256,1024]{1,0:T(8,128)S(1)} %copy-done.15), channel_id=1, source_target_pairs={{0,1},{1,0},{2,3},{3,2},{4,5},{5,4},{6,7},{7,6},{8,9},{9,8},{10,11... | collective-permute-start | bytes 3145736 | tf_op jit(solution)/shard_map/ppermute | solution.py:26
  51.9 6.6 %collective-permute-start.5 = (bf16[256,1024]{1,0:T(8,128)(2,1)S(1)}, bf16[256,1024]{1,0:T(8,128)(2,1)S(1)}, u32[]{:S(2)}, u32[]{:S(2)}) collective-permute-start(bf16[256,1024]{1,0:T(8,128)(2,1)S(1)} %get-tuple-element.66), channel_id=1, source_target_pairs={{0,1},{1,0},{2,3},{3,2},{4,5},{5,4},{6,7},{7,6},{8,9},{9,8},{10,11... | collective-permute-start | bytes 1572872 | tf_op jit(solution)/shard_map/ppermute | solution.py:26
  58.6 14.3 %collective-permute-start.7 = (bf16[256,1024]{1,0:T(8,128)(2,1)S(1)}, bf16[256,1024]{1,0:T(8,128)(2,1)S(1)}, u32[]{:S(2)}, u32[]{:S(2)}) collective-permute-start(bf16[256,1024]{1,0:T(8,128)(2,1)S(1)} %add_convert_fusion.1), channel_id=1, source_target_pairs={{0,32},{32,0},{1,33},{33,1},{2,34},{34,2},{3,35},{35,3},{4,36},{36... | collective-permute-start | bytes 1572872 | tf_op jit(solution)/shard_map/ppermute | solution.py:30
  60.0 12.9 %collective-permute-start.6 = (bf16[256,1024]{1,0:T(8,128)(2,1)S(1)}, bf16[256,1024]{1,0:T(8,128)(2,1)S(1)}, u32[]{:S(2)}, u32[]{:S(2)}) collective-permute-start(bf16[256,1024]{1,0:T(8,128)(2,1)S(1)} %get-tuple-element.71), channel_id=1, source_target_pairs={{0,1},{1,0},{2,3},{3,2},{4,5},{5,4},{6,7},{7,6},{8,9},{9,8},{10,11... | collective-permute-start | bytes 1572872 | tf_op jit(solution)/shard_map/ppermute | solution.py:26
  74.9 16.0 %collective-permute-start.8 = (bf16[256,1152]{1,0:T(8,128)(2,1)S(1)}, bf16[256,1152]{1,0:T(8,128)(2,1)}, u32[]{:S(2)}, u32[]{:S(2)}) collective-permute-start(bf16[256,1152]{1,0:T(8,128)(2,1)S(1)} %get-tuple-element.83.refs_9_), channel_id=1, source_target_pairs={{0,32},{32,0},{1,33},{33,1},{2,34},{34,2},{3,35},{35,3},{4,36},{36... | collective-permute-start | bytes 1769480 | tf_op jit(solution)/shard_map/ppermute | solution.py:30
  75.7 12.2 %all-to-all-start.2 = ((bf16[16,8,1024]{2,1,0:T(8,128)(2,1)}), bf16[16,8,1024]{2,1,0:T(8,128)(2,1)S(1)}, u32[]{:S(2)}, u32[]{:S(2)}) async-start(bf16[16,8,1024]{2,1,0:T(8,128)(2,1)} %bitcast.9), calls=%async_computation.2 | async-start | bytes 524288 | tf_op jit(solution)/shard_map/all_to_all | solution.py:50
  80.5 30.6 %collective-permute-start.13 = (bf16[256,1152]{1,0:T(8,128)(2,1)S(1)}, bf16[256,1152]{1,0:T(8,128)(2,1)}, u32[]{:S(2)}, u32[]{:S(2)}) collective-permute-start(bf16[256,1152]{1,0:T(8,128)(2,1)S(1)} %get-tuple-element.83.refs_9_), channel_id=1, source_target_pairs={{0,1},{1,0},{2,3},{3,2},{4,5},{5,4},{6,7},{7,6},{8,9},{9,8},{10,11... | collective-permute-start | bytes 1769480 | tf_op jit(solution)/shard_map/ppermute | solution.py:26
  90.9 21.6 %collective-permute-start.12 = (bf16[256,1152]{1,0:T(8,128)(2,1)}, bf16[256,1152]{1,0:T(8,128)(2,1)S(1)}, u32[]{:S(2)}, u32[]{:S(2)}) collective-permute-start(bf16[256,1152]{1,0:T(8,128)(2,1)} %collective-permute-done.8.refs_7_), channel_id=1, source_target_pairs={{0,1},{1,0},{2,3},{3,2},{4,5},{5,4},{6,7},{7,6},{8,9},{9,8},{10,11... | collective-permute-start | bytes 1769480 | tf_op jit(solution)/shard_map/ppermute | solution.py:26
  93.5 12.0 %all-to-all-start.3 = ((bf16[16,8,1280]{2,1,0:T(8,128)(2,1)}), bf16[16,8,1280]{2,1,0:T(8,128)(2,1)S(1)}, u32[]{:S(2)}, u32[]{:S(2)}) async-start(bf16[16,8,1280]{2,1,0:T(8,128)(2,1)} %bitcast.11), calls=%async_computation.3 | async-start | bytes 655360 | tf_op jit(solution)/shard_map/all_to_all | solution.py:509
  106.7 4.4 %collective-permute-start.11 = (f32[8,1024]{1,0:T(8,128)S(1)}, f32[8,1024]{1,0:T(8,128)S(1)}, u32[]{:S(2)}, u32[]{:S(2)}) collective-permute-start(f32[8,1024]{1,0:T(8,128)S(1)} %get-tuple-element.87.refs_3_), channel_id=1, source_target_pairs={{0,1},{1,0},{2,3},{3,2},{4,5},{5,4},{6,7},{7,6},{8,9},{9,8},{10,11... | collective-permute-start | bytes 98312 | tf_op jit(solution)/shard_map/ppermute | solution.py:26
  108.8 3.7 %collective-permute-start.9 = (f32[8,1024]{1,0:T(8,128)S(1)}, f32[8,1024]{1,0:T(8,128)S(1)}, u32[]{:S(2)}, u32[]{:S(2)}) collective-permute-start(f32[8,1024]{1,0:T(8,128)S(1)} %get-tuple-element.87.refs_3_), channel_id=1, source_target_pairs={{0,33},{33,0},{1,32},{32,1},{2,35},{35,2},{3,34},{34,3},{4,37},{37... | collective-permute-start | bytes 98312 | tf_op jit(solution)/shard_map/ppermute | solution.py:34
  122.5 4.3 %collective-permute-start.14 = (bf16[256,1024]{1,0:T(8,128)(2,1)}, bf16[256,1024]{1,0:T(8,128)(2,1)}, u32[]{:S(2)}, u32[]{:S(2)}) collective-permute-start(bf16[256,1024]{1,0:T(8,128)(2,1)} %get-tuple-element.97), channel_id=1, source_target_pairs={{0,1},{1,0},{2,3},{3,2},{4,5},{5,4},{6,7},{7,6},{8,9},{9,8},{10,11... | collective-permute-start | bytes 1572872 | tf_op jit(solution)/shard_map/ppermute | solution.py:26
  123.0 33.1 %all-to-all-start.4 = ((bf16[16,64,1024]{2,1,0:T(8,128)(2,1)}), bf16[16,64,1024]{2,1,0:T(8,128)(2,1)S(1)}, u32[]{:S(2)}, u32[]{:S(2)}) async-start(bf16[16,64,1024]{2,1,0:T(8,128)(2,1)} %get-tuple-element.98), calls=%async_computation.4 | async-start | bytes 4194304 | tf_op jit(solution)/shard_map/all_to_all | solution.py:536
  128.1 7.8 %collective-permute-start.15 = (bf16[128,1024]{1,0:T(8,128)(2,1)S(1)}, bf16[128,1024]{1,0:T(8,128)(2,1)S(1)}, u32[]{:S(2)}, u32[]{:S(2)}) collective-permute-start(bf16[128,1024]{1,0:T(8,128)(2,1)S(1)} %get-tuple-element.111), channel_id=1, source_target_pairs={{0,32},{32,0},{1,33},{33,1},{2,34},{34,2},{3,35},{35,3},{4,36},{36... | collective-permute-start | bytes 786440 | tf_op jit(solution)/shard_map/ppermute | solution.py:30
  129.1 8.6 %collective-permute-start.17 = (bf16[128,1024]{1,0:T(8,128)(2,1)S(1)}, bf16[128,1024]{1,0:T(8,128)(2,1)S(1)}, u32[]{:S(2)}, u32[]{:S(2)}) collective-permute-start(bf16[128,1024]{1,0:T(8,128)(2,1)S(1)} %get-tuple-element.112), channel_id=1, source_target_pairs={{0,96},{96,0},{32,64},{64,32},{1,97},{97,1},{33,65},{65,33},{2,98}... | collective-permute-start | bytes 786440 | tf_op jit(solution)/shard_map/ppermute | solution.py:42
  137.9 7.7 %collective-permute-start.16 = (bf16[128,1024]{1,0:T(8,128)(2,1)S(1)}, bf16[128,1024]{1,0:T(8,128)(2,1)S(1)}, u32[]{:S(2)}, u32[]{:S(2)}) collective-permute-start(bf16[128,1024]{1,0:T(8,128)(2,1)S(1)} %get-tuple-element.109), channel_id=1, source_target_pairs={{0,96},{96,0},{32,64},{64,32},{1,97},{97,1},{33,65},{65,33},{2,98}... | collective-permute-start | bytes 786440 | tf_op jit(solution)/shard_map/ppermute | solution.py:42
  140.3 18.6 %collective-permute-start.18 = (bf16[128,1024]{1,0:T(8,128)(2,1)S(1)}, bf16[128,1024]{1,0:T(8,128)(2,1)}, u32[]{:S(2)}, u32[]{:S(2)}) collective-permute-start(bf16[128,1024]{1,0:T(8,128)(2,1)S(1)} %get-tuple-element.110), channel_id=1, source_target_pairs={{0,32},{32,0},{1,33},{33,1},{2,34},{34,2},{3,35},{35,3},{4,36},{36... | collective-permute-start | bytes 786440 | tf_op jit(solution)/shard_map/ppermute | solution.py:30
  159.9 6.5 %collective-permute-start.22 = (bf16[64,1024]{1,0:T(8,128)(2,1)S(1)}, bf16[64,1024]{1,0:T(8,128)(2,1)S(1)}, u32[]{:S(2)}, u32[]{:S(2)}) collective-permute-start(bf16[64,1024]{1,0:T(8,128)(2,1)S(1)} %maximum_maximum_fusion.own), channel_id=1, source_target_pairs={{0,64},{64,0},{1,65},{65,1},{2,66},{66,2},{3,67},{67,3},{4,68},{68... | collective-permute-start | bytes 393224 | tf_op jit(solution)/shard_map/ppermute | solution.py:38
  162.8 6.3 %collective-permute-start.21 = (bf16[64,1024]{1,0:T(8,128)(2,1)S(1)}, bf16[64,1024]{1,0:T(8,128)(2,1)S(1)}, u32[]{:S(2)}, u32[]{:S(2)}) collective-permute-start(bf16[64,1024]{1,0:T(8,128)(2,1)S(1)} %maximum_maximum_fusion.own), channel_id=1, source_target_pairs={{0,96},{96,0},{32,64},{64,32},{1,97},{97,1},{33,65},{65,33},{2,98}... | collective-permute-start | bytes 393224 | tf_op jit(solution)/shard_map/ppermute | solution.py:42
  163.3 5.9 %collective-permute-start.20 = (bf16[64,1024]{1,0:T(8,128)(2,1)S(1)}, bf16[64,1024]{1,0:T(8,128)(2,1)S(1)}, u32[]{:S(2)}, u32[]{:S(2)}) collective-permute-start(bf16[64,1024]{1,0:T(8,128)(2,1)S(1)} %maximum_maximum_fusion.own), channel_id=1, source_target_pairs={{0,32},{32,0},{1,33},{33,1},{2,34},{34,2},{3,35},{35,3},{4,36},{36... | collective-permute-start | bytes 393224 | tf_op jit(solution)/shard_map/ppermute | solution.py:30
  (34 other events, 277.3 us)

commit v10 on v9

--- a/solution.py
+++ b/solution.py
@@ -74,9 +74,8 @@
     return core, high + low - 2 * high * low
 
 
-def pick_kernel(w_in, w_out, mine, theirs, top):
+def pick_kernel(w_in, mine, theirs):
     core, role = place_of()
-    top[...] = jnp.where(role == 0, w_out[:32], w_out[32:])
     part = jnp.where(iota((512, 256), 1) < 128, core * 2 + role, 2 - core * 2 + role)
     at = iota((512, 256), 1) % 128
     spread = (iota((512, 256), 0) == at // 32 * 128 + part * 32 + at % 32).astype(BF16)
@@ -86,14 +85,17 @@
         theirs[:, i * 128 : i * 128 + 128] = got[:, 128:]
 
 
-def lay_kernel(mine, theirs, top, out, block, sems):
+def lay_kernel(mine, theirs, w_out, out, block, sems):
     core, role = place_of()
-    block[:32] = top[...]
-    block[32:, :512] = jnp.where(core == 0, mine[...], theirs[...])
-    block[32:, 512:] = jnp.where(core == 0, theirs[...], mine[...])
-    copies = [pltpu.make_async_copy(block, out.at[i], sems.at[i]) for i in range(16)]
+    top = w_out.at[pl.ds(pl.multiple_of(role * 32, 32), 32)]
+    copies = [pltpu.make_async_copy(top, out.at[i, 0:32], sems.at[i]) for i in range(16)]
     for copy in copies:
         copy.start()
+    block[:, :512] = jnp.where(core == 0, mine[...], theirs[...])
+    block[:, 512:] = jnp.where(core == 0, theirs[...], mine[...])
+    for i in range(16):
+        copies.append(pltpu.make_async_copy(block, out.at[i, 32:64], sems.at[16 + i]))
+        copies[-1].start()
     for copy in copies:
         copy.wait()
 
@@ -144,6 +146,13 @@
         compiler_params=LIMIT,
         cost_estimate=cost(flops, 6 * 2**20, 2**19),
     )(tok_a, tok_b, weights)
+
+
+def hit_kernel(positives, labels, share):
+    total = jnp.zeros(share.shape, F32)
+    for p in range(POS):
+        total = total + (positives[:, p : p + 1] == labels[...]).astype(F32)
+    share[...] = total * (1.0 / POS)
 
 
 def norm_kernel(lengths, tok, part, from_core, from_near, gain, rows, emb_hbm, emb, sem):
@@ -415,23 +424,23 @@
     gain = norm_gain.reshape(1, width)
     own_tok = states.reshape(docs * length, width)
 
-    mine, theirs, top = pl.pallas_call(
+    mine, theirs = pl.pallas_call(
         pick_kernel,
-        out_shape=(shape((32, 512), BF16),) * 2 + (shape((32, width), BF16),),
-        in_specs=[WHOLE, WHOLE],
-        out_specs=(WHOLE,) * 3,
+        out_shape=(shape((32, 512), BF16),) * 2,
+        in_specs=[WHOLE],
+        out_specs=(WHOLE,) * 2,
         compiler_params=LIMIT,
         cost_estimate=cost(2**25, 2**18),
-    )(w_in, w_out)
+    )(w_in)
     block = pl.pallas_call(
         lay_kernel,
         out_shape=shape((16, 64, width), BF16),
-        in_specs=[WHOLE, WHOLE, WHOLE],
+        in_specs=[WHOLE, WHOLE, ANYWHERE],
         out_specs=ANYWHERE,
-        scratch_shapes=[pltpu.VMEM((64, width), BF16), pltpu.SemaphoreType.DMA((16,))],
+        scratch_shapes=[pltpu.VMEM((32, width), BF16), pltpu.SemaphoreType.DMA((32,))],
         compiler_params=LIMIT,
         cost_estimate=cost(0, 2**21),
-    )(mine, swap_core(theirs), top)
+    )(mine, swap_core(theirs), w_out)
     block, own_tok, label_tiles, shortlist, positives, owner_map = lax.optimization_barrier(
         (block, own_tok, label_tiles, shortlist, positives, owner_map)
     )
@@ -454,12 +463,15 @@
     tiles = jnp.concatenate([label_tiles, oth_tiles], axis=0)
     tiles_top = round_bf16(tiles)
     tiles_hi, tiles_lo = tiles_top.astype(BF16), (tiles - tiles_top).astype(BF16)
-    cluster_hit = (posit[:, :, None] // LPC == cluster_ids[None, None, :]).astype(F32)
-    offset_hit = (
-        posit[:, :, None] % LPC == jnp.arange(LPC, dtype=jnp.int32)[None, None, :]
-    ).astype(F32)
-    hits = jnp.sum(cluster_hit[:, :, :, None] * offset_hit[:, :, None, :], axis=1).reshape(128, 512)
-    share_hit = hits / POS
+    label_ids = (jnp.repeat(cluster_ids, LPC) * LPC + jnp.arange(512) % LPC).astype(jnp.int32)
+    share_hit = pl.pallas_call(
+        hit_kernel,
+        out_shape=shape((128, 512), F32),
+        in_specs=[WHOLE, WHOLE],
+        out_specs=WHOLE,
+        compiler_params=LIMIT,
+        cost_estimate=cost(2**18, 2**18),
+    )(posit, label_ids[None, :])
     hit = share_hit.astype(BF16)
     pos_part = jnp.dot(hit, tiles_hi, preferred_element_type=F32) + jnp.dot(
         hit, tiles_lo, preferred_element_type=F32
@@ -470,13 +482,11 @@
     )
 
     near_a, near_b, near_hidden, near_slope = forward(diag_tok, near_tok, weights, 2**30)
-    near_a, core_tok = lax.optimization_barrier((near_a, core_tok))
-    own_a, own_b, own_hidden, own_slope = forward(core_tok, own_tok, weights, 2**30)
-    near_a, own_a, own_b = lax.optimization_barrier((swap_core(near_a), own_a, own_b))
-    near_sum = (near_b + near_a.astype(F32)).astype(BF16)
+    near_sum = (near_b + swap_core(near_a).astype(F32)).astype(BF16)
     near_sum, pos_part = lax.optimization_barrier((near_sum, pos_part))
     from_near = swap_near(near_sum)
     pos_got = gather_chips(pos_part.reshape(16, docs, width))
+    own_a, own_b, own_hidden, own_slope = forward(core_tok, own_tok, weights, 2**36)
     from_near, pos_got = lax.optimization_barrier((from_near, pos_got))
     pos_mean = jnp.sum(pos_got.astype(F32), axis=0) * (1.0 / POS_SCALE)
     own_rows, emb = pl.pallas_call(

time: 172 us -> 172 us (level)
  waiting for transfers between devices: 53.7 us -> 58.6 us
  local copies, waits for them, and re-layouts: 10.4 us -> 7.03 us
    unnamed x63 -> x65, local copies, waits for them, and re-layouts: 6.93 us -> 4.31 us
  transfers between devices with their start and end apart: 27 -> 27, of which waited for: 13 -> 13; matrix products, arithmetic and copies ran while one was open for 13% -> 12% of each run, Pallas kernels for 7% -> 5%
where the time goes in v10:
time: 172 us; the launch traced here: 171 us
  waiting for transfers between devices  58.6 us (34%)
  starting transfers between devices  45.6 us (27%)
  Pallas kernels  27.2 us (16%)
  other arithmetic  17.2 us (10%)
  blocking collectives  13.1 us (8%)
  local copies, waits for them, and re-layouts  7.03 us (4%)
    all_to_all x2, waiting for transfers between devices, gather_chips(): return lax.all_to_all(a, CHIPS, 0, 0, tiled=True)  20.4 us
    all_to_all x1, blocking collectives, gather_chips(): return lax.all_to_all(a, CHIPS, 0, 0, tiled=True)  13.1 us
    ppermute x10, starting transfers between devices, swap_core(): return lax.ppermute(a, 'c', [(0, 1), (1, 0)])  12.7 us
    all_to_all x2, starting transfers between devices, gather_chips(): return lax.all_to_all(a, CHIPS, 0, 0, tiled=True)  11.8 us
    reduce_max x1, other arithmetic, on_device(): jnp.max((short[:, :, None] == cluster_ids[None, None, :]).astype(F32), ax...  9.9 us
    all_to_all x1, waiting for transfers between devices, on_device(): got = lax.all_to_all(send, CHIPS, 0, 0, tiled=True)  9.27 us
    pallas_call x1, Pallas kernels, backward(): pl.pallas_call(backward_kernel, out_shape=(shape((16, 64, 1024), BF16), s...  9.24 us
    ppermute x3, waiting for transfers between devices, swap_wrap(): return lax.ppermute(a, ('h', 'l'), [(0, 3), (3, 0), (1, 2), (2, 1)])  9.1 us
  transfers between devices with their start and end apart: 27, of which 13 were waited for; matrix products, arithmetic and copies ran while one was open for 12% of the time, Pallas kernels for 5%

profile of v10, /device:TPU:1, one launch (start us, length us, event | category | flops | bytes accessed | tf_op | source)
XLA Modules:
  0.0 171.3 jit_solution(8443191498995630670)
XLA Ops:
  9.2 7.9 %all-to-all-start = ((bf16[16,64,1024]{2,1,0:T(8,128)(2,1)}), bf16[16,64,1024]{2,1,0:T(8,128)(2,1)}, u32[]{:S(2)}, u32[]{:S(2)}) async-start(bf16[16,64,1024]{2,1,0:T(8,128)(2,1)} %shard_map.155), calls=%async_computation | async-start | bytes 4194304 | tf_op jit(solution)/shard_map/all_to_all | solution.py:50
  18.5 9.9 %convert_reduce_fusion.live = bf16[128,128]{1,0:T(8,128)(2,1)S(1)} fusion(s32[128]{0:T(128)S(1)} %select_reduce_fusion, s32[128,400]{1,0:T(8,128)S(1)} %dynamic-slice_bitcast_fusion), kind=kLoop, calls=%fused_computation | loop fusion | flops 19644416 | bytes 238080 | tf_op jit(solution)/shard_map/reduce_max | solution.py:460
  31.5 14.8 %all-to-all-done.weights.refs_18_ = bf16[16,64,1024]{2,1,0:T(8,128)(2,1)} async-done(((bf16[16,64,1024]{2,1,0:T(8,128)(2,1)}), bf16[16,64,1024]{2,1,0:T(8,128)(2,1)}, u32[]{:S(2)}, u32[]{:S(2)}) %all-to-all-start) | async-done | bytes 2097184 | tf_op jit(solution)/shard_map/all_to_all | solution.py:50
  46.4 4.3 %shard_map.158 = (bf16[256,1024]{1,0:T(8,128)(2,1)S(1)}, f32[256,1024]{1,0:T(8,128)S(1)}, bf16[512,512]{1,0:T(8,128)(2,1)S(1)}, f32[512,512]{1,0:T(8,128)S(1)}) custom-call(bf16[256,1024]{1,0:T(8,128)(2,1)} %collective-permute-done.4.tok_a.refs_10_, bf16[256,1024]{1,0:T(8,128)(2,1)S(1)} %collective-permute-done.5.tok_b.refs_11_, ...), custom_call_target="tpu_custom_call" | custom-call | flops 1073741824 | bytes 6291456 | tf_op jit(solution)/shard_map/pallas_call | solution.py:131
  55.5 3.2 %shard_map.157 = (bf16[256,1024]{1,0:T(8,128)(2,1)S(1)}, f32[256,1024]{1,0:T(8,128)S(1)}, bf16[512,512]{1,0:T(8,128)(2,1)S(1)}, f32[512,512]{1,0:T(8,128)S(1)}) custom-call(bf16[256,1024]{1,0:T(8,128)(2,1)S(1)} %collective-permute-done.1.tok_a.refs_12_, bf16[256,1024]{1,0:T(8,128)(2,1)S(1)} %bitcast.23, bf16[16,64,1024]{2,1,0:T(8,128)(2,1)} %all-to-all-done.weights.refs_18_), custom_call_target="tpu_custom_call" | custom-call | flops 68719476736 | bytes 6291456 | tf_op jit(solution)/shard_map/pallas_call | solution.py:131
  60.2 13.1 %all_to_all.25 = f16[16,8,1024]{2,1,0:T(8,128)(2,1)} all-to-all(f16[16,8,1024]{2,1,0:T(8,128)(2,1)S(1)} %bitcast.29), channel_id=1, replica_groups=mesh['h'=2,'l'=2,'x'=4,'z'=4,'c'=2] {'x','z'}, dimensions={0} | all-to-all | bytes 524288 | tf_op jit(solution)/shard_map/all_to_all | solution.py:50
  73.3 1.9 %shard_map.159 = (bf16[256,1152]{1,0:T(8,128)(2,1)S(1)}, bf16[128,1024]{1,0:T(8,128)(2,1)}) custom-call(s32[8]{0:T(128)S(1)} %copy-done.6, bf16[256,1024]{1,0:T(8,128)(2,1)S(1)} %bitcast.24, f32[256,1024]{1,0:T(8,128)S(1)} %get-tuple-element.58.part, bf16[256,1024]{1,0:T(8,128)(2,1)S(1)} %collective-permute-done.3.from_core, ...), custom_call_target="tpu_custom_call" | custom-call | flops 4194304 | bytes 4194304 | tf_op jit(solution)/shard_map/pallas_call | solution.py:492
  75.5 3.9 %all-to-all-start.2 = ((bf16[16,8,1024]{2,1,0:T(8,128)(2,1)}), bf16[16,8,1024]{2,1,0:T(8,128)(2,1)S(1)}, u32[]{:S(2)}, u32[]{:S(2)}) async-start(bf16[16,8,1024]{2,1,0:T(8,128)(2,1)} %bitcast.9), calls=%async_computation.2 | async-start | bytes 524288 | tf_op jit(solution)/shard_map/all_to_all | solution.py:50
  81.2 5.5 %all-to-all-done.2 = bf16[16,8,1024]{2,1,0:T(8,128)(2,1)S(1)} async-done(((bf16[16,8,1024]{2,1,0:T(8,128)(2,1)}), bf16[16,8,1024]{2,1,0:T(8,128)(2,1)S(1)}, u32[]{:S(2)}, u32[]{:S(2)}) %all-to-all-start.2) | async-done | bytes 262176 | tf_op jit(solution)/shard_map/all_to_all | solution.py:50
  86.7 2.3 %shard_map.160 = (bf16[128,1280]{1,0:T(8,128)(2,1)}, f32[128,512]{1,0:T(8,128)S(1)}) custom-call(bf16[128,1024]{1,0:T(8,128)(2,1)S(1)} %bitcast.17, bf16[512,1024]{1,0:T(8,128)(2,1)S(1)} %get-tuple-element.67.tiles_hi, bf16[512,1024]{1,0:T(8,128)(2,1)S(1)} %get-tuple-element.68.tiles_lo, bf16[128,128]{1,0:T(8,128)(2,1)S(1)} %convert_reduce_fusion.live), custom_call_target="tpu_custom_call" | custom-call | flops 536870912 | bytes 3145728 | tf_op jit(solution)/shard_map/pallas_call | solution.py:504
  89.8 2.8 %collective-permute-start.12 = (bf16[256,1152]{1,0:T(8,128)(2,1)}, bf16[256,1152]{1,0:T(8,128)(2,1)S(1)}, u32[]{:S(2)}, u32[]{:S(2)}) collective-permute-start(bf16[256,1152]{1,0:T(8,128)(2,1)} %collective-permute-done.8.refs_7_), channel_id=1, source_target_pairs={{0,1},{1,0},{2,3},{3,2},{4,5},{5,4},{6,7},{7,6},{8,9},{9,8},{10,11... | collective-permute-start | bytes 1769480 | tf_op jit(solution)/shard_map/ppermute | solution.py:26
  92.7 3.5 %all-to-all-start.3 = ((bf16[16,8,1280]{2,1,0:T(8,128)(2,1)}), bf16[16,8,1280]{2,1,0:T(8,128)(2,1)S(1)}, u32[]{:S(2)}, u32[]{:S(2)}) async-start(bf16[16,8,1280]{2,1,0:T(8,128)(2,1)} %bitcast.11), calls=%async_computation.3 | async-start | bytes 655360 | tf_op jit(solution)/shard_map/all_to_all | solution.py:519
  96.3 8.4 %all-to-all-done.3.got_hbm = bf16[16,8,1280]{2,1,0:T(8,128)(2,1)S(1)} async-done(((bf16[16,8,1280]{2,1,0:T(8,128)(2,1)}), bf16[16,8,1280]{2,1,0:T(8,128)(2,1)S(1)}, u32[]{:S(2)}, u32[]{:S(2)}) %all-to-all-start.3) | async-done | bytes 327712 | tf_op jit(solution)/shard_map/all_to_all | solution.py:519
  113.2 9.2 %shard_map.162 = (bf16[16,64,1024]{2,1,0:T(8,128)(2,1)}, f32[256,1024]{1,0:T(8,128)}, bf16[256,1024]{1,0:T(8,128)(2,1)}) custom-call(f32[8,1024]{1,0:T(8,128)} %copy-done.31, f32[8,1024]{1,0:T(8,128)} %copy-done.30, f32[8,1024]{1,0:T(8,128)} %copy-done.29, f32[8,1024]{1,0:T(8,128)} %copy-done.11, f32[1,1024]{1,0:T(1,128)} %bitcast.26, f32[8,128]{1,0:T(8,128)} %copy-done.12, ...), custom_call_target="tpu_custom_call" | custom-call | flops 3221225472 | bytes 10485760 | tf_op jit(solution)/shard_map/pallas_call | solution.py:331
  122.9 3.8 %all-to-all-start.4 = ((bf16[16,64,1024]{2,1,0:T(8,128)(2,1)}), bf16[16,64,1024]{2,1,0:T(8,128)(2,1)S(1)}, u32[]{:S(2)}, u32[]{:S(2)}) async-start(bf16[16,64,1024]{2,1,0:T(8,128)(2,1)} %get-tuple-element.86), calls=%async_computation.4 | async-start | bytes 4194304 | tf_op jit(solution)/shard_map/all_to_all | solution.py:546
  128.6 2.4 %collective-permute-start.17 = (bf16[128,1024]{1,0:T(8,128)(2,1)S(1)}, bf16[128,1024]{1,0:T(8,128)(2,1)S(1)}, u32[]{:S(2)}, u32[]{:S(2)}) collective-permute-start(bf16[128,1024]{1,0:T(8,128)(2,1)S(1)} %get-tuple-element.100), channel_id=1, source_target_pairs={{0,96},{96,0},{32,64},{64,32},{1,97},{97,1},{33,65},{65,33},{2,98}... | collective-permute-start | bytes 786440 | tf_op jit(solution)/shard_map/ppermute | solution.py:42
  131.0 4.8 %collective-permute-done.15 = bf16[128,1024]{1,0:T(8,128)(2,1)S(1)} collective-permute-done((bf16[128,1024]{1,0:T(8,128)(2,1)S(1)}, bf16[128,1024]{1,0:T(8,128)(2,1)S(1)}, u32[]{:S(2)}, u32[]{:S(2)}) %collective-permute-start.15) | collective-permute-done | bytes 262176 | tf_op jit(solution)/shard_map/ppermute | solution.py:30
  138.2 2.4 %collective-permute-start.16 = (bf16[128,1024]{1,0:T(8,128)(2,1)S(1)}, bf16[128,1024]{1,0:T(8,128)(2,1)S(1)}, u32[]{:S(2)}, u32[]{:S(2)}) collective-permute-start(bf16[128,1024]{1,0:T(8,128)(2,1)S(1)} %get-tuple-element.97), channel_id=1, source_target_pairs={{0,96},{96,0},{32,64},{64,32},{1,97},{97,1},{33,65},{65,33},{2,98}... | collective-permute-start | bytes 786440 | tf_op jit(solution)/shard_map/ppermute | solution.py:42
  141.2 4.7 %collective-permute-done.16 = bf16[128,1024]{1,0:T(8,128)(2,1)S(1)} collective-permute-done((bf16[128,1024]{1,0:T(8,128)(2,1)S(1)}, bf16[128,1024]{1,0:T(8,128)(2,1)S(1)}, u32[]{:S(2)}, u32[]{:S(2)}) %collective-permute-start.16) | collective-permute-done | bytes 262176 | tf_op jit(solution)/shard_map/ppermute | solution.py:42
  146.8 9.3 %all-to-all-done.4.got = bf16[16,64,1024]{2,1,0:T(8,128)(2,1)S(1)} async-done(((bf16[16,64,1024]{2,1,0:T(8,128)(2,1)}), bf16[16,64,1024]{2,1,0:T(8,128)(2,1)S(1)}, u32[]{:S(2)}, u32[]{:S(2)}) %all-to-all-start.4) | async-done | bytes 2097184 | tf_op jit(solution)/shard_map/all_to_all | solution.py:546
  159.9 2.7 %collective-permute-start.22 = (bf16[64,1024]{1,0:T(8,128)(2,1)S(1)}, bf16[64,1024]{1,0:T(8,128)(2,1)S(1)}, u32[]{:S(2)}, u32[]{:S(2)}) collective-permute-start(bf16[64,1024]{1,0:T(8,128)(2,1)S(1)} %maximum_maximum_fusion.own), channel_id=1, source_target_pairs={{0,64},{64,0},{1,65},{65,1},{2,66},{66,2},{3,67},{67,3},{4,68},{68... | collective-permute-start | bytes 393224 | tf_op jit(solution)/shard_map/ppermute | solution.py:38
  162.9 2.1 %divide_subtract_fusion = (f32[256,1024]{1,0:T(8,128)}, f32[256,1024]{1,0:T(8,128)}, f32[256,1024]{1,0:T(8,128)}) fusion(f32[256,1024]{1,0:T(8,128)S(1)} %copy-done.18, f32[128,1024]{1,0:T(8,128)S(1)} %convert_add_fusion, f32[128,1024]{1,0:T(8,128)S(1)} %copy-done.19, f32[256,1024]{1,0:T(8,128)S(1)} %copy-done.20, f32[256,1024]{1,0:T(8,128)S(1)} %copy-done.21), kind=kLoop, calls=%fused_computation.10 | loop fusion | flops 3407872 | bytes 7340032 | tf_op jit(solution)/shard_map/sub | solution.py:584
  166.5 2.9 %collective-permute-done.21.wrap = bf16[64,1024]{1,0:T(8,128)(2,1)S(1)} collective-permute-done((bf16[64,1024]{1,0:T(8,128)(2,1)S(1)}, bf16[64,1024]{1,0:T(8,128)(2,1)S(1)}, u32[]{:S(2)}, u32[]{:S(2)}) %collective-permute-start.21) | collective-permute-done | bytes 131104 | tf_op jit(solution)/shard_map/ppermute | solution.py:42
  169.5 1.9 %shard_map.164 = (f32[32,2048]{1,0:T(8,128)}, f32[64,1024]{1,0:T(8,128)}) custom-call(s32[3]{0:T(128)S(1)} %pad_add_fusion.meta, bf16[64,1024]{1,0:T(8,128)(2,1)S(1)} %maximum_maximum_fusion.own, bf16[64,1024]{1,0:T(8,128)(2,1)S(1)} %collective-permute-done.20.near, bf16[64,1024]{1,0:T(8,128)(2,1)S(1)} %collective-permute-done.21.wrap, ...), custom_call_target="tpu_custom_call" | custom-call | flops 67108864 | bytes 1048576 | tf_op jit(solution)/shard_map/pallas_call | solution.py:561
  (136 shorter events, 42.1 us)
Async XLA Ops:
  6.8 39.6 %collective-permute-start.5 = (bf16[256,1024]{1,0:T(8,128)(2,1)S(1)}, bf16[256,1024]{1,0:T(8,128)(2,1)S(1)}, u32[]{:S(2)}, u32[]{:S(2)}) collective-permute-start(bf16[256,1024]{1,0:T(8,128)(2,1)S(1)} %bitcast.20), channel_id=1, source_target_pairs={{0,32},{32,0},{1,33},{33,1},{2,34},{34,2},{3,35},{35,3},{4,36},{36... | collective-permute-start | bytes 1572872 | tf_op jit(solution)/shard_map/ppermute | solution.py:30
  8.2 38.2 %collective-permute-start.4 = (bf16[256,1024]{1,0:T(8,128)(2,1)S(1)}, bf16[256,1024]{1,0:T(8,128)(2,1)}, u32[]{:S(2)}, u32[]{:S(2)}) collective-permute-start(bf16[256,1024]{1,0:T(8,128)(2,1)S(1)} %bitcast.21), channel_id=1, source_target_pairs={{0,33},{33,0},{1,32},{32,1},{2,35},{35,2},{3,34},{34,3},{4,37},{37... | collective-permute-start | bytes 1572872 | tf_op jit(solution)/shard_map/ppermute | solution.py:34
  9.2 37.2 %all-to-all-start = ((bf16[16,64,1024]{2,1,0:T(8,128)(2,1)}), bf16[16,64,1024]{2,1,0:T(8,128)(2,1)}, u32[]{:S(2)}, u32[]{:S(2)}) async-start(bf16[16,64,1024]{2,1,0:T(8,128)(2,1)} %shard_map.155), calls=%async_computation | async-start | bytes 4194304 | tf_op jit(solution)/shard_map/all_to_all | solution.py:50
  17.3 11.1 %collective-permute-start.2 = (f32[256,1024]{1,0:T(8,128)S(1)}, f32[256,1024]{1,0:T(8,128)}, u32[]{:S(2)}, u32[]{:S(2)}) collective-permute-start(f32[256,1024]{1,0:T(8,128)S(1)} %copy-done.17), channel_id=1, source_target_pairs={{0,1},{1,0},{2,3},{3,2},{4,5},{5,4},{6,7},{7,6},{8,9},{9,8},{10,11... | collective-permute-start | bytes 3145736 | tf_op jit(solution)/shard_map/ppermute | solution.py:26
  50.7 3.2 %collective-permute-start.6 = (bf16[256,1024]{1,0:T(8,128)(2,1)S(1)}, bf16[256,1024]{1,0:T(8,128)(2,1)S(1)}, u32[]{:S(2)}, u32[]{:S(2)}) collective-permute-start(bf16[256,1024]{1,0:T(8,128)(2,1)S(1)} %get-tuple-element.61), channel_id=1, source_target_pairs={{0,1},{1,0},{2,3},{3,2},{4,5},{5,4},{6,7},{7,6},{8,9},{9,8},{10,11... | collective-permute-start | bytes 1572872 | tf_op jit(solution)/shard_map/ppermute | solution.py:26
  52.4 3.1 %collective-permute-start.1 = (bf16[256,1024]{1,0:T(8,128)(2,1)S(1)}, bf16[256,1024]{1,0:T(8,128)(2,1)S(1)}, u32[]{:S(2)}, u32[]{:S(2)}) collective-permute-start(bf16[256,1024]{1,0:T(8,128)(2,1)S(1)} %bitcast.22), channel_id=1, source_target_pairs={{0,1},{1,0},{2,3},{3,2},{4,5},{5,4},{6,7},{7,6},{8,9},{9,8},{10,11... | collective-permute-start | bytes 1572872 | tf_op jit(solution)/shard_map/ppermute | solution.py:26
  54.1 19.2 %collective-permute-start.7 = (bf16[256,1024]{1,0:T(8,128)(2,1)S(1)}, bf16[256,1024]{1,0:T(8,128)(2,1)S(1)}, u32[]{:S(2)}, u32[]{:S(2)}) collective-permute-start(bf16[256,1024]{1,0:T(8,128)(2,1)S(1)} %add_convert_fusion.1), channel_id=1, source_target_pairs={{0,32},{32,0},{1,33},{33,1},{2,34},{34,2},{3,35},{35,3},{4,36},{36... | collective-permute-start | bytes 1572872 | tf_op jit(solution)/shard_map/ppermute | solution.py:30
  59.6 13.7 %collective-permute-start.3 = (bf16[256,1024]{1,0:T(8,128)(2,1)S(1)}, bf16[256,1024]{1,0:T(8,128)(2,1)S(1)}, u32[]{:S(2)}, u32[]{:S(2)}) collective-permute-start(bf16[256,1024]{1,0:T(8,128)(2,1)S(1)} %get-tuple-element.59), channel_id=1, source_target_pairs={{0,1},{1,0},{2,3},{3,2},{4,5},{5,4},{6,7},{7,6},{8,9},{9,8},{10,11... | collective-permute-start | bytes 1572872 | tf_op jit(solution)/shard_map/ppermute | solution.py:26
  75.3 14.5 %collective-permute-start.8 = (bf16[256,1152]{1,0:T(8,128)(2,1)S(1)}, bf16[256,1152]{1,0:T(8,128)(2,1)}, u32[]{:S(2)}, u32[]{:S(2)}) collective-permute-start(bf16[256,1152]{1,0:T(8,128)(2,1)S(1)} %get-tuple-element.71.refs_9_), channel_id=1, source_target_pairs={{0,32},{32,0},{1,33},{33,1},{2,34},{34,2},{3,35},{35,3},{4,36},{36... | collective-permute-start | bytes 1769480 | tf_op jit(solution)/shard_map/ppermute | solution.py:30
  75.5 11.2 %all-to-all-start.2 = ((bf16[16,8,1024]{2,1,0:T(8,128)(2,1)}), bf16[16,8,1024]{2,1,0:T(8,128)(2,1)S(1)}, u32[]{:S(2)}, u32[]{:S(2)}) async-start(bf16[16,8,1024]{2,1,0:T(8,128)(2,1)} %bitcast.9), calls=%async_computation.2 | async-start | bytes 524288 | tf_op jit(solution)/shard_map/all_to_all | solution.py:50
  79.4 30.1 %collective-permute-start.13 = (bf16[256,1152]{1,0:T(8,128)(2,1)S(1)}, bf16[256,1152]{1,0:T(8,128)(2,1)}, u32[]{:S(2)}, u32[]{:S(2)}) collective-permute-start(bf16[256,1152]{1,0:T(8,128)(2,1)S(1)} %get-tuple-element.71.refs_9_), channel_id=1, source_target_pairs={{0,1},{1,0},{2,3},{3,2},{4,5},{5,4},{6,7},{7,6},{8,9},{9,8},{10,11... | collective-permute-start | bytes 1769480 | tf_op jit(solution)/shard_map/ppermute | solution.py:26
  89.8 22.6 %collective-permute-start.12 = (bf16[256,1152]{1,0:T(8,128)(2,1)}, bf16[256,1152]{1,0:T(8,128)(2,1)S(1)}, u32[]{:S(2)}, u32[]{:S(2)}) collective-permute-start(bf16[256,1152]{1,0:T(8,128)(2,1)} %collective-permute-done.8.refs_7_), channel_id=1, source_target_pairs={{0,1},{1,0},{2,3},{3,2},{4,5},{5,4},{6,7},{7,6},{8,9},{9,8},{10,11... | collective-permute-start | bytes 1769480 | tf_op jit(solution)/shard_map/ppermute | solution.py:26
  92.7 12.0 %all-to-all-start.3 = ((bf16[16,8,1280]{2,1,0:T(8,128)(2,1)}), bf16[16,8,1280]{2,1,0:T(8,128)(2,1)S(1)}, u32[]{:S(2)}, u32[]{:S(2)}) async-start(bf16[16,8,1280]{2,1,0:T(8,128)(2,1)} %bitcast.11), calls=%async_computation.3 | async-start | bytes 655360 | tf_op jit(solution)/shard_map/all_to_all | solution.py:519
  105.9 3.5 %collective-permute-start.11 = (f32[8,1024]{1,0:T(8,128)S(1)}, f32[8,1024]{1,0:T(8,128)S(1)}, u32[]{:S(2)}, u32[]{:S(2)}) collective-permute-start(f32[8,1024]{1,0:T(8,128)S(1)} %get-tuple-element.75.refs_3_), channel_id=1, source_target_pairs={{0,1},{1,0},{2,3},{3,2},{4,5},{5,4},{6,7},{7,6},{8,9},{9,8},{10,11... | collective-permute-start | bytes 98312 | tf_op jit(solution)/shard_map/ppermute | solution.py:26
  109.0 3.4 %collective-permute-start.9 = (f32[8,1024]{1,0:T(8,128)S(1)}, f32[8,1024]{1,0:T(8,128)S(1)}, u32[]{:S(2)}, u32[]{:S(2)}) collective-permute-start(f32[8,1024]{1,0:T(8,128)S(1)} %get-tuple-element.75.refs_3_), channel_id=1, source_target_pairs={{0,33},{33,0},{1,32},{32,1},{2,35},{35,2},{3,34},{34,3},{4,37},{37... | collective-permute-start | bytes 98312 | tf_op jit(solution)/shard_map/ppermute | solution.py:34
  122.5 4.3 %collective-permute-start.14 = (bf16[256,1024]{1,0:T(8,128)(2,1)}, bf16[256,1024]{1,0:T(8,128)(2,1)}, u32[]{:S(2)}, u32[]{:S(2)}) collective-permute-start(bf16[256,1024]{1,0:T(8,128)(2,1)} %get-tuple-element.85), channel_id=1, source_target_pairs={{0,1},{1,0},{2,3},{3,2},{4,5},{5,4},{6,7},{7,6},{8,9},{9,8},{10,11... | collective-permute-start | bytes 1572872 | tf_op jit(solution)/shard_map/ppermute | solution.py:26
  122.9 33.1 %all-to-all-start.4 = ((bf16[16,64,1024]{2,1,0:T(8,128)(2,1)}), bf16[16,64,1024]{2,1,0:T(8,128)(2,1)S(1)}, u32[]{:S(2)}, u32[]{:S(2)}) async-start(bf16[16,64,1024]{2,1,0:T(8,128)(2,1)} %get-tuple-element.86), calls=%async_computation.4 | async-start | bytes 4194304 | tf_op jit(solution)/shard_map/all_to_all | solution.py:546
  128.0 7.8 %collective-permute-start.15 = (bf16[128,1024]{1,0:T(8,128)(2,1)S(1)}, bf16[128,1024]{1,0:T(8,128)(2,1)S(1)}, u32[]{:S(2)}, u32[]{:S(2)}) collective-permute-start(bf16[128,1024]{1,0:T(8,128)(2,1)S(1)} %get-tuple-element.99), channel_id=1, source_target_pairs={{0,32},{32,0},{1,33},{33,1},{2,34},{34,2},{3,35},{35,3},{4,36},{36... | collective-permute-start | bytes 786440 | tf_op jit(solution)/shard_map/ppermute | solution.py:30
  128.6 8.6 %collective-permute-start.17 = (bf16[128,1024]{1,0:T(8,128)(2,1)S(1)}, bf16[128,1024]{1,0:T(8,128)(2,1)S(1)}, u32[]{:S(2)}, u32[]{:S(2)}) collective-permute-start(bf16[128,1024]{1,0:T(8,128)(2,1)S(1)} %get-tuple-element.100), channel_id=1, source_target_pairs={{0,96},{96,0},{32,64},{64,32},{1,97},{97,1},{33,65},{65,33},{2,98}... | collective-permute-start | bytes 786440 | tf_op jit(solution)/shard_map/ppermute | solution.py:42
  138.2 7.7 %collective-permute-start.16 = (bf16[128,1024]{1,0:T(8,128)(2,1)S(1)}, bf16[128,1024]{1,0:T(8,128)(2,1)S(1)}, u32[]{:S(2)}, u32[]{:S(2)}) collective-permute-start(bf16[128,1024]{1,0:T(8,128)(2,1)S(1)} %get-tuple-element.97), channel_id=1, source_target_pairs={{0,96},{96,0},{32,64},{64,32},{1,97},{97,1},{33,65},{65,33},{2,98}... | collective-permute-start | bytes 786440 | tf_op jit(solution)/shard_map/ppermute | solution.py:42
  140.5 18.2 %collective-permute-start.18 = (bf16[128,1024]{1,0:T(8,128)(2,1)}, bf16[128,1024]{1,0:T(8,128)(2,1)}, u32[]{:S(2)}, u32[]{:S(2)}) collective-permute-start(bf16[128,1024]{1,0:T(8,128)(2,1)} %get-tuple-element.98), channel_id=1, source_target_pairs={{0,32},{32,0},{1,33},{33,1},{2,34},{34,2},{3,35},{35,3},{4,36},{36... | collective-permute-start | bytes 786440 | tf_op jit(solution)/shard_map/ppermute | solution.py:30
  159.9 6.6 %collective-permute-start.22 = (bf16[64,1024]{1,0:T(8,128)(2,1)S(1)}, bf16[64,1024]{1,0:T(8,128)(2,1)S(1)}, u32[]{:S(2)}, u32[]{:S(2)}) collective-permute-start(bf16[64,1024]{1,0:T(8,128)(2,1)S(1)} %maximum_maximum_fusion.own), channel_id=1, source_target_pairs={{0,64},{64,0},{1,65},{65,1},{2,66},{66,2},{3,67},{67,3},{4,68},{68... | collective-permute-start | bytes 393224 | tf_op jit(solution)/shard_map/ppermute | solution.py:38
  162.6 6.9 %collective-permute-start.21 = (bf16[64,1024]{1,0:T(8,128)(2,1)S(1)}, bf16[64,1024]{1,0:T(8,128)(2,1)S(1)}, u32[]{:S(2)}, u32[]{:S(2)}) collective-permute-start(bf16[64,1024]{1,0:T(8,128)(2,1)S(1)} %maximum_maximum_fusion.own), channel_id=1, source_target_pairs={{0,96},{96,0},{32,64},{64,32},{1,97},{97,1},{33,65},{65,33},{2,98}... | collective-permute-start | bytes 393224 | tf_op jit(solution)/shard_map/ppermute | solution.py:42
  162.9 6.6 %collective-permute-start.20 = (bf16[64,1024]{1,0:T(8,128)(2,1)S(1)}, bf16[64,1024]{1,0:T(8,128)(2,1)S(1)}, u32[]{:S(2)}, u32[]{:S(2)}) collective-permute-start(bf16[64,1024]{1,0:T(8,128)(2,1)S(1)} %maximum_maximum_fusion.own), channel_id=1, source_target_pairs={{0,32},{32,0},{1,33},{33,1},{2,34},{34,2},{3,35},{35,3},{4,36},{36... | collective-permute-start | bytes 393224 | tf_op jit(solution)/shard_map/ppermute | solution.py:30
  (35 other events, 281.7 us)

commit v11 on v10

--- a/solution.py
+++ b/solution.py
@@ -85,9 +85,8 @@
         theirs[:, i * 128 : i * 128 + 128] = got[:, 128:]
 
 
-def lay_kernel(mine, theirs, w_out, out, block, sems):
+def lay_kernel(mine, theirs, top, out, block, sems):
     core, role = place_of()
-    top = w_out.at[pl.ds(pl.multiple_of(role * 32, 32), 32)]
     copies = [pltpu.make_async_copy(top, out.at[i, 0:32], sems.at[i]) for i in range(16)]
     for copy in copies:
         copy.start()
@@ -243,12 +242,13 @@
     ]
     for copy in tile_copies:
         copy.start()
-    first.start()
     row_copies, tok_copies, hid_copies, slope_copies = [], [], [], []
     for k in range(4):
         at = pl.ds(k * 256, 256)
         row_copies.append(pltpu.make_async_copy(rows[k], row_buf.at[at], sems.at[1 + k]))
         row_copies[k].start()
+        if k == 0:
+            first.start()
     for k in range(2):
         at = pl.ds(k * 512, 512)
         slope_copies.append(pltpu.make_async_copy(slopes[k], slope_buf.at[at], sems.at[5 + k]))
@@ -435,12 +435,12 @@
     block = pl.pallas_call(
         lay_kernel,
         out_shape=shape((16, 64, width), BF16),
-        in_specs=[WHOLE, WHOLE, ANYWHERE],
+        in_specs=[WHOLE, WHOLE, WHOLE],
         out_specs=ANYWHERE,
         scratch_shapes=[pltpu.VMEM((32, width), BF16), pltpu.SemaphoreType.DMA((32,))],
         compiler_params=LIMIT,
         cost_estimate=cost(0, 2**21),
-    )(mine, swap_core(theirs), w_out)
+    )(mine, swap_core(theirs), lax.dynamic_slice_in_dim(w_out, role * 32, 32, 0))
     block, own_tok, label_tiles, shortlist, positives, owner_map = lax.optimization_barrier(
         (block, own_tok, label_tiles, shortlist, positives, owner_map)
     )

time: 172 us -> 172 us (level)
    unnamed x65 -> x59, local copies, waits for them, and re-layouts: 4.31 us -> 3.41 us
where the time goes in v11:
time: 172 us; the launch traced here: 171 us
  waiting for transfers between devices  58.5 us (34%)
  starting transfers between devices  45.8 us (27%)
  Pallas kernels  28.1 us (16%)
  other arithmetic  17.2 us (10%)
  blocking collectives  13 us (8%)
  local copies, waits for them, and re-layouts  6.14 us (4%)
    all_to_all x2, waiting for transfers between devices, gather_chips(): return lax.all_to_all(a, CHIPS, 0, 0, tiled=True)  20.3 us
    all_to_all x1, blocking collectives, gather_chips(): return lax.all_to_all(a, CHIPS, 0, 0, tiled=True)  13 us
    ppermute x10, starting transfers between devices, swap_core(): return lax.ppermute(a, 'c', [(0, 1), (1, 0)])  13 us
    all_to_all x2, starting transfers between devices, gather_chips(): return lax.all_to_all(a, CHIPS, 0, 0, tiled=True)  11.6 us
    reduce_max x1, other arithmetic, on_device(): jnp.max((short[:, :, None] == cluster_ids[None, None, :]).astype(F32), ax...  9.9 us
    pallas_call x1, Pallas kernels, backward(): pl.pallas_call(backward_kernel, out_shape=(shape((16, 64, 1024), BF16), s...  9.28 us
    all_to_all x1, waiting for transfers between devices, on_device(): got = lax.all_to_all(send, CHIPS, 0, 0, tiled=True)  9.28 us
    ppermute x3, waiting for transfers between devices, swap_wrap(): return lax.ppermute(a, ('h', 'l'), [(0, 3), (3, 0), (1, 2), (2, 1)])  9.07 us
  transfers between devices with their start and end apart: 27, of which 13 were waited for; matrix products, arithmetic and copies ran while one was open for 12% of the time, Pallas kernels for 5%

profile of v11, /device:TPU:1, one launch (start us, length us, event | category | flops | bytes accessed | tf_op | source)
XLA Modules:
  0.0 171.2 jit_solution(3590797148968973155)
XLA Ops:
  8.4 7.9 %all-to-all-start = ((bf16[16,64,1024]{2,1,0:T(8,128)(2,1)}), bf16[16,64,1024]{2,1,0:T(8,128)(2,1)}, u32[]{:S(2)}, u32[]{:S(2)}) async-start(bf16[16,64,1024]{2,1,0:T(8,128)(2,1)} %shard_map.155), calls=%async_computation | async-start | bytes 4194304 | tf_op jit(solution)/shard_map/all_to_all | solution.py:50
  17.7 9.9 %convert_reduce_fusion.live = bf16[128,128]{1,0:T(8,128)(2,1)S(1)} fusion(s32[128]{0:T(128)S(1)} %select_reduce_fusion, s32[128,400]{1,0:T(8,128)S(1)} %dynamic-slice_bitcast_fusion), kind=kLoop, calls=%fused_computation | loop fusion | flops 19644416 | bytes 238080 | tf_op jit(solution)/shard_map/reduce_max | solution.py:460
  30.7 14.8 %all-to-all-done.weights.refs_18_ = bf16[16,64,1024]{2,1,0:T(8,128)(2,1)} async-done(((bf16[16,64,1024]{2,1,0:T(8,128)(2,1)}), bf16[16,64,1024]{2,1,0:T(8,128)(2,1)}, u32[]{:S(2)}, u32[]{:S(2)}) %all-to-all-start) | async-done | bytes 2097184 | tf_op jit(solution)/shard_map/all_to_all | solution.py:50
  45.5 4.2 %shard_map.158 = (bf16[256,1024]{1,0:T(8,128)(2,1)S(1)}, f32[256,1024]{1,0:T(8,128)S(1)}, bf16[512,512]{1,0:T(8,128)(2,1)S(1)}, f32[512,512]{1,0:T(8,128)S(1)}) custom-call(bf16[256,1024]{1,0:T(8,128)(2,1)} %collective-permute-done.4.tok_a.refs_10_, bf16[256,1024]{1,0:T(8,128)(2,1)} %collective-permute-done.5.tok_b.refs_11_, ...), custom_call_target="tpu_custom_call" | custom-call | flops 1073741824 | bytes 6291456 | tf_op jit(solution)/shard_map/pallas_call | solution.py:130
  54.6 3.2 %shard_map.157 = (bf16[256,1024]{1,0:T(8,128)(2,1)S(1)}, f32[256,1024]{1,0:T(8,128)S(1)}, bf16[512,512]{1,0:T(8,128)(2,1)S(1)}, f32[512,512]{1,0:T(8,128)S(1)}) custom-call(bf16[256,1024]{1,0:T(8,128)(2,1)S(1)} %collective-permute-done.1.tok_a.refs_12_, bf16[256,1024]{1,0:T(8,128)(2,1)S(1)} %bitcast.23, bf16[16,64,1024]{2,1,0:T(8,128)(2,1)} %all-to-all-done.weights.refs_18_), custom_call_target="tpu_custom_call" | custom-call | flops 68719476736 | bytes 6291456 | tf_op jit(solution)/shard_map/pallas_call | solution.py:130
  59.3 13.0 %all_to_all.25 = f16[16,8,1024]{2,1,0:T(8,128)(2,1)S(1)} all-to-all(f16[16,8,1024]{2,1,0:T(8,128)(2,1)S(1)} %bitcast.29), channel_id=1, replica_groups=mesh['h'=2,'l'=2,'x'=4,'z'=4,'c'=2] {'x','z'}, dimensions={0} | all-to-all | bytes 524288 | tf_op jit(solution)/shard_map/all_to_all | solution.py:50
  72.3 2.8 %shard_map.159 = (bf16[256,1152]{1,0:T(8,128)(2,1)}, bf16[128,1024]{1,0:T(8,128)(2,1)}) custom-call(s32[8]{0:T(128)S(1)} %copy-done.6, bf16[256,1024]{1,0:T(8,128)(2,1)S(1)} %bitcast.24, f32[256,1024]{1,0:T(8,128)S(1)} %get-tuple-element.58.part, bf16[256,1024]{1,0:T(8,128)(2,1)S(1)} %collective-permute-done.3.from_core, ...), custom_call_target="tpu_custom_call" | custom-call | flops 4194304 | bytes 4194304 | tf_op jit(solution)/shard_map/pallas_call | solution.py:492
  75.3 3.8 %all-to-all-start.2 = ((bf16[16,8,1024]{2,1,0:T(8,128)(2,1)}), bf16[16,8,1024]{2,1,0:T(8,128)(2,1)S(1)}, u32[]{:S(2)}, u32[]{:S(2)}) async-start(bf16[16,8,1024]{2,1,0:T(8,128)(2,1)} %bitcast.9), calls=%async_computation.2 | async-start | bytes 524288 | tf_op jit(solution)/shard_map/all_to_all | solution.py:50
  79.1 1.9 %collective-permute-start.13 = (bf16[256,1152]{1,0:T(8,128)(2,1)}, bf16[256,1152]{1,0:T(8,128)(2,1)}, u32[]{:S(2)}, u32[]{:S(2)}) collective-permute-start(bf16[256,1152]{1,0:T(8,128)(2,1)} %get-tuple-element.71.refs_9_), channel_id=1, source_target_pairs={{0,1},{1,0},{2,3},{3,2},{4,5},{5,4},{6,7},{7,6},{8,9},{9,8},{10,11... | collective-permute-start | bytes 1769480 | tf_op jit(solution)/shard_map/ppermute | solution.py:26
  81.0 5.4 %all-to-all-done.2 = bf16[16,8,1024]{2,1,0:T(8,128)(2,1)S(1)} async-done(((bf16[16,8,1024]{2,1,0:T(8,128)(2,1)}), bf16[16,8,1024]{2,1,0:T(8,128)(2,1)S(1)}, u32[]{:S(2)}, u32[]{:S(2)}) %all-to-all-start.2) | async-done | bytes 262176 | tf_op jit(solution)/shard_map/all_to_all | solution.py:50
  86.4 2.3 %shard_map.160 = (bf16[128,1280]{1,0:T(8,128)(2,1)}, f32[128,512]{1,0:T(8,128)S(1)}) custom-call(bf16[128,1024]{1,0:T(8,128)(2,1)S(1)} %bitcast.17, bf16[512,1024]{1,0:T(8,128)(2,1)S(1)} %get-tuple-element.67.tiles_hi, bf16[512,1024]{1,0:T(8,128)(2,1)S(1)} %get-tuple-element.68.tiles_lo, bf16[128,128]{1,0:T(8,128)(2,1)S(1)} %convert_reduce_fusion.live), custom_call_target="tpu_custom_call" | custom-call | flops 536870912 | bytes 3145728 | tf_op jit(solution)/shard_map/pallas_call | solution.py:504
  89.4 3.0 %collective-permute-start.12 = (bf16[256,1152]{1,0:T(8,128)(2,1)}, bf16[256,1152]{1,0:T(8,128)(2,1)S(1)}, u32[]{:S(2)}, u32[]{:S(2)}) collective-permute-start(bf16[256,1152]{1,0:T(8,128)(2,1)} %collective-permute-done.8.refs_7_), channel_id=1, source_target_pairs={{0,1},{1,0},{2,3},{3,2},{4,5},{5,4},{6,7},{7,6},{8,9},{9,8},{10,11... | collective-permute-start | bytes 1769480 | tf_op jit(solution)/shard_map/ppermute | solution.py:26
  92.5 3.5 %all-to-all-start.3 = ((bf16[16,8,1280]{2,1,0:T(8,128)(2,1)}), bf16[16,8,1280]{2,1,0:T(8,128)(2,1)S(1)}, u32[]{:S(2)}, u32[]{:S(2)}) async-start(bf16[16,8,1280]{2,1,0:T(8,128)(2,1)} %bitcast.11), calls=%async_computation.3 | async-start | bytes 655360 | tf_op jit(solution)/shard_map/all_to_all | solution.py:519
  96.1 8.4 %all-to-all-done.3.got_hbm = bf16[16,8,1280]{2,1,0:T(8,128)(2,1)S(1)} async-done(((bf16[16,8,1280]{2,1,0:T(8,128)(2,1)}), bf16[16,8,1280]{2,1,0:T(8,128)(2,1)S(1)}, u32[]{:S(2)}, u32[]{:S(2)}) %all-to-all-start.3) | async-done | bytes 327712 | tf_op jit(solution)/shard_map/all_to_all | solution.py:519
  113.0 9.3 %shard_map.162 = (bf16[16,64,1024]{2,1,0:T(8,128)(2,1)}, f32[256,1024]{1,0:T(8,128)}, bf16[256,1024]{1,0:T(8,128)(2,1)}) custom-call(f32[8,1024]{1,0:T(8,128)} %copy-done.28, f32[8,1024]{1,0:T(8,128)} %copy-done.27, f32[8,1024]{1,0:T(8,128)} %copy-done.26, f32[8,1024]{1,0:T(8,128)} %copy-done.9, f32[1,1024]{1,0:T(1,128)} %bitcast.26, f32[8,128]{1,0:T(8,128)} %copy-done.10, ...), custom_call_target="tpu_custom_call" | custom-call | flops 3221225472 | bytes 10485760 | tf_op jit(solution)/shard_map/pallas_call | solution.py:331
  122.7 3.8 %all-to-all-start.4 = ((bf16[16,64,1024]{2,1,0:T(8,128)(2,1)}), bf16[16,64,1024]{2,1,0:T(8,128)(2,1)S(1)}, u32[]{:S(2)}, u32[]{:S(2)}) async-start(bf16[16,64,1024]{2,1,0:T(8,128)(2,1)} %get-tuple-element.86), calls=%async_computation.4 | async-start | bytes 4194304 | tf_op jit(solution)/shard_map/all_to_all | solution.py:546
  128.5 2.4 %collective-permute-start.17 = (bf16[128,1024]{1,0:T(8,128)(2,1)S(1)}, bf16[128,1024]{1,0:T(8,128)(2,1)S(1)}, u32[]{:S(2)}, u32[]{:S(2)}) collective-permute-start(bf16[128,1024]{1,0:T(8,128)(2,1)S(1)} %get-tuple-element.100), channel_id=1, source_target_pairs={{0,96},{96,0},{32,64},{64,32},{1,97},{97,1},{33,65},{65,33},{2,98}... | collective-permute-start | bytes 786440 | tf_op jit(solution)/shard_map/ppermute | solution.py:42
  130.9 4.8 %collective-permute-done.15 = bf16[128,1024]{1,0:T(8,128)(2,1)S(1)} collective-permute-done((bf16[128,1024]{1,0:T(8,128)(2,1)S(1)}, bf16[128,1024]{1,0:T(8,128)(2,1)S(1)}, u32[]{:S(2)}, u32[]{:S(2)}) %collective-permute-start.15) | collective-permute-done | bytes 262176 | tf_op jit(solution)/shard_map/ppermute | solution.py:30
  138.0 2.4 %collective-permute-start.16 = (bf16[128,1024]{1,0:T(8,128)(2,1)S(1)}, bf16[128,1024]{1,0:T(8,128)(2,1)S(1)}, u32[]{:S(2)}, u32[]{:S(2)}) collective-permute-start(bf16[128,1024]{1,0:T(8,128)(2,1)S(1)} %get-tuple-element.97), channel_id=1, source_target_pairs={{0,96},{96,0},{32,64},{64,32},{1,97},{97,1},{33,65},{65,33},{2,98}... | collective-permute-start | bytes 786440 | tf_op jit(solution)/shard_map/ppermute | solution.py:42
  141.1 4.7 %collective-permute-done.16 = bf16[128,1024]{1,0:T(8,128)(2,1)S(1)} collective-permute-done((bf16[128,1024]{1,0:T(8,128)(2,1)S(1)}, bf16[128,1024]{1,0:T(8,128)(2,1)S(1)}, u32[]{:S(2)}, u32[]{:S(2)}) %collective-permute-start.16) | collective-permute-done | bytes 262176 | tf_op jit(solution)/shard_map/ppermute | solution.py:42
  146.6 9.3 %all-to-all-done.4.got = bf16[16,64,1024]{2,1,0:T(8,128)(2,1)S(1)} async-done(((bf16[16,64,1024]{2,1,0:T(8,128)(2,1)}), bf16[16,64,1024]{2,1,0:T(8,128)(2,1)S(1)}, u32[]{:S(2)}, u32[]{:S(2)}) %all-to-all-start.4) | async-done | bytes 2097184 | tf_op jit(solution)/shard_map/all_to_all | solution.py:546
  159.7 2.7 %collective-permute-start.22 = (bf16[64,1024]{1,0:T(8,128)(2,1)S(1)}, bf16[64,1024]{1,0:T(8,128)(2,1)S(1)}, u32[]{:S(2)}, u32[]{:S(2)}) collective-permute-start(bf16[64,1024]{1,0:T(8,128)(2,1)S(1)} %maximum_maximum_fusion.own), channel_id=1, source_target_pairs={{0,64},{64,0},{1,65},{65,1},{2,66},{66,2},{3,67},{67,3},{4,68},{68... | collective-permute-start | bytes 393224 | tf_op jit(solution)/shard_map/ppermute | solution.py:38
  162.8 2.1 %divide_subtract_fusion = (f32[256,1024]{1,0:T(8,128)}, f32[256,1024]{1,0:T(8,128)}, f32[256,1024]{1,0:T(8,128)}) fusion(f32[256,1024]{1,0:T(8,128)S(1)} %copy-done.16, f32[128,1024]{1,0:T(8,128)S(1)} %convert_add_fusion, f32[128,1024]{1,0:T(8,128)S(1)} %copy-done.17, f32[256,1024]{1,0:T(8,128)S(1)} %copy-done.18, f32[256,1024]{1,0:T(8,128)S(1)} %copy-done.19), kind=kLoop, calls=%fused_computation.10 | loop fusion | flops 3407872 | bytes 7340032 | tf_op jit(solution)/shard_map/sub | solution.py:584
  166.4 3.0 %collective-permute-done.21.wrap = bf16[64,1024]{1,0:T(8,128)(2,1)S(1)} collective-permute-done((bf16[64,1024]{1,0:T(8,128)(2,1)S(1)}, bf16[64,1024]{1,0:T(8,128)(2,1)S(1)}, u32[]{:S(2)}, u32[]{:S(2)}) %collective-permute-start.21) | collective-permute-done | bytes 131104 | tf_op jit(solution)/shard_map/ppermute | solution.py:42
  (131 shorter events, 41.3 us)
Async XLA Ops:
  5.9 39.6 %collective-permute-start.5 = (bf16[256,1024]{1,0:T(8,128)(2,1)S(1)}, bf16[256,1024]{1,0:T(8,128)(2,1)}, u32[]{:S(2)}, u32[]{:S(2)}) collective-permute-start(bf16[256,1024]{1,0:T(8,128)(2,1)S(1)} %bitcast.20), channel_id=1, source_target_pairs={{0,32},{32,0},{1,33},{33,1},{2,34},{34,2},{3,35},{35,3},{4,36},{36... | collective-permute-start | bytes 1572872 | tf_op jit(solution)/shard_map/ppermute | solution.py:30
  7.4 38.2 %collective-permute-start.4 = (bf16[256,1024]{1,0:T(8,128)(2,1)S(1)}, bf16[256,1024]{1,0:T(8,128)(2,1)}, u32[]{:S(2)}, u32[]{:S(2)}) collective-permute-start(bf16[256,1024]{1,0:T(8,128)(2,1)S(1)} %bitcast.21), channel_id=1, source_target_pairs={{0,33},{33,0},{1,32},{32,1},{2,35},{35,2},{3,34},{34,3},{4,37},{37... | collective-permute-start | bytes 1572872 | tf_op jit(solution)/shard_map/ppermute | solution.py:34
  8.4 37.2 %all-to-all-start = ((bf16[16,64,1024]{2,1,0:T(8,128)(2,1)}), bf16[16,64,1024]{2,1,0:T(8,128)(2,1)}, u32[]{:S(2)}, u32[]{:S(2)}) async-start(bf16[16,64,1024]{2,1,0:T(8,128)(2,1)} %shard_map.155), calls=%async_computation | async-start | bytes 4194304 | tf_op jit(solution)/shard_map/all_to_all | solution.py:50
  16.4 11.1 %collective-permute-start.2 = (f32[256,1024]{1,0:T(8,128)S(1)}, f32[256,1024]{1,0:T(8,128)}, u32[]{:S(2)}, u32[]{:S(2)}) collective-permute-start(f32[256,1024]{1,0:T(8,128)S(1)} %copy-done.15), channel_id=1, source_target_pairs={{0,1},{1,0},{2,3},{3,2},{4,5},{5,4},{6,7},{7,6},{8,9},{9,8},{10,11... | collective-permute-start | bytes 3145736 | tf_op jit(solution)/shard_map/ppermute | solution.py:26
  49.8 3.2 %collective-permute-start.6 = (bf16[256,1024]{1,0:T(8,128)(2,1)S(1)}, bf16[256,1024]{1,0:T(8,128)(2,1)S(1)}, u32[]{:S(2)}, u32[]{:S(2)}) collective-permute-start(bf16[256,1024]{1,0:T(8,128)(2,1)S(1)} %get-tuple-element.61), channel_id=1, source_target_pairs={{0,1},{1,0},{2,3},{3,2},{4,5},{5,4},{6,7},{7,6},{8,9},{9,8},{10,11... | collective-permute-start | bytes 1572872 | tf_op jit(solution)/shard_map/ppermute | solution.py:26
  51.5 3.1 %collective-permute-start.1 = (bf16[256,1024]{1,0:T(8,128)(2,1)S(1)}, bf16[256,1024]{1,0:T(8,128)(2,1)S(1)}, u32[]{:S(2)}, u32[]{:S(2)}) collective-permute-start(bf16[256,1024]{1,0:T(8,128)(2,1)S(1)} %bitcast.22), channel_id=1, source_target_pairs={{0,1},{1,0},{2,3},{3,2},{4,5},{5,4},{6,7},{7,6},{8,9},{9,8},{10,11... | collective-permute-start | bytes 1572872 | tf_op jit(solution)/shard_map/ppermute | solution.py:26
  53.2 19.1 %collective-permute-start.7 = (bf16[256,1024]{1,0:T(8,128)(2,1)S(1)}, bf16[256,1024]{1,0:T(8,128)(2,1)S(1)}, u32[]{:S(2)}, u32[]{:S(2)}) collective-permute-start(bf16[256,1024]{1,0:T(8,128)(2,1)S(1)} %add_convert_fusion.1), channel_id=1, source_target_pairs={{0,32},{32,0},{1,33},{33,1},{2,34},{34,2},{3,35},{35,3},{4,36},{36... | collective-permute-start | bytes 1572872 | tf_op jit(solution)/shard_map/ppermute | solution.py:30
  58.7 13.6 %collective-permute-start.3 = (bf16[256,1024]{1,0:T(8,128)(2,1)S(1)}, bf16[256,1024]{1,0:T(8,128)(2,1)S(1)}, u32[]{:S(2)}, u32[]{:S(2)}) collective-permute-start(bf16[256,1024]{1,0:T(8,128)(2,1)S(1)} %get-tuple-element.59), channel_id=1, source_target_pairs={{0,1},{1,0},{2,3},{3,2},{4,5},{5,4},{6,7},{7,6},{8,9},{9,8},{10,11... | collective-permute-start | bytes 1572872 | tf_op jit(solution)/shard_map/ppermute | solution.py:26
  75.1 14.3 %collective-permute-start.8 = (bf16[256,1152]{1,0:T(8,128)(2,1)}, bf16[256,1152]{1,0:T(8,128)(2,1)}, u32[]{:S(2)}, u32[]{:S(2)}) collective-permute-start(bf16[256,1152]{1,0:T(8,128)(2,1)} %get-tuple-element.71.refs_9_), channel_id=1, source_target_pairs={{0,32},{32,0},{1,33},{33,1},{2,34},{34,2},{3,35},{35,3},{4,36},{36... | collective-permute-start | bytes 1769480 | tf_op jit(solution)/shard_map/ppermute | solution.py:30
  75.3 11.1 %all-to-all-start.2 = ((bf16[16,8,1024]{2,1,0:T(8,128)(2,1)}), bf16[16,8,1024]{2,1,0:T(8,128)(2,1)S(1)}, u32[]{:S(2)}, u32[]{:S(2)}) async-start(bf16[16,8,1024]{2,1,0:T(8,128)(2,1)} %bitcast.9), calls=%async_computation.2 | async-start | bytes 524288 | tf_op jit(solution)/shard_map/all_to_all | solution.py:50
  79.1 30.2 %collective-permute-start.13 = (bf16[256,1152]{1,0:T(8,128)(2,1)}, bf16[256,1152]{1,0:T(8,128)(2,1)}, u32[]{:S(2)}, u32[]{:S(2)}) collective-permute-start(bf16[256,1152]{1,0:T(8,128)(2,1)} %get-tuple-element.71.refs_9_), channel_id=1, source_target_pairs={{0,1},{1,0},{2,3},{3,2},{4,5},{5,4},{6,7},{7,6},{8,9},{9,8},{10,11... | collective-permute-start | bytes 1769480 | tf_op jit(solution)/shard_map/ppermute | solution.py:26
  89.4 22.8 %collective-permute-start.12 = (bf16[256,1152]{1,0:T(8,128)(2,1)}, bf16[256,1152]{1,0:T(8,128)(2,1)S(1)}, u32[]{:S(2)}, u32[]{:S(2)}) collective-permute-start(bf16[256,1152]{1,0:T(8,128)(2,1)} %collective-permute-done.8.refs_7_), channel_id=1, source_target_pairs={{0,1},{1,0},{2,3},{3,2},{4,5},{5,4},{6,7},{7,6},{8,9},{9,8},{10,11... | collective-permute-start | bytes 1769480 | tf_op jit(solution)/shard_map/ppermute | solution.py:26
  92.5 12.0 %all-to-all-start.3 = ((bf16[16,8,1280]{2,1,0:T(8,128)(2,1)}), bf16[16,8,1280]{2,1,0:T(8,128)(2,1)S(1)}, u32[]{:S(2)}, u32[]{:S(2)}) async-start(bf16[16,8,1280]{2,1,0:T(8,128)(2,1)} %bitcast.11), calls=%async_computation.3 | async-start | bytes 655360 | tf_op jit(solution)/shard_map/all_to_all | solution.py:519
  105.7 3.6 %collective-permute-start.11 = (f32[8,1024]{1,0:T(8,128)S(1)}, f32[8,1024]{1,0:T(8,128)S(1)}, u32[]{:S(2)}, u32[]{:S(2)}) collective-permute-start(f32[8,1024]{1,0:T(8,128)S(1)} %get-tuple-element.75.refs_3_), channel_id=1, source_target_pairs={{0,1},{1,0},{2,3},{3,2},{4,5},{5,4},{6,7},{7,6},{8,9},{9,8},{10,11... | collective-permute-start | bytes 98312 | tf_op jit(solution)/shard_map/ppermute | solution.py:26
  108.8 3.4 %collective-permute-start.9 = (f32[8,1024]{1,0:T(8,128)S(1)}, f32[8,1024]{1,0:T(8,128)S(1)}, u32[]{:S(2)}, u32[]{:S(2)}) collective-permute-start(f32[8,1024]{1,0:T(8,128)S(1)} %get-tuple-element.75.refs_3_), channel_id=1, source_target_pairs={{0,33},{33,0},{1,32},{32,1},{2,35},{35,2},{3,34},{34,3},{4,37},{37... | collective-permute-start | bytes 98312 | tf_op jit(solution)/shard_map/ppermute | solution.py:34
  122.3 4.3 %collective-permute-start.14 = (bf16[256,1024]{1,0:T(8,128)(2,1)}, bf16[256,1024]{1,0:T(8,128)(2,1)}, u32[]{:S(2)}, u32[]{:S(2)}) collective-permute-start(bf16[256,1024]{1,0:T(8,128)(2,1)} %get-tuple-element.85), channel_id=1, source_target_pairs={{0,1},{1,0},{2,3},{3,2},{4,5},{5,4},{6,7},{7,6},{8,9},{9,8},{10,11... | collective-permute-start | bytes 1572872 | tf_op jit(solution)/shard_map/ppermute | solution.py:26
  122.7 33.1 %all-to-all-start.4 = ((bf16[16,64,1024]{2,1,0:T(8,128)(2,1)}), bf16[16,64,1024]{2,1,0:T(8,128)(2,1)S(1)}, u32[]{:S(2)}, u32[]{:S(2)}) async-start(bf16[16,64,1024]{2,1,0:T(8,128)(2,1)} %get-tuple-element.86), calls=%async_computation.4 | async-start | bytes 4194304 | tf_op jit(solution)/shard_map/all_to_all | solution.py:546
  127.9 7.8 %collective-permute-start.15 = (bf16[128,1024]{1,0:T(8,128)(2,1)S(1)}, bf16[128,1024]{1,0:T(8,128)(2,1)S(1)}, u32[]{:S(2)}, u32[]{:S(2)}) collective-permute-start(bf16[128,1024]{1,0:T(8,128)(2,1)S(1)} %get-tuple-element.99), channel_id=1, source_target_pairs={{0,32},{32,0},{1,33},{33,1},{2,34},{34,2},{3,35},{35,3},{4,36},{36... | collective-permute-start | bytes 786440 | tf_op jit(solution)/shard_map/ppermute | solution.py:30
  128.5 8.6 %collective-permute-start.17 = (bf16[128,1024]{1,0:T(8,128)(2,1)S(1)}, bf16[128,1024]{1,0:T(8,128)(2,1)S(1)}, u32[]{:S(2)}, u32[]{:S(2)}) collective-permute-start(bf16[128,1024]{1,0:T(8,128)(2,1)S(1)} %get-tuple-element.100), channel_id=1, source_target_pairs={{0,96},{96,0},{32,64},{64,32},{1,97},{97,1},{33,65},{65,33},{2,98}... | collective-permute-start | bytes 786440 | tf_op jit(solution)/shard_map/ppermute | solution.py:42
  138.0 7.7 %collective-permute-start.16 = (bf16[128,1024]{1,0:T(8,128)(2,1)S(1)}, bf16[128,1024]{1,0:T(8,128)(2,1)S(1)}, u32[]{:S(2)}, u32[]{:S(2)}) collective-permute-start(bf16[128,1024]{1,0:T(8,128)(2,1)S(1)} %get-tuple-element.97), channel_id=1, source_target_pairs={{0,96},{96,0},{32,64},{64,32},{1,97},{97,1},{33,65},{65,33},{2,98}... | collective-permute-start | bytes 786440 | tf_op jit(solution)/shard_map/ppermute | solution.py:42
  140.4 18.2 %collective-permute-start.18 = (bf16[128,1024]{1,0:T(8,128)(2,1)}, bf16[128,1024]{1,0:T(8,128)(2,1)}, u32[]{:S(2)}, u32[]{:S(2)}) collective-permute-start(bf16[128,1024]{1,0:T(8,128)(2,1)} %get-tuple-element.98), channel_id=1, source_target_pairs={{0,32},{32,0},{1,33},{33,1},{2,34},{34,2},{3,35},{35,3},{4,36},{36... | collective-permute-start | bytes 786440 | tf_op jit(solution)/shard_map/ppermute | solution.py:30
  159.7 6.6 %collective-permute-start.22 = (bf16[64,1024]{1,0:T(8,128)(2,1)S(1)}, bf16[64,1024]{1,0:T(8,128)(2,1)S(1)}, u32[]{:S(2)}, u32[]{:S(2)}) collective-permute-start(bf16[64,1024]{1,0:T(8,128)(2,1)S(1)} %maximum_maximum_fusion.own), channel_id=1, source_target_pairs={{0,64},{64,0},{1,65},{65,1},{2,66},{66,2},{3,67},{67,3},{4,68},{68... | collective-permute-start | bytes 393224 | tf_op jit(solution)/shard_map/ppermute | solution.py:38
  162.5 6.9 %collective-permute-start.21 = (bf16[64,1024]{1,0:T(8,128)(2,1)S(1)}, bf16[64,1024]{1,0:T(8,128)(2,1)S(1)}, u32[]{:S(2)}, u32[]{:S(2)}) collective-permute-start(bf16[64,1024]{1,0:T(8,128)(2,1)S(1)} %maximum_maximum_fusion.own), channel_id=1, source_target_pairs={{0,96},{96,0},{32,64},{64,32},{1,97},{97,1},{33,65},{65,33},{2,98}... | collective-permute-start | bytes 393224 | tf_op jit(solution)/shard_map/ppermute | solution.py:42
  162.7 6.6 %collective-permute-start.20 = (bf16[64,1024]{1,0:T(8,128)(2,1)S(1)}, bf16[64,1024]{1,0:T(8,128)(2,1)S(1)}, u32[]{:S(2)}, u32[]{:S(2)}) collective-permute-start(bf16[64,1024]{1,0:T(8,128)(2,1)S(1)} %maximum_maximum_fusion.own), channel_id=1, source_target_pairs={{0,32},{32,0},{1,33},{33,1},{2,34},{34,2},{3,35},{35,3},{4,36},{36... | collective-permute-start | bytes 393224 | tf_op jit(solution)/shard_map/ppermute | solution.py:30
  (32 other events, 226.9 us)

commit v12 on v11

--- a/solution.py
+++ b/solution.py
@@ -54,7 +54,7 @@
 SCALARS = pl.BlockSpec(memory_space=pltpu.SMEM)
 ANYWHERE = pl.BlockSpec(memory_space=pl.ANY)
 LIMIT = pltpu.CompilerParams(vmem_limit_bytes=20 * 1024 * 1024)
-MOST = pltpu.CompilerParams(vmem_limit_bytes=60 * 1024 * 1024)
+MOST = pltpu.CompilerParams(vmem_limit_bytes=56 * 1024 * 1024)
 
 
 def shape(dims, dtype):

time: 172 us -> 172 us (level)
  no operation moved by 1% of the time
where the time goes in v12:
time: 172 us; the launch traced here: 171 us
  waiting for transfers between devices  58.5 us (34%)
  starting transfers between devices  45.8 us (27%)
  Pallas kernels  28.1 us (16%)
  other arithmetic  17.2 us (10%)
  blocking collectives  13 us (8%)
  local copies, waits for them, and re-layouts  6.14 us (4%)
    all_to_all x2, waiting for transfers between devices, gather_chips(): return lax.all_to_all(a, CHIPS, 0, 0, tiled=True)  20.3 us
    all_to_all x1, blocking collectives, gather_chips(): return lax.all_to_all(a, CHIPS, 0, 0, tiled=True)  13 us
    ppermute x10, starting transfers between devices, swap_core(): return lax.ppermute(a, 'c', [(0, 1), (1, 0)])  13 us
    all_to_all x2, starting transfers between devices, gather_chips(): return lax.all_to_all(a, CHIPS, 0, 0, tiled=True)  11.6 us
    reduce_max x1, other arithmetic, on_device(): jnp.max((short[:, :, None] == cluster_ids[None, None, :]).astype(F32), ax...  9.9 us
    pallas_call x1, Pallas kernels, backward(): pl.pallas_call(backward_kernel, out_shape=(shape((16, 64, 1024), BF16), s...  9.28 us
    all_to_all x1, waiting for transfers between devices, on_device(): got = lax.all_to_all(send, CHIPS, 0, 0, tiled=True)  9.28 us
    ppermute x3, waiting for transfers between devices, swap_wrap(): return lax.ppermute(a, ('h', 'l'), [(0, 3), (3, 0), (1, 2), (2, 1)])  9.07 us
  transfers between devices with their start and end apart: 27, of which 13 were waited for; matrix products, arithmetic and copies ran while one was open for 12% of the time, Pallas kernels for 5%

profile of v12, /device:TPU:1, one launch (start us, length us, event | category | flops | bytes accessed | tf_op | source)
XLA Modules:
  0.0 171.2 jit_solution(7059525724763878177)
XLA Ops:
  8.4 7.9 %all-to-all-start = ((bf16[16,64,1024]{2,1,0:T(8,128)(2,1)}), bf16[16,64,1024]{2,1,0:T(8,128)(2,1)}, u32[]{:S(2)}, u32[]{:S(2)}) async-start(bf16[16,64,1024]{2,1,0:T(8,128)(2,1)} %shard_map.155), calls=%async_computation | async-start | bytes 4194304 | tf_op jit(solution)/shard_map/all_to_all | solution.py:50
  17.7 9.9 %convert_reduce_fusion.live = bf16[128,128]{1,0:T(8,128)(2,1)S(1)} fusion(s32[128]{0:T(128)S(1)} %select_reduce_fusion, s32[128,400]{1,0:T(8,128)S(1)} %dynamic-slice_bitcast_fusion), kind=kLoop, calls=%fused_computation | loop fusion | flops 19644416 | bytes 238080 | tf_op jit(solution)/shard_map/reduce_max | solution.py:460
  30.7 14.8 %all-to-all-done.weights.refs_18_ = bf16[16,64,1024]{2,1,0:T(8,128)(2,1)} async-done(((bf16[16,64,1024]{2,1,0:T(8,128)(2,1)}), bf16[16,64,1024]{2,1,0:T(8,128)(2,1)}, u32[]{:S(2)}, u32[]{:S(2)}) %all-to-all-start) | async-done | bytes 2097184 | tf_op jit(solution)/shard_map/all_to_all | solution.py:50
  45.5 4.2 %shard_map.158 = (bf16[256,1024]{1,0:T(8,128)(2,1)S(1)}, f32[256,1024]{1,0:T(8,128)S(1)}, bf16[512,512]{1,0:T(8,128)(2,1)S(1)}, f32[512,512]{1,0:T(8,128)S(1)}) custom-call(bf16[256,1024]{1,0:T(8,128)(2,1)} %collective-permute-done.4.tok_a.refs_10_, bf16[256,1024]{1,0:T(8,128)(2,1)} %collective-permute-done.5.tok_b.refs_11_, ...), custom_call_target="tpu_custom_call" | custom-call | flops 1073741824 | bytes 6291456 | tf_op jit(solution)/shard_map/pallas_call | solution.py:130
  54.6 3.2 %shard_map.157 = (bf16[256,1024]{1,0:T(8,128)(2,1)S(1)}, f32[256,1024]{1,0:T(8,128)S(1)}, bf16[512,512]{1,0:T(8,128)(2,1)S(1)}, f32[512,512]{1,0:T(8,128)S(1)}) custom-call(bf16[256,1024]{1,0:T(8,128)(2,1)S(1)} %collective-permute-done.1.tok_a.refs_12_, bf16[256,1024]{1,0:T(8,128)(2,1)S(1)} %bitcast.23, bf16[16,64,1024]{2,1,0:T(8,128)(2,1)} %all-to-all-done.weights.refs_18_), custom_call_target="tpu_custom_call" | custom-call | flops 68719476736 | bytes 6291456 | tf_op jit(solution)/shard_map/pallas_call | solution.py:130
  59.3 13.0 %all_to_all.25 = f16[16,8,1024]{2,1,0:T(8,128)(2,1)S(1)} all-to-all(f16[16,8,1024]{2,1,0:T(8,128)(2,1)S(1)} %bitcast.29), channel_id=1, replica_groups=mesh['h'=2,'l'=2,'x'=4,'z'=4,'c'=2] {'x','z'}, dimensions={0} | all-to-all | bytes 524288 | tf_op jit(solution)/shard_map/all_to_all | solution.py:50
  72.3 2.8 %shard_map.159 = (bf16[256,1152]{1,0:T(8,128)(2,1)}, bf16[128,1024]{1,0:T(8,128)(2,1)}) custom-call(s32[8]{0:T(128)S(1)} %copy-done.6, bf16[256,1024]{1,0:T(8,128)(2,1)S(1)} %bitcast.24, f32[256,1024]{1,0:T(8,128)S(1)} %get-tuple-element.58.part, bf16[256,1024]{1,0:T(8,128)(2,1)S(1)} %collective-permute-done.3.from_core, ...), custom_call_target="tpu_custom_call" | custom-call | flops 4194304 | bytes 4194304 | tf_op jit(solution)/shard_map/pallas_call | solution.py:492
  75.3 3.8 %all-to-all-start.2 = ((bf16[16,8,1024]{2,1,0:T(8,128)(2,1)}), bf16[16,8,1024]{2,1,0:T(8,128)(2,1)S(1)}, u32[]{:S(2)}, u32[]{:S(2)}) async-start(bf16[16,8,1024]{2,1,0:T(8,128)(2,1)} %bitcast.9), calls=%async_computation.2 | async-start | bytes 524288 | tf_op jit(solution)/shard_map/all_to_all | solution.py:50
  79.1 1.9 %collective-permute-start.13 = (bf16[256,1152]{1,0:T(8,128)(2,1)}, bf16[256,1152]{1,0:T(8,128)(2,1)}, u32[]{:S(2)}, u32[]{:S(2)}) collective-permute-start(bf16[256,1152]{1,0:T(8,128)(2,1)} %get-tuple-element.71.refs_9_), channel_id=1, source_target_pairs={{0,1},{1,0},{2,3},{3,2},{4,5},{5,4},{6,7},{7,6},{8,9},{9,8},{10,11... | collective-permute-start | bytes 1769480 | tf_op jit(solution)/shard_map/ppermute | solution.py:26
  81.0 5.4 %all-to-all-done.2 = bf16[16,8,1024]{2,1,0:T(8,128)(2,1)S(1)} async-done(((bf16[16,8,1024]{2,1,0:T(8,128)(2,1)}), bf16[16,8,1024]{2,1,0:T(8,128)(2,1)S(1)}, u32[]{:S(2)}, u32[]{:S(2)}) %all-to-all-start.2) | async-done | bytes 262176 | tf_op jit(solution)/shard_map/all_to_all | solution.py:50
  86.4 2.3 %shard_map.160 = (bf16[128,1280]{1,0:T(8,128)(2,1)}, f32[128,512]{1,0:T(8,128)S(1)}) custom-call(bf16[128,1024]{1,0:T(8,128)(2,1)S(1)} %bitcast.17, bf16[512,1024]{1,0:T(8,128)(2,1)S(1)} %get-tuple-element.67.tiles_hi, bf16[512,1024]{1,0:T(8,128)(2,1)S(1)} %get-tuple-element.68.tiles_lo, bf16[128,128]{1,0:T(8,128)(2,1)S(1)} %convert_reduce_fusion.live), custom_call_target="tpu_custom_call" | custom-call | flops 536870912 | bytes 3145728 | tf_op jit(solution)/shard_map/pallas_call | solution.py:504
  89.4 3.0 %collective-permute-start.12 = (bf16[256,1152]{1,0:T(8,128)(2,1)}, bf16[256,1152]{1,0:T(8,128)(2,1)S(1)}, u32[]{:S(2)}, u32[]{:S(2)}) collective-permute-start(bf16[256,1152]{1,0:T(8,128)(2,1)} %collective-permute-done.8.refs_7_), channel_id=1, source_target_pairs={{0,1},{1,0},{2,3},{3,2},{4,5},{5,4},{6,7},{7,6},{8,9},{9,8},{10,11... | collective-permute-start | bytes 1769480 | tf_op jit(solution)/shard_map/ppermute | solution.py:26
  92.5 3.5 %all-to-all-start.3 = ((bf16[16,8,1280]{2,1,0:T(8,128)(2,1)}), bf16[16,8,1280]{2,1,0:T(8,128)(2,1)S(1)}, u32[]{:S(2)}, u32[]{:S(2)}) async-start(bf16[16,8,1280]{2,1,0:T(8,128)(2,1)} %bitcast.11), calls=%async_computation.3 | async-start | bytes 655360 | tf_op jit(solution)/shard_map/all_to_all | solution.py:519
  96.1 8.4 %all-to-all-done.3.got_hbm = bf16[16,8,1280]{2,1,0:T(8,128)(2,1)S(1)} async-done(((bf16[16,8,1280]{2,1,0:T(8,128)(2,1)}), bf16[16,8,1280]{2,1,0:T(8,128)(2,1)S(1)}, u32[]{:S(2)}, u32[]{:S(2)}) %all-to-all-start.3) | async-done | bytes 327712 | tf_op jit(solution)/shard_map/all_to_all | solution.py:519
  113.0 9.3 %shard_map.162 = (bf16[16,64,1024]{2,1,0:T(8,128)(2,1)}, f32[256,1024]{1,0:T(8,128)}, bf16[256,1024]{1,0:T(8,128)(2,1)}) custom-call(f32[8,1024]{1,0:T(8,128)} %copy-done.28, f32[8,1024]{1,0:T(8,128)} %copy-done.27, f32[8,1024]{1,0:T(8,128)} %copy-done.26, f32[8,1024]{1,0:T(8,128)} %copy-done.9, f32[1,1024]{1,0:T(1,128)} %bitcast.26, f32[8,128]{1,0:T(8,128)} %copy-done.10, ...), custom_call_target="tpu_custom_call" | custom-call | flops 3221225472 | bytes 10485760 | tf_op jit(solution)/shard_map/pallas_call | solution.py:331
  122.7 3.8 %all-to-all-start.4 = ((bf16[16,64,1024]{2,1,0:T(8,128)(2,1)}), bf16[16,64,1024]{2,1,0:T(8,128)(2,1)S(1)}, u32[]{:S(2)}, u32[]{:S(2)}) async-start(bf16[16,64,1024]{2,1,0:T(8,128)(2,1)} %get-tuple-element.86), calls=%async_computation.4 | async-start | bytes 4194304 | tf_op jit(solution)/shard_map/all_to_all | solution.py:546
  128.5 2.4 %collective-permute-start.17 = (bf16[128,1024]{1,0:T(8,128)(2,1)S(1)}, bf16[128,1024]{1,0:T(8,128)(2,1)S(1)}, u32[]{:S(2)}, u32[]{:S(2)}) collective-permute-start(bf16[128,1024]{1,0:T(8,128)(2,1)S(1)} %get-tuple-element.100), channel_id=1, source_target_pairs={{0,96},{96,0},{32,64},{64,32},{1,97},{97,1},{33,65},{65,33},{2,98}... | collective-permute-start | bytes 786440 | tf_op jit(solution)/shard_map/ppermute | solution.py:42
  130.9 4.8 %collective-permute-done.15 = bf16[128,1024]{1,0:T(8,128)(2,1)S(1)} collective-permute-done((bf16[128,1024]{1,0:T(8,128)(2,1)S(1)}, bf16[128,1024]{1,0:T(8,128)(2,1)S(1)}, u32[]{:S(2)}, u32[]{:S(2)}) %collective-permute-start.15) | collective-permute-done | bytes 262176 | tf_op jit(solution)/shard_map/ppermute | solution.py:30
  138.0 2.4 %collective-permute-start.16 = (bf16[128,1024]{1,0:T(8,128)(2,1)S(1)}, bf16[128,1024]{1,0:T(8,128)(2,1)S(1)}, u32[]{:S(2)}, u32[]{:S(2)}) collective-permute-start(bf16[128,1024]{1,0:T(8,128)(2,1)S(1)} %get-tuple-element.97), channel_id=1, source_target_pairs={{0,96},{96,0},{32,64},{64,32},{1,97},{97,1},{33,65},{65,33},{2,98}... | collective-permute-start | bytes 786440 | tf_op jit(solution)/shard_map/ppermute | solution.py:42
  141.1 4.7 %collective-permute-done.16 = bf16[128,1024]{1,0:T(8,128)(2,1)S(1)} collective-permute-done((bf16[128,1024]{1,0:T(8,128)(2,1)S(1)}, bf16[128,1024]{1,0:T(8,128)(2,1)S(1)}, u32[]{:S(2)}, u32[]{:S(2)}) %collective-permute-start.16) | collective-permute-done | bytes 262176 | tf_op jit(solution)/shard_map/ppermute | solution.py:42
  146.6 9.3 %all-to-all-done.4.got = bf16[16,64,1024]{2,1,0:T(8,128)(2,1)S(1)} async-done(((bf16[16,64,1024]{2,1,0:T(8,128)(2,1)}), bf16[16,64,1024]{2,1,0:T(8,128)(2,1)S(1)}, u32[]{:S(2)}, u32[]{:S(2)}) %all-to-all-start.4) | async-done | bytes 2097184 | tf_op jit(solution)/shard_map/all_to_all | solution.py:546
  159.7 2.7 %collective-permute-start.22 = (bf16[64,1024]{1,0:T(8,128)(2,1)S(1)}, bf16[64,1024]{1,0:T(8,128)(2,1)S(1)}, u32[]{:S(2)}, u32[]{:S(2)}) collective-permute-start(bf16[64,1024]{1,0:T(8,128)(2,1)S(1)} %maximum_maximum_fusion.own), channel_id=1, source_target_pairs={{0,64},{64,0},{1,65},{65,1},{2,66},{66,2},{3,67},{67,3},{4,68},{68... | collective-permute-start | bytes 393224 | tf_op jit(solution)/shard_map/ppermute | solution.py:38
  162.8 2.1 %divide_subtract_fusion = (f32[256,1024]{1,0:T(8,128)}, f32[256,1024]{1,0:T(8,128)}, f32[256,1024]{1,0:T(8,128)}) fusion(f32[256,1024]{1,0:T(8,128)S(1)} %copy-done.16, f32[128,1024]{1,0:T(8,128)S(1)} %convert_add_fusion, f32[128,1024]{1,0:T(8,128)S(1)} %copy-done.17, f32[256,1024]{1,0:T(8,128)S(1)} %copy-done.18, f32[256,1024]{1,0:T(8,128)S(1)} %copy-done.19), kind=kLoop, calls=%fused_computation.10 | loop fusion | flops 3407872 | bytes 7340032 | tf_op jit(solution)/shard_map/sub | solution.py:584
  166.4 3.0 %collective-permute-done.21.wrap = bf16[64,1024]{1,0:T(8,128)(2,1)S(1)} collective-permute-done((bf16[64,1024]{1,0:T(8,128)(2,1)S(1)}, bf16[64,1024]{1,0:T(8,128)(2,1)S(1)}, u32[]{:S(2)}, u32[]{:S(2)}) %collective-permute-start.21) | collective-permute-done | bytes 131104 | tf_op jit(solution)/shard_map/ppermute | solution.py:42
  (131 shorter events, 41.3 us)
Async XLA Ops:
  5.9 39.6 %collective-permute-start.5 = (bf16[256,1024]{1,0:T(8,128)(2,1)S(1)}, bf16[256,1024]{1,0:T(8,128)(2,1)}, u32[]{:S(2)}, u32[]{:S(2)}) collective-permute-start(bf16[256,1024]{1,0:T(8,128)(2,1)S(1)} %bitcast.20), channel_id=1, source_target_pairs={{0,32},{32,0},{1,33},{33,1},{2,34},{34,2},{3,35},{35,3},{4,36},{36... | collective-permute-start | bytes 1572872 | tf_op jit(solution)/shard_map/ppermute | solution.py:30
  7.4 38.2 %collective-permute-start.4 = (bf16[256,1024]{1,0:T(8,128)(2,1)S(1)}, bf16[256,1024]{1,0:T(8,128)(2,1)}, u32[]{:S(2)}, u32[]{:S(2)}) collective-permute-start(bf16[256,1024]{1,0:T(8,128)(2,1)S(1)} %bitcast.21), channel_id=1, source_target_pairs={{0,33},{33,0},{1,32},{32,1},{2,35},{35,2},{3,34},{34,3},{4,37},{37... | collective-permute-start | bytes 1572872 | tf_op jit(solution)/shard_map/ppermute | solution.py:34
  8.4 37.2 %all-to-all-start = ((bf16[16,64,1024]{2,1,0:T(8,128)(2,1)}), bf16[16,64,1024]{2,1,0:T(8,128)(2,1)}, u32[]{:S(2)}, u32[]{:S(2)}) async-start(bf16[16,64,1024]{2,1,0:T(8,128)(2,1)} %shard_map.155), calls=%async_computation | async-start | bytes 4194304 | tf_op jit(solution)/shard_map/all_to_all | solution.py:50
  16.4 11.1 %collective-permute-start.2 = (f32[256,1024]{1,0:T(8,128)S(1)}, f32[256,1024]{1,0:T(8,128)}, u32[]{:S(2)}, u32[]{:S(2)}) collective-permute-start(f32[256,1024]{1,0:T(8,128)S(1)} %copy-done.15), channel_id=1, source_target_pairs={{0,1},{1,0},{2,3},{3,2},{4,5},{5,4},{6,7},{7,6},{8,9},{9,8},{10,11... | collective-permute-start | bytes 3145736 | tf_op jit(solution)/shard_map/ppermute | solution.py:26
  49.8 3.2 %collective-permute-start.6 = (bf16[256,1024]{1,0:T(8,128)(2,1)S(1)}, bf16[256,1024]{1,0:T(8,128)(2,1)S(1)}, u32[]{:S(2)}, u32[]{:S(2)}) collective-permute-start(bf16[256,1024]{1,0:T(8,128)(2,1)S(1)} %get-tuple-element.61), channel_id=1, source_target_pairs={{0,1},{1,0},{2,3},{3,2},{4,5},{5,4},{6,7},{7,6},{8,9},{9,8},{10,11... | collective-permute-start | bytes 1572872 | tf_op jit(solution)/shard_map/ppermute | solution.py:26
  51.5 3.1 %collective-permute-start.1 = (bf16[256,1024]{1,0:T(8,128)(2,1)S(1)}, bf16[256,1024]{1,0:T(8,128)(2,1)S(1)}, u32[]{:S(2)}, u32[]{:S(2)}) collective-permute-start(bf16[256,1024]{1,0:T(8,128)(2,1)S(1)} %bitcast.22), channel_id=1, source_target_pairs={{0,1},{1,0},{2,3},{3,2},{4,5},{5,4},{6,7},{7,6},{8,9},{9,8},{10,11... | collective-permute-start | bytes 1572872 | tf_op jit(solution)/shard_map/ppermute | solution.py:26
  53.2 19.1 %collective-permute-start.7 = (bf16[256,1024]{1,0:T(8,128)(2,1)S(1)}, bf16[256,1024]{1,0:T(8,128)(2,1)S(1)}, u32[]{:S(2)}, u32[]{:S(2)}) collective-permute-start(bf16[256,1024]{1,0:T(8,128)(2,1)S(1)} %add_convert_fusion.1), channel_id=1, source_target_pairs={{0,32},{32,0},{1,33},{33,1},{2,34},{34,2},{3,35},{35,3},{4,36},{36... | collective-permute-start | bytes 1572872 | tf_op jit(solution)/shard_map/ppermute | solution.py:30
  58.7 13.6 %collective-permute-start.3 = (bf16[256,1024]{1,0:T(8,128)(2,1)S(1)}, bf16[256,1024]{1,0:T(8,128)(2,1)S(1)}, u32[]{:S(2)}, u32[]{:S(2)}) collective-permute-start(bf16[256,1024]{1,0:T(8,128)(2,1)S(1)} %get-tuple-element.59), channel_id=1, source_target_pairs={{0,1},{1,0},{2,3},{3,2},{4,5},{5,4},{6,7},{7,6},{8,9},{9,8},{10,11... | collective-permute-start | bytes 1572872 | tf_op jit(solution)/shard_map/ppermute | solution.py:26
  75.1 14.3 %collective-permute-start.8 = (bf16[256,1152]{1,0:T(8,128)(2,1)}, bf16[256,1152]{1,0:T(8,128)(2,1)}, u32[]{:S(2)}, u32[]{:S(2)}) collective-permute-start(bf16[256,1152]{1,0:T(8,128)(2,1)} %get-tuple-element.71.refs_9_), channel_id=1, source_target_pairs={{0,32},{32,0},{1,33},{33,1},{2,34},{34,2},{3,35},{35,3},{4,36},{36... | collective-permute-start | bytes 1769480 | tf_op jit(solution)/shard_map/ppermute | solution.py:30
  75.3 11.1 %all-to-all-start.2 = ((bf16[16,8,1024]{2,1,0:T(8,128)(2,1)}), bf16[16,8,1024]{2,1,0:T(8,128)(2,1)S(1)}, u32[]{:S(2)}, u32[]{:S(2)}) async-start(bf16[16,8,1024]{2,1,0:T(8,128)(2,1)} %bitcast.9), calls=%async_computation.2 | async-start | bytes 524288 | tf_op jit(solution)/shard_map/all_to_all | solution.py:50
  79.1 30.2 %collective-permute-start.13 = (bf16[256,1152]{1,0:T(8,128)(2,1)}, bf16[256,1152]{1,0:T(8,128)(2,1)}, u32[]{:S(2)}, u32[]{:S(2)}) collective-permute-start(bf16[256,1152]{1,0:T(8,128)(2,1)} %get-tuple-element.71.refs_9_), channel_id=1, source_target_pairs={{0,1},{1,0},{2,3},{3,2},{4,5},{5,4},{6,7},{7,6},{8,9},{9,8},{10,11... | collective-permute-start | bytes 1769480 | tf_op jit(solution)/shard_map/ppermute | solution.py:26
  89.4 22.8 %collective-permute-start.12 = (bf16[256,1152]{1,0:T(8,128)(2,1)}, bf16[256,1152]{1,0:T(8,128)(2,1)S(1)}, u32[]{:S(2)}, u32[]{:S(2)}) collective-permute-start(bf16[256,1152]{1,0:T(8,128)(2,1)} %collective-permute-done.8.refs_7_), channel_id=1, source_target_pairs={{0,1},{1,0},{2,3},{3,2},{4,5},{5,4},{6,7},{7,6},{8,9},{9,8},{10,11... | collective-permute-start | bytes 1769480 | tf_op jit(solution)/shard_map/ppermute | solution.py:26
  92.5 12.0 %all-to-all-start.3 = ((bf16[16,8,1280]{2,1,0:T(8,128)(2,1)}), bf16[16,8,1280]{2,1,0:T(8,128)(2,1)S(1)}, u32[]{:S(2)}, u32[]{:S(2)}) async-start(bf16[16,8,1280]{2,1,0:T(8,128)(2,1)} %bitcast.11), calls=%async_computation.3 | async-start | bytes 655360 | tf_op jit(solution)/shard_map/all_to_all | solution.py:519
  105.7 3.6 %collective-permute-start.11 = (f32[8,1024]{1,0:T(8,128)S(1)}, f32[8,1024]{1,0:T(8,128)S(1)}, u32[]{:S(2)}, u32[]{:S(2)}) collective-permute-start(f32[8,1024]{1,0:T(8,128)S(1)} %get-tuple-element.75.refs_3_), channel_id=1, source_target_pairs={{0,1},{1,0},{2,3},{3,2},{4,5},{5,4},{6,7},{7,6},{8,9},{9,8},{10,11... | collective-permute-start | bytes 98312 | tf_op jit(solution)/shard_map/ppermute | solution.py:26
  108.8 3.4 %collective-permute-start.9 = (f32[8,1024]{1,0:T(8,128)S(1)}, f32[8,1024]{1,0:T(8,128)S(1)}, u32[]{:S(2)}, u32[]{:S(2)}) collective-permute-start(f32[8,1024]{1,0:T(8,128)S(1)} %get-tuple-element.75.refs_3_), channel_id=1, source_target_pairs={{0,33},{33,0},{1,32},{32,1},{2,35},{35,2},{3,34},{34,3},{4,37},{37... | collective-permute-start | bytes 98312 | tf_op jit(solution)/shard_map/ppermute | solution.py:34
  122.3 4.3 %collective-permute-start.14 = (bf16[256,1024]{1,0:T(8,128)(2,1)}, bf16[256,1024]{1,0:T(8,128)(2,1)}, u32[]{:S(2)}, u32[]{:S(2)}) collective-permute-start(bf16[256,1024]{1,0:T(8,128)(2,1)} %get-tuple-element.85), channel_id=1, source_target_pairs={{0,1},{1,0},{2,3},{3,2},{4,5},{5,4},{6,7},{7,6},{8,9},{9,8},{10,11... | collective-permute-start | bytes 1572872 | tf_op jit(solution)/shard_map/ppermute | solution.py:26
  122.7 33.1 %all-to-all-start.4 = ((bf16[16,64,1024]{2,1,0:T(8,128)(2,1)}), bf16[16,64,1024]{2,1,0:T(8,128)(2,1)S(1)}, u32[]{:S(2)}, u32[]{:S(2)}) async-start(bf16[16,64,1024]{2,1,0:T(8,128)(2,1)} %get-tuple-element.86), calls=%async_computation.4 | async-start | bytes 4194304 | tf_op jit(solution)/shard_map/all_to_all | solution.py:546
  127.9 7.8 %collective-permute-start.15 = (bf16[128,1024]{1,0:T(8,128)(2,1)S(1)}, bf16[128,1024]{1,0:T(8,128)(2,1)S(1)}, u32[]{:S(2)}, u32[]{:S(2)}) collective-permute-start(bf16[128,1024]{1,0:T(8,128)(2,1)S(1)} %get-tuple-element.99), channel_id=1, source_target_pairs={{0,32},{32,0},{1,33},{33,1},{2,34},{34,2},{3,35},{35,3},{4,36},{36... | collective-permute-start | bytes 786440 | tf_op jit(solution)/shard_map/ppermute | solution.py:30
  128.5 8.6 %collective-permute-start.17 = (bf16[128,1024]{1,0:T(8,128)(2,1)S(1)}, bf16[128,1024]{1,0:T(8,128)(2,1)S(1)}, u32[]{:S(2)}, u32[]{:S(2)}) collective-permute-start(bf16[128,1024]{1,0:T(8,128)(2,1)S(1)} %get-tuple-element.100), channel_id=1, source_target_pairs={{0,96},{96,0},{32,64},{64,32},{1,97},{97,1},{33,65},{65,33},{2,98}... | collective-permute-start | bytes 786440 | tf_op jit(solution)/shard_map/ppermute | solution.py:42
  138.0 7.7 %collective-permute-start.16 = (bf16[128,1024]{1,0:T(8,128)(2,1)S(1)}, bf16[128,1024]{1,0:T(8,128)(2,1)S(1)}, u32[]{:S(2)}, u32[]{:S(2)}) collective-permute-start(bf16[128,1024]{1,0:T(8,128)(2,1)S(1)} %get-tuple-element.97), channel_id=1, source_target_pairs={{0,96},{96,0},{32,64},{64,32},{1,97},{97,1},{33,65},{65,33},{2,98}... | collective-permute-start | bytes 786440 | tf_op jit(solution)/shard_map/ppermute | solution.py:42
  140.4 18.2 %collective-permute-start.18 = (bf16[128,1024]{1,0:T(8,128)(2,1)}, bf16[128,1024]{1,0:T(8,128)(2,1)}, u32[]{:S(2)}, u32[]{:S(2)}) collective-permute-start(bf16[128,1024]{1,0:T(8,128)(2,1)} %get-tuple-element.98), channel_id=1, source_target_pairs={{0,32},{32,0},{1,33},{33,1},{2,34},{34,2},{3,35},{35,3},{4,36},{36... | collective-permute-start | bytes 786440 | tf_op jit(solution)/shard_map/ppermute | solution.py:30
  159.7 6.6 %collective-permute-start.22 = (bf16[64,1024]{1,0:T(8,128)(2,1)S(1)}, bf16[64,1024]{1,0:T(8,128)(2,1)S(1)}, u32[]{:S(2)}, u32[]{:S(2)}) collective-permute-start(bf16[64,1024]{1,0:T(8,128)(2,1)S(1)} %maximum_maximum_fusion.own), channel_id=1, source_target_pairs={{0,64},{64,0},{1,65},{65,1},{2,66},{66,2},{3,67},{67,3},{4,68},{68... | collective-permute-start | bytes 393224 | tf_op jit(solution)/shard_map/ppermute | solution.py:38
  162.5 6.9 %collective-permute-start.21 = (bf16[64,1024]{1,0:T(8,128)(2,1)S(1)}, bf16[64,1024]{1,0:T(8,128)(2,1)S(1)}, u32[]{:S(2)}, u32[]{:S(2)}) collective-permute-start(bf16[64,1024]{1,0:T(8,128)(2,1)S(1)} %maximum_maximum_fusion.own), channel_id=1, source_target_pairs={{0,96},{96,0},{32,64},{64,32},{1,97},{97,1},{33,65},{65,33},{2,98}... | collective-permute-start | bytes 393224 | tf_op jit(solution)/shard_map/ppermute | solution.py:42
  162.7 6.6 %collective-permute-start.20 = (bf16[64,1024]{1,0:T(8,128)(2,1)S(1)}, bf16[64,1024]{1,0:T(8,128)(2,1)S(1)}, u32[]{:S(2)}, u32[]{:S(2)}) collective-permute-start(bf16[64,1024]{1,0:T(8,128)(2,1)S(1)} %maximum_maximum_fusion.own), channel_id=1, source_target_pairs={{0,32},{32,0},{1,33},{33,1},{2,34},{34,2},{3,35},{35,3},{4,36},{36... | collective-permute-start | bytes 393224 | tf_op jit(solution)/shard_map/ppermute | solution.py:30
  (32 other events, 226.9 us)
